TPU v7x, 32 devices: a whole 2x2x4 slice. The times are simulated.
32 devices in a mesh: groups: 2 (over y), space: 4 (over z), tm: 2 (over x), freq: 2 (over core).
Axes of the slice: x: 2, y: 2, z: 4, core: 2. Of those that a mesh axis runs over, the one named last changes fastest.
Arguments:
- snapshots: float32 [16, 64, 16384], P(None, 'space', ('groups', 'tm')), parts along dimension 2, may hold values from -28 to 28, as said below
- weights: float32 [16384], P(('groups', 'tm', 'space')), parts along dimension 0, may hold values from 0.3 to 3
Outputs:
- modes: float32 [16, 2, 16, 16384], P('freq', None, None, ('groups', 'tm', 'space')), parts along dimension 3
- r_factor: float32 [4, 16, 16, 16], P('groups', 'freq'), parts along dimension 0
There are 2 independent parts, one for each index of `groups`. A program takes and returns all parts, laid end to end along the dimension named above; each array names one. Nothing has to cross between parts.
Inputs may be any that keep to these rules, and one draw needn't show every extreme that they name: `snapshots`: velocity fluctuations of the jet.
All inputs are finite; a program needn't handle non-finite values.
Results may differ from a plain program's by a relative error of at most 0.00009.
Values sent between devices are 32-bit elements; how exact they have to be, the bound alone decides.
No kernel may reach another device: no remote copies, remote signals or barrier semaphores. Data moves between devices by JAX's collectives and lax.ppermute only.
A program may use at most 64 MiB of HBM per device.

v0:
```python
import functools

import numpy as np
import jax
import jax.numpy as jnp
from jax import lax
from jax.experimental import pallas as pl
from jax.experimental.pallas import tpu as pltpu
from jax.sharding import PartitionSpec as P

NB = 16
SEGMENT_FRAMES = 64
NF = 16
HALF = NB // 2
STEP = 16
epsilon = 1e-05
VMEM_BYTES = 48 * 1024 * 1024


def dft_blocks(freq_count):
    times = np.arange(SEGMENT_FRAMES)
    taper = 0.5 - 0.5 * np.cos(2.0 * np.pi * times / SEGMENT_FRAMES)
    taper = taper / np.sqrt(np.sum(taper * taper))
    bins = 1 + np.arange(NF)
    angles = 2.0 * np.pi * (bins[:, None] * times[None, :] % SEGMENT_FRAMES) / SEGMENT_FRAMES
    table = np.stack([np.cos(angles) * taper, -np.sin(angles) * taper])
    local = NF // freq_count
    table = table.reshape(2, freq_count, local, SEGMENT_FRAMES // STEP, STEP)
    eye = np.eye(HALF)
    spread = np.einsum("rhfgt,bc->hrfbgct", table, eye)
    return spread.reshape(freq_count, 2 * local * HALF, SEGMENT_FRAMES * HALF).astype(np.float32)


def dot(a, b):
    return jnp.dot(a, b, precision=lax.Precision.HIGHEST, preferred_element_type=jnp.float32)


def cut_kernel(n, rows, share, x_ref, o_ref, sem):
    first = lax.axis_index("freq") * share
    copies = []
    for s in range(n):
        start = pl.multiple_of(s * rows + first, 128)
        copies.append(
            pltpu.make_async_copy(x_ref.at[:, :, pl.ds(start, share)], o_ref.at[s], sem.at[s])
        )
    for copy in copies:
        copy.start()
    for copy in copies:
        copy.wait()


def cut(snapshots, n, rows, share):
    blocks, local_times, _ = snapshots.shape
    if local_times % 8 == 0:
        return pl.pallas_call(
            functools.partial(cut_kernel, n, rows, share),
            out_shape=jax.ShapeDtypeStruct((n, blocks, local_times, share), jnp.float32),
            in_specs=[pl.BlockSpec(memory_space=pl.ANY)],
            out_specs=pl.BlockSpec(memory_space=pl.ANY),
            scratch_shapes=[pltpu.SemaphoreType.DMA((n,))],
        )(snapshots)
    shaped = snapshots.reshape(blocks, local_times, n, rows // share, share)
    own = lax.dynamic_index_in_dim(shaped, lax.axis_index("freq"), 3, keepdims=False)
    return own.transpose(2, 0, 1, 3)


def spectra_kernel(local, targets, freq_count, x_ref, t_ref, w_ref, own_ref, other_ref, gram_ref):
    share = x_ref.shape[3]
    half_rows = 2 * local * HALF
    for h, out_ref in ((0, own_ref), (1, other_ref)):
        for g in range(NB // HALF):
            data = x_ref[:, g * HALF : (g + 1) * HALF].reshape(SEGMENT_FRAMES * HALF, share)
            part = dot(t_ref[h], data)
            out_ref[:, g] = part.reshape(2 * local, HALF, share)
    width = local * NB
    line = lax.broadcasted_iota(jnp.int32, (width, width), 0) // NB
    lane = lax.broadcasted_iota(jnp.int32, (width, width), 1) // NB
    row = lax.broadcasted_iota(jnp.int32, (NB, width), 0)
    col = lax.broadcasted_iota(jnp.int32, (NB, width), 1) % NB
    packed = []
    for out_ref in (own_ref, other_ref):
        z = out_ref[...].reshape(2 * width, share)
        zw = z * w_ref[...]
        full = lax.dot_general(
            zw,
            z,
            (((1,), (1,)), ((), ())),
            precision=lax.Precision.HIGHEST,
            preferred_element_type=jnp.float32,
        )
        gram_re = full[:width, :width] + full[width:, width:]
        gram_im = full[:width, width:] - full[width:, :width]
        both = []
        for part in (gram_re, gram_im):
            kept = jnp.where(line == lane, part, 0.0)
            both.append(jnp.sum(kept.reshape(local, NB, width), axis=0))
        packed.append(jnp.where(row >= col, both[0], both[1]))
    me = lax.axis_index("freq")
    for d in range(targets):
        gram_ref[d] = jnp.where(me == d % freq_count, packed[0], packed[1])


def spectra_and_gram(pieces, tables, weights, local, targets, freq_count):
    share = pieces.shape[3]
    shape = jax.ShapeDtypeStruct((2 * local, NB // HALF, HALF, share), jnp.float32)
    return pl.pallas_call(
        functools.partial(spectra_kernel, local, targets, freq_count),
        out_shape=(
            shape,
            shape,
            jax.ShapeDtypeStruct((targets, NB, local * NB), jnp.float32),
        ),
        compiler_params=pltpu.CompilerParams(vmem_limit_bytes=VMEM_BYTES),
    )(pieces, tables, weights)


def inv_sqrt(x):
    y = lax.rsqrt(x)
    return y * (1.5 - 0.5 * x * (y * y))


def finish_kernel(local, total, gram_ref, own_ref, other_ref, modes_ref, factor_ref):
    width = local * NB
    share = own_ref.shape[3]
    gram = jnp.sum(gram_ref[...], axis=0) / total
    row = lax.broadcasted_iota(jnp.int32, (NB, width), 0)
    col = lax.broadcasted_iota(jnp.int32, (NB, width), 1) % NB
    stacked = [jnp.where(col == j, gram, 0.0) for j in range(NB)]
    for j in range(NB):
        line = jnp.broadcast_to(gram[j : j + 1, :], (NB, width))
        stacked.append(jnp.where((col == row) & (row > j), -line, 0.0))
    stacked = jnp.concatenate(stacked, axis=0)
    group_r = lax.broadcasted_iota(jnp.int32, (width, width), 0) // NB
    group_c = lax.broadcasted_iota(jnp.int32, (width, width), 1) // NB
    same = group_r == group_c
    ones = jnp.where(same, 1.0, 0.0).astype(jnp.bfloat16)
    spread = jnp.zeros(stacked.shape, jnp.float32)
    rest = stacked
    for _ in range(3):
        piece = rest.astype(jnp.bfloat16)
        rest = rest - piece.astype(jnp.float32)
        spread = spread + jnp.dot(piece, ones, preferred_element_type=jnp.float32)
    col_re = [[spread[j * NB + 8 * h : j * NB + 8 * h + 8] for h in (0, 1)] for j in range(NB)]
    base = NB * NB
    col_im = [
        [spread[base + j * NB + 8 * h : base + j * NB + 8 * h + 8] for h in (0, 1)]
        for j in range(NB)
    ]
    rows = [lax.broadcasted_iota(jnp.int32, (8, width), 0) + 8 * h for h in (0, 1)]
    lanes = lax.broadcasted_iota(jnp.int32, (8, width), 1) % NB
    inv_re = [jnp.where(rows[h] == lanes, 1.0, 0.0) for h in (0, 1)]
    inv_im = [jnp.zeros((8, width), jnp.float32) for h in (0, 1)]
    low_re = [jnp.zeros((8, width), jnp.float32) for h in (0, 1)]
    low_im = [jnp.zeros((8, width), jnp.float32) for h in (0, 1)]

    def pick(halves, i):
        return jnp.broadcast_to(halves[i // 8][i % 8 : i % 8 + 1, :], (8, width))

    for p in range(NB):
        pivot = pick(col_re[p], p) + epsilon
        scale = inv_sqrt(pivot)
        coef_re, coef_im = [None, None], [None, None]
        for h in range(p // 8, 2):
            below = rows[h] > p
            coef_re[h] = jnp.where(below, col_re[p][h] * scale, 0.0)
            coef_im[h] = jnp.where(below, col_im[p][h] * scale, 0.0)
            here = lanes == p
            diag = jnp.where(rows[h] == p, pivot * scale, coef_re[h])
            low_re[h] = jnp.where(here, diag, low_re[h])
            low_im[h] = jnp.where(here, coef_im[h], low_im[h])
        for j in range(p + 1, NB):
            a_re, a_im = pick(coef_re, j), pick(coef_im, j)
            for h in range(j // 8, 2):
                col_re[j][h] = col_re[j][h] - (coef_re[h] * a_re + coef_im[h] * a_im)
                col_im[j][h] = col_im[j][h] - (coef_im[h] * a_re - coef_re[h] * a_im)
        line_re = pick(inv_re, p) * scale
        line_im = pick(inv_im, p) * scale
        for h in range(p // 8, 2):
            at = rows[h] == p
            new_re = inv_re[h] - (coef_re[h] * line_re - coef_im[h] * line_im)
            new_im = inv_im[h] - (coef_re[h] * line_im + coef_im[h] * line_re)
            inv_re[h] = jnp.where(at, line_re, new_re)
            inv_im[h] = jnp.where(at, line_im, new_im)

    block_re = jnp.where(same, jnp.concatenate(inv_re * local, axis=0), 0.0)
    block_im = jnp.where(same, jnp.concatenate(inv_im * local, axis=0), 0.0)
    mixing = jnp.concatenate(
        [
            jnp.concatenate([block_re, block_im], axis=1),
            jnp.concatenate([-block_im, block_re], axis=1),
        ],
        axis=0,
    )
    me = lax.axis_index("freq")
    for k, ref in ((0, own_ref), (1, other_ref)):
        start = pl.multiple_of(((me + k) % 2) * share, 128)
        out = dot(mixing, ref[...].reshape(2 * width, share))
        for part in range(2):
            for f in range(local):
                at = part * width + f * NB
                modes_ref[f, part, :, pl.ds(start, share)] = out[at : at + NB]
    pad = jnp.zeros((width - NB, width), jnp.float32)
    turned_re = jnp.transpose(jnp.concatenate(low_re + [pad], axis=0))
    turned_im = jnp.transpose(jnp.concatenate(low_im + [pad], axis=0))
    for f in range(local):
        factor_ref[0, f] = turned_re[f * NB : (f + 1) * NB, :NB]
        factor_ref[1, f] = -turned_im[f * NB : (f + 1) * NB, :NB]


def finish(grams, own, other, local, total):
    share = own.shape[3]
    return pl.pallas_call(
        functools.partial(finish_kernel, local, total),
        out_shape=(
            jax.ShapeDtypeStruct((local, 2, NB, 2 * share), jnp.float32),
            jax.ShapeDtypeStruct((2, local, NB, NB), jnp.float32),
        ),
        compiler_params=pltpu.CompilerParams(vmem_limit_bytes=VMEM_BYTES),
    )(grams, own, other)


def on_device(snapshots, weights):
    n = lax.axis_size("space")
    tm_count = lax.axis_size("tm")
    freq_count = lax.axis_size("freq")
    local = NF // freq_count
    blocks, local_times, columns = snapshots.shape
    rows = columns // n
    share = rows // freq_count
    me = lax.axis_index("freq")

    tables = jnp.asarray(dft_blocks(freq_count))
    tables = jnp.where(me == 0, tables, tables[::-1])
    own_weights = lax.dynamic_index_in_dim(weights.reshape(freq_count, 1, share), me, 0, False)

    sent = cut(snapshots, n, rows, share)
    pieces = lax.all_to_all(sent, "space", split_axis=0, concat_axis=0, tiled=True)
    if local_times != STEP:
        pieces = pieces.transpose(1, 0, 2, 3).reshape(blocks, SEGMENT_FRAMES // STEP, STEP, share)
        pieces = pieces.transpose(1, 0, 2, 3)

    targets = n * tm_count * freq_count
    own, other, gram = spectra_and_gram(pieces, tables, own_weights, local, targets, freq_count)
    swap = [(i, freq_count - 1 - i) for i in range(freq_count)]
    other = lax.ppermute(other, "freq", swap)
    grams = lax.all_to_all(gram, ("space", "tm", "freq"), split_axis=0, concat_axis=0, tiled=True)
    total = rows * n * tm_count
    return finish(grams, own, other, local, total)


def solution(mesh):
    return jax.shard_map(
        on_device,
        mesh=mesh,
        in_specs=(P(None, "space", ("groups", "tm")), P(("groups", "tm", "space"))),
        out_specs=(
            P("freq", None, None, ("groups", "tm", "space")),
            P("groups", "freq", None, None),
        ),
        check_vma=False,
    )
```

profile of v0, /device:TPU:0, one launch (start us, length us, event | category | flops | bytes accessed | tf_op | source)
XLA Modules:
  0.0 137.6 jit_solution(14766619896580891045)
XLA Ops:
  0.6 0.0 copy-start
  0.6 64.7 %shard_map.50 = f32[4,16,16,512]{3,2,1,0:T(8,128)} custom-call(f32[16,16,4096]{2,1,0:T(8,128)} %x_ref.1), custom_call_target="tpu_custom_call" | custom-call | tf_op jit(solution)/shard_map/pallas_call | solution.py:55
  65.3 0.0 copy-start.1
  65.3 6.5 %all-to-all-start = ((f32[4,16,16,512]{3,2,1,0:T(8,128)}), f32[4,16,16,512]{3,2,1,0:T(8,128)S(1)}, u32[]{:S(2)}, u32[]{:S(2)}) async-start(f32[4,16,16,512]{3,2,1,0:T(8,128)} %shard_map.50), calls=%async_computation | async-start | bytes 4194304 | tf_op jit(solution)/shard_map/all_to_all | solution.py:237
  71.8 0.0 copy-done
  71.8 0.0 copy-done.1
  71.8 0.1 broadcast_select_fusion.t_ref
  71.9 48.1 %all-to-all-done.x_ref = f32[4,16,16,512]{3,2,1,0:T(8,128)S(1)} async-done(((f32[4,16,16,512]{3,2,1,0:T(8,128)}), f32[4,16,16,512]{3,2,1,0:T(8,128)S(1)}, u32[]{:S(2)}, u32[]{:S(2)}) %all-to-all-start) | async-done | bytes 2097184 | tf_op jit(solution)/shard_map/all_to_all | solution.py:237
  120.0 3.3 %shard_map.51 = (f32[16,2,8,512]{3,2,1,0:T(8,128)S(1)}, f32[16,2,8,512]{3,2,1,0:T(8,128)S(1)}, f32[16,16,128]{2,1,0:T(8,128)S(1)}) custom-call(f32[4,16,16,512]{3,2,1,0:T(8,128)S(1)} %all-to-all-done.x_ref, f32[2,128,512]{2,1,0:T(8,128)S(1)} %broadcast_select_fusion.t_ref, f32[1,512]{1,0:T(1,128)S(1)} %dynamic-slice_bitcast_fusion.w_ref), custom_call_target="tpu_custom_call" | custom-call | tf_op jit(solution)/shard_map/pallas_call | solution.py:106
  123.3 0.1 collective-permute-start
  123.4 11.6 %all_to_all.10.gram_ref = f32[16,16,128]{2,1,0:T(8,128)S(1)} all-to-all(f32[16,16,128]{2,1,0:T(8,128)S(1)} %get-tuple-element.5), channel_id=1, replica_groups=mesh['groups'=2,'space'=4,'tm'=2,'freq'=2] {'space','tm','freq'}, dimensions={0} | all-to-all | bytes 262144 | tf_op jit(solution)/shard_map/all_to_all | solution.py:246
  135.0 0.0 collective-permute-done.other_ref
  135.0 2.6 %shard_map.52 = (f32[8,2,16,1024]{3,2,1,0:T(8,128)}, f32[2,8,16,16]{3,2,1,0:T(8,128)}) custom-call(f32[16,16,128]{2,1,0:T(8,128)S(1)} %all_to_all.10.gram_ref, f32[16,2,8,512]{3,2,1,0:T(8,128)S(1)} %get-tuple-element.6.own_ref, f32[16,2,8,512]{3,2,1,0:T(8,128)S(1)} %collective-permute-done.other_ref), custom_call_target="tpu_custom_call" | custom-call | tf_op jit(solution)/shard_map/pallas_call | solution.py:212
  (1 shorter events, 0.0 us)
Async XLA Ops:
  0.6 71.2 %copy-start = (f32[1024]{0:T(1024)S(1)}, f32[1024]{0:T(1024)}, u32[]{:S(2)}) copy-start(f32[1024]{0:T(1024)} %param.4) | copy-start | bytes 12292
  65.3 6.5 %copy-start.1 = (f32[2,128,512]{2,1,0:T(8,128)S(1)}, f32[2,128,512]{2,1,0:T(8,128)}, u32[]{:S(2)}) copy-start(f32[2,128,512]{2,1,0:T(8,128)} %constant.13.clone) | copy-start | bytes 1572868
  65.3 54.7 %all-to-all-start = ((f32[4,16,16,512]{3,2,1,0:T(8,128)}), f32[4,16,16,512]{3,2,1,0:T(8,128)S(1)}, u32[]{:S(2)}, u32[]{:S(2)}) async-start(f32[4,16,16,512]{3,2,1,0:T(8,128)} %shard_map.50), calls=%async_computation | async-start | bytes 4194304 | tf_op jit(solution)/shard_map/all_to_all | solution.py:237
  123.3 11.7 %collective-permute-start = (f32[16,2,8,512]{3,2,1,0:T(8,128)S(1)}, f32[16,2,8,512]{3,2,1,0:T(8,128)S(1)}, u32[]{:S(2)}, u32[]{:S(2)}) collective-permute-start(f32[16,2,8,512]{3,2,1,0:T(8,128)S(1)} %get-tuple-element.7), channel_id=1, source_target_pairs={{0,1},{1,0},{2,3},{3,2},{4,5},{5,4},{6,7},{7,6},{8,9},{9,8},{10,11... | collective-permute-start | bytes 1572872 | tf_op jit(solution)/shard_map/ppermute | solution.py:245
where the time goes:
time: 138 us
  Pallas kernels  70.6 us (51%)
  waiting for transfers between devices  48.1 us (35%)
  blocking collectives  11.6 us (8%)
  starting transfers between devices  6.53 us (5%)
    pallas_call x1, Pallas kernels, cut(): pl.pallas_call(functools.partial(cut_kernel, n, rows, share), out_shape=j...  64.7 us
    all_to_all x1, waiting for transfers between devices, on_device(): lax.all_to_all(sent, 'space', split_axis=0, concat_axis=0, tiled=True)  48.1 us
    all_to_all x1, blocking collectives, on_device(): lax.all_to_all(gram, ('space', 'tm', 'freq'), split_axis=0, concat_axis=0...  11.6 us
    all_to_all x1, starting transfers between devices, on_device(): lax.all_to_all(sent, 'space', split_axis=0, concat_axis=0, tiled=True)  6.46 us
    pallas_call x1, Pallas kernels, spectra_and_gram(): pl.pallas_call(functools.partial(spectra_kernel, local, targets, freq_cou...  3.32 us
  transfers between devices with their start and end apart: 2, of which 1 were waited for; matrix products, arithmetic and copies ran while one was open for 0% of the time, Pallas kernels for 0%

commit v1 on v0

--- a/solution.py
+++ b/solution.py
@@ -11,37 +11,39 @@
 NB = 16
 SEGMENT_FRAMES = 64
 NF = 16
-HALF = NB // 2
-STEP = 16
+CUTS = 4
 epsilon = 1e-05
 VMEM_BYTES = 48 * 1024 * 1024
 
 
-def dft_blocks(freq_count):
+def dft_blocks(groups):
     times = np.arange(SEGMENT_FRAMES)
     taper = 0.5 - 0.5 * np.cos(2.0 * np.pi * times / SEGMENT_FRAMES)
     taper = taper / np.sqrt(np.sum(taper * taper))
     bins = 1 + np.arange(NF)
     angles = 2.0 * np.pi * (bins[:, None] * times[None, :] % SEGMENT_FRAMES) / SEGMENT_FRAMES
     table = np.stack([np.cos(angles) * taper, -np.sin(angles) * taper])
-    local = NF // freq_count
-    table = table.reshape(2, freq_count, local, SEGMENT_FRAMES // STEP, STEP)
-    eye = np.eye(HALF)
-    spread = np.einsum("rhfgt,bc->hrfbgct", table, eye)
-    return spread.reshape(freq_count, 2 * local * HALF, SEGMENT_FRAMES * HALF).astype(np.float32)
+    step = SEGMENT_FRAMES // groups
+    table = table.reshape(2, 2, NF // 2, groups, step)
+    spread = np.einsum("rhfgt,bc->ghrfbct", table, np.eye(NB))
+    return spread.reshape(groups, 2 * NF * NB, NB * step).astype(np.float32)
 
 
 def dot(a, b):
     return jnp.dot(a, b, precision=lax.Precision.HIGHEST, preferred_element_type=jnp.float32)
 
 
-def cut_kernel(n, rows, share, x_ref, o_ref, sem):
-    first = lax.axis_index("freq") * share
+def cut_kernel(n, k, rows, share, x_ref, o_ref, sem):
+    to = lax.rem(lax.axis_index("space") + k, n)
+    start = pl.multiple_of(to * rows + lax.axis_index("freq") * share, 128)
+    part = NB // CUTS
     copies = []
-    for s in range(n):
-        start = pl.multiple_of(s * rows + first, 128)
+    for i in range(CUTS):
+        blocks = pl.ds(i * part, part)
         copies.append(
-            pltpu.make_async_copy(x_ref.at[:, :, pl.ds(start, share)], o_ref.at[s], sem.at[s])
+            pltpu.make_async_copy(
+                x_ref.at[blocks, :, pl.ds(start, share)], o_ref.at[blocks], sem.at[i]
+            )
         )
     for copy in copies:
         copy.start()
@@ -49,40 +51,60 @@
         copy.wait()
 
 
-def cut(snapshots, n, rows, share):
+def cut(snapshots, n, k, rows, share):
     blocks, local_times, _ = snapshots.shape
     if local_times % 8 == 0:
-        return pl.pallas_call(
-            functools.partial(cut_kernel, n, rows, share),
-            out_shape=jax.ShapeDtypeStruct((n, blocks, local_times, share), jnp.float32),
+        piece = pl.pallas_call(
+            functools.partial(cut_kernel, n, k, rows, share),
+            out_shape=jax.ShapeDtypeStruct((blocks, local_times, share), jnp.float32),
             in_specs=[pl.BlockSpec(memory_space=pl.ANY)],
-            out_specs=pl.BlockSpec(memory_space=pl.ANY),
-            scratch_shapes=[pltpu.SemaphoreType.DMA((n,))],
+            out_specs=pl.BlockSpec(memory_space=pltpu.VMEM),
+            scratch_shapes=[pltpu.SemaphoreType.DMA((CUTS,))],
         )(snapshots)
-    shaped = snapshots.reshape(blocks, local_times, n, rows // share, share)
-    own = lax.dynamic_index_in_dim(shaped, lax.axis_index("freq"), 3, keepdims=False)
-    return own.transpose(2, 0, 1, 3)
-
-
-def spectra_kernel(local, targets, freq_count, x_ref, t_ref, w_ref, own_ref, other_ref, gram_ref):
-    share = x_ref.shape[3]
-    half_rows = 2 * local * HALF
-    for h, out_ref in ((0, own_ref), (1, other_ref)):
-        for g in range(NB // HALF):
-            data = x_ref[:, g * HALF : (g + 1) * HALF].reshape(SEGMENT_FRAMES * HALF, share)
-            part = dot(t_ref[h], data)
-            out_ref[:, g] = part.reshape(2 * local, HALF, share)
-    width = local * NB
+    else:
+        to = lax.rem(lax.axis_index("space") + k, n)
+        start = to * rows + lax.axis_index("freq") * share
+        piece = lax.dynamic_slice_in_dim(snapshots, start, share, axis=2)
+    return piece.reshape(blocks * local_times, share)
+
+
+def early_kernel(n, offsets, t_ref, *refs):
+    out_ref = refs[-1]
+    me = lax.axis_index("space")
+    total = None
+    for k, ref in zip(offsets, refs):
+        part = dot(t_ref[lax.rem(me - k + n, n)], ref[...])
+        total = part if total is None else total + part
+    out_ref[...] = total
+
+
+def early(tables, n, offsets, pieces):
+    share = pieces[0].shape[1]
+    return pl.pallas_call(
+        functools.partial(early_kernel, n, offsets),
+        out_shape=jax.ShapeDtypeStruct((tables.shape[1], share), jnp.float32),
+        compiler_params=pltpu.CompilerParams(vmem_limit_bytes=VMEM_BYTES),
+    )(tables, *pieces)
+
+
+def late_kernel(n, k, targets, t_ref, sum_ref, x_ref, w_ref, own_ref, other_ref, gram_ref):
+    src = lax.rem(lax.axis_index("space") - k + n, n)
+    spectra = sum_ref[...] + dot(t_ref[src], x_ref[...])
+    half = spectra.shape[0] // 2
+    width = half // 2
+    local = width // NB
     line = lax.broadcasted_iota(jnp.int32, (width, width), 0) // NB
     lane = lax.broadcasted_iota(jnp.int32, (width, width), 1) // NB
     row = lax.broadcasted_iota(jnp.int32, (NB, width), 0)
     col = lax.broadcasted_iota(jnp.int32, (NB, width), 1) % NB
+    first = lax.axis_index("freq") == 0
+    halves = [spectra[:half], spectra[half:]]
+    own_ref[...] = jnp.where(first, halves[0], halves[1])
+    other_ref[...] = jnp.where(first, halves[1], halves[0])
     packed = []
-    for out_ref in (own_ref, other_ref):
-        z = out_ref[...].reshape(2 * width, share)
-        zw = z * w_ref[...]
+    for z in halves:
         full = lax.dot_general(
-            zw,
+            z * w_ref[...],
             z,
             (((1,), (1,)), ((), ())),
             precision=lax.Precision.HIGHEST,
@@ -95,23 +117,23 @@
             kept = jnp.where(line == lane, part, 0.0)
             both.append(jnp.sum(kept.reshape(local, NB, width), axis=0))
         packed.append(jnp.where(row >= col, both[0], both[1]))
-    me = lax.axis_index("freq")
     for d in range(targets):
-        gram_ref[d] = jnp.where(me == d % freq_count, packed[0], packed[1])
-
-
-def spectra_and_gram(pieces, tables, weights, local, targets, freq_count):
-    share = pieces.shape[3]
-    shape = jax.ShapeDtypeStruct((2 * local, NB // HALF, HALF, share), jnp.float32)
+        gram_ref[d] = packed[d % 2]
+
+
+def late(tables, n, k, partial_sum, piece, weights, targets):
+    share = piece.shape[1]
+    half = tables.shape[1] // 2
+    shape = jax.ShapeDtypeStruct((half, share), jnp.float32)
     return pl.pallas_call(
-        functools.partial(spectra_kernel, local, targets, freq_count),
+        functools.partial(late_kernel, n, k, targets),
         out_shape=(
             shape,
             shape,
-            jax.ShapeDtypeStruct((targets, NB, local * NB), jnp.float32),
+            jax.ShapeDtypeStruct((targets, NB, half // 2), jnp.float32),
         ),
         compiler_params=pltpu.CompilerParams(vmem_limit_bytes=VMEM_BYTES),
-    )(pieces, tables, weights)
+    )(tables, partial_sum, piece, weights)
 
 
 def inv_sqrt(x):
@@ -121,7 +143,7 @@
 
 def finish_kernel(local, total, gram_ref, own_ref, other_ref, modes_ref, factor_ref):
     width = local * NB
-    share = own_ref.shape[3]
+    share = own_ref.shape[1]
     gram = jnp.sum(gram_ref[...], axis=0) / total
     row = lax.broadcasted_iota(jnp.int32, (NB, width), 0)
     col = lax.broadcasted_iota(jnp.int32, (NB, width), 1) % NB
@@ -194,7 +216,7 @@
     me = lax.axis_index("freq")
     for k, ref in ((0, own_ref), (1, other_ref)):
         start = pl.multiple_of(((me + k) % 2) * share, 128)
-        out = dot(mixing, ref[...].reshape(2 * width, share))
+        out = dot(mixing, ref[...])
         for part in range(2):
             for f in range(local):
                 at = part * width + f * NB
@@ -208,7 +230,7 @@
 
 
 def finish(grams, own, other, local, total):
-    share = own.shape[3]
+    share = own.shape[1]
     return pl.pallas_call(
         functools.partial(finish_kernel, local, total),
         out_shape=(
@@ -229,20 +251,21 @@
     share = rows // freq_count
     me = lax.axis_index("freq")
 
-    tables = jnp.asarray(dft_blocks(freq_count))
-    tables = jnp.where(me == 0, tables, tables[::-1])
+    tables = jnp.asarray(dft_blocks(n))
     own_weights = lax.dynamic_index_in_dim(weights.reshape(freq_count, 1, share), me, 0, False)
 
-    sent = cut(snapshots, n, rows, share)
-    pieces = lax.all_to_all(sent, "space", split_axis=0, concat_axis=0, tiled=True)
-    if local_times != STEP:
-        pieces = pieces.transpose(1, 0, 2, 3).reshape(blocks, SEGMENT_FRAMES // STEP, STEP, share)
-        pieces = pieces.transpose(1, 0, 2, 3)
+    order = [n // 2] + [k for k in range(1, n) if k != n // 2]
+    pieces = []
+    for k in order:
+        sent = cut(snapshots, n, k, rows, share)
+        pieces.append(lax.ppermute(sent, "space", [(i, (i + k) % n) for i in range(n)]))
+    pieces = [cut(snapshots, n, 0, rows, share)] + pieces
+    order = [0] + order
 
     targets = n * tm_count * freq_count
-    own, other, gram = spectra_and_gram(pieces, tables, own_weights, local, targets, freq_count)
-    swap = [(i, freq_count - 1 - i) for i in range(freq_count)]
-    other = lax.ppermute(other, "freq", swap)
+    before = early(tables, n, order[:-1], pieces[:-1])
+    own, other, gram = late(tables, n, order[-1], before, pieces[-1], own_weights, targets)
+    other = lax.ppermute(other, "freq", [(0, 1), (1, 0)])
     grams = lax.all_to_all(gram, ("space", "tm", "freq"), split_axis=0, concat_axis=0, tiled=True)
     total = rows * n * tm_count
     return finish(grams, own, other, local, total)

time: 138 us -> 75.3 us (0.55)
  Pallas kernels: 70.6 us -> 16.1 us
  waiting for transfers between devices: 48.1 us -> 25.7 us
  blocking collectives: 11.6 us -> 23.3 us
  starting transfers between devices: 6.53 us -> 8.1 us
    pallas_call x2 -> x6, Pallas kernels: 68 us -> 13.5 us  [the longest x4 7.69 us: cut(): pl.pallas_call(functools.partial(cut_kernel, n, k, rows, share), out_shap...]
    all_to_all x1 -> x0, waiting for transfers between devices: 48.1 us -> none  [on_device(): lax.all_to_all(sent, 'space', split_axis=0, concat_axis=0, tiled=True)]
    ppermute x1 -> x4, waiting for transfers between devices: 0.01 us -> 25.7 us  [the longest x3 25.7 us: on_device(): lax.ppermute(sent, 'space', [(i, (i + k) % n) for i in range(n)])]
    all_to_all x1, blocking collectives: 11.6 us -> 23.3 us  [on_device(): lax.all_to_all(gram, ('space', 'tm', 'freq'), split_axis=0, concat_axis=0...]
    ppermute x1 -> x4, starting transfers between devices: 0.07 us -> 8.1 us  [the longest x3 8.03 us: on_device(): lax.ppermute(sent, 'space', [(i, (i + k) % n) for i in range(n)])]
    all_to_all x1 -> x0, starting transfers between devices: 6.46 us -> none  [on_device(): lax.all_to_all(sent, 'space', split_axis=0, concat_axis=0, tiled=True)]
  transfers between devices with their start and end apart: 2 -> 4, of which waited for: 1 -> 1; matrix products, arithmetic and copies ran while one was open for 0% -> 0% of each run, Pallas kernels for 0% -> 13%
where the time goes in v1:
time: 75.3 us; the launch traced here: 75 us
  waiting for transfers between devices  25.7 us (34%)
  blocking collectives  23.3 us (31%)
  Pallas kernels  16.1 us (21%)
  starting transfers between devices  8.1 us (11%)
  local copies, waits for them, and re-layouts  1.06 us (1%)
    ppermute x3, waiting for transfers between devices, on_device(): lax.ppermute(sent, 'space', [(i, (i + k) % n) for i in range(n)])  25.7 us
    all_to_all x1, blocking collectives, on_device(): lax.all_to_all(gram, ('space', 'tm', 'freq'), split_axis=0, concat_axis=0...  23.3 us
    ppermute x3, starting transfers between devices, on_device(): lax.ppermute(sent, 'space', [(i, (i + k) % n) for i in range(n)])  8.03 us
    pallas_call x4, Pallas kernels, cut(): pl.pallas_call(functools.partial(cut_kernel, n, k, rows, share), out_shap...  7.69 us
    pallas_call x1, Pallas kernels, early(): pl.pallas_call(functools.partial(early_kernel, n, offsets), out_shape=jax...  3.7 us
    pallas_call x1, Pallas kernels, finish(): pl.pallas_call(functools.partial(finish_kernel, local, total), out_shape=...  2.56 us
    pallas_call x1, Pallas kernels, late(): pl.pallas_call(functools.partial(late_kernel, n, k, targets), out_shape=(...  2.11 us
  transfers between devices with their start and end apart: 4, of which 1 were waited for; matrix products, arithmetic and copies ran while one was open for 0% of the time, Pallas kernels for 13%

profile of v1, /device:TPU:0, one launch (start us, length us, event | category | flops | bytes accessed | tf_op | source)
XLA Modules:
  0.0 75.0 jit_solution(7315509521982120894)
XLA Ops:
  0.6 0.0 copy-start
  0.6 1.9 %shard_map.51 = f32[16,16,512]{2,1,0:T(8,128)} custom-call(f32[16,16,4096]{2,1,0:T(8,128)} %x_ref.7), custom_call_target="tpu_custom_call" | custom-call | tf_op jit(solution)/shard_map/pallas_call | solution.py:57
  2.6 4.1 %collective-permute-start = (f32[256,512]{1,0:T(8,128)}, f32[256,512]{1,0:T(8,128)S(1)}, u32[]{:S(2)}, u32[]{:S(2)}) collective-permute-start(f32[256,512]{1,0:T(8,128)} %bitcast.10), channel_id=1, source_target_pairs={{0,8},{4,12},{8,0},{12,4},{1,9},{5,13},{9,1},{13,5},{2,10},{6,14},... | collective-permute-start | bytes 1572872 | tf_op jit(solution)/shard_map/ppermute | solution.py:261
  6.7 1.9 %shard_map.52 = f32[16,16,512]{2,1,0:T(8,128)} custom-call(f32[16,16,4096]{2,1,0:T(8,128)} %x_ref.7), custom_call_target="tpu_custom_call" | custom-call | tf_op jit(solution)/shard_map/pallas_call | solution.py:57
  8.6 0.0 copy-start.1
  8.6 1.6 %collective-permute-start.1 = (f32[256,512]{1,0:T(8,128)}, f32[256,512]{1,0:T(8,128)}, u32[]{:S(2)}, u32[]{:S(2)}) collective-permute-start(f32[256,512]{1,0:T(8,128)} %bitcast.11), channel_id=1, source_target_pairs={{0,4},{4,8},{8,12},{12,0},{1,5},{5,9},{9,13},{13,1},{2,6},{6,10},{... | collective-permute-start | bytes 1572872 | tf_op jit(solution)/shard_map/ppermute | solution.py:261
  10.3 1.9 %shard_map.54 = f32[16,16,512]{2,1,0:T(8,128)} custom-call(f32[16,16,4096]{2,1,0:T(8,128)} %x_ref.7), custom_call_target="tpu_custom_call" | custom-call | tf_op jit(solution)/shard_map/pallas_call | solution.py:57
  12.2 2.3 %collective-permute-start.2 = (f32[256,512]{1,0:T(8,128)}, f32[256,512]{1,0:T(8,128)S(1)}, u32[]{:S(2)}, u32[]{:S(2)}) collective-permute-start(f32[256,512]{1,0:T(8,128)} %bitcast.9), channel_id=1, source_target_pairs={{0,12},{4,0},{8,4},{12,8},{1,13},{5,1},{9,5},{13,9},{2,14},{6,2},{... | collective-permute-start | bytes 1572872 | tf_op jit(solution)/shard_map/ppermute | solution.py:261
  14.5 1.9 %shard_map.50 = f32[16,16,512]{2,1,0:T(8,128)} custom-call(f32[16,16,4096]{2,1,0:T(8,128)} %x_ref.7), custom_call_target="tpu_custom_call" | custom-call | tf_op jit(solution)/shard_map/pallas_call | solution.py:57
  16.4 0.0 copy-done
  16.4 25.7 %collective-permute-done.refs_1_ = f32[256,512]{1,0:T(8,128)S(1)} collective-permute-done((f32[256,512]{1,0:T(8,128)}, f32[256,512]{1,0:T(8,128)S(1)}, u32[]{:S(2)}, u32[]{:S(2)}) %collective-permute-start) | collective-permute-done | bytes 524320 | tf_op jit(solution)/shard_map/ppermute | solution.py:261
  42.2 0.0 collective-permute-done.1.refs_2_
  42.2 0.0 copy-done.1
  42.2 0.0 copy-start.2
  42.2 1.0 %copy-done.2 = f32[16,16,512]{2,1,0:T(8,128)S(1)} copy-done((f32[16,16,512]{2,1,0:T(8,128)S(1)}, f32[16,16,512]{2,1,0:T(8,128)}, u32[]{:S(2)}) %copy-start.2) | copy-done | bytes 524312
  43.2 3.7 %shard_map.53.sum_ref = f32[512,512]{1,0:T(8,128)S(1)} custom-call(f32[4,512,256]{2,1,0:T(8,128)S(1)} %copy-done.1, f32[256,512]{1,0:T(8,128)S(1)} %bitcast.8, f32[256,512]{1,0:T(8,128)S(1)} %collective-permute-done.refs_1_, f32[256,512]{1,0:T(8,128)} %collective-permute-done.1.refs_2_), custom_call_target="tpu_custom_call" | custom-call | tf_op jit(solution)/shard_map/pallas_call | solution.py:83
  46.9 0.0 collective-permute-done.2.x_ref
  46.9 2.1 %shard_map.55 = (f32[256,512]{1,0:T(8,128)S(1)}, f32[256,512]{1,0:T(8,128)S(1)}, f32[16,16,128]{2,1,0:T(8,128)S(1)}) custom-call(f32[4,512,256]{2,1,0:T(8,128)S(1)} %copy-done.1, f32[512,512]{1,0:T(8,128)S(1)} %shard_map.53.sum_ref, f32[256,512]{1,0:T(8,128)S(1)} %collective-permute-done.2.x_ref, f32[1,512]{1,0:T(1,128)S(1)} %dynamic-slice_bitcast_fusion.w_ref), custom_call_target="tpu_custom_call" | custom-call | tf_op jit(solution)/shard_map/pallas_call | solution.py:128
  49.1 0.1 collective-permute-start.3
  49.1 23.3 %all_to_all.5.gram_ref = f32[16,16,128]{2,1,0:T(8,128)S(1)} all-to-all(f32[16,16,128]{2,1,0:T(8,128)S(1)} %get-tuple-element.5), channel_id=1, replica_groups=mesh['groups'=2,'space'=4,'tm'=2,'freq'=2] {'space','tm','freq'}, dimensions={0} | all-to-all | bytes 262144 | tf_op jit(solution)/shard_map/all_to_all | solution.py:269
  72.4 0.0 collective-permute-done.3.other_ref
  72.4 2.6 %shard_map.56 = (f32[8,2,16,1024]{3,2,1,0:T(8,128)}, f32[2,8,16,16]{3,2,1,0:T(8,128)}) custom-call(f32[16,16,128]{2,1,0:T(8,128)S(1)} %all_to_all.5.gram_ref, f32[256,512]{1,0:T(8,128)S(1)} %get-tuple-element.6.own_ref, f32[256,512]{1,0:T(8,128)S(1)} %collective-permute-done.3.other_ref), custom_call_target="tpu_custom_call" | custom-call | tf_op jit(solution)/shard_map/pallas_call | solution.py:234
  (1 shorter events, 0.0 us)
Async XLA Ops:
  0.6 15.8 %copy-start = (f32[1024]{0:T(1024)S(1)}, f32[1024]{0:T(1024)}, u32[]{:S(2)}) copy-start(f32[1024]{0:T(1024)} %param.4) | copy-start | bytes 12292
  2.6 39.6 %collective-permute-start = (f32[256,512]{1,0:T(8,128)}, f32[256,512]{1,0:T(8,128)S(1)}, u32[]{:S(2)}, u32[]{:S(2)}) collective-permute-start(f32[256,512]{1,0:T(8,128)} %bitcast.10), channel_id=1, source_target_pairs={{0,8},{4,12},{8,0},{12,4},{1,9},{5,13},{9,1},{13,5},{2,10},{6,14},... | collective-permute-start | bytes 1572872 | tf_op jit(solution)/shard_map/ppermute | solution.py:261
  8.6 33.6 %copy-start.1 = (f32[4,512,256]{2,1,0:T(8,128)S(1)}, f32[4,512,256]{2,1,0:T(8,128)}, u32[]{:S(2)}) copy-start(f32[4,512,256]{2,1,0:T(8,128)} %constant.12.clone.t_ref) | copy-start | bytes 6291460
  8.6 33.5 %collective-permute-start.1 = (f32[256,512]{1,0:T(8,128)}, f32[256,512]{1,0:T(8,128)}, u32[]{:S(2)}, u32[]{:S(2)}) collective-permute-start(f32[256,512]{1,0:T(8,128)} %bitcast.11), channel_id=1, source_target_pairs={{0,4},{4,8},{8,12},{12,0},{1,5},{5,9},{9,13},{13,1},{2,6},{6,10},{... | collective-permute-start | bytes 1572872 | tf_op jit(solution)/shard_map/ppermute | solution.py:261
  12.2 34.7 %collective-permute-start.2 = (f32[256,512]{1,0:T(8,128)}, f32[256,512]{1,0:T(8,128)S(1)}, u32[]{:S(2)}, u32[]{:S(2)}) collective-permute-start(f32[256,512]{1,0:T(8,128)} %bitcast.9), channel_id=1, source_target_pairs={{0,12},{4,0},{8,4},{12,8},{1,13},{5,1},{9,5},{13,9},{2,14},{6,2},{... | collective-permute-start | bytes 1572872 | tf_op jit(solution)/shard_map/ppermute | solution.py:261
  42.2 1.0 %copy-start.2 = (f32[16,16,512]{2,1,0:T(8,128)S(1)}, f32[16,16,512]{2,1,0:T(8,128)}, u32[]{:S(2)}) copy-start(f32[16,16,512]{2,1,0:T(8,128)} %shard_map.50) | copy-start | bytes 1572868
  49.1 23.4 %collective-permute-start.3 = (f32[256,512]{1,0:T(8,128)S(1)}, f32[256,512]{1,0:T(8,128)S(1)}, u32[]{:S(2)}, u32[]{:S(2)}) collective-permute-start(f32[256,512]{1,0:T(8,128)S(1)} %get-tuple-element.7), channel_id=1, source_target_pairs={{0,1},{1,0},{2,3},{3,2},{4,5},{5,4},{6,7},{7,6},{8,9},{9,8},{10,11... | collective-permute-start | bytes 1572872 | tf_op jit(solution)/shard_map/ppermute | solution.py:268

commit v2 on v1

--- a/solution.py
+++ b/solution.py
@@ -11,7 +11,7 @@
 NB = 16
 SEGMENT_FRAMES = 64
 NF = 16
-CUTS = 4
+CUTS = 16
 epsilon = 1e-05
 VMEM_BYTES = 48 * 1024 * 1024
 
@@ -68,23 +68,19 @@
     return piece.reshape(blocks * local_times, share)
 
 
-def early_kernel(n, offsets, t_ref, *refs):
-    out_ref = refs[-1]
-    me = lax.axis_index("space")
-    total = None
-    for k, ref in zip(offsets, refs):
-        part = dot(t_ref[lax.rem(me - k + n, n)], ref[...])
-        total = part if total is None else total + part
-    out_ref[...] = total
-
-
-def early(tables, n, offsets, pieces):
-    share = pieces[0].shape[1]
-    return pl.pallas_call(
-        functools.partial(early_kernel, n, offsets),
+def early_kernel(n, k, t_ref, x_ref, *refs):
+    src = lax.rem(lax.axis_index("space") - k + n, n)
+    part = dot(t_ref[src], x_ref[...])
+    refs[-1][...] = part if len(refs) == 1 else refs[0][...] + part
+
+
+def early(tables, n, k, piece, *before):
+    share = piece.shape[1]
+    return pl.pallas_call(
+        functools.partial(early_kernel, n, k),
         out_shape=jax.ShapeDtypeStruct((tables.shape[1], share), jnp.float32),
         compiler_params=pltpu.CompilerParams(vmem_limit_bytes=VMEM_BYTES),
-    )(tables, *pieces)
+    )(tables, piece, *before)
 
 
 def late_kernel(n, k, targets, t_ref, sum_ref, x_ref, w_ref, own_ref, other_ref, gram_ref):
@@ -134,6 +130,19 @@
         ),
         compiler_params=pltpu.CompilerParams(vmem_limit_bytes=VMEM_BYTES),
     )(tables, partial_sum, piece, weights)
+
+
+def share_kernel(gram_ref, out_ref):
+    total = jnp.sum(gram_ref[...], axis=0)
+    for d in range(out_ref.shape[0]):
+        out_ref[d] = total
+
+
+def add_and_repeat(grams, times):
+    return pl.pallas_call(
+        share_kernel,
+        out_shape=jax.ShapeDtypeStruct((times,) + grams.shape[1:], jnp.float32),
+    )(grams)
 
 
 def inv_sqrt(x):
@@ -254,19 +263,22 @@
     tables = jnp.asarray(dft_blocks(n))
     own_weights = lax.dynamic_index_in_dim(weights.reshape(freq_count, 1, share), me, 0, False)
 
-    order = [n // 2] + [k for k in range(1, n) if k != n // 2]
-    pieces = []
-    for k in order:
+    offsets = [n // 2] + [k for k in range(1, n) if k != n // 2]
+    pieces = {}
+    for k in offsets:
         sent = cut(snapshots, n, k, rows, share)
-        pieces.append(lax.ppermute(sent, "space", [(i, (i + k) % n) for i in range(n)]))
-    pieces = [cut(snapshots, n, 0, rows, share)] + pieces
-    order = [0] + order
-
-    targets = n * tm_count * freq_count
-    before = early(tables, n, order[:-1], pieces[:-1])
-    own, other, gram = late(tables, n, order[-1], before, pieces[-1], own_weights, targets)
+        pieces[k] = lax.ppermute(sent, "space", [(i, (i + k) % n) for i in range(n)])
+    pieces[0] = cut(snapshots, n, 0, rows, share)
+
+    before = early(tables, n, 0, pieces[0])
+    for k in [n // 2] + [k for k in range(n - 1, 1, -1) if k != n // 2]:
+        before = early(tables, n, k, pieces[k], before)
+    targets = tm_count * freq_count
+    own, other, gram = late(tables, n, 1, before, pieces[1], own_weights, targets)
     other = lax.ppermute(other, "freq", [(0, 1), (1, 0)])
-    grams = lax.all_to_all(gram, ("space", "tm", "freq"), split_axis=0, concat_axis=0, tiled=True)
+    grams = lax.all_to_all(gram, ("tm", "freq"), split_axis=0, concat_axis=0, tiled=True)
+    grams = add_and_repeat(grams, n)
+    grams = lax.all_to_all(grams, "space", split_axis=0, concat_axis=0, tiled=True)
     total = rows * n * tm_count
     return finish(grams, own, other, local, total)
 

time: 75.3 us -> 76 us (level)
  Pallas kernels: 16.1 us -> 17.9 us
  starting transfers between devices: 8.1 us -> 6.42 us
  blocking collectives: 23.3 us -> 24.5 us
  waiting for transfers between devices: 25.7 us -> 24.7 us
    pallas_call x1 -> x4, Pallas kernels: 3.7 us -> 5.44 us  [the longest x3 4.06 us: early(): pl.pallas_call(functools.partial(early_kernel, n, k), out_shape=jax.Shape...]
    ppermute x3, starting transfers between devices: 8.03 us -> 6.35 us  [on_device(): lax.ppermute(sent, 'space', [(i, (i + k) % n) for i in range(n)])]
    all_to_all x1 -> x2, blocking collectives: 23.3 us -> 24.5 us  [the longest x1 16.6 us: on_device(): lax.all_to_all(grams, 'space', split_axis=0, concat_axis=0, tiled=True)]
    ppermute x3, waiting for transfers between devices: 25.7 us -> 24.7 us  [on_device(): lax.ppermute(sent, 'space', [(i, (i + k) % n) for i in range(n)])]
  transfers between devices with their start and end apart: 4 -> 4, of which waited for: 1 -> 2; matrix products, arithmetic and copies ran while one was open for 0% -> 0% of each run, Pallas kernels for 13% -> 15%
where the time goes in v2:
time: 76 us; the launch traced here: 75.3 us
  waiting for transfers between devices  24.7 us (32%)
  blocking collectives  24.5 us (32%)
  Pallas kernels  17.9 us (24%)
  starting transfers between devices  6.42 us (8%)
  local copies, waits for them, and re-layouts  1.06 us (1%)
  between operations  0.76 us (1%)
    ppermute x3, waiting for transfers between devices, on_device(): lax.ppermute(sent, 'space', [(i, (i + k) % n) for i in range(n)])  24.7 us
    all_to_all x1, blocking collectives, on_device(): lax.all_to_all(grams, 'space', split_axis=0, concat_axis=0, tiled=True)  16.6 us
    all_to_all x1, blocking collectives, on_device(): lax.all_to_all(gram, ('tm', 'freq'), split_axis=0, concat_axis=0, tiled=T...  7.86 us
    pallas_call x4, Pallas kernels, cut(): pl.pallas_call(functools.partial(cut_kernel, n, k, rows, share), out_shap...  7.76 us
    ppermute x3, starting transfers between devices, on_device(): lax.ppermute(sent, 'space', [(i, (i + k) % n) for i in range(n)])  6.35 us
    pallas_call x3, Pallas kernels, early(): pl.pallas_call(functools.partial(early_kernel, n, k), out_shape=jax.Shape...  4.06 us
    pallas_call x1, Pallas kernels, finish(): pl.pallas_call(functools.partial(finish_kernel, local, total), out_shape=...  2.56 us
    pallas_call x1, Pallas kernels, late(): pl.pallas_call(functools.partial(late_kernel, n, k, targets), out_shape=(...  2.11 us
  transfers between devices with their start and end apart: 4, of which 2 were waited for; matrix products, arithmetic and copies ran while one was open for 0% of the time, Pallas kernels for 15%

profile of v2, /device:TPU:0, one launch (start us, length us, event | category | flops | bytes accessed | tf_op | source)
XLA Modules:
  0.0 75.3 jit_solution(16289225156201895776)
XLA Ops:
  0.6 0.0 copy-start
  0.6 1.9 %shard_map.51 = f32[16,16,512]{2,1,0:T(8,128)} custom-call(f32[16,16,4096]{2,1,0:T(8,128)} %x_ref.7), custom_call_target="tpu_custom_call" | custom-call | tf_op jit(solution)/shard_map/pallas_call | solution.py:57
  2.6 4.1 %collective-permute-start.1 = (f32[256,512]{1,0:T(8,128)}, f32[256,512]{1,0:T(8,128)}, u32[]{:S(2)}, u32[]{:S(2)}) collective-permute-start(f32[256,512]{1,0:T(8,128)} %bitcast.11), channel_id=1, source_target_pairs={{0,8},{4,12},{8,0},{12,4},{1,9},{5,13},{9,1},{13,5},{2,10},{6,14},... | collective-permute-start | bytes 1572872 | tf_op jit(solution)/shard_map/ppermute | solution.py:270
  6.7 1.9 %shard_map.50 = f32[16,16,512]{2,1,0:T(8,128)} custom-call(f32[16,16,4096]{2,1,0:T(8,128)} %x_ref.7), custom_call_target="tpu_custom_call" | custom-call | tf_op jit(solution)/shard_map/pallas_call | solution.py:57
  8.6 0.0 copy-start.1
  8.6 1.4 %collective-permute-start = (f32[256,512]{1,0:T(8,128)}, f32[256,512]{1,0:T(8,128)S(1)}, u32[]{:S(2)}, u32[]{:S(2)}) collective-permute-start(f32[256,512]{1,0:T(8,128)} %bitcast.10), channel_id=1, source_target_pairs={{0,12},{4,0},{8,4},{12,8},{1,13},{5,1},{9,5},{13,9},{2,14},{6,2},{... | collective-permute-start | bytes 1572872 | tf_op jit(solution)/shard_map/ppermute | solution.py:270
  10.0 1.9 %shard_map.56 = f32[16,16,512]{2,1,0:T(8,128)} custom-call(f32[16,16,4096]{2,1,0:T(8,128)} %x_ref.7), custom_call_target="tpu_custom_call" | custom-call | tf_op jit(solution)/shard_map/pallas_call | solution.py:57
  12.0 0.8 %collective-permute-start.2 = (f32[256,512]{1,0:T(8,128)}, f32[256,512]{1,0:T(8,128)S(1)}, u32[]{:S(2)}, u32[]{:S(2)}) collective-permute-start(f32[256,512]{1,0:T(8,128)} %bitcast.9), channel_id=1, source_target_pairs={{0,4},{4,8},{8,12},{12,0},{1,5},{5,9},{9,13},{13,1},{2,6},{6,10},{... | collective-permute-start | bytes 1572872 | tf_op jit(solution)/shard_map/ppermute | solution.py:270
  12.9 1.9 %shard_map.52 = f32[16,16,512]{2,1,0:T(8,128)} custom-call(f32[16,16,4096]{2,1,0:T(8,128)} %x_ref.7), custom_call_target="tpu_custom_call" | custom-call | tf_op jit(solution)/shard_map/pallas_call | solution.py:57
  14.8 0.0 copy-done.1
  14.8 0.0 copy-start.2
  14.8 1.0 %copy-done.2 = f32[16,16,512]{2,1,0:T(8,128)S(1)} copy-done((f32[16,16,512]{2,1,0:T(8,128)S(1)}, f32[16,16,512]{2,1,0:T(8,128)}, u32[]{:S(2)}) %copy-start.2) | copy-done | bytes 524312
  15.8 1.0 %shard_map.53.refs_0_ = f32[512,512]{1,0:T(8,128)S(1)} custom-call(f32[4,512,256]{2,1,0:T(8,128)S(1)} %copy-done.1, f32[256,512]{1,0:T(8,128)S(1)} %bitcast.8), custom_call_target="tpu_custom_call" | custom-call | tf_op jit(solution)/shard_map/pallas_call | solution.py:79
  16.9 0.0 copy-done
  16.9 15.0 %collective-permute-done.1.x_ref = f32[256,512]{1,0:T(8,128)} collective-permute-done((f32[256,512]{1,0:T(8,128)}, f32[256,512]{1,0:T(8,128)}, u32[]{:S(2)}, u32[]{:S(2)}) %collective-permute-start.1) | collective-permute-done | bytes 524320 | tf_op jit(solution)/shard_map/ppermute | solution.py:270
  31.9 2.0 %shard_map.54.refs_0_ = f32[512,512]{1,0:T(8,128)S(1)} custom-call(f32[4,512,256]{2,1,0:T(8,128)S(1)} %copy-done.1, f32[256,512]{1,0:T(8,128)} %collective-permute-done.1.x_ref, f32[512,512]{1,0:T(8,128)S(1)} %shard_map.53.refs_0_), custom_call_target="tpu_custom_call" | custom-call | tf_op jit(solution)/shard_map/pallas_call | solution.py:79
  34.0 9.7 %collective-permute-done.x_ref = f32[256,512]{1,0:T(8,128)S(1)} collective-permute-done((f32[256,512]{1,0:T(8,128)}, f32[256,512]{1,0:T(8,128)S(1)}, u32[]{:S(2)}, u32[]{:S(2)}) %collective-permute-start) | collective-permute-done | bytes 524320 | tf_op jit(solution)/shard_map/ppermute | solution.py:270
  43.6 1.0 %shard_map.55.sum_ref = f32[512,512]{1,0:T(8,128)S(1)} custom-call(f32[4,512,256]{2,1,0:T(8,128)S(1)} %copy-done.1, f32[256,512]{1,0:T(8,128)S(1)} %collective-permute-done.x_ref, f32[512,512]{1,0:T(8,128)S(1)} %shard_map.54.refs_0_), custom_call_target="tpu_custom_call" | custom-call | tf_op jit(solution)/shard_map/pallas_call | solution.py:79
  44.6 0.0 collective-permute-done.2.x_ref
  44.6 2.1 %shard_map.57 = (f32[256,512]{1,0:T(8,128)S(1)}, f32[256,512]{1,0:T(8,128)}, f32[4,16,128]{2,1,0:T(8,128)S(1)}) custom-call(f32[4,512,256]{2,1,0:T(8,128)S(1)} %copy-done.1, f32[512,512]{1,0:T(8,128)S(1)} %shard_map.55.sum_ref, f32[256,512]{1,0:T(8,128)S(1)} %collective-permute-done.2.x_ref, f32[1,512]{1,0:T(1,128)S(1)} %dynamic-slice_bitcast_fusion.w_ref), custom_call_target="tpu_custom_call" | custom-call | tf_op jit(solution)/shard_map/pallas_call | solution.py:124
  46.8 0.1 collective-permute-start.3
  46.8 7.9 %all_to_all.10.gram_ref = f32[4,16,128]{2,1,0:T(8,128)} all-to-all(f32[4,16,128]{2,1,0:T(8,128)S(1)} %get-tuple-element.5), channel_id=1, replica_groups=mesh['groups'=2,'space'=4,'tm'=2,'freq'=2] {'tm','freq'}, dimensions={0} | all-to-all | bytes 65536 | tf_op jit(solution)/shard_map/all_to_all | solution.py:279
  54.7 1.4 %shard_map.58 = f32[4,16,128]{2,1,0:T(8,128)} custom-call(f32[4,16,128]{2,1,0:T(8,128)} %all_to_all.10.gram_ref), custom_call_target="tpu_custom_call" | custom-call | tf_op jit(solution)/shard_map/pallas_call | solution.py:142
  56.1 16.6 %all_to_all.11.gram_ref = f32[4,16,128]{2,1,0:T(8,128)S(1)} all-to-all(f32[4,16,128]{2,1,0:T(8,128)} %shard_map.58), channel_id=1, replica_groups=mesh['groups'=2,'space'=4,'tm'=2,'freq'=2] {'space'}, dimensions={0} | all-to-all | bytes 65536 | tf_op jit(solution)/shard_map/all_to_all | solution.py:281
  72.7 0.0 collective-permute-done.3.other_ref
  72.7 2.6 %shard_map.59 = (f32[8,2,16,1024]{3,2,1,0:T(8,128)}, f32[2,8,16,16]{3,2,1,0:T(8,128)}) custom-call(f32[4,16,128]{2,1,0:T(8,128)S(1)} %all_to_all.11.gram_ref, f32[256,512]{1,0:T(8,128)S(1)} %get-tuple-element.6.own_ref, f32[256,512]{1,0:T(8,128)S(1)} %collective-permute-done.3.other_ref), custom_call_target="tpu_custom_call" | custom-call | tf_op jit(solution)/shard_map/pallas_call | solution.py:243
  (1 shorter events, 0.0 us)
Async XLA Ops:
  0.6 16.2 %copy-start = (f32[1024]{0:T(1024)S(1)}, f32[1024]{0:T(1024)}, u32[]{:S(2)}) copy-start(f32[1024]{0:T(1024)} %param.4) | copy-start | bytes 12292
  2.6 29.3 %collective-permute-start.1 = (f32[256,512]{1,0:T(8,128)}, f32[256,512]{1,0:T(8,128)}, u32[]{:S(2)}, u32[]{:S(2)}) collective-permute-start(f32[256,512]{1,0:T(8,128)} %bitcast.11), channel_id=1, source_target_pairs={{0,8},{4,12},{8,0},{12,4},{1,9},{5,13},{9,1},{13,5},{2,10},{6,14},... | collective-permute-start | bytes 1572872 | tf_op jit(solution)/shard_map/ppermute | solution.py:270
  8.6 6.2 %copy-start.1 = (f32[4,512,256]{2,1,0:T(8,128)S(1)}, f32[4,512,256]{2,1,0:T(8,128)}, u32[]{:S(2)}) copy-start(f32[4,512,256]{2,1,0:T(8,128)} %constant.12.clone.t_ref) | copy-start | bytes 6291460
  8.6 35.0 %collective-permute-start = (f32[256,512]{1,0:T(8,128)}, f32[256,512]{1,0:T(8,128)S(1)}, u32[]{:S(2)}, u32[]{:S(2)}) collective-permute-start(f32[256,512]{1,0:T(8,128)} %bitcast.10), channel_id=1, source_target_pairs={{0,12},{4,0},{8,4},{12,8},{1,13},{5,1},{9,5},{13,9},{2,14},{6,2},{... | collective-permute-start | bytes 1572872 | tf_op jit(solution)/shard_map/ppermute | solution.py:270
  12.0 32.6 %collective-permute-start.2 = (f32[256,512]{1,0:T(8,128)}, f32[256,512]{1,0:T(8,128)S(1)}, u32[]{:S(2)}, u32[]{:S(2)}) collective-permute-start(f32[256,512]{1,0:T(8,128)} %bitcast.9), channel_id=1, source_target_pairs={{0,4},{4,8},{8,12},{12,0},{1,5},{5,9},{9,13},{13,1},{2,6},{6,10},{... | collective-permute-start | bytes 1572872 | tf_op jit(solution)/shard_map/ppermute | solution.py:270
  14.8 1.0 %copy-start.2 = (f32[16,16,512]{2,1,0:T(8,128)S(1)}, f32[16,16,512]{2,1,0:T(8,128)}, u32[]{:S(2)}) copy-start(f32[16,16,512]{2,1,0:T(8,128)} %shard_map.52) | copy-start | bytes 1572868
  46.8 26.0 %collective-permute-start.3 = (f32[256,512]{1,0:T(8,128)}, f32[256,512]{1,0:T(8,128)S(1)}, u32[]{:S(2)}, u32[]{:S(2)}) collective-permute-start(f32[256,512]{1,0:T(8,128)} %get-tuple-element.7), channel_id=1, source_target_pairs={{0,1},{1,0},{2,3},{3,2},{4,5},{5,4},{6,7},{7,6},{8,9},{9,8},{10,11... | collective-permute-start | bytes 1572872 | tf_op jit(solution)/shard_map/ppermute | solution.py:278

commit v3 on v2

--- a/solution.py
+++ b/solution.py
@@ -13,7 +13,7 @@
 NF = 16
 CUTS = 16
 epsilon = 1e-05
-VMEM_BYTES = 48 * 1024 * 1024
+MIB = 1024 * 1024
 
 
 def dft_blocks(groups):
@@ -57,9 +57,10 @@
         piece = pl.pallas_call(
             functools.partial(cut_kernel, n, k, rows, share),
             out_shape=jax.ShapeDtypeStruct((blocks, local_times, share), jnp.float32),
-            in_specs=[pl.BlockSpec(memory_space=pl.ANY)],
+            in_specs=[pl.BlockSpec(memory_space=pltpu.HBM)],
             out_specs=pl.BlockSpec(memory_space=pltpu.VMEM),
             scratch_shapes=[pltpu.SemaphoreType.DMA((CUTS,))],
+            compiler_params=pltpu.CompilerParams(vmem_limit_bytes=4 * MIB),
         )(snapshots)
     else:
         to = lax.rem(lax.axis_index("space") + k, n)
@@ -79,11 +80,11 @@
     return pl.pallas_call(
         functools.partial(early_kernel, n, k),
         out_shape=jax.ShapeDtypeStruct((tables.shape[1], share), jnp.float32),
-        compiler_params=pltpu.CompilerParams(vmem_limit_bytes=VMEM_BYTES),
+        compiler_params=pltpu.CompilerParams(vmem_limit_bytes=16 * MIB),
     )(tables, piece, *before)
 
 
-def late_kernel(n, k, targets, t_ref, sum_ref, x_ref, w_ref, own_ref, other_ref, gram_ref):
+def late_kernel(n, k, t_ref, sum_ref, x_ref, w_ref, own_ref, other_ref, gram_ref, lent_ref):
     src = lax.rem(lax.axis_index("space") - k + n, n)
     spectra = sum_ref[...] + dot(t_ref[src], x_ref[...])
     half = spectra.shape[0] // 2
@@ -113,36 +114,20 @@
             kept = jnp.where(line == lane, part, 0.0)
             both.append(jnp.sum(kept.reshape(local, NB, width), axis=0))
         packed.append(jnp.where(row >= col, both[0], both[1]))
-    for d in range(targets):
-        gram_ref[d] = packed[d % 2]
-
-
-def late(tables, n, k, partial_sum, piece, weights, targets):
+    gram_ref[...] = jnp.where(first, packed[0], packed[1])
+    lent_ref[...] = jnp.where(first, packed[1], packed[0])
+
+
+def late(tables, n, k, partial_sum, piece, weights):
     share = piece.shape[1]
     half = tables.shape[1] // 2
     shape = jax.ShapeDtypeStruct((half, share), jnp.float32)
+    gram_shape = jax.ShapeDtypeStruct((NB, half // 2), jnp.float32)
     return pl.pallas_call(
-        functools.partial(late_kernel, n, k, targets),
-        out_shape=(
-            shape,
-            shape,
-            jax.ShapeDtypeStruct((targets, NB, half // 2), jnp.float32),
-        ),
-        compiler_params=pltpu.CompilerParams(vmem_limit_bytes=VMEM_BYTES),
+        functools.partial(late_kernel, n, k),
+        out_shape=(shape, shape, gram_shape, gram_shape),
+        compiler_params=pltpu.CompilerParams(vmem_limit_bytes=16 * MIB),
     )(tables, partial_sum, piece, weights)
-
-
-def share_kernel(gram_ref, out_ref):
-    total = jnp.sum(gram_ref[...], axis=0)
-    for d in range(out_ref.shape[0]):
-        out_ref[d] = total
-
-
-def add_and_repeat(grams, times):
-    return pl.pallas_call(
-        share_kernel,
-        out_shape=jax.ShapeDtypeStruct((times,) + grams.shape[1:], jnp.float32),
-    )(grams)
 
 
 def inv_sqrt(x):
@@ -150,10 +135,11 @@
     return y * (1.5 - 0.5 * x * (y * y))
 
 
-def finish_kernel(local, total, gram_ref, own_ref, other_ref, modes_ref, factor_ref):
+def finish_kernel(local, total, own_ref, other_ref, *refs):
+    gram_refs, (modes_ref, factor_ref) = refs[:-2], refs[-2:]
     width = local * NB
     share = own_ref.shape[1]
-    gram = jnp.sum(gram_ref[...], axis=0) / total
+    gram = sum(ref[...] for ref in gram_refs) / total
     row = lax.broadcasted_iota(jnp.int32, (NB, width), 0)
     col = lax.broadcasted_iota(jnp.int32, (NB, width), 1) % NB
     stacked = [jnp.where(col == j, gram, 0.0) for j in range(NB)]
@@ -246,8 +232,15 @@
             jax.ShapeDtypeStruct((local, 2, NB, 2 * share), jnp.float32),
             jax.ShapeDtypeStruct((2, local, NB, NB), jnp.float32),
         ),
-        compiler_params=pltpu.CompilerParams(vmem_limit_bytes=VMEM_BYTES),
-    )(grams, own, other)
+        compiler_params=pltpu.CompilerParams(vmem_limit_bytes=16 * MIB),
+    )(own, other, *grams)
+
+
+def copies(value, axis, size):
+    return [value] + [
+        lax.ppermute(value, axis, [(i, (i + k) % size) for i in range(size)])
+        for k in range(1, size)
+    ]
 
 
 def on_device(snapshots, weights):
@@ -273,12 +266,13 @@
     before = early(tables, n, 0, pieces[0])
     for k in [n // 2] + [k for k in range(n - 1, 1, -1) if k != n // 2]:
         before = early(tables, n, k, pieces[k], before)
-    targets = tm_count * freq_count
-    own, other, gram = late(tables, n, 1, before, pieces[1], own_weights, targets)
-    other = lax.ppermute(other, "freq", [(0, 1), (1, 0)])
-    grams = lax.all_to_all(gram, ("tm", "freq"), split_axis=0, concat_axis=0, tiled=True)
-    grams = add_and_repeat(grams, n)
-    grams = lax.all_to_all(grams, "space", split_axis=0, concat_axis=0, tiled=True)
+    own, other, gram, lent = late(tables, n, 1, before, pieces[1], own_weights)
+    swap = [(0, 1), (1, 0)]
+    gram = gram + lax.ppermute(lent, "freq", swap)
+    gram, other = lax.optimization_barrier((gram, other))
+    other = lax.ppermute(other, "freq", swap)
+    gram = sum(copies(gram, "tm", tm_count))
+    grams = copies(gram, "space", n)
     total = rows * n * tm_count
     return finish(grams, own, other, local, total)
 

time: 76 us -> 71.4 us (0.939)
  blocking collectives: 24.5 us -> 0 us
  starting transfers between devices: 6.42 us -> 21.5 us
  waiting for transfers between devices: 24.7 us -> 32.5 us
  Pallas kernels: 17.9 us -> 14.1 us
  local copies, waits for them, and re-layouts: 1.06 us -> 2.21 us
    all_to_all x2 -> x0, blocking collectives: 24.5 us -> none  [the longest x1 16.6 us: on_device(): lax.all_to_all(grams, 'space', split_axis=0, concat_axis=0, tiled=True)]
    ppermute x1 -> x6, starting transfers between devices: 0.07 us -> 15.3 us  [the longest x4 15 us: copies(): lax.ppermute(value, axis, [(i, (i + k) % size) for i in range(size)])]
    ppermute x1 -> x6, waiting for transfers between devices: 0.01 us -> 4.52 us  [the longest x4 3.36 us: copies(): lax.ppermute(value, axis, [(i, (i + k) % size) for i in range(size)])]
    pallas_call x4, Pallas kernels: 7.76 us -> 4.37 us  [cut(): pl.pallas_call(functools.partial(cut_kernel, n, k, rows, share), out_shap...]
    ppermute x3, waiting for transfers between devices: 24.7 us -> 28 us  [on_device(): lax.ppermute(sent, 'space', [(i, (i + k) % n) for i in range(n)])]
    pallas_call x2 -> x1, Pallas kernels: 3.49 us -> 2.1 us  [late(): pl.pallas_call(functools.partial(late_kernel, n, k), out_shape=(shape, sh...]
    unnamed x6, local copies, waits for them, and re-layouts: 1.05 us -> 2.2 us
    pallas_call x3, Pallas kernels: 4.06 us -> 5.12 us  [early(): pl.pallas_call(functools.partial(early_kernel, n, k), out_shape=jax.Shape...]
  transfers between devices with their start and end apart: 4 -> 9, of which waited for: 2 -> 5; matrix products, arithmetic and copies ran while one was open for 0% -> 0% of each run, Pallas kernels for 15% -> 12%
where the time goes in v3:
time: 71.4 us; the launch traced here: 71.2 us
  waiting for transfers between devices  32.5 us (46%)
  starting transfers between devices  21.5 us (30%)
  Pallas kernels  14.1 us (20%)
  local copies, waits for them, and re-layouts  2.21 us (3%)
  between operations  0.77 us (1%)
    ppermute x3, waiting for transfers between devices, on_device(): lax.ppermute(sent, 'space', [(i, (i + k) % n) for i in range(n)])  28 us
    ppermute x4, starting transfers between devices, copies(): lax.ppermute(value, axis, [(i, (i + k) % size) for i in range(size)])  15 us
    ppermute x3, starting transfers between devices, on_device(): lax.ppermute(sent, 'space', [(i, (i + k) % n) for i in range(n)])  6.23 us
    pallas_call x3, Pallas kernels, early(): pl.pallas_call(functools.partial(early_kernel, n, k), out_shape=jax.Shape...  5.12 us
    pallas_call x4, Pallas kernels, cut(): pl.pallas_call(functools.partial(cut_kernel, n, k, rows, share), out_shap...  4.37 us
    ppermute x4, waiting for transfers between devices, copies(): lax.ppermute(value, axis, [(i, (i + k) % size) for i in range(size)])  3.36 us
    pallas_call x1, Pallas kernels, finish(): pl.pallas_call(functools.partial(finish_kernel, local, total), out_shape=...  2.56 us
    unnamed x6, local copies, waits for them, and re-layouts  2.2 us
  transfers between devices with their start and end apart: 9, of which 5 were waited for; matrix products, arithmetic and copies ran while one was open for 0% of the time, Pallas kernels for 12%

profile of v3, /device:TPU:0, one launch (start us, length us, event | category | flops | bytes accessed | tf_op | source)
XLA Modules:
  0.0 71.2 jit_solution(70011327862363474)
XLA Ops:
  0.6 0.0 copy-start
  0.6 0.0 copy-start.1
  0.7 2.2 %copy-done.1 = f32[16,16,4096]{2,1,0:T(8,128)S(1)} copy-done((f32[16,16,4096]{2,1,0:T(8,128)S(1)}, f32[16,16,4096]{2,1,0:T(8,128)}, u32[]{:S(2)}) %copy-start.1) | copy-done | bytes 4194328
  2.8 1.3 %shard_map.51 = f32[16,16,512]{2,1,0:T(8,128)} custom-call(f32[16,16,4096]{2,1,0:T(8,128)S(1)} %copy-done.1), custom_call_target="tpu_custom_call" | custom-call | tf_op jit(solution)/shard_map/pallas_call | solution.py:57
  4.1 4.1 %collective-permute-start.1 = (f32[256,512]{1,0:T(8,128)}, f32[256,512]{1,0:T(8,128)}, u32[]{:S(2)}, u32[]{:S(2)}) collective-permute-start(f32[256,512]{1,0:T(8,128)} %bitcast.1), channel_id=1, source_target_pairs={{0,8},{4,12},{8,0},{12,4},{1,9},{5,13},{9,1},{13,5},{2,10},{6,14},... | collective-permute-start | bytes 1572872 | tf_op jit(solution)/shard_map/ppermute | solution.py:263
  8.2 1.3 %shard_map.50 = f32[16,16,512]{2,1,0:T(8,128)} custom-call(f32[16,16,4096]{2,1,0:T(8,128)S(1)} %copy-done.1), custom_call_target="tpu_custom_call" | custom-call | tf_op jit(solution)/shard_map/pallas_call | solution.py:57
  9.5 0.0 copy-start.2
  9.5 1.4 %collective-permute-start = (f32[256,512]{1,0:T(8,128)}, f32[256,512]{1,0:T(8,128)}, u32[]{:S(2)}, u32[]{:S(2)}) collective-permute-start(f32[256,512]{1,0:T(8,128)} %bitcast), channel_id=1, source_target_pairs={{0,12},{4,0},{8,4},{12,8},{1,13},{5,1},{9,5},{13,9},{2,14},{6,2},{... | collective-permute-start | bytes 1572872 | tf_op jit(solution)/shard_map/ppermute | solution.py:263
  10.9 1.3 %shard_map.56 = f32[16,16,512]{2,1,0:T(8,128)} custom-call(f32[16,16,4096]{2,1,0:T(8,128)S(1)} %copy-done.1), custom_call_target="tpu_custom_call" | custom-call | tf_op jit(solution)/shard_map/pallas_call | solution.py:57
  12.3 0.7 %collective-permute-start.2 = (f32[256,512]{1,0:T(8,128)}, f32[256,512]{1,0:T(8,128)S(1)}, u32[]{:S(2)}, u32[]{:S(2)}) collective-permute-start(f32[256,512]{1,0:T(8,128)} %bitcast.3), channel_id=1, source_target_pairs={{0,4},{4,8},{8,12},{12,0},{1,5},{5,9},{9,13},{13,1},{2,6},{6,10},{... | collective-permute-start | bytes 1572872 | tf_op jit(solution)/shard_map/ppermute | solution.py:263
  13.0 0.5 shard_map.52
  13.5 1.0 %shard_map.53.refs_0_ = f32[512,512]{1,0:T(8,128)S(1)} custom-call(f32[4,512,256]{2,1,0:T(8,128)S(1)} %copy-done.2, f32[256,512]{1,0:T(8,128)S(1)} %bitcast.8), custom_call_target="tpu_custom_call" | custom-call | tf_op jit(solution)/shard_map/pallas_call | solution.py:80
  14.5 0.0 copy-done
  14.5 18.9 %collective-permute-done.1.x_ref = f32[256,512]{1,0:T(8,128)} collective-permute-done((f32[256,512]{1,0:T(8,128)}, f32[256,512]{1,0:T(8,128)}, u32[]{:S(2)}, u32[]{:S(2)}) %collective-permute-start.1) | collective-permute-done | bytes 524320 | tf_op jit(solution)/shard_map/ppermute | solution.py:263
  33.5 2.1 %shard_map.54.refs_0_ = f32[512,512]{1,0:T(8,128)S(1)} custom-call(f32[4,512,256]{2,1,0:T(8,128)S(1)} %copy-done.2, f32[256,512]{1,0:T(8,128)} %collective-permute-done.1.x_ref, f32[512,512]{1,0:T(8,128)S(1)} %shard_map.53.refs_0_), custom_call_target="tpu_custom_call" | custom-call | tf_op jit(solution)/shard_map/pallas_call | solution.py:80
  35.5 9.1 %collective-permute-done.x_ref = f32[256,512]{1,0:T(8,128)} collective-permute-done((f32[256,512]{1,0:T(8,128)}, f32[256,512]{1,0:T(8,128)}, u32[]{:S(2)}, u32[]{:S(2)}) %collective-permute-start) | collective-permute-done | bytes 524320 | tf_op jit(solution)/shard_map/ppermute | solution.py:263
  44.6 2.0 %shard_map.55.sum_ref = f32[512,512]{1,0:T(8,128)S(1)} custom-call(f32[4,512,256]{2,1,0:T(8,128)S(1)} %copy-done.2, f32[256,512]{1,0:T(8,128)} %collective-permute-done.x_ref, f32[512,512]{1,0:T(8,128)S(1)} %shard_map.54.refs_0_), custom_call_target="tpu_custom_call" | custom-call | tf_op jit(solution)/shard_map/pallas_call | solution.py:80
  46.7 0.0 collective-permute-done.2.x_ref
  46.7 2.1 %shard_map.57 = (f32[256,512]{1,0:T(8,128)S(1)}, f32[256,512]{1,0:T(8,128)S(1)}, f32[16,128]{1,0:T(8,128)S(1)}, f32[16,128]{1,0:T(8,128)S(1)}) custom-call(f32[4,512,256]{2,1,0:T(8,128)S(1)} %copy-done.2, f32[512,512]{1,0:T(8,128)S(1)} %shard_map.55.sum_ref, f32[256,512]{1,0:T(8,128)S(1)} %collective-permute-done.2.x_ref, ...), custom_call_target="tpu_custom_call" | custom-call | tf_op jit(solution)/shard_map/pallas_call | solution.py:126
  48.8 0.1 collective-permute-start.3
  48.9 1.2 %collective-permute-done.3 = f32[16,128]{1,0:T(8,128)S(1)} collective-permute-done((f32[16,128]{1,0:T(8,128)S(1)}, f32[16,128]{1,0:T(8,128)S(1)}, u32[]{:S(2)}, u32[]{:S(2)}) %collective-permute-start.3) | collective-permute-done | bytes 8224 | tf_op jit(solution)/shard_map/ppermute | solution.py:271
  50.0 0.2 collective-permute-start.4
  50.2 3.2 %collective-permute-start.5 = (f32[16,128]{1,0:T(8,128)S(1)}, f32[16,128]{1,0:T(8,128)S(1)}, u32[]{:S(2)}, u32[]{:S(2)}) collective-permute-start(f32[16,128]{1,0:T(8,128)S(1)} %add.11), channel_id=1, source_target_pairs={{0,2},{2,0},{1,3},{3,1},{4,6},{6,4},{5,7},{7,5},{8,10},{10,8},{9,1... | collective-permute-start | bytes 24584 | tf_op jit(solution)/shard_map/ppermute | solution.py:241
  53.4 1.6 %collective-permute-done.5 = f32[16,128]{1,0:T(8,128)S(1)} collective-permute-done((f32[16,128]{1,0:T(8,128)S(1)}, f32[16,128]{1,0:T(8,128)S(1)}, u32[]{:S(2)}, u32[]{:S(2)}) %collective-permute-start.5) | collective-permute-done | bytes 8224 | tf_op jit(solution)/shard_map/ppermute | solution.py:241
  55.0 9.0 %collective-permute-start.6 = (f32[16,128]{1,0:T(8,128)S(1)}, f32[16,128]{1,0:T(8,128)S(1)}, u32[]{:S(2)}, u32[]{:S(2)}) collective-permute-start(f32[16,128]{1,0:T(8,128)S(1)} %add.12.refs_0_), channel_id=1, source_target_pairs={{0,4},{4,8},{8,12},{12,0},{1,5},{5,9},{9,13},{13,1},{2,6},{6,10},{... | collective-permute-start | bytes 24584 | tf_op jit(solution)/shard_map/ppermute | solution.py:241
  64.0 0.0 collective-permute-start.7
  64.0 2.8 %collective-permute-start.8 = (f32[16,128]{1,0:T(8,128)S(1)}, f32[16,128]{1,0:T(8,128)S(1)}, u32[]{:S(2)}, u32[]{:S(2)}) collective-permute-start(f32[16,128]{1,0:T(8,128)S(1)} %add.12.refs_0_), channel_id=1, source_target_pairs={{0,12},{4,0},{8,4},{12,8},{1,13},{5,1},{9,5},{13,9},{2,14},{6,2},{... | collective-permute-start | bytes 24584 | tf_op jit(solution)/shard_map/ppermute | solution.py:241
  66.9 0.0 collective-permute-done.6.refs_1_
  66.9 1.7 %collective-permute-done.7.refs_2_ = f32[16,128]{1,0:T(8,128)S(1)} collective-permute-done((f32[16,128]{1,0:T(8,128)S(1)}, f32[16,128]{1,0:T(8,128)S(1)}, u32[]{:S(2)}, u32[]{:S(2)}) %collective-permute-start.7) | collective-permute-done | bytes 8224 | tf_op jit(solution)/shard_map/ppermute | solution.py:241
  68.6 0.0 collective-permute-done.8.refs_3_
  68.6 0.0 collective-permute-done.4.other_ref
  68.6 2.6 %shard_map.58 = (f32[8,2,16,1024]{3,2,1,0:T(8,128)}, f32[2,8,16,16]{3,2,1,0:T(8,128)}) custom-call(f32[256,512]{1,0:T(8,128)S(1)} %get-tuple-element.8.own_ref, f32[256,512]{1,0:T(8,128)S(1)} %collective-permute-done.4.other_ref, f32[16,128]{1,0:T(8,128)S(1)} %add.12.refs_0_, f32[16,128]{1,0:T(8,128)S(1)} %collective-permute-done.6.refs_1_, ...), custom_call_target="tpu_custom_call" | custom-call | tf_op jit(solution)/shard_map/pallas_call | solution.py:229
  (4 shorter events, 0.0 us)
Async XLA Ops:
  0.6 13.9 %copy-start = (f32[1024]{0:T(1024)S(1)}, f32[1024]{0:T(1024)}, u32[]{:S(2)}) copy-start(f32[1024]{0:T(1024)} %param.4) | copy-start | bytes 12292
  0.6 2.2 %copy-start.1 = (f32[16,16,4096]{2,1,0:T(8,128)S(1)}, f32[16,16,4096]{2,1,0:T(8,128)}, u32[]{:S(2)}) copy-start(f32[16,16,4096]{2,1,0:T(8,128)} %x_ref.7) | copy-start | bytes 12582916
  4.1 29.3 %collective-permute-start.1 = (f32[256,512]{1,0:T(8,128)}, f32[256,512]{1,0:T(8,128)}, u32[]{:S(2)}, u32[]{:S(2)}) collective-permute-start(f32[256,512]{1,0:T(8,128)} %bitcast.1), channel_id=1, source_target_pairs={{0,8},{4,12},{8,0},{12,4},{1,9},{5,13},{9,1},{13,5},{2,10},{6,14},... | collective-permute-start | bytes 1572872 | tf_op jit(solution)/shard_map/ppermute | solution.py:263
  9.5 4.0 %copy-start.2 = (f32[4,512,256]{2,1,0:T(8,128)S(1)}, f32[4,512,256]{2,1,0:T(8,128)}, u32[]{:S(2)}) copy-start(f32[4,512,256]{2,1,0:T(8,128)} %constant.12.clone.t_ref) | copy-start | bytes 6291460
  9.5 35.1 %collective-permute-start = (f32[256,512]{1,0:T(8,128)}, f32[256,512]{1,0:T(8,128)}, u32[]{:S(2)}, u32[]{:S(2)}) collective-permute-start(f32[256,512]{1,0:T(8,128)} %bitcast), channel_id=1, source_target_pairs={{0,12},{4,0},{8,4},{12,8},{1,13},{5,1},{9,5},{13,9},{2,14},{6,2},{... | collective-permute-start | bytes 1572872 | tf_op jit(solution)/shard_map/ppermute | solution.py:263
  12.3 34.4 %collective-permute-start.2 = (f32[256,512]{1,0:T(8,128)}, f32[256,512]{1,0:T(8,128)S(1)}, u32[]{:S(2)}, u32[]{:S(2)}) collective-permute-start(f32[256,512]{1,0:T(8,128)} %bitcast.3), channel_id=1, source_target_pairs={{0,4},{4,8},{8,12},{12,0},{1,5},{5,9},{9,13},{13,1},{2,6},{6,10},{... | collective-permute-start | bytes 1572872 | tf_op jit(solution)/shard_map/ppermute | solution.py:263
  48.8 1.2 %collective-permute-start.3 = (f32[16,128]{1,0:T(8,128)S(1)}, f32[16,128]{1,0:T(8,128)S(1)}, u32[]{:S(2)}, u32[]{:S(2)}) collective-permute-start(f32[16,128]{1,0:T(8,128)S(1)} %get-tuple-element.10), channel_id=1, source_target_pairs={{0,1},{1,0},{2,3},{3,2},{4,5},{5,4},{6,7},{7,6},{8,9},{9,8},{10,11... | collective-permute-start | bytes 24584 | tf_op jit(solution)/shard_map/ppermute | solution.py:271
  50.0 18.6 %collective-permute-start.4 = (f32[256,512]{1,0:T(8,128)S(1)}, f32[256,512]{1,0:T(8,128)S(1)}, u32[]{:S(2)}, u32[]{:S(2)}) collective-permute-start(f32[256,512]{1,0:T(8,128)S(1)} %get-tuple-element.12), channel_id=1, source_target_pairs={{0,1},{1,0},{2,3},{3,2},{4,5},{5,4},{6,7},{7,6},{8,9},{9,8},{10,11... | collective-permute-start | bytes 1572872 | tf_op jit(solution)/shard_map/ppermute | solution.py:273
  50.2 4.8 %collective-permute-start.5 = (f32[16,128]{1,0:T(8,128)S(1)}, f32[16,128]{1,0:T(8,128)S(1)}, u32[]{:S(2)}, u32[]{:S(2)}) collective-permute-start(f32[16,128]{1,0:T(8,128)S(1)} %add.11), channel_id=1, source_target_pairs={{0,2},{2,0},{1,3},{3,1},{4,6},{6,4},{5,7},{7,5},{8,10},{10,8},{9,1... | collective-permute-start | bytes 24584 | tf_op jit(solution)/shard_map/ppermute | solution.py:241
  55.0 11.9 %collective-permute-start.6 = (f32[16,128]{1,0:T(8,128)S(1)}, f32[16,128]{1,0:T(8,128)S(1)}, u32[]{:S(2)}, u32[]{:S(2)}) collective-permute-start(f32[16,128]{1,0:T(8,128)S(1)} %add.12.refs_0_), channel_id=1, source_target_pairs={{0,4},{4,8},{8,12},{12,0},{1,5},{5,9},{9,13},{13,1},{2,6},{6,10},{... | collective-permute-start | bytes 24584 | tf_op jit(solution)/shard_map/ppermute | solution.py:241
  64.0 4.5 %collective-permute-start.7 = (f32[16,128]{1,0:T(8,128)S(1)}, f32[16,128]{1,0:T(8,128)S(1)}, u32[]{:S(2)}, u32[]{:S(2)}) collective-permute-start(f32[16,128]{1,0:T(8,128)S(1)} %add.12.refs_0_), channel_id=1, source_target_pairs={{0,8},{4,12},{8,0},{12,4},{1,9},{5,13},{9,1},{13,5},{2,10},{6,14},... | collective-permute-start | bytes 24584 | tf_op jit(solution)/shard_map/ppermute | solution.py:241
  64.0 4.5 %collective-permute-start.8 = (f32[16,128]{1,0:T(8,128)S(1)}, f32[16,128]{1,0:T(8,128)S(1)}, u32[]{:S(2)}, u32[]{:S(2)}) collective-permute-start(f32[16,128]{1,0:T(8,128)S(1)} %add.12.refs_0_), channel_id=1, source_target_pairs={{0,12},{4,0},{8,4},{12,8},{1,13},{5,1},{9,5},{13,9},{2,14},{6,2},{... | collective-permute-start | bytes 24584 | tf_op jit(solution)/shard_map/ppermute | solution.py:241

commit v4 on v3

--- a/solution.py
+++ b/solution.py
@@ -33,16 +33,18 @@
     return jnp.dot(a, b, precision=lax.Precision.HIGHEST, preferred_element_type=jnp.float32)
 
 
-def cut_kernel(n, k, rows, share, x_ref, o_ref, sem):
+def cut_kernel(n, k, rows, skip, x_ref, o_ref, sem):
+    size = o_ref.shape[2]
     to = lax.rem(lax.axis_index("space") + k, n)
-    start = pl.multiple_of(to * rows + lax.axis_index("freq") * share, 128)
+    share = rows // 2
+    start = pl.multiple_of(to * rows + lax.axis_index("freq") * share + skip, 128)
     part = NB // CUTS
     copies = []
     for i in range(CUTS):
         blocks = pl.ds(i * part, part)
         copies.append(
             pltpu.make_async_copy(
-                x_ref.at[blocks, :, pl.ds(start, share)], o_ref.at[blocks], sem.at[i]
+                x_ref.at[blocks, :, pl.ds(start, size)], o_ref.at[blocks], sem.at[i]
             )
         )
     for copy in copies:
@@ -51,22 +53,22 @@
         copy.wait()
 
 
-def cut(snapshots, n, k, rows, share):
+def cut(snapshots, n, k, rows, skip, size):
     blocks, local_times, _ = snapshots.shape
     if local_times % 8 == 0:
         piece = pl.pallas_call(
-            functools.partial(cut_kernel, n, k, rows, share),
-            out_shape=jax.ShapeDtypeStruct((blocks, local_times, share), jnp.float32),
+            functools.partial(cut_kernel, n, k, rows, skip),
+            out_shape=pltpu.VMEM((blocks, local_times, size), jnp.float32),
             in_specs=[pl.BlockSpec(memory_space=pltpu.HBM)],
             out_specs=pl.BlockSpec(memory_space=pltpu.VMEM),
             scratch_shapes=[pltpu.SemaphoreType.DMA((CUTS,))],
             compiler_params=pltpu.CompilerParams(vmem_limit_bytes=4 * MIB),
-        )(snapshots)
+        )(pltpu.with_memory_space_constraint(snapshots, pltpu.HBM))
     else:
         to = lax.rem(lax.axis_index("space") + k, n)
-        start = to * rows + lax.axis_index("freq") * share
-        piece = lax.dynamic_slice_in_dim(snapshots, start, share, axis=2)
-    return piece.reshape(blocks * local_times, share)
+        start = to * rows + lax.axis_index("freq") * (rows // 2) + skip
+        piece = lax.dynamic_slice_in_dim(snapshots, start, size, axis=2)
+    return piece.reshape(blocks * local_times, size)
 
 
 def early_kernel(n, k, t_ref, x_ref, *refs):
@@ -84,9 +86,11 @@
     )(tables, piece, *before)
 
 
-def late_kernel(n, k, t_ref, sum_ref, x_ref, w_ref, own_ref, other_ref, gram_ref, lent_ref):
+def late_kernel(n, k, skip, t_ref, sum_ref, x_ref, w_ref, *refs):
+    *before, own_ref, other_ref, gram_ref, lent_ref = refs
+    cols = pl.ds(skip, x_ref.shape[1])
     src = lax.rem(lax.axis_index("space") - k + n, n)
-    spectra = sum_ref[...] + dot(t_ref[src], x_ref[...])
+    spectra = sum_ref[:, cols] + dot(t_ref[src], x_ref[...])
     half = spectra.shape[0] // 2
     width = half // 2
     local = width // NB
@@ -101,7 +105,7 @@
     packed = []
     for z in halves:
         full = lax.dot_general(
-            z * w_ref[...],
+            z * w_ref[:, cols],
             z,
             (((1,), (1,)), ((), ())),
             precision=lax.Precision.HIGHEST,
@@ -114,20 +118,22 @@
             kept = jnp.where(line == lane, part, 0.0)
             both.append(jnp.sum(kept.reshape(local, NB, width), axis=0))
         packed.append(jnp.where(row >= col, both[0], both[1]))
-    gram_ref[...] = jnp.where(first, packed[0], packed[1])
-    lent_ref[...] = jnp.where(first, packed[1], packed[0])
-
-
-def late(tables, n, k, partial_sum, piece, weights):
+    gram = jnp.where(first, packed[0], packed[1])
+    lent = jnp.where(first, packed[1], packed[0])
+    gram_ref[...] = gram + before[0][...] if before else gram
+    lent_ref[...] = lent + before[1][...] if before else lent
+
+
+def late(tables, n, k, skip, partial_sum, piece, weights, *before):
     share = piece.shape[1]
     half = tables.shape[1] // 2
     shape = jax.ShapeDtypeStruct((half, share), jnp.float32)
     gram_shape = jax.ShapeDtypeStruct((NB, half // 2), jnp.float32)
     return pl.pallas_call(
-        functools.partial(late_kernel, n, k),
+        functools.partial(late_kernel, n, k, skip),
         out_shape=(shape, shape, gram_shape, gram_shape),
         compiler_params=pltpu.CompilerParams(vmem_limit_bytes=16 * MIB),
-    )(tables, partial_sum, piece, weights)
+    )(tables, partial_sum, piece, weights, *before)
 
 
 def inv_sqrt(x):
@@ -135,10 +141,11 @@
     return y * (1.5 - 0.5 * x * (y * y))
 
 
-def finish_kernel(local, total, own_ref, other_ref, *refs):
-    gram_refs, (modes_ref, factor_ref) = refs[:-2], refs[-2:]
+def finish_kernel(local, total, parts, *refs):
+    own_refs, other_refs = refs[:parts], refs[parts : 2 * parts]
+    *gram_refs, modes_ref, factor_ref = refs[2 * parts :]
     width = local * NB
-    share = own_ref.shape[1]
+    share = modes_ref.shape[3] // 2
     gram = sum(ref[...] for ref in gram_refs) / total
     row = lax.broadcasted_iota(jnp.int32, (NB, width), 0)
     col = lax.broadcasted_iota(jnp.int32, (NB, width), 1) % NB
@@ -209,13 +216,15 @@
         axis=0,
     )
     me = lax.axis_index("freq")
-    for k, ref in ((0, own_ref), (1, other_ref)):
-        start = pl.multiple_of(((me + k) % 2) * share, 128)
-        out = dot(mixing, ref[...])
-        for part in range(2):
-            for f in range(local):
-                at = part * width + f * NB
-                modes_ref[f, part, :, pl.ds(start, share)] = out[at : at + NB]
+    size = share // parts
+    for k, refs_of in ((0, own_refs), (1, other_refs)):
+        for i, ref in enumerate(refs_of):
+            start = pl.multiple_of(((me + k) % 2) * share + i * size, 128)
+            out = dot(mixing, ref[...])
+            for part in range(2):
+                for f in range(local):
+                    at = part * width + f * NB
+                    modes_ref[f, part, :, pl.ds(start, size)] = out[at : at + NB]
     pad = jnp.zeros((width - NB, width), jnp.float32)
     turned_re = jnp.transpose(jnp.concatenate(low_re + [pad], axis=0))
     turned_im = jnp.transpose(jnp.concatenate(low_im + [pad], axis=0))
@@ -225,22 +234,23 @@
 
 
 def finish(grams, own, other, local, total):
-    share = own.shape[1]
+    share = sum(part.shape[1] for part in own)
     return pl.pallas_call(
-        functools.partial(finish_kernel, local, total),
+        functools.partial(finish_kernel, local, total, len(own)),
         out_shape=(
             jax.ShapeDtypeStruct((local, 2, NB, 2 * share), jnp.float32),
             jax.ShapeDtypeStruct((2, local, NB, NB), jnp.float32),
         ),
         compiler_params=pltpu.CompilerParams(vmem_limit_bytes=16 * MIB),
-    )(own, other, *grams)
-
-
-def copies(value, axis, size):
-    return [value] + [
-        lax.ppermute(value, axis, [(i, (i + k) % size) for i in range(size)])
-        for k in range(1, size)
-    ]
+    )(*own, *other, *grams)
+
+
+def partner(value, axis, size, step):
+    return lax.ppermute(value, axis, [(i, i ^ step) for i in range(size)])
+
+
+def steps(size):
+    return [1 << b for b in range(size.bit_length() - 1)]
 
 
 def on_device(snapshots, weights):
@@ -256,23 +266,36 @@
     tables = jnp.asarray(dft_blocks(n))
     own_weights = lax.dynamic_index_in_dim(weights.reshape(freq_count, 1, share), me, 0, False)
 
-    offsets = [n // 2] + [k for k in range(1, n) if k != n // 2]
-    pieces = {}
-    for k in offsets:
-        sent = cut(snapshots, n, k, rows, share)
-        pieces[k] = lax.ppermute(sent, "space", [(i, (i + k) % n) for i in range(n)])
-    pieces[0] = cut(snapshots, n, 0, rows, share)
-
-    before = early(tables, n, 0, pieces[0])
-    for k in [n // 2] + [k for k in range(n - 1, 1, -1) if k != n // 2]:
-        before = early(tables, n, k, pieces[k], before)
-    own, other, gram, lent = late(tables, n, 1, before, pieces[1], own_weights)
-    swap = [(0, 1), (1, 0)]
-    gram = gram + lax.ppermute(lent, "freq", swap)
-    gram, other = lax.optimization_barrier((gram, other))
-    other = lax.ppermute(other, "freq", swap)
-    gram = sum(copies(gram, "tm", tm_count))
-    grams = copies(gram, "space", n)
+    last = n // 2
+    halves = (0, share // 2)
+
+    def send(k, skip, size):
+        sent = cut(snapshots, n, k, rows, skip, size)
+        return lax.ppermute(sent, "space", [(i, (i + k) % n) for i in range(n)])
+
+    offsets = [k for k in range(1, n) if k != last]
+    pieces = [send(k, 0, share) for k in offsets]
+    last_pieces = [send(last, skip, share // 2) for skip in halves]
+    before = early(tables, n, 0, cut(snapshots, n, 0, rows, 0, share))
+    for k, piece in zip(offsets, pieces):
+        before = early(tables, n, k, piece, before)
+    own, other, grams = [], [], []
+    for skip, piece in zip(halves, last_pieces):
+        if other:
+            other[-1] = partner(other[-1], "freq", freq_count, 1)
+            piece, other[-1] = lax.optimization_barrier((piece, other[-1]))
+        mine, traded, *grams = late(tables, n, last, skip, before, piece, own_weights, *grams)
+        own.append(mine)
+        other.append(traded)
+    gram, lent = grams
+    gram = gram + partner(lent, "freq", freq_count, 1)
+    for step in steps(tm_count):
+        gram = gram + partner(gram, "tm", tm_count, step)
+    for step in steps(n)[:-1]:
+        gram = gram + partner(gram, "space", n, step)
+    gram, traded = lax.optimization_barrier((gram, other[1]))
+    other[1] = partner(traded, "freq", freq_count, 1)
+    grams = [gram, partner(gram, "space", n, steps(n)[-1])]
     total = rows * n * tm_count
     return finish(grams, own, other, local, total)
 

time: 71.4 us -> 71.7 us (level)
  starting transfers between devices: 21.5 us -> 10.1 us
  waiting for transfers between devices: 32.5 us -> 40.4 us
  Pallas kernels: 14.1 us -> 19.8 us
  local copies, waits for them, and re-layouts: 2.21 us -> 0.03 us
    ppermute x9 -> x10, starting transfers between devices: 21.5 us -> 10.1 us  [the longest x4 8.24 us: send(): return lax.ppermute(sent, 'space', [(i, (i + k) % n) for i in range(n)])]
    ppermute x9 -> x10, waiting for transfers between devices: 32.5 us -> 40.4 us  [the longest x4 29.1 us: send(): return lax.ppermute(sent, 'space', [(i, (i + k) % n) for i in range(n)])]
    pallas_call x6 -> x8, Pallas kernels: 9.03 us -> 15.7 us  [the longest x5 8.51 us: cut(): pl.pallas_call(functools.partial(cut_kernel, n, k, rows, skip), out_shape...]
    unnamed x6 -> x4, local copies, waits for them, and re-layouts: 2.2 us -> 0.02 us
    pallas_call x3, Pallas kernels: 5.12 us -> 4.07 us  [early(): pl.pallas_call(functools.partial(early_kernel, n, k), out_shape=jax.Shape...]
  transfers between devices with their start and end apart: 9 -> 10, of which waited for: 5 -> 8; matrix products, arithmetic and copies ran while one was open for 0% -> 0% of each run, Pallas kernels for 12% -> 19%
where the time goes in v4:
time: 71.7 us; the launch traced here: 71.1 us
  waiting for transfers between devices  40.4 us (56%)
  Pallas kernels  19.8 us (28%)
  starting transfers between devices  10.1 us (14%)
  between operations  0.76 us (1%)
    ppermute x4, waiting for transfers between devices, send(): return lax.ppermute(sent, 'space', [(i, (i + k) % n) for i in range(n)])  29.1 us
    ppermute x6, waiting for transfers between devices, partner(): return lax.ppermute(value, axis, [(i, i ^ step) for i in range(size)])  11.3 us
    pallas_call x5, Pallas kernels, cut(): pl.pallas_call(functools.partial(cut_kernel, n, k, rows, skip), out_shape...  8.51 us
    ppermute x4, starting transfers between devices, send(): return lax.ppermute(sent, 'space', [(i, (i + k) % n) for i in range(n)])  8.24 us
    pallas_call x2, Pallas kernels, late(): pl.pallas_call(functools.partial(late_kernel, n, k, skip), out_shape=(sha...  4.67 us
    pallas_call x3, Pallas kernels, early(): pl.pallas_call(functools.partial(early_kernel, n, k), out_shape=jax.Shape...  4.07 us
    pallas_call x1, Pallas kernels, finish(): pl.pallas_call(functools.partial(finish_kernel, local, total, len(own)),...  2.56 us
    ppermute x6, starting transfers between devices, partner(): return lax.ppermute(value, axis, [(i, i ^ step) for i in range(size)])  1.86 us
  transfers between devices with their start and end apart: 10, of which 8 were waited for; matrix products, arithmetic and copies ran while one was open for 0% of the time, Pallas kernels for 19%

profile of v4, /device:TPU:0, one launch (start us, length us, event | category | flops | bytes accessed | tf_op | source)
XLA Modules:
  0.0 71.1 jit_solution(15104477515025718916)
XLA Ops:
  0.6 0.0 copy-start
  0.6 1.9 %shard_map.51 = f32[16,16,512]{2,1,0:T(8,128)} custom-call(f32[16,16,4096]{2,1,0:T(8,128)} %x_ref.9), custom_call_target="tpu_custom_call" | custom-call | tf_op jit(solution)/shard_map/pallas_call | solution.py:59
  2.6 3.1 %collective-permute-start.1 = (f32[256,512]{1,0:T(8,128)}, f32[256,512]{1,0:T(8,128)}, u32[]{:S(2)}, u32[]{:S(2)}) collective-permute-start(f32[256,512]{1,0:T(8,128)} %bitcast.1), channel_id=1, source_target_pairs={{0,4},{4,8},{8,12},{12,0},{1,5},{5,9},{9,13},{13,1},{2,6},{6,10},{... | collective-permute-start | bytes 1572872 | tf_op jit(solution)/shard_map/ppermute | solution.py:274
  5.7 1.9 %shard_map.50 = f32[16,16,512]{2,1,0:T(8,128)} custom-call(f32[16,16,4096]{2,1,0:T(8,128)} %x_ref.9), custom_call_target="tpu_custom_call" | custom-call | tf_op jit(solution)/shard_map/pallas_call | solution.py:59
  7.6 2.1 %collective-permute-start = (f32[256,512]{1,0:T(8,128)}, f32[256,512]{1,0:T(8,128)S(1)}, u32[]{:S(2)}, u32[]{:S(2)}) collective-permute-start(f32[256,512]{1,0:T(8,128)} %bitcast), channel_id=1, source_target_pairs={{0,12},{4,0},{8,4},{12,8},{1,13},{5,1},{9,5},{13,9},{2,14},{6,2},{... | collective-permute-start | bytes 1572872 | tf_op jit(solution)/shard_map/ppermute | solution.py:274
  9.7 1.8 %shard_map.56 = f32[16,16,256]{2,1,0:T(8,128)} custom-call(f32[16,16,4096]{2,1,0:T(8,128)} %x_ref.9), custom_call_target="tpu_custom_call" | custom-call | tf_op jit(solution)/shard_map/pallas_call | solution.py:59
  11.5 0.0 copy-start.1
  11.5 1.0 %collective-permute-start.2 = (f32[256,256]{1,0:T(8,128)}, f32[256,256]{1,0:T(8,128)}, u32[]{:S(2)}, u32[]{:S(2)}) collective-permute-start(f32[256,256]{1,0:T(8,128)} %bitcast.3), channel_id=1, source_target_pairs={{0,8},{4,12},{8,0},{12,4},{1,9},{5,13},{9,1},{13,5},{2,10},{6,14},... | collective-permute-start | bytes 786440 | tf_op jit(solution)/shard_map/ppermute | solution.py:274
  12.5 1.7 %shard_map.58 = f32[16,16,256]{2,1,0:T(8,128)} custom-call(f32[16,16,4096]{2,1,0:T(8,128)} %x_ref.9), custom_call_target="tpu_custom_call" | custom-call | tf_op jit(solution)/shard_map/pallas_call | solution.py:59
  14.3 2.0 %collective-permute-start.3 = (f32[256,256]{1,0:T(8,128)}, f32[256,256]{1,0:T(8,128)S(1)}, u32[]{:S(2)}, u32[]{:S(2)}) collective-permute-start(f32[256,256]{1,0:T(8,128)} %bitcast.6), channel_id=1, source_target_pairs={{0,8},{4,12},{8,0},{12,4},{1,9},{5,13},{9,1},{13,5},{2,10},{6,14},... | collective-permute-start | bytes 786440 | tf_op jit(solution)/shard_map/ppermute | solution.py:274
  16.3 1.1 %shard_map.52 = f32[16,16,512]{2,1,0:T(8,128)S(1)} custom-call(f32[16,16,4096]{2,1,0:T(8,128)} %x_ref.9), custom_call_target="tpu_custom_call" | custom-call | tf_op jit(solution)/shard_map/pallas_call | solution.py:59
  17.5 1.0 %shard_map.53.refs_0_ = f32[512,512]{1,0:T(8,128)S(1)} custom-call(f32[4,512,256]{2,1,0:T(8,128)S(1)} %copy-done.1, f32[256,512]{1,0:T(8,128)S(1)} %bitcast.9), custom_call_target="tpu_custom_call" | custom-call | tf_op jit(solution)/shard_map/pallas_call | solution.py:82
  18.5 2.3 %collective-permute-done.1.x_ref = f32[256,512]{1,0:T(8,128)} collective-permute-done((f32[256,512]{1,0:T(8,128)}, f32[256,512]{1,0:T(8,128)}, u32[]{:S(2)}, u32[]{:S(2)}) %collective-permute-start.1) | collective-permute-done | bytes 524320 | tf_op jit(solution)/shard_map/ppermute | solution.py:274
  20.8 2.0 %shard_map.54.refs_0_ = f32[512,512]{1,0:T(8,128)S(1)} custom-call(f32[4,512,256]{2,1,0:T(8,128)S(1)} %copy-done.1, f32[256,512]{1,0:T(8,128)} %collective-permute-done.1.x_ref, f32[512,512]{1,0:T(8,128)S(1)} %shard_map.53.refs_0_), custom_call_target="tpu_custom_call" | custom-call | tf_op jit(solution)/shard_map/pallas_call | solution.py:82
  22.9 8.2 %collective-permute-done.x_ref = f32[256,512]{1,0:T(8,128)S(1)} collective-permute-done((f32[256,512]{1,0:T(8,128)}, f32[256,512]{1,0:T(8,128)S(1)}, u32[]{:S(2)}, u32[]{:S(2)}) %collective-permute-start) | collective-permute-done | bytes 524320 | tf_op jit(solution)/shard_map/ppermute | solution.py:274
  31.1 1.0 %shard_map.55.sum_ref = f32[512,512]{1,0:T(8,128)S(1)} custom-call(f32[4,512,256]{2,1,0:T(8,128)S(1)} %copy-done.1, f32[256,512]{1,0:T(8,128)S(1)} %collective-permute-done.x_ref, f32[512,512]{1,0:T(8,128)S(1)} %shard_map.54.refs_0_), custom_call_target="tpu_custom_call" | custom-call | tf_op jit(solution)/shard_map/pallas_call | solution.py:82
  32.1 16.0 %collective-permute-done.2.x_ref = f32[256,256]{1,0:T(8,128)} collective-permute-done((f32[256,256]{1,0:T(8,128)}, f32[256,256]{1,0:T(8,128)}, u32[]{:S(2)}, u32[]{:S(2)}) %collective-permute-start.2) | collective-permute-done | bytes 262176 | tf_op jit(solution)/shard_map/ppermute | solution.py:274
  48.1 2.8 %shard_map.57 = (f32[256,256]{1,0:T(8,128)S(1)}, f32[256,256]{1,0:T(8,128)S(1)}, f32[16,128]{1,0:T(8,128)S(1)}, f32[16,128]{1,0:T(8,128)S(1)}) custom-call(f32[4,512,256]{2,1,0:T(8,128)S(1)} %copy-done.1, f32[512,512]{1,0:T(8,128)S(1)} %shard_map.55.sum_ref, f32[256,256]{1,0:T(8,128)} %collective-permute-done.2.x_ref, ...), custom_call_target="tpu_custom_call" | custom-call | tf_op jit(solution)/shard_map/pallas_call | solution.py:132
  50.9 0.1 collective-permute-start.4
  51.0 2.5 %collective-permute-done.3.x_ref = f32[256,256]{1,0:T(8,128)S(1)} collective-permute-done((f32[256,256]{1,0:T(8,128)}, f32[256,256]{1,0:T(8,128)S(1)}, u32[]{:S(2)}, u32[]{:S(2)}) %collective-permute-start.3) | collective-permute-done | bytes 262176 | tf_op jit(solution)/shard_map/ppermute | solution.py:274
  53.5 0.0 collective-permute-done.4.refs_2_
  53.5 1.9 %shard_map.59 = (f32[256,256]{1,0:T(8,128)S(1)}, f32[256,256]{1,0:T(8,128)S(1)}, f32[16,128]{1,0:T(8,128)S(1)}, f32[16,128]{1,0:T(8,128)S(1)}) custom-call(f32[4,512,256]{2,1,0:T(8,128)S(1)} %copy-done.1, f32[512,512]{1,0:T(8,128)S(1)} %shard_map.55.sum_ref, f32[256,256]{1,0:T(8,128)S(1)} %collective-permute-done.3.x_ref, ...), custom_call_target="tpu_custom_call" | custom-call | tf_op jit(solution)/shard_map/pallas_call | solution.py:132
  55.4 0.1 collective-permute-start.5
  55.5 1.2 %collective-permute-done.5 = f32[16,128]{1,0:T(8,128)S(1)} collective-permute-done((f32[16,128]{1,0:T(8,128)S(1)}, f32[16,128]{1,0:T(8,128)S(1)}, u32[]{:S(2)}, u32[]{:S(2)}) %collective-permute-start.5) | collective-permute-done | bytes 8224 | tf_op jit(solution)/shard_map/ppermute | solution.py:249
  56.7 1.5 %collective-permute-start.6 = (f32[16,128]{1,0:T(8,128)S(1)}, f32[16,128]{1,0:T(8,128)S(1)}, u32[]{:S(2)}, u32[]{:S(2)}) collective-permute-start(f32[16,128]{1,0:T(8,128)S(1)} %add.14), channel_id=1, source_target_pairs={{0,2},{2,0},{1,3},{3,1},{4,6},{6,4},{5,7},{7,5},{8,10},{10,8},{9,1... | collective-permute-start | bytes 24584 | tf_op jit(solution)/shard_map/ppermute | solution.py:249
  58.1 2.2 %collective-permute-done.6 = f32[16,128]{1,0:T(8,128)S(1)} collective-permute-done((f32[16,128]{1,0:T(8,128)S(1)}, f32[16,128]{1,0:T(8,128)S(1)}, u32[]{:S(2)}, u32[]{:S(2)}) %collective-permute-start.6) | collective-permute-done | bytes 8224 | tf_op jit(solution)/shard_map/ppermute | solution.py:249
  60.3 0.0 collective-permute-start.7
  60.3 3.6 %collective-permute-done.7 = f32[16,128]{1,0:T(8,128)S(1)} collective-permute-done((f32[16,128]{1,0:T(8,128)S(1)}, f32[16,128]{1,0:T(8,128)S(1)}, u32[]{:S(2)}, u32[]{:S(2)}) %collective-permute-start.7) | collective-permute-done | bytes 8224 | tf_op jit(solution)/shard_map/ppermute | solution.py:249
  64.0 0.2 collective-permute-start.9
  64.2 4.3 %collective-permute-done.9.refs_5_ = f32[16,128]{1,0:T(8,128)S(1)} collective-permute-done((f32[16,128]{1,0:T(8,128)S(1)}, f32[16,128]{1,0:T(8,128)S(1)}, u32[]{:S(2)}, u32[]{:S(2)}) %collective-permute-start.9) | collective-permute-done | bytes 8224 | tf_op jit(solution)/shard_map/ppermute | solution.py:249
  68.5 0.0 collective-permute-done.8.refs_3_
  68.5 2.6 %shard_map.60 = (f32[8,2,16,1024]{3,2,1,0:T(8,128)}, f32[2,8,16,16]{3,2,1,0:T(8,128)}) custom-call(f32[256,256]{1,0:T(8,128)S(1)} %get-tuple-element.14.refs_0_, f32[256,256]{1,0:T(8,128)S(1)} %get-tuple-element.19.refs_1_, f32[256,256]{1,0:T(8,128)S(1)} %collective-permute-done.4.refs_2_, f32[256,256]{1,0:T(8,128)S(1)} %collective-permute-done.8.refs_3_, ...), custom_call_target="tpu_custom_call" | custom-call | tf_op jit(solution)/shard_map/pallas_call | solution.py:238
  (7 shorter events, 0.0 us)
Async XLA Ops:
  0.6 17.9 %copy-start = (f32[1024]{0:T(1024)S(1)}, f32[1024]{0:T(1024)}, u32[]{:S(2)}) copy-start(f32[1024]{0:T(1024)} %param.4) | copy-start | bytes 12292
  2.6 18.2 %collective-permute-start.1 = (f32[256,512]{1,0:T(8,128)}, f32[256,512]{1,0:T(8,128)}, u32[]{:S(2)}, u32[]{:S(2)}) collective-permute-start(f32[256,512]{1,0:T(8,128)} %bitcast.1), channel_id=1, source_target_pairs={{0,4},{4,8},{8,12},{12,0},{1,5},{5,9},{9,13},{13,1},{2,6},{6,10},{... | collective-permute-start | bytes 1572872 | tf_op jit(solution)/shard_map/ppermute | solution.py:274
  7.6 23.5 %collective-permute-start = (f32[256,512]{1,0:T(8,128)}, f32[256,512]{1,0:T(8,128)S(1)}, u32[]{:S(2)}, u32[]{:S(2)}) collective-permute-start(f32[256,512]{1,0:T(8,128)} %bitcast), channel_id=1, source_target_pairs={{0,12},{4,0},{8,4},{12,8},{1,13},{5,1},{9,5},{13,9},{2,14},{6,2},{... | collective-permute-start | bytes 1572872 | tf_op jit(solution)/shard_map/ppermute | solution.py:274
  11.5 6.0 %copy-start.1 = (f32[4,512,256]{2,1,0:T(8,128)S(1)}, f32[4,512,256]{2,1,0:T(8,128)}, u32[]{:S(2)}) copy-start(f32[4,512,256]{2,1,0:T(8,128)} %constant.12.clone.t_ref) | copy-start | bytes 6291460
  11.5 36.6 %collective-permute-start.2 = (f32[256,256]{1,0:T(8,128)}, f32[256,256]{1,0:T(8,128)}, u32[]{:S(2)}, u32[]{:S(2)}) collective-permute-start(f32[256,256]{1,0:T(8,128)} %bitcast.3), channel_id=1, source_target_pairs={{0,8},{4,12},{8,0},{12,4},{1,9},{5,13},{9,1},{13,5},{2,10},{6,14},... | collective-permute-start | bytes 786440 | tf_op jit(solution)/shard_map/ppermute | solution.py:274
  14.3 39.3 %collective-permute-start.3 = (f32[256,256]{1,0:T(8,128)}, f32[256,256]{1,0:T(8,128)S(1)}, u32[]{:S(2)}, u32[]{:S(2)}) collective-permute-start(f32[256,256]{1,0:T(8,128)} %bitcast.6), channel_id=1, source_target_pairs={{0,8},{4,12},{8,0},{12,4},{1,9},{5,13},{9,1},{13,5},{2,10},{6,14},... | collective-permute-start | bytes 786440 | tf_op jit(solution)/shard_map/ppermute | solution.py:274
  50.9 2.6 %collective-permute-start.4 = (f32[256,256]{1,0:T(8,128)S(1)}, f32[256,256]{1,0:T(8,128)S(1)}, u32[]{:S(2)}, u32[]{:S(2)}) collective-permute-start(f32[256,256]{1,0:T(8,128)S(1)} %get-tuple-element.15), channel_id=1, source_target_pairs={{0,1},{1,0},{2,3},{3,2},{4,5},{5,4},{6,7},{7,6},{8,9},{9,8},{10,11... | collective-permute-start | bytes 786440 | tf_op jit(solution)/shard_map/ppermute | solution.py:249
  55.4 1.2 %collective-permute-start.5 = (f32[16,128]{1,0:T(8,128)S(1)}, f32[16,128]{1,0:T(8,128)S(1)}, u32[]{:S(2)}, u32[]{:S(2)}) collective-permute-start(f32[16,128]{1,0:T(8,128)S(1)} %get-tuple-element.22), channel_id=1, source_target_pairs={{0,1},{1,0},{2,3},{3,2},{4,5},{5,4},{6,7},{7,6},{8,9},{9,8},{10,11... | collective-permute-start | bytes 24584 | tf_op jit(solution)/shard_map/ppermute | solution.py:249
  56.7 3.7 %collective-permute-start.6 = (f32[16,128]{1,0:T(8,128)S(1)}, f32[16,128]{1,0:T(8,128)S(1)}, u32[]{:S(2)}, u32[]{:S(2)}) collective-permute-start(f32[16,128]{1,0:T(8,128)S(1)} %add.14), channel_id=1, source_target_pairs={{0,2},{2,0},{1,3},{3,1},{4,6},{6,4},{5,7},{7,5},{8,10},{10,8},{9,1... | collective-permute-start | bytes 24584 | tf_op jit(solution)/shard_map/ppermute | solution.py:249
  60.3 3.7 %collective-permute-start.7 = (f32[16,128]{1,0:T(8,128)S(1)}, f32[16,128]{1,0:T(8,128)S(1)}, u32[]{:S(2)}, u32[]{:S(2)}) collective-permute-start(f32[16,128]{1,0:T(8,128)S(1)} %add.15), channel_id=1, source_target_pairs={{0,4},{4,0},{8,12},{12,8},{1,5},{5,1},{9,13},{13,9},{2,6},{6,2},{1... | collective-permute-start | bytes 24584 | tf_op jit(solution)/shard_map/ppermute | solution.py:249
  64.0 4.6 %collective-permute-start.8 = (f32[256,256]{1,0:T(8,128)S(1)}, f32[256,256]{1,0:T(8,128)S(1)}, u32[]{:S(2)}, u32[]{:S(2)}) collective-permute-start(f32[256,256]{1,0:T(8,128)S(1)} %get-tuple-element.24), channel_id=1, source_target_pairs={{0,1},{1,0},{2,3},{3,2},{4,5},{5,4},{6,7},{7,6},{8,9},{9,8},{10,11... | collective-permute-start | bytes 786440 | tf_op jit(solution)/shard_map/ppermute | solution.py:249
  64.0 4.6 %collective-permute-start.9 = (f32[16,128]{1,0:T(8,128)S(1)}, f32[16,128]{1,0:T(8,128)S(1)}, u32[]{:S(2)}, u32[]{:S(2)}) collective-permute-start(f32[16,128]{1,0:T(8,128)S(1)} %add.16.refs_4_), channel_id=1, source_target_pairs={{0,8},{4,12},{8,0},{12,4},{1,9},{5,13},{9,1},{13,5},{2,10},{6,14},... | collective-permute-start | bytes 24584 | tf_op jit(solution)/shard_map/ppermute | solution.py:249

commit v5 on v4

--- a/solution.py
+++ b/solution.py
@@ -88,7 +88,10 @@
 
 def late_kernel(n, k, skip, t_ref, sum_ref, x_ref, w_ref, *refs):
     *before, own_ref, other_ref, gram_ref, lent_ref = refs
-    cols = pl.ds(skip, x_ref.shape[1])
+    size = x_ref.shape[1]
+    cols = pl.ds(skip, size)
+    at = lax.axis_index("freq") * sum_ref.shape[1] + skip
+    weights = w_ref[:, pl.ds(pl.multiple_of(at, 128), size)]
     src = lax.rem(lax.axis_index("space") - k + n, n)
     spectra = sum_ref[:, cols] + dot(t_ref[src], x_ref[...])
     half = spectra.shape[0] // 2
@@ -105,7 +108,7 @@
     packed = []
     for z in halves:
         full = lax.dot_general(
-            z * w_ref[:, cols],
+            z * weights,
             z,
             (((1,), (1,)), ((), ())),
             precision=lax.Precision.HIGHEST,
@@ -143,10 +146,10 @@
 
 def finish_kernel(local, total, parts, *refs):
     own_refs, other_refs = refs[:parts], refs[parts : 2 * parts]
-    *gram_refs, modes_ref, factor_ref = refs[2 * parts :]
+    grams_ref, modes_ref, factor_ref = refs[2 * parts :]
     width = local * NB
     share = modes_ref.shape[3] // 2
-    gram = sum(ref[...] for ref in gram_refs) / total
+    gram = jnp.sum(grams_ref[...].reshape(-1, NB, width), axis=0) / total
     row = lax.broadcasted_iota(jnp.int32, (NB, width), 0)
     col = lax.broadcasted_iota(jnp.int32, (NB, width), 1) % NB
     stacked = [jnp.where(col == j, gram, 0.0) for j in range(NB)]
@@ -242,7 +245,7 @@
             jax.ShapeDtypeStruct((2, local, NB, NB), jnp.float32),
         ),
         compiler_params=pltpu.CompilerParams(vmem_limit_bytes=16 * MIB),
-    )(*own, *other, *grams)
+    )(*own, *other, grams)
 
 
 def partner(value, axis, size, step):
@@ -261,10 +264,8 @@
     blocks, local_times, columns = snapshots.shape
     rows = columns // n
     share = rows // freq_count
-    me = lax.axis_index("freq")
 
     tables = jnp.asarray(dft_blocks(n))
-    own_weights = lax.dynamic_index_in_dim(weights.reshape(freq_count, 1, share), me, 0, False)
 
     last = n // 2
     halves = (0, share // 2)
@@ -284,18 +285,14 @@
         if other:
             other[-1] = partner(other[-1], "freq", freq_count, 1)
             piece, other[-1] = lax.optimization_barrier((piece, other[-1]))
-        mine, traded, *grams = late(tables, n, last, skip, before, piece, own_weights, *grams)
+        mine, traded, *grams = late(tables, n, last, skip, before, piece, weights.reshape(1, rows), *grams)
         own.append(mine)
         other.append(traded)
     gram, lent = grams
     gram = gram + partner(lent, "freq", freq_count, 1)
-    for step in steps(tm_count):
-        gram = gram + partner(gram, "tm", tm_count, step)
-    for step in steps(n)[:-1]:
-        gram = gram + partner(gram, "space", n, step)
     gram, traded = lax.optimization_barrier((gram, other[1]))
     other[1] = partner(traded, "freq", freq_count, 1)
-    grams = [gram, partner(gram, "space", n, steps(n)[-1])]
+    grams = lax.all_gather(gram, ("space", "tm"), tiled=True)
     total = rows * n * tm_count
     return finish(grams, own, other, local, total)
 

time: 71.7 us -> 89.4 us (1.25)
  blocking collectives: 0 us -> 30.5 us
  waiting for transfers between devices: 40.4 us -> 34.2 us
  Pallas kernels: 19.8 us -> 14.8 us
  starting transfers between devices: 10.1 us -> 8.56 us
    all_gather x0 -> x1, blocking collectives: none -> 30.5 us  [on_device(): grams = lax.all_gather(gram, ('space', 'tm'), tiled=True)]
    ppermute x6 -> x3, waiting for transfers between devices: 11.3 us -> 1.16 us  [partner(): return lax.ppermute(value, axis, [(i, i ^ step) for i in range(size)])]
    ppermute x4, waiting for transfers between devices: 29.1 us -> 33.1 us  [send(): return lax.ppermute(sent, 'space', [(i, (i + k) % n) for i in range(n)])]
    pallas_call x5, Pallas kernels: 8.51 us -> 5.51 us  [cut(): pl.pallas_call(functools.partial(cut_kernel, n, k, rows, skip), out_shape...]
    ppermute x6 -> x3, starting transfers between devices: 1.86 us -> 0.32 us  [partner(): return lax.ppermute(value, axis, [(i, i ^ step) for i in range(size)])]
    pallas_call x3, Pallas kernels: 4.07 us -> 3.03 us  [early(): pl.pallas_call(functools.partial(early_kernel, n, k), out_shape=jax.Shape...]
    pallas_call x2, Pallas kernels: 4.67 us -> 3.71 us  [late(): pl.pallas_call(functools.partial(late_kernel, n, k, skip), out_shape=(sha...]
  transfers between devices with their start and end apart: 10 -> 7, of which waited for: 8 -> 5; matrix products, arithmetic and copies ran while one was open for 0% -> 0% of each run, Pallas kernels for 19% -> 10%
where the time goes in v5:
time: 89.4 us; the launch traced here: 88.9 us
  waiting for transfers between devices  34.2 us (38%)
  blocking collectives  30.5 us (34%)
  Pallas kernels  14.8 us (17%)
  starting transfers between devices  8.56 us (10%)
    ppermute x4, waiting for transfers between devices, send(): return lax.ppermute(sent, 'space', [(i, (i + k) % n) for i in range(n)])  33.1 us
    all_gather x1, blocking collectives, on_device(): grams = lax.all_gather(gram, ('space', 'tm'), tiled=True)  30.5 us
    ppermute x4, starting transfers between devices, send(): return lax.ppermute(sent, 'space', [(i, (i + k) % n) for i in range(n)])  8.24 us
    pallas_call x5, Pallas kernels, cut(): pl.pallas_call(functools.partial(cut_kernel, n, k, rows, skip), out_shape...  5.51 us
    pallas_call x2, Pallas kernels, late(): pl.pallas_call(functools.partial(late_kernel, n, k, skip), out_shape=(sha...  3.71 us
    pallas_call x3, Pallas kernels, early(): pl.pallas_call(functools.partial(early_kernel, n, k), out_shape=jax.Shape...  3.03 us
    pallas_call x1, Pallas kernels, finish(): pl.pallas_call(functools.partial(finish_kernel, local, total, len(own)),...  2.56 us
  transfers between devices with their start and end apart: 7, of which 5 were waited for; matrix products, arithmetic and copies ran while one was open for 0% of the time, Pallas kernels for 10%

profile of v5, /device:TPU:0, one launch (start us, length us, event | category | flops | bytes accessed | tf_op | source)
XLA Modules:
  0.0 88.9 jit_solution(8867237988455507468)
XLA Ops:
  0.6 1.2 %shard_map.51 = f32[16,16,512]{2,1,0:T(8,128)S(1)} custom-call(f32[16,16,4096]{2,1,0:T(8,128)} %x_ref.9), custom_call_target="tpu_custom_call" | custom-call | tf_op jit(solution)/shard_map/pallas_call | solution.py:59
  1.8 3.1 %collective-permute-start.1 = (f32[256,512]{1,0:T(8,128)S(1)}, f32[256,512]{1,0:T(8,128)S(1)}, u32[]{:S(2)}, u32[]{:S(2)}) collective-permute-start(f32[256,512]{1,0:T(8,128)S(1)} %bitcast.8), channel_id=1, source_target_pairs={{0,4},{4,8},{8,12},{12,0},{1,5},{5,9},{9,13},{13,1},{2,6},{6,10},{... | collective-permute-start | bytes 1572872 | tf_op jit(solution)/shard_map/ppermute | solution.py:275
  4.9 1.1 %shard_map.50 = f32[16,16,512]{2,1,0:T(8,128)S(1)} custom-call(f32[16,16,4096]{2,1,0:T(8,128)} %x_ref.9), custom_call_target="tpu_custom_call" | custom-call | tf_op jit(solution)/shard_map/pallas_call | solution.py:59
  6.0 2.1 %collective-permute-start = (f32[256,512]{1,0:T(8,128)S(1)}, f32[256,512]{1,0:T(8,128)S(1)}, u32[]{:S(2)}, u32[]{:S(2)}) collective-permute-start(f32[256,512]{1,0:T(8,128)S(1)} %bitcast.7), channel_id=1, source_target_pairs={{0,12},{4,0},{8,4},{12,8},{1,13},{5,1},{9,5},{13,9},{2,14},{6,2},{... | collective-permute-start | bytes 1572872 | tf_op jit(solution)/shard_map/ppermute | solution.py:275
  8.1 1.0 %shard_map.56 = f32[16,16,256]{2,1,0:T(8,128)S(1)} custom-call(f32[16,16,4096]{2,1,0:T(8,128)} %x_ref.9), custom_call_target="tpu_custom_call" | custom-call | tf_op jit(solution)/shard_map/pallas_call | solution.py:59
  9.2 0.0 copy-start
  9.2 1.0 %collective-permute-start.2 = (f32[256,256]{1,0:T(8,128)S(1)}, f32[256,256]{1,0:T(8,128)S(1)}, u32[]{:S(2)}, u32[]{:S(2)}) collective-permute-start(f32[256,256]{1,0:T(8,128)S(1)} %bitcast.10), channel_id=1, source_target_pairs={{0,8},{4,12},{8,0},{12,4},{1,9},{5,13},{9,1},{13,5},{2,10},{6,14},... | collective-permute-start | bytes 786440 | tf_op jit(solution)/shard_map/ppermute | solution.py:275
  10.2 1.0 %shard_map.58 = f32[16,16,256]{2,1,0:T(8,128)S(1)} custom-call(f32[16,16,4096]{2,1,0:T(8,128)} %x_ref.9), custom_call_target="tpu_custom_call" | custom-call | tf_op jit(solution)/shard_map/pallas_call | solution.py:59
  11.3 2.0 %collective-permute-start.3 = (f32[256,256]{1,0:T(8,128)S(1)}, f32[256,256]{1,0:T(8,128)S(1)}, u32[]{:S(2)}, u32[]{:S(2)}) collective-permute-start(f32[256,256]{1,0:T(8,128)S(1)} %bitcast.9), channel_id=1, source_target_pairs={{0,8},{4,12},{8,0},{12,4},{1,9},{5,13},{9,1},{13,5},{2,10},{6,14},... | collective-permute-start | bytes 786440 | tf_op jit(solution)/shard_map/ppermute | solution.py:275
  13.3 1.1 %shard_map.52 = f32[16,16,512]{2,1,0:T(8,128)S(1)} custom-call(f32[16,16,4096]{2,1,0:T(8,128)} %x_ref.9), custom_call_target="tpu_custom_call" | custom-call | tf_op jit(solution)/shard_map/pallas_call | solution.py:59
  14.4 0.0 copy-done
  14.4 1.0 %shard_map.53.refs_0_ = f32[512,512]{1,0:T(8,128)S(1)} custom-call(f32[4,512,256]{2,1,0:T(8,128)S(1)} %copy-done, f32[256,512]{1,0:T(8,128)S(1)} %bitcast.6), custom_call_target="tpu_custom_call" | custom-call | tf_op jit(solution)/shard_map/pallas_call | solution.py:82
  15.4 0.0 copy-start.1
  15.5 4.2 %collective-permute-done.1.x_ref = f32[256,512]{1,0:T(8,128)S(1)} collective-permute-done((f32[256,512]{1,0:T(8,128)S(1)}, f32[256,512]{1,0:T(8,128)S(1)}, u32[]{:S(2)}, u32[]{:S(2)}) %collective-permute-start.1) | collective-permute-done | bytes 524320 | tf_op jit(solution)/shard_map/ppermute | solution.py:275
  19.7 1.0 %shard_map.54.refs_0_ = f32[512,512]{1,0:T(8,128)S(1)} custom-call(f32[4,512,256]{2,1,0:T(8,128)S(1)} %copy-done, f32[256,512]{1,0:T(8,128)S(1)} %collective-permute-done.1.x_ref, f32[512,512]{1,0:T(8,128)S(1)} %shard_map.53.refs_0_), custom_call_target="tpu_custom_call" | custom-call | tf_op jit(solution)/shard_map/pallas_call | solution.py:82
  20.7 9.3 %collective-permute-done.x_ref = f32[256,512]{1,0:T(8,128)S(1)} collective-permute-done((f32[256,512]{1,0:T(8,128)S(1)}, f32[256,512]{1,0:T(8,128)S(1)}, u32[]{:S(2)}, u32[]{:S(2)}) %collective-permute-start) | collective-permute-done | bytes 524320 | tf_op jit(solution)/shard_map/ppermute | solution.py:275
  30.1 1.0 %shard_map.55.sum_ref = f32[512,512]{1,0:T(8,128)S(1)} custom-call(f32[4,512,256]{2,1,0:T(8,128)S(1)} %copy-done, f32[256,512]{1,0:T(8,128)S(1)} %collective-permute-done.x_ref, f32[512,512]{1,0:T(8,128)S(1)} %shard_map.54.refs_0_), custom_call_target="tpu_custom_call" | custom-call | tf_op jit(solution)/shard_map/pallas_call | solution.py:82
  31.1 15.9 %collective-permute-done.2.x_ref = f32[256,256]{1,0:T(8,128)S(1)} collective-permute-done((f32[256,256]{1,0:T(8,128)S(1)}, f32[256,256]{1,0:T(8,128)S(1)}, u32[]{:S(2)}, u32[]{:S(2)}) %collective-permute-start.2) | collective-permute-done | bytes 262176 | tf_op jit(solution)/shard_map/ppermute | solution.py:275
  47.0 0.0 copy-done.1
  47.0 1.9 %shard_map.57 = (f32[256,256]{1,0:T(8,128)S(1)}, f32[256,256]{1,0:T(8,128)S(1)}, f32[16,128]{1,0:T(8,128)S(1)}, f32[16,128]{1,0:T(8,128)S(1)}) custom-call(f32[4,512,256]{2,1,0:T(8,128)S(1)} %copy-done, f32[512,512]{1,0:T(8,128)S(1)} %shard_map.55.sum_ref, f32[256,256]{1,0:T(8,128)S(1)} %collective-permute-done.2.x_ref, f32[1,1024]{1,0:T(1,128)S(1)} %bitcast.11), custom_call_target="tpu_custom_call" | custom-call | tf_op jit(solution)/shard_map/pallas_call | solution.py:135
  48.9 0.1 collective-permute-start.4
  48.9 3.6 %collective-permute-done.3.x_ref = f32[256,256]{1,0:T(8,128)S(1)} collective-permute-done((f32[256,256]{1,0:T(8,128)S(1)}, f32[256,256]{1,0:T(8,128)S(1)}, u32[]{:S(2)}, u32[]{:S(2)}) %collective-permute-start.3) | collective-permute-done | bytes 262176 | tf_op jit(solution)/shard_map/ppermute | solution.py:275
  52.5 0.0 collective-permute-done.4.refs_2_
  52.5 1.9 %shard_map.59 = (f32[256,256]{1,0:T(8,128)S(1)}, f32[256,256]{1,0:T(8,128)S(1)}, f32[16,128]{1,0:T(8,128)S(1)}, f32[16,128]{1,0:T(8,128)S(1)}) custom-call(f32[4,512,256]{2,1,0:T(8,128)S(1)} %copy-done, f32[512,512]{1,0:T(8,128)S(1)} %shard_map.55.sum_ref, f32[256,256]{1,0:T(8,128)S(1)} %collective-permute-done.3.x_ref, f32[1,1024]{1,0:T(1,128)S(1)} %bitcast.12, ...), custom_call_target="tpu_custom_call" | custom-call | tf_op jit(solution)/shard_map/pallas_call | solution.py:135
  54.4 0.1 collective-permute-start.5
  54.5 1.2 %collective-permute-done.5 = f32[16,128]{1,0:T(8,128)S(1)} collective-permute-done((f32[16,128]{1,0:T(8,128)S(1)}, f32[16,128]{1,0:T(8,128)S(1)}, u32[]{:S(2)}, u32[]{:S(2)}) %collective-permute-start.5) | collective-permute-done | bytes 8224 | tf_op jit(solution)/shard_map/ppermute | solution.py:252
  55.6 0.2 collective-permute-start.6
  55.8 30.5 %all_gather.3.refs_4_ = f32[128,128]{1,0:T(8,128)S(1)} all-gather(f32[16,128]{1,0:T(8,128)S(1)} %add.3), channel_id=1, replica_groups=mesh['groups'=2,'space'=4,'tm'=2,'freq'=2] {'space','tm'}, dimensions={0}, use_global_device_ids=true | all-gather | bytes 73728 | tf_op jit(solution)/shard_map/all_gather | solution.py:295
  86.3 0.0 collective-permute-done.6.refs_3_
  86.3 2.6 %shard_map.60 = (f32[8,2,16,1024]{3,2,1,0:T(8,128)}, f32[2,8,16,16]{3,2,1,0:T(8,128)}) custom-call(f32[256,256]{1,0:T(8,128)S(1)} %get-tuple-element.14.refs_0_, f32[256,256]{1,0:T(8,128)S(1)} %get-tuple-element.19.refs_1_, f32[256,256]{1,0:T(8,128)S(1)} %collective-permute-done.4.refs_2_, f32[256,256]{1,0:T(8,128)S(1)} %collective-permute-done.6.refs_3_, ...), custom_call_target="tpu_custom_call" | custom-call | tf_op jit(solution)/shard_map/pallas_call | solution.py:241
  (1 shorter events, 0.0 us)
Async XLA Ops:
  1.8 17.9 %collective-permute-start.1 = (f32[256,512]{1,0:T(8,128)S(1)}, f32[256,512]{1,0:T(8,128)S(1)}, u32[]{:S(2)}, u32[]{:S(2)}) collective-permute-start(f32[256,512]{1,0:T(8,128)S(1)} %bitcast.8), channel_id=1, source_target_pairs={{0,4},{4,8},{8,12},{12,0},{1,5},{5,9},{9,13},{13,1},{2,6},{6,10},{... | collective-permute-start | bytes 1572872 | tf_op jit(solution)/shard_map/ppermute | solution.py:275
  6.0 24.0 %collective-permute-start = (f32[256,512]{1,0:T(8,128)S(1)}, f32[256,512]{1,0:T(8,128)S(1)}, u32[]{:S(2)}, u32[]{:S(2)}) collective-permute-start(f32[256,512]{1,0:T(8,128)S(1)} %bitcast.7), channel_id=1, source_target_pairs={{0,12},{4,0},{8,4},{12,8},{1,13},{5,1},{9,5},{13,9},{2,14},{6,2},{... | collective-permute-start | bytes 1572872 | tf_op jit(solution)/shard_map/ppermute | solution.py:275
  9.2 5.3 %copy-start = (f32[4,512,256]{2,1,0:T(8,128)S(1)}, f32[4,512,256]{2,1,0:T(8,128)}, u32[]{:S(2)}) copy-start(f32[4,512,256]{2,1,0:T(8,128)} %constant.2.clone.t_ref) | copy-start | bytes 6291460
  9.2 37.8 %collective-permute-start.2 = (f32[256,256]{1,0:T(8,128)S(1)}, f32[256,256]{1,0:T(8,128)S(1)}, u32[]{:S(2)}, u32[]{:S(2)}) collective-permute-start(f32[256,256]{1,0:T(8,128)S(1)} %bitcast.10), channel_id=1, source_target_pairs={{0,8},{4,12},{8,0},{12,4},{1,9},{5,13},{9,1},{13,5},{2,10},{6,14},... | collective-permute-start | bytes 786440 | tf_op jit(solution)/shard_map/ppermute | solution.py:275
  11.3 41.2 %collective-permute-start.3 = (f32[256,256]{1,0:T(8,128)S(1)}, f32[256,256]{1,0:T(8,128)S(1)}, u32[]{:S(2)}, u32[]{:S(2)}) collective-permute-start(f32[256,256]{1,0:T(8,128)S(1)} %bitcast.9), channel_id=1, source_target_pairs={{0,8},{4,12},{8,0},{12,4},{1,9},{5,13},{9,1},{13,5},{2,10},{6,14},... | collective-permute-start | bytes 786440 | tf_op jit(solution)/shard_map/ppermute | solution.py:275
  15.4 31.6 %copy-start.1 = (f32[1024]{0:T(1024)S(1)}, f32[1024]{0:T(1024)}, u32[]{:S(2)}) copy-start(f32[1024]{0:T(1024)} %param.4) | copy-start | bytes 12292
  48.9 3.7 %collective-permute-start.4 = (f32[256,256]{1,0:T(8,128)S(1)}, f32[256,256]{1,0:T(8,128)S(1)}, u32[]{:S(2)}, u32[]{:S(2)}) collective-permute-start(f32[256,256]{1,0:T(8,128)S(1)} %get-tuple-element.15), channel_id=1, source_target_pairs={{0,1},{1,0},{2,3},{3,2},{4,5},{5,4},{6,7},{7,6},{8,9},{9,8},{10,11... | collective-permute-start | bytes 786440 | tf_op jit(solution)/shard_map/ppermute | solution.py:252
  54.4 1.2 %collective-permute-start.5 = (f32[16,128]{1,0:T(8,128)S(1)}, f32[16,128]{1,0:T(8,128)S(1)}, u32[]{:S(2)}, u32[]{:S(2)}) collective-permute-start(f32[16,128]{1,0:T(8,128)S(1)} %get-tuple-element.22), channel_id=1, source_target_pairs={{0,1},{1,0},{2,3},{3,2},{4,5},{5,4},{6,7},{7,6},{8,9},{9,8},{10,11... | collective-permute-start | bytes 24584 | tf_op jit(solution)/shard_map/ppermute | solution.py:252
  55.6 30.7 %collective-permute-start.6 = (f32[256,256]{1,0:T(8,128)S(1)}, f32[256,256]{1,0:T(8,128)S(1)}, u32[]{:S(2)}, u32[]{:S(2)}) collective-permute-start(f32[256,256]{1,0:T(8,128)S(1)} %get-tuple-element.24), channel_id=1, source_target_pairs={{0,1},{1,0},{2,3},{3,2},{4,5},{5,4},{6,7},{7,6},{8,9},{9,8},{10,11... | collective-permute-start | bytes 786440 | tf_op jit(solution)/shard_map/ppermute | solution.py:252

commit v6 on v5

--- a/solution.py
+++ b/solution.py
@@ -149,7 +149,7 @@
     grams_ref, modes_ref, factor_ref = refs[2 * parts :]
     width = local * NB
     share = modes_ref.shape[3] // 2
-    gram = jnp.sum(grams_ref[...].reshape(-1, NB, width), axis=0) / total
+    gram = jnp.sum(grams_ref[...], axis=0) / total
     row = lax.broadcasted_iota(jnp.int32, (NB, width), 0)
     col = lax.broadcasted_iota(jnp.int32, (NB, width), 1) % NB
     stacked = [jnp.where(col == j, gram, 0.0) for j in range(NB)]
@@ -292,7 +292,8 @@
     gram = gram + partner(lent, "freq", freq_count, 1)
     gram, traded = lax.optimization_barrier((gram, other[1]))
     other[1] = partner(traded, "freq", freq_count, 1)
-    grams = lax.all_gather(gram, ("space", "tm"), tiled=True)
+    grams = jnp.broadcast_to(gram, (n * tm_count,) + gram.shape)
+    grams = lax.all_to_all(grams, ("space", "tm"), split_axis=0, concat_axis=0, tiled=True)
     total = rows * n * tm_count
     return finish(grams, own, other, local, total)
 

time: 89.4 us -> 69.4 us (0.78)
  blocking collectives: 30.5 us -> 10.5 us
    all_gather x1 -> x0, blocking collectives: 30.5 us -> none  [on_device(): grams = lax.all_gather(gram, ('space', 'tm'), tiled=True)]
    all_to_all x0 -> x1, blocking collectives: none -> 10.5 us  [on_device(): lax.all_to_all(grams, ('space', 'tm'), split_axis=0, concat_axis=0, tiled...]
  transfers between devices with their start and end apart: 7 -> 7, of which waited for: 5 -> 5; matrix products, arithmetic and copies ran while one was open for 0% -> 0% of each run, Pallas kernels for 10% -> 13%
where the time goes in v6:
time: 69.4 us; the launch traced here: 68.9 us
  waiting for transfers between devices  34.2 us (49%)
  Pallas kernels  14.8 us (21%)
  blocking collectives  10.5 us (15%)
  starting transfers between devices  8.56 us (12%)
  between operations  0.75 us (1%)
    ppermute x4, waiting for transfers between devices, send(): return lax.ppermute(sent, 'space', [(i, (i + k) % n) for i in range(n)])  33.1 us
    all_to_all x1, blocking collectives, on_device(): lax.all_to_all(grams, ('space', 'tm'), split_axis=0, concat_axis=0, tiled...  10.5 us
    ppermute x4, starting transfers between devices, send(): return lax.ppermute(sent, 'space', [(i, (i + k) % n) for i in range(n)])  8.24 us
    pallas_call x5, Pallas kernels, cut(): pl.pallas_call(functools.partial(cut_kernel, n, k, rows, skip), out_shape...  5.51 us
    pallas_call x2, Pallas kernels, late(): pl.pallas_call(functools.partial(late_kernel, n, k, skip), out_shape=(sha...  3.71 us
    pallas_call x3, Pallas kernels, early(): pl.pallas_call(functools.partial(early_kernel, n, k), out_shape=jax.Shape...  3.03 us
    pallas_call x1, Pallas kernels, finish(): pl.pallas_call(functools.partial(finish_kernel, local, total, len(own)),...  2.56 us
  transfers between devices with their start and end apart: 7, of which 5 were waited for; matrix products, arithmetic and copies ran while one was open for 0% of the time, Pallas kernels for 13%

profile of v6, /device:TPU:0, one launch (start us, length us, event | category | flops | bytes accessed | tf_op | source)
XLA Modules:
  0.0 68.9 jit_solution(6158087753558266495)
XLA Ops:
  0.6 1.2 %shard_map.51 = f32[16,16,512]{2,1,0:T(8,128)S(1)} custom-call(f32[16,16,4096]{2,1,0:T(8,128)} %x_ref.9), custom_call_target="tpu_custom_call" | custom-call | tf_op jit(solution)/shard_map/pallas_call | solution.py:59
  1.8 3.1 %collective-permute-start.1 = (f32[256,512]{1,0:T(8,128)S(1)}, f32[256,512]{1,0:T(8,128)S(1)}, u32[]{:S(2)}, u32[]{:S(2)}) collective-permute-start(f32[256,512]{1,0:T(8,128)S(1)} %bitcast.8), channel_id=1, source_target_pairs={{0,4},{4,8},{8,12},{12,0},{1,5},{5,9},{9,13},{13,1},{2,6},{6,10},{... | collective-permute-start | bytes 1572872 | tf_op jit(solution)/shard_map/ppermute | solution.py:275
  4.9 1.1 %shard_map.50 = f32[16,16,512]{2,1,0:T(8,128)S(1)} custom-call(f32[16,16,4096]{2,1,0:T(8,128)} %x_ref.9), custom_call_target="tpu_custom_call" | custom-call | tf_op jit(solution)/shard_map/pallas_call | solution.py:59
  6.0 2.1 %collective-permute-start = (f32[256,512]{1,0:T(8,128)S(1)}, f32[256,512]{1,0:T(8,128)S(1)}, u32[]{:S(2)}, u32[]{:S(2)}) collective-permute-start(f32[256,512]{1,0:T(8,128)S(1)} %bitcast.7), channel_id=1, source_target_pairs={{0,12},{4,0},{8,4},{12,8},{1,13},{5,1},{9,5},{13,9},{2,14},{6,2},{... | collective-permute-start | bytes 1572872 | tf_op jit(solution)/shard_map/ppermute | solution.py:275
  8.1 1.0 %shard_map.56 = f32[16,16,256]{2,1,0:T(8,128)S(1)} custom-call(f32[16,16,4096]{2,1,0:T(8,128)} %x_ref.9), custom_call_target="tpu_custom_call" | custom-call | tf_op jit(solution)/shard_map/pallas_call | solution.py:59
  9.2 0.0 copy-start
  9.2 1.0 %collective-permute-start.2 = (f32[256,256]{1,0:T(8,128)S(1)}, f32[256,256]{1,0:T(8,128)S(1)}, u32[]{:S(2)}, u32[]{:S(2)}) collective-permute-start(f32[256,256]{1,0:T(8,128)S(1)} %bitcast.10), channel_id=1, source_target_pairs={{0,8},{4,12},{8,0},{12,4},{1,9},{5,13},{9,1},{13,5},{2,10},{6,14},... | collective-permute-start | bytes 786440 | tf_op jit(solution)/shard_map/ppermute | solution.py:275
  10.2 1.0 %shard_map.58 = f32[16,16,256]{2,1,0:T(8,128)S(1)} custom-call(f32[16,16,4096]{2,1,0:T(8,128)} %x_ref.9), custom_call_target="tpu_custom_call" | custom-call | tf_op jit(solution)/shard_map/pallas_call | solution.py:59
  11.3 2.0 %collective-permute-start.3 = (f32[256,256]{1,0:T(8,128)S(1)}, f32[256,256]{1,0:T(8,128)S(1)}, u32[]{:S(2)}, u32[]{:S(2)}) collective-permute-start(f32[256,256]{1,0:T(8,128)S(1)} %bitcast.9), channel_id=1, source_target_pairs={{0,8},{4,12},{8,0},{12,4},{1,9},{5,13},{9,1},{13,5},{2,10},{6,14},... | collective-permute-start | bytes 786440 | tf_op jit(solution)/shard_map/ppermute | solution.py:275
  13.3 1.1 %shard_map.52 = f32[16,16,512]{2,1,0:T(8,128)S(1)} custom-call(f32[16,16,4096]{2,1,0:T(8,128)} %x_ref.9), custom_call_target="tpu_custom_call" | custom-call | tf_op jit(solution)/shard_map/pallas_call | solution.py:59
  14.4 0.0 copy-done
  14.4 1.0 %shard_map.53.refs_0_ = f32[512,512]{1,0:T(8,128)S(1)} custom-call(f32[4,512,256]{2,1,0:T(8,128)S(1)} %copy-done, f32[256,512]{1,0:T(8,128)S(1)} %bitcast.6), custom_call_target="tpu_custom_call" | custom-call | tf_op jit(solution)/shard_map/pallas_call | solution.py:82
  15.4 0.0 copy-start.1
  15.5 4.2 %collective-permute-done.1.x_ref = f32[256,512]{1,0:T(8,128)S(1)} collective-permute-done((f32[256,512]{1,0:T(8,128)S(1)}, f32[256,512]{1,0:T(8,128)S(1)}, u32[]{:S(2)}, u32[]{:S(2)}) %collective-permute-start.1) | collective-permute-done | bytes 524320 | tf_op jit(solution)/shard_map/ppermute | solution.py:275
  19.7 1.0 %shard_map.54.refs_0_ = f32[512,512]{1,0:T(8,128)S(1)} custom-call(f32[4,512,256]{2,1,0:T(8,128)S(1)} %copy-done, f32[256,512]{1,0:T(8,128)S(1)} %collective-permute-done.1.x_ref, f32[512,512]{1,0:T(8,128)S(1)} %shard_map.53.refs_0_), custom_call_target="tpu_custom_call" | custom-call | tf_op jit(solution)/shard_map/pallas_call | solution.py:82
  20.7 9.3 %collective-permute-done.x_ref = f32[256,512]{1,0:T(8,128)S(1)} collective-permute-done((f32[256,512]{1,0:T(8,128)S(1)}, f32[256,512]{1,0:T(8,128)S(1)}, u32[]{:S(2)}, u32[]{:S(2)}) %collective-permute-start) | collective-permute-done | bytes 524320 | tf_op jit(solution)/shard_map/ppermute | solution.py:275
  30.1 1.0 %shard_map.55.sum_ref = f32[512,512]{1,0:T(8,128)S(1)} custom-call(f32[4,512,256]{2,1,0:T(8,128)S(1)} %copy-done, f32[256,512]{1,0:T(8,128)S(1)} %collective-permute-done.x_ref, f32[512,512]{1,0:T(8,128)S(1)} %shard_map.54.refs_0_), custom_call_target="tpu_custom_call" | custom-call | tf_op jit(solution)/shard_map/pallas_call | solution.py:82
  31.1 15.9 %collective-permute-done.2.x_ref = f32[256,256]{1,0:T(8,128)S(1)} collective-permute-done((f32[256,256]{1,0:T(8,128)S(1)}, f32[256,256]{1,0:T(8,128)S(1)}, u32[]{:S(2)}, u32[]{:S(2)}) %collective-permute-start.2) | collective-permute-done | bytes 262176 | tf_op jit(solution)/shard_map/ppermute | solution.py:275
  47.0 0.0 copy-done.1
  47.0 1.9 %shard_map.57 = (f32[256,256]{1,0:T(8,128)S(1)}, f32[256,256]{1,0:T(8,128)S(1)}, f32[16,128]{1,0:T(8,128)S(1)}, f32[16,128]{1,0:T(8,128)S(1)}) custom-call(f32[4,512,256]{2,1,0:T(8,128)S(1)} %copy-done, f32[512,512]{1,0:T(8,128)S(1)} %shard_map.55.sum_ref, f32[256,256]{1,0:T(8,128)S(1)} %collective-permute-done.2.x_ref, f32[1,1024]{1,0:T(1,128)S(1)} %bitcast.11), custom_call_target="tpu_custom_call" | custom-call | tf_op jit(solution)/shard_map/pallas_call | solution.py:135
  48.9 0.1 collective-permute-start.4
  48.9 3.6 %collective-permute-done.3.x_ref = f32[256,256]{1,0:T(8,128)S(1)} collective-permute-done((f32[256,256]{1,0:T(8,128)S(1)}, f32[256,256]{1,0:T(8,128)S(1)}, u32[]{:S(2)}, u32[]{:S(2)}) %collective-permute-start.3) | collective-permute-done | bytes 262176 | tf_op jit(solution)/shard_map/ppermute | solution.py:275
  52.5 0.0 collective-permute-done.4.refs_2_
  52.5 1.9 %shard_map.59 = (f32[256,256]{1,0:T(8,128)S(1)}, f32[256,256]{1,0:T(8,128)S(1)}, f32[16,128]{1,0:T(8,128)S(1)}, f32[16,128]{1,0:T(8,128)S(1)}) custom-call(f32[4,512,256]{2,1,0:T(8,128)S(1)} %copy-done, f32[512,512]{1,0:T(8,128)S(1)} %shard_map.55.sum_ref, f32[256,256]{1,0:T(8,128)S(1)} %collective-permute-done.3.x_ref, f32[1,1024]{1,0:T(1,128)S(1)} %bitcast.12, ...), custom_call_target="tpu_custom_call" | custom-call | tf_op jit(solution)/shard_map/pallas_call | solution.py:135
  54.4 0.1 collective-permute-start.5
  54.5 1.2 %collective-permute-done.5 = f32[16,128]{1,0:T(8,128)S(1)} collective-permute-done((f32[16,128]{1,0:T(8,128)S(1)}, f32[16,128]{1,0:T(8,128)S(1)}, u32[]{:S(2)}, u32[]{:S(2)}) %collective-permute-start.5) | collective-permute-done | bytes 8224 | tf_op jit(solution)/shard_map/ppermute | solution.py:252
  55.6 0.2 collective-permute-start.6
  55.8 10.5 %all_to_all.5.refs_4_ = f32[8,16,128]{2,1,0:T(8,128)S(1)} all-to-all(f32[8,16,128]{2,1,0:T(8,128)S(1)} %broadcast_in_dim.3), channel_id=1, replica_groups=mesh['groups'=2,'space'=4,'tm'=2,'freq'=2] {'space','tm'}, dimensions={0} | all-to-all | bytes 131072 | tf_op jit(solution)/shard_map/all_to_all | solution.py:296
  66.3 0.0 collective-permute-done.6.refs_3_
  66.3 2.6 %shard_map.60 = (f32[8,2,16,1024]{3,2,1,0:T(8,128)}, f32[2,8,16,16]{3,2,1,0:T(8,128)}) custom-call(f32[256,256]{1,0:T(8,128)S(1)} %get-tuple-element.14.refs_0_, f32[256,256]{1,0:T(8,128)S(1)} %get-tuple-element.19.refs_1_, f32[256,256]{1,0:T(8,128)S(1)} %collective-permute-done.4.refs_2_, f32[256,256]{1,0:T(8,128)S(1)} %collective-permute-done.6.refs_3_, ...), custom_call_target="tpu_custom_call" | custom-call | tf_op jit(solution)/shard_map/pallas_call | solution.py:241
  (2 shorter events, 0.0 us)
Async XLA Ops:
  1.8 17.9 %collective-permute-start.1 = (f32[256,512]{1,0:T(8,128)S(1)}, f32[256,512]{1,0:T(8,128)S(1)}, u32[]{:S(2)}, u32[]{:S(2)}) collective-permute-start(f32[256,512]{1,0:T(8,128)S(1)} %bitcast.8), channel_id=1, source_target_pairs={{0,4},{4,8},{8,12},{12,0},{1,5},{5,9},{9,13},{13,1},{2,6},{6,10},{... | collective-permute-start | bytes 1572872 | tf_op jit(solution)/shard_map/ppermute | solution.py:275
  6.0 24.0 %collective-permute-start = (f32[256,512]{1,0:T(8,128)S(1)}, f32[256,512]{1,0:T(8,128)S(1)}, u32[]{:S(2)}, u32[]{:S(2)}) collective-permute-start(f32[256,512]{1,0:T(8,128)S(1)} %bitcast.7), channel_id=1, source_target_pairs={{0,12},{4,0},{8,4},{12,8},{1,13},{5,1},{9,5},{13,9},{2,14},{6,2},{... | collective-permute-start | bytes 1572872 | tf_op jit(solution)/shard_map/ppermute | solution.py:275
  9.2 5.3 %copy-start = (f32[4,512,256]{2,1,0:T(8,128)S(1)}, f32[4,512,256]{2,1,0:T(8,128)}, u32[]{:S(2)}) copy-start(f32[4,512,256]{2,1,0:T(8,128)} %constant.2.clone.t_ref) | copy-start | bytes 6291460
  9.2 37.8 %collective-permute-start.2 = (f32[256,256]{1,0:T(8,128)S(1)}, f32[256,256]{1,0:T(8,128)S(1)}, u32[]{:S(2)}, u32[]{:S(2)}) collective-permute-start(f32[256,256]{1,0:T(8,128)S(1)} %bitcast.10), channel_id=1, source_target_pairs={{0,8},{4,12},{8,0},{12,4},{1,9},{5,13},{9,1},{13,5},{2,10},{6,14},... | collective-permute-start | bytes 786440 | tf_op jit(solution)/shard_map/ppermute | solution.py:275
  11.3 41.2 %collective-permute-start.3 = (f32[256,256]{1,0:T(8,128)S(1)}, f32[256,256]{1,0:T(8,128)S(1)}, u32[]{:S(2)}, u32[]{:S(2)}) collective-permute-start(f32[256,256]{1,0:T(8,128)S(1)} %bitcast.9), channel_id=1, source_target_pairs={{0,8},{4,12},{8,0},{12,4},{1,9},{5,13},{9,1},{13,5},{2,10},{6,14},... | collective-permute-start | bytes 786440 | tf_op jit(solution)/shard_map/ppermute | solution.py:275
  15.4 31.6 %copy-start.1 = (f32[1024]{0:T(1024)S(1)}, f32[1024]{0:T(1024)}, u32[]{:S(2)}) copy-start(f32[1024]{0:T(1024)} %param.4) | copy-start | bytes 12292
  48.9 3.7 %collective-permute-start.4 = (f32[256,256]{1,0:T(8,128)S(1)}, f32[256,256]{1,0:T(8,128)S(1)}, u32[]{:S(2)}, u32[]{:S(2)}) collective-permute-start(f32[256,256]{1,0:T(8,128)S(1)} %get-tuple-element.15), channel_id=1, source_target_pairs={{0,1},{1,0},{2,3},{3,2},{4,5},{5,4},{6,7},{7,6},{8,9},{9,8},{10,11... | collective-permute-start | bytes 786440 | tf_op jit(solution)/shard_map/ppermute | solution.py:252
  54.4 1.2 %collective-permute-start.5 = (f32[16,128]{1,0:T(8,128)S(1)}, f32[16,128]{1,0:T(8,128)S(1)}, u32[]{:S(2)}, u32[]{:S(2)}) collective-permute-start(f32[16,128]{1,0:T(8,128)S(1)} %get-tuple-element.22), channel_id=1, source_target_pairs={{0,1},{1,0},{2,3},{3,2},{4,5},{5,4},{6,7},{7,6},{8,9},{9,8},{10,11... | collective-permute-start | bytes 24584 | tf_op jit(solution)/shard_map/ppermute | solution.py:252
  55.6 10.7 %collective-permute-start.6 = (f32[256,256]{1,0:T(8,128)S(1)}, f32[256,256]{1,0:T(8,128)S(1)}, u32[]{:S(2)}, u32[]{:S(2)}) collective-permute-start(f32[256,256]{1,0:T(8,128)S(1)} %get-tuple-element.24), channel_id=1, source_target_pairs={{0,1},{1,0},{2,3},{3,2},{4,5},{5,4},{6,7},{7,6},{8,9},{9,8},{10,11... | collective-permute-start | bytes 786440 | tf_op jit(solution)/shard_map/ppermute | solution.py:252

commit v7 on v6

--- a/solution.py
+++ b/solution.py
@@ -26,11 +26,32 @@
     step = SEGMENT_FRAMES // groups
     table = table.reshape(2, 2, NF // 2, groups, step)
     spread = np.einsum("rhfgt,bc->ghrfbct", table, np.eye(NB))
-    return spread.reshape(groups, 2 * NF * NB, NB * step).astype(np.float32)
-
-
-def dot(a, b):
-    return jnp.dot(a, b, precision=lax.Precision.HIGHEST, preferred_element_type=jnp.float32)
+    spread = spread.reshape(groups, 2 * NF * NB, NB * step).astype(np.float32)
+    high = spread.astype(jnp.bfloat16)
+    low = (spread - high.astype(np.float32)).astype(jnp.bfloat16)
+    return np.concatenate([high, high, low], axis=2)
+
+
+def split(x):
+    high = x.astype(jnp.bfloat16)
+    return high, (x - high.astype(jnp.float32)).astype(jnp.bfloat16)
+
+
+def times_split(left, x):
+    high, low = split(x)
+    right = jnp.concatenate([high, low, high], axis=0)
+    return jnp.dot(left, right, preferred_element_type=jnp.float32)
+
+
+def rows_product(a, b):
+    a_high, a_low = split(a)
+    b_high, b_low = split(b)
+    total = 0.0
+    for x, y in ((a_high, b_high), (a_high, b_low), (a_low, b_high)):
+        total = total + lax.dot_general(
+            x, y, (((1,), (1,)), ((), ())), preferred_element_type=jnp.float32
+        )
+    return total
 
 
 def cut_kernel(n, k, rows, skip, x_ref, o_ref, sem):
@@ -73,7 +94,7 @@
 
 def early_kernel(n, k, t_ref, x_ref, *refs):
     src = lax.rem(lax.axis_index("space") - k + n, n)
-    part = dot(t_ref[src], x_ref[...])
+    part = times_split(t_ref[src], x_ref[...])
     refs[-1][...] = part if len(refs) == 1 else refs[0][...] + part
 
 
@@ -87,13 +108,13 @@
 
 
 def late_kernel(n, k, skip, t_ref, sum_ref, x_ref, w_ref, *refs):
-    *before, own_ref, other_ref, gram_ref, lent_ref = refs
+    *before, own_ref, other_ref, gram_ref = refs
     size = x_ref.shape[1]
     cols = pl.ds(skip, size)
     at = lax.axis_index("freq") * sum_ref.shape[1] + skip
     weights = w_ref[:, pl.ds(pl.multiple_of(at, 128), size)]
     src = lax.rem(lax.axis_index("space") - k + n, n)
-    spectra = sum_ref[:, cols] + dot(t_ref[src], x_ref[...])
+    spectra = sum_ref[:, cols] + times_split(t_ref[src], x_ref[...])
     half = spectra.shape[0] // 2
     width = half // 2
     local = width // NB
@@ -107,13 +128,7 @@
     other_ref[...] = jnp.where(first, halves[1], halves[0])
     packed = []
     for z in halves:
-        full = lax.dot_general(
-            z * weights,
-            z,
-            (((1,), (1,)), ((), ())),
-            precision=lax.Precision.HIGHEST,
-            preferred_element_type=jnp.float32,
-        )
+        full = rows_product(z * weights, z)
         gram_re = full[:width, :width] + full[width:, width:]
         gram_im = full[:width, width:] - full[width:, :width]
         both = []
@@ -121,20 +136,20 @@
             kept = jnp.where(line == lane, part, 0.0)
             both.append(jnp.sum(kept.reshape(local, NB, width), axis=0))
         packed.append(jnp.where(row >= col, both[0], both[1]))
-    gram = jnp.where(first, packed[0], packed[1])
-    lent = jnp.where(first, packed[1], packed[0])
-    gram_ref[...] = gram + before[0][...] if before else gram
-    lent_ref[...] = lent + before[1][...] if before else lent
-
-
-def late(tables, n, k, skip, partial_sum, piece, weights, *before):
+    if before:
+        packed = [packed[h] + before[0][h] for h in range(2)]
+    for d in range(gram_ref.shape[0]):
+        gram_ref[d] = packed[d % 2]
+
+
+def late(tables, n, k, skip, targets, partial_sum, piece, weights, *before):
     share = piece.shape[1]
     half = tables.shape[1] // 2
     shape = jax.ShapeDtypeStruct((half, share), jnp.float32)
-    gram_shape = jax.ShapeDtypeStruct((NB, half // 2), jnp.float32)
+    gram_shape = jax.ShapeDtypeStruct((targets, NB, half // 2), jnp.float32)
     return pl.pallas_call(
         functools.partial(late_kernel, n, k, skip),
-        out_shape=(shape, shape, gram_shape, gram_shape),
+        out_shape=(shape, shape, gram_shape),
         compiler_params=pltpu.CompilerParams(vmem_limit_bytes=16 * MIB),
     )(tables, partial_sum, piece, weights, *before)
 
@@ -146,7 +161,7 @@
 
 def finish_kernel(local, total, parts, *refs):
     own_refs, other_refs = refs[:parts], refs[parts : 2 * parts]
-    grams_ref, modes_ref, factor_ref = refs[2 * parts :]
+    grams_ref, modes_ref, factor_ref, *slots, sem = refs[2 * parts :]
     width = local * NB
     share = modes_ref.shape[3] // 2
     gram = jnp.sum(grams_ref[...], axis=0) / total
@@ -219,21 +234,35 @@
         axis=0,
     )
     me = lax.axis_index("freq")
-    size = share // parts
+    high, low = split(mixing)
+    mixing = jnp.concatenate([high, high, low], axis=1)
+    moves = []
     for k, refs_of in ((0, own_refs), (1, other_refs)):
-        for i, ref in enumerate(refs_of):
-            start = pl.multiple_of(((me + k) % 2) * share + i * size, 128)
-            out = dot(mixing, ref[...])
+        skip = 0
+        for ref in refs_of:
+            size = ref.shape[1]
+            out = times_split(mixing, ref[...])
+            slot = slots[len(moves)]
             for part in range(2):
                 for f in range(local):
                     at = part * width + f * NB
-                    modes_ref[f, part, :, pl.ds(start, size)] = out[at : at + NB]
+                    slot[f, part] = out[at : at + NB]
+            start = pl.multiple_of(((me + k) % 2) * share + skip, 128)
+            moves.append(
+                pltpu.make_async_copy(
+                    slot, modes_ref.at[:, :, :, pl.ds(start, size)], sem.at[len(moves)]
+                )
+            )
+            moves[-1].start()
+            skip += size
     pad = jnp.zeros((width - NB, width), jnp.float32)
     turned_re = jnp.transpose(jnp.concatenate(low_re + [pad], axis=0))
     turned_im = jnp.transpose(jnp.concatenate(low_im + [pad], axis=0))
     for f in range(local):
         factor_ref[0, f] = turned_re[f * NB : (f + 1) * NB, :NB]
         factor_ref[1, f] = -turned_im[f * NB : (f + 1) * NB, :NB]
+    for move in moves:
+        move.wait()
 
 
 def finish(grams, own, other, local, total):
@@ -244,16 +273,20 @@
             jax.ShapeDtypeStruct((local, 2, NB, 2 * share), jnp.float32),
             jax.ShapeDtypeStruct((2, local, NB, NB), jnp.float32),
         ),
+        out_specs=(
+            pl.BlockSpec(memory_space=pltpu.HBM),
+            pl.BlockSpec(memory_space=pltpu.VMEM),
+        ),
+        scratch_shapes=[
+            *[pltpu.VMEM((local, 2, NB, part.shape[1]), jnp.float32) for part in own + other],
+            pltpu.SemaphoreType.DMA((len(own + other),)),
+        ],
         compiler_params=pltpu.CompilerParams(vmem_limit_bytes=16 * MIB),
     )(*own, *other, grams)
 
 
 def partner(value, axis, size, step):
     return lax.ppermute(value, axis, [(i, i ^ step) for i in range(size)])
-
-
-def steps(size):
-    return [1 << b for b in range(size.bit_length() - 1)]
 
 
 def on_device(snapshots, weights):
@@ -268,7 +301,9 @@
     tables = jnp.asarray(dft_blocks(n))
 
     last = n // 2
-    halves = (0, share // 2)
+    early_rows = share - share // 4
+    parts = ((0, early_rows), (early_rows, share - early_rows))
+    targets = n * tm_count * freq_count
 
     def send(k, skip, size):
         sent = cut(snapshots, n, k, rows, skip, size)
@@ -276,24 +311,25 @@
 
     offsets = [k for k in range(1, n) if k != last]
     pieces = [send(k, 0, share) for k in offsets]
-    last_pieces = [send(last, skip, share // 2) for skip in halves]
+    last_pieces = [send(last, skip, size) for skip, size in parts]
     before = early(tables, n, 0, cut(snapshots, n, 0, rows, 0, share))
     for k, piece in zip(offsets, pieces):
         before = early(tables, n, k, piece, before)
     own, other, grams = [], [], []
-    for skip, piece in zip(halves, last_pieces):
+    for (skip, _), piece in zip(parts, last_pieces):
         if other:
             other[-1] = partner(other[-1], "freq", freq_count, 1)
             piece, other[-1] = lax.optimization_barrier((piece, other[-1]))
-        mine, traded, *grams = late(tables, n, last, skip, before, piece, weights.reshape(1, rows), *grams)
+        copies = targets if own else 2
+        mine, traded, *grams = late(
+            tables, n, last, skip, copies, before, piece, weights.reshape(1, rows), *grams
+        )
         own.append(mine)
         other.append(traded)
-    gram, lent = grams
-    gram = gram + partner(lent, "freq", freq_count, 1)
-    gram, traded = lax.optimization_barrier((gram, other[1]))
-    other[1] = partner(traded, "freq", freq_count, 1)
-    grams = jnp.broadcast_to(gram, (n * tm_count,) + gram.shape)
-    grams = lax.all_to_all(grams, ("space", "tm"), split_axis=0, concat_axis=0, tiled=True)
+    other[-1] = partner(other[-1], "freq", freq_count, 1)
+    grams = lax.all_to_all(
+        grams[0], ("space", "tm", "freq"), split_axis=0, concat_axis=0, tiled=True
+    )
     total = rows * n * tm_count
     return finish(grams, own, other, local, total)
 

time: 69.4 us -> 75.1 us (1.082)
  waiting for transfers between devices: 34.2 us -> 49.6 us
  blocking collectives: 10.5 us -> 0 us
  starting transfers between devices: 8.56 us -> 11.5 us
  Pallas kernels: 14.8 us -> 12.7 us
    all_to_all x1 -> x0, blocking collectives: 10.5 us -> none  [on_device(): lax.all_to_all(grams, ('space', 'tm'), split_axis=0, concat_axis=0, tiled...]
    ppermute x4, waiting for transfers between devices: 33.1 us -> 42 us  [send(): return lax.ppermute(sent, 'space', [(i, (i + k) % n) for i in range(n)])]
    all_to_all x0 -> x1, waiting for transfers between devices: none -> 6.52 us  [on_device(): lax.all_to_all(grams[0], ('space', 'tm', 'freq'), split_axis=0, concat_ax...]
    all_to_all x0 -> x1, starting transfers between devices: none -> 4.5 us  [on_device(): lax.all_to_all(grams[0], ('space', 'tm', 'freq'), split_axis=0, concat_ax...]
    ppermute x4, starting transfers between devices: 8.24 us -> 6.53 us  [send(): return lax.ppermute(sent, 'space', [(i, (i + k) % n) for i in range(n)])]
    pallas_call x3, Pallas kernels: 3.03 us -> 1.74 us  [early(): pl.pallas_call(functools.partial(early_kernel, n, k), out_shape=jax.Shape...]
    pallas_call x2, Pallas kernels: 3.71 us -> 2.54 us  [late(): pl.pallas_call(functools.partial(late_kernel, n, k, skip), out_shape=(sha...]
  transfers between devices with their start and end apart: 7 -> 7, of which waited for: 5 -> 6; matrix products, arithmetic and copies ran while one was open for 0% -> 0% of each run, Pallas kernels for 13% -> 8%
where the time goes in v7:
time: 75.1 us; the launch traced here: 74.5 us
  waiting for transfers between devices  49.6 us (66%)
  Pallas kernels  12.7 us (17%)
  starting transfers between devices  11.5 us (15%)
    ppermute x4, waiting for transfers between devices, send(): return lax.ppermute(sent, 'space', [(i, (i + k) % n) for i in range(n)])  42 us
    ppermute x4, starting transfers between devices, send(): return lax.ppermute(sent, 'space', [(i, (i + k) % n) for i in range(n)])  6.53 us
    all_to_all x1, waiting for transfers between devices, on_device(): lax.all_to_all(grams[0], ('space', 'tm', 'freq'), split_axis=0, concat_ax...  6.52 us
    pallas_call x5, Pallas kernels, cut(): pl.pallas_call(functools.partial(cut_kernel, n, k, rows, skip), out_shape...  5.53 us
    all_to_all x1, starting transfers between devices, on_device(): lax.all_to_all(grams[0], ('space', 'tm', 'freq'), split_axis=0, concat_ax...  4.5 us
    pallas_call x1, Pallas kernels, finish(): pl.pallas_call(functools.partial(finish_kernel, local, total, len(own)),...  2.87 us
    pallas_call x2, Pallas kernels, late(): pl.pallas_call(functools.partial(late_kernel, n, k, skip), out_shape=(sha...  2.54 us
    pallas_call x3, Pallas kernels, early(): pl.pallas_call(functools.partial(early_kernel, n, k), out_shape=jax.Shape...  1.74 us
  transfers between devices with their start and end apart: 7, of which 6 were waited for; matrix products, arithmetic and copies ran while one was open for 0% of the time, Pallas kernels for 8%

profile of v7, /device:TPU:0, one launch (start us, length us, event | category | flops | bytes accessed | tf_op | source)
XLA Modules:
  0.0 74.5 jit_solution(10224213298542161072)
XLA Ops:
  0.6 1.2 %shard_map.51 = f32[16,16,512]{2,1,0:T(8,128)S(1)} custom-call(f32[16,16,4096]{2,1,0:T(8,128)} %x_ref.9), custom_call_target="tpu_custom_call" | custom-call | tf_op jit(solution)/shard_map/pallas_call | solution.py:80
  1.8 3.1 %collective-permute-start.1 = (f32[256,512]{1,0:T(8,128)S(1)}, f32[256,512]{1,0:T(8,128)S(1)}, u32[]{:S(2)}, u32[]{:S(2)}) collective-permute-start(f32[256,512]{1,0:T(8,128)S(1)} %bitcast.8), channel_id=1, source_target_pairs={{0,4},{4,8},{8,12},{12,0},{1,5},{5,9},{9,13},{13,1},{2,6},{6,10},{... | collective-permute-start | bytes 1572872 | tf_op jit(solution)/shard_map/ppermute | solution.py:310
  4.9 1.1 %shard_map.50 = f32[16,16,512]{2,1,0:T(8,128)S(1)} custom-call(f32[16,16,4096]{2,1,0:T(8,128)} %x_ref.9), custom_call_target="tpu_custom_call" | custom-call | tf_op jit(solution)/shard_map/pallas_call | solution.py:80
  6.0 0.0 copy-start
  6.0 2.1 %collective-permute-start = (f32[256,512]{1,0:T(8,128)S(1)}, f32[256,512]{1,0:T(8,128)S(1)}, u32[]{:S(2)}, u32[]{:S(2)}) collective-permute-start(f32[256,512]{1,0:T(8,128)S(1)} %bitcast.7), channel_id=1, source_target_pairs={{0,12},{4,0},{8,4},{12,8},{1,13},{5,1},{9,5},{13,9},{2,14},{6,2},{... | collective-permute-start | bytes 1572872 | tf_op jit(solution)/shard_map/ppermute | solution.py:310
  8.1 1.1 %shard_map.56 = f32[16,16,384]{2,1,0:T(8,128)S(1)} custom-call(f32[16,16,4096]{2,1,0:T(8,128)} %x_ref.9), custom_call_target="tpu_custom_call" | custom-call | tf_op jit(solution)/shard_map/pallas_call | solution.py:80
  9.2 1.3 %collective-permute-start.2 = (f32[256,384]{1,0:T(8,128)S(1)}, f32[256,384]{1,0:T(8,128)S(1)}, u32[]{:S(2)}, u32[]{:S(2)}) collective-permute-start(f32[256,384]{1,0:T(8,128)S(1)} %bitcast.9), channel_id=1, source_target_pairs={{0,8},{4,12},{8,0},{12,4},{1,9},{5,13},{9,1},{13,5},{2,10},{6,14},... | collective-permute-start | bytes 1179656 | tf_op jit(solution)/shard_map/ppermute | solution.py:310
  10.5 1.1 %shard_map.52 = f32[16,16,512]{2,1,0:T(8,128)S(1)} custom-call(f32[16,16,4096]{2,1,0:T(8,128)} %x_ref.9), custom_call_target="tpu_custom_call" | custom-call | tf_op jit(solution)/shard_map/pallas_call | solution.py:80
  11.6 0.0 copy-done
  11.7 0.6 shard_map.53.refs_0_
  12.2 7.4 %collective-permute-done.1.x_ref = f32[256,512]{1,0:T(8,128)S(1)} collective-permute-done((f32[256,512]{1,0:T(8,128)S(1)}, f32[256,512]{1,0:T(8,128)S(1)}, u32[]{:S(2)}, u32[]{:S(2)}) %collective-permute-start.1) | collective-permute-done | bytes 524320 | tf_op jit(solution)/shard_map/ppermute | solution.py:310
  19.7 0.6 shard_map.54.refs_0_
  20.3 0.0 copy-start.1
  20.3 9.8 %collective-permute-done.x_ref = f32[256,512]{1,0:T(8,128)S(1)} collective-permute-done((f32[256,512]{1,0:T(8,128)S(1)}, f32[256,512]{1,0:T(8,128)S(1)}, u32[]{:S(2)}, u32[]{:S(2)}) %collective-permute-start) | collective-permute-done | bytes 524320 | tf_op jit(solution)/shard_map/ppermute | solution.py:310
  30.1 0.6 shard_map.55.sum_ref
  30.6 16.3 %collective-permute-done.2.x_ref = f32[256,384]{1,0:T(8,128)S(1)} collective-permute-done((f32[256,384]{1,0:T(8,128)S(1)}, f32[256,384]{1,0:T(8,128)S(1)}, u32[]{:S(2)}, u32[]{:S(2)}) %collective-permute-start.2) | collective-permute-done | bytes 393248 | tf_op jit(solution)/shard_map/ppermute | solution.py:310
  46.9 0.0 copy-done.1
  46.9 1.2 %shard_map.57 = (f32[256,384]{1,0:T(8,128)S(1)}, f32[256,384]{1,0:T(8,128)S(1)}, f32[2,16,128]{2,1,0:T(8,128)S(1)}) custom-call(bf16[4,512,768]{2,1,0:T(8,128)(2,1)S(1)} %copy-done, f32[512,512]{1,0:T(8,128)S(1)} %shard_map.55.sum_ref, f32[256,384]{1,0:T(8,128)S(1)} %collective-permute-done.2.x_ref, f32[1,1024]{1,0:T(1,128)S(1)} %bitcast.11), custom_call_target="tpu_custom_call" | custom-call | tf_op jit(solution)/shard_map/pallas_call | solution.py:150
  48.1 0.1 collective-permute-start.4
  48.2 1.0 %shard_map.58 = f32[16,16,128]{2,1,0:T(8,128)S(1)} custom-call(f32[16,16,4096]{2,1,0:T(8,128)} %x_ref.9), custom_call_target="tpu_custom_call" | custom-call | tf_op jit(solution)/shard_map/pallas_call | solution.py:80
  49.2 0.1 collective-permute-start.3
  49.3 8.6 %collective-permute-done.3.x_ref = f32[256,128]{1,0:T(8,128)S(1)} collective-permute-done((f32[256,128]{1,0:T(8,128)S(1)}, f32[256,128]{1,0:T(8,128)S(1)}, u32[]{:S(2)}, u32[]{:S(2)}) %collective-permute-start.3) | collective-permute-done | bytes 131104 | tf_op jit(solution)/shard_map/ppermute | solution.py:310
  57.8 0.0 collective-permute-done.4.refs_2_
  57.8 1.4 %shard_map.59 = (f32[256,128]{1,0:T(8,128)S(1)}, f32[256,128]{1,0:T(8,128)S(1)}, f32[16,16,128]{2,1,0:T(8,128)}) custom-call(bf16[4,512,768]{2,1,0:T(8,128)(2,1)S(1)} %copy-done, f32[512,512]{1,0:T(8,128)S(1)} %shard_map.55.sum_ref, f32[256,128]{1,0:T(8,128)S(1)} %collective-permute-done.3.x_ref, f32[1,1024]{1,0:T(1,128)S(1)} %bitcast.12, ...), custom_call_target="tpu_custom_call" | custom-call | tf_op jit(solution)/shard_map/pallas_call | solution.py:150
  59.2 4.5 %all-to-all-start = ((f32[16,16,128]{2,1,0:T(8,128)}), f32[16,16,128]{2,1,0:T(8,128)S(1)}, u32[]{:S(2)}, u32[]{:S(2)}) async-start(f32[16,16,128]{2,1,0:T(8,128)} %get-tuple-element.17), calls=%async_computation | async-start | bytes 262144 | tf_op jit(solution)/shard_map/all_to_all | solution.py:330
  63.7 0.4 collective-permute-start.5
  64.1 1.0 %collective-permute-done.5.refs_3_ = f32[256,128]{1,0:T(8,128)S(1)} collective-permute-done((f32[256,128]{1,0:T(8,128)S(1)}, f32[256,128]{1,0:T(8,128)S(1)}, u32[]{:S(2)}, u32[]{:S(2)}) %collective-permute-start.5) | collective-permute-done | bytes 131104 | tf_op jit(solution)/shard_map/ppermute | solution.py:289
  65.1 6.5 %all-to-all-done.refs_4_ = f32[16,16,128]{2,1,0:T(8,128)S(1)} async-done(((f32[16,16,128]{2,1,0:T(8,128)}), f32[16,16,128]{2,1,0:T(8,128)S(1)}, u32[]{:S(2)}, u32[]{:S(2)}) %all-to-all-start) | async-done | bytes 131104 | tf_op jit(solution)/shard_map/all_to_all | solution.py:330
  71.7 2.9 %shard_map.60 = (f32[8,2,16,1024]{3,2,1,0:T(8,128)}, f32[2,8,16,16]{3,2,1,0:T(8,128)}) custom-call(f32[256,384]{1,0:T(8,128)S(1)} %get-tuple-element.10.refs_0_, f32[256,128]{1,0:T(8,128)S(1)} %get-tuple-element.14.refs_1_, f32[256,384]{1,0:T(8,128)S(1)} %collective-permute-done.4.refs_2_, f32[256,128]{1,0:T(8,128)S(1)} %collective-permute-done.5.refs_3_, ...), custom_call_target="tpu_custom_call" | custom-call | tf_op jit(solution)/shard_map/pallas_call | solution.py:270
Async XLA Ops:
  1.8 17.9 %collective-permute-start.1 = (f32[256,512]{1,0:T(8,128)S(1)}, f32[256,512]{1,0:T(8,128)S(1)}, u32[]{:S(2)}, u32[]{:S(2)}) collective-permute-start(f32[256,512]{1,0:T(8,128)S(1)} %bitcast.8), channel_id=1, source_target_pairs={{0,4},{4,8},{8,12},{12,0},{1,5},{5,9},{9,13},{13,1},{2,6},{6,10},{... | collective-permute-start | bytes 1572872 | tf_op jit(solution)/shard_map/ppermute | solution.py:310
  6.0 5.6 %copy-start = (bf16[4,512,768]{2,1,0:T(8,128)(2,1)S(1)}, bf16[4,512,768]{2,1,0:T(8,128)(2,1)}, u32[]{:S(2)}) copy-start(bf16[4,512,768]{2,1,0:T(8,128)(2,1)} %constant.2.clone.t_ref) | copy-start | bytes 9437188
  6.0 24.0 %collective-permute-start = (f32[256,512]{1,0:T(8,128)S(1)}, f32[256,512]{1,0:T(8,128)S(1)}, u32[]{:S(2)}, u32[]{:S(2)}) collective-permute-start(f32[256,512]{1,0:T(8,128)S(1)} %bitcast.7), channel_id=1, source_target_pairs={{0,12},{4,0},{8,4},{12,8},{1,13},{5,1},{9,5},{13,9},{2,14},{6,2},{... | collective-permute-start | bytes 1572872 | tf_op jit(solution)/shard_map/ppermute | solution.py:310
  9.2 37.7 %collective-permute-start.2 = (f32[256,384]{1,0:T(8,128)S(1)}, f32[256,384]{1,0:T(8,128)S(1)}, u32[]{:S(2)}, u32[]{:S(2)}) collective-permute-start(f32[256,384]{1,0:T(8,128)S(1)} %bitcast.9), channel_id=1, source_target_pairs={{0,8},{4,12},{8,0},{12,4},{1,9},{5,13},{9,1},{13,5},{2,10},{6,14},... | collective-permute-start | bytes 1179656 | tf_op jit(solution)/shard_map/ppermute | solution.py:310
  20.3 26.6 %copy-start.1 = (f32[1024]{0:T(1024)S(1)}, f32[1024]{0:T(1024)}, u32[]{:S(2)}) copy-start(f32[1024]{0:T(1024)} %param.4) | copy-start | bytes 12292
  48.1 9.7 %collective-permute-start.4 = (f32[256,384]{1,0:T(8,128)S(1)}, f32[256,384]{1,0:T(8,128)S(1)}, u32[]{:S(2)}, u32[]{:S(2)}) collective-permute-start(f32[256,384]{1,0:T(8,128)S(1)} %get-tuple-element.11), channel_id=1, source_target_pairs={{0,1},{1,0},{2,3},{3,2},{4,5},{5,4},{6,7},{7,6},{8,9},{9,8},{10,11... | collective-permute-start | bytes 1179656 | tf_op jit(solution)/shard_map/ppermute | solution.py:289
  49.2 8.6 %collective-permute-start.3 = (f32[256,128]{1,0:T(8,128)S(1)}, f32[256,128]{1,0:T(8,128)S(1)}, u32[]{:S(2)}, u32[]{:S(2)}) collective-permute-start(f32[256,128]{1,0:T(8,128)S(1)} %bitcast.10), channel_id=1, source_target_pairs={{0,8},{4,12},{8,0},{12,4},{1,9},{5,13},{9,1},{13,5},{2,10},{6,14},... | collective-permute-start | bytes 393224 | tf_op jit(solution)/shard_map/ppermute | solution.py:310
  59.2 12.4 %all-to-all-start = ((f32[16,16,128]{2,1,0:T(8,128)}), f32[16,16,128]{2,1,0:T(8,128)S(1)}, u32[]{:S(2)}, u32[]{:S(2)}) async-start(f32[16,16,128]{2,1,0:T(8,128)} %get-tuple-element.17), calls=%async_computation | async-start | bytes 262144 | tf_op jit(solution)/shard_map/all_to_all | solution.py:330
  63.7 1.4 %collective-permute-start.5 = (f32[256,128]{1,0:T(8,128)S(1)}, f32[256,128]{1,0:T(8,128)S(1)}, u32[]{:S(2)}, u32[]{:S(2)}) collective-permute-start(f32[256,128]{1,0:T(8,128)S(1)} %get-tuple-element.16), channel_id=1, source_target_pairs={{0,1},{1,0},{2,3},{3,2},{4,5},{5,4},{6,7},{7,6},{8,9},{9,8},{10,11... | collective-permute-start | bytes 393224 | tf_op jit(solution)/shard_map/ppermute | solution.py:289

commit v8 on v7

--- a/solution.py
+++ b/solution.py
@@ -14,6 +14,7 @@
 CUTS = 16
 epsilon = 1e-05
 MIB = 1024 * 1024
+SMALL = pl.CostEstimate(flops=1, transcendentals=0, bytes_accessed=1)
 
 
 def dft_blocks(groups):
@@ -84,6 +85,7 @@
             out_specs=pl.BlockSpec(memory_space=pltpu.VMEM),
             scratch_shapes=[pltpu.SemaphoreType.DMA((CUTS,))],
             compiler_params=pltpu.CompilerParams(vmem_limit_bytes=4 * MIB),
+            cost_estimate=SMALL,
         )(pltpu.with_memory_space_constraint(snapshots, pltpu.HBM))
     else:
         to = lax.rem(lax.axis_index("space") + k, n)
@@ -104,14 +106,15 @@
         functools.partial(early_kernel, n, k),
         out_shape=jax.ShapeDtypeStruct((tables.shape[1], share), jnp.float32),
         compiler_params=pltpu.CompilerParams(vmem_limit_bytes=16 * MIB),
+        cost_estimate=SMALL,
     )(tables, piece, *before)
 
 
 def late_kernel(n, k, skip, t_ref, sum_ref, x_ref, w_ref, *refs):
-    *before, own_ref, other_ref, gram_ref = refs
     size = x_ref.shape[1]
+    share = sum_ref.shape[1]
     cols = pl.ds(skip, size)
-    at = lax.axis_index("freq") * sum_ref.shape[1] + skip
+    at = lax.axis_index("freq") * share + skip
     weights = w_ref[:, pl.ds(pl.multiple_of(at, 128), size)]
     src = lax.rem(lax.axis_index("space") - k + n, n)
     spectra = sum_ref[:, cols] + times_split(t_ref[src], x_ref[...])
@@ -124,8 +127,14 @@
     col = lax.broadcasted_iota(jnp.int32, (NB, width), 1) % NB
     first = lax.axis_index("freq") == 0
     halves = [spectra[:half], spectra[half:]]
+    if skip:
+        before_ref, own_ref, gram_ref = refs
+    else:
+        own_ref, gram_ref, other_ref, rest_ref = refs
+        rest = sum_ref[:, size:]
+        other_ref[...] = jnp.where(first, halves[1], halves[0])
+        rest_ref[...] = jnp.where(first, rest[half:], rest[:half])
     own_ref[...] = jnp.where(first, halves[0], halves[1])
-    other_ref[...] = jnp.where(first, halves[1], halves[0])
     packed = []
     for z in halves:
         full = rows_product(z * weights, z)
@@ -136,21 +145,23 @@
             kept = jnp.where(line == lane, part, 0.0)
             both.append(jnp.sum(kept.reshape(local, NB, width), axis=0))
         packed.append(jnp.where(row >= col, both[0], both[1]))
-    if before:
-        packed = [packed[h] + before[0][h] for h in range(2)]
+    if skip:
+        packed = [packed[h] + before_ref[h] for h in range(2)]
     for d in range(gram_ref.shape[0]):
         gram_ref[d] = packed[d % 2]
 
 
 def late(tables, n, k, skip, targets, partial_sum, piece, weights, *before):
-    share = piece.shape[1]
+    share = partial_sum.shape[1]
     half = tables.shape[1] // 2
-    shape = jax.ShapeDtypeStruct((half, share), jnp.float32)
-    gram_shape = jax.ShapeDtypeStruct((targets, NB, half // 2), jnp.float32)
+    shapes = [(half, piece.shape[1]), (targets, NB, half // 2)]
+    if not skip:
+        shapes += [(half, piece.shape[1]), (half, share - piece.shape[1])]
     return pl.pallas_call(
         functools.partial(late_kernel, n, k, skip),
-        out_shape=(shape, shape, gram_shape),
+        out_shape=[jax.ShapeDtypeStruct(shape, jnp.float32) for shape in shapes],
         compiler_params=pltpu.CompilerParams(vmem_limit_bytes=16 * MIB),
+        cost_estimate=SMALL,
     )(tables, partial_sum, piece, weights, *before)
 
 
@@ -159,9 +170,10 @@
     return y * (1.5 - 0.5 * x * (y * y))
 
 
-def finish_kernel(local, total, parts, *refs):
-    own_refs, other_refs = refs[:parts], refs[parts : 2 * parts]
-    grams_ref, modes_ref, factor_ref, *slots, sem = refs[2 * parts :]
+def finish_kernel(
+    n, k, total, t_ref, first_ref, second_ref, other_ref, rest_ref, raw_ref, grams_ref, modes_ref, factor_ref
+):
+    local = modes_ref.shape[0]
     width = local * NB
     share = modes_ref.shape[3] // 2
     gram = jnp.sum(grams_ref[...], axis=0) / total
@@ -236,53 +248,37 @@
     me = lax.axis_index("freq")
     high, low = split(mixing)
     mixing = jnp.concatenate([high, high, low], axis=1)
-    moves = []
-    for k, refs_of in ((0, own_refs), (1, other_refs)):
-        skip = 0
-        for ref in refs_of:
-            size = ref.shape[1]
-            out = times_split(mixing, ref[...])
-            slot = slots[len(moves)]
-            for part in range(2):
-                for f in range(local):
-                    at = part * width + f * NB
-                    slot[f, part] = out[at : at + NB]
-            start = pl.multiple_of(((me + k) % 2) * share + skip, 128)
-            moves.append(
-                pltpu.make_async_copy(
-                    slot, modes_ref.at[:, :, :, pl.ds(start, size)], sem.at[len(moves)]
-                )
-            )
-            moves[-1].start()
-            skip += size
+    src = lax.rem(lax.axis_index("space") - k + n, n)
+    lines = pl.ds(pl.multiple_of(me * 2 * width, 128), 2 * width)
+    own = [first_ref[...], second_ref[...]]
+    added = times_split(t_ref[src, lines], raw_ref[...])
+    other = [other_ref[...], rest_ref[...] + added]
+    for place, parts in ((me, own), (1 - me, other)):
+        out = times_split(mixing, jnp.concatenate(parts, axis=1))
+        cols = pl.ds(pl.multiple_of(place * share, 128), share)
+        for part in range(2):
+            for f in range(local):
+                at = part * width + f * NB
+                modes_ref[f, part, :, cols] = out[at : at + NB]
     pad = jnp.zeros((width - NB, width), jnp.float32)
     turned_re = jnp.transpose(jnp.concatenate(low_re + [pad], axis=0))
     turned_im = jnp.transpose(jnp.concatenate(low_im + [pad], axis=0))
     for f in range(local):
         factor_ref[0, f] = turned_re[f * NB : (f + 1) * NB, :NB]
         factor_ref[1, f] = -turned_im[f * NB : (f + 1) * NB, :NB]
-    for move in moves:
-        move.wait()
-
-
-def finish(grams, own, other, local, total):
-    share = sum(part.shape[1] for part in own)
+
+
+def finish(tables, n, k, total, first, second, other, rest, raw, grams):
+    local = tables.shape[1] // (4 * NB)
+    share = other.shape[1] + rest.shape[1]
     return pl.pallas_call(
-        functools.partial(finish_kernel, local, total, len(own)),
+        functools.partial(finish_kernel, n, k, total),
         out_shape=(
             jax.ShapeDtypeStruct((local, 2, NB, 2 * share), jnp.float32),
             jax.ShapeDtypeStruct((2, local, NB, NB), jnp.float32),
         ),
-        out_specs=(
-            pl.BlockSpec(memory_space=pltpu.HBM),
-            pl.BlockSpec(memory_space=pltpu.VMEM),
-        ),
-        scratch_shapes=[
-            *[pltpu.VMEM((local, 2, NB, part.shape[1]), jnp.float32) for part in own + other],
-            pltpu.SemaphoreType.DMA((len(own + other),)),
-        ],
         compiler_params=pltpu.CompilerParams(vmem_limit_bytes=16 * MIB),
-    )(*own, *other, grams)
+    )(tables, first, second, other, rest, raw, grams)
 
 
 def partner(value, axis, size, step):
@@ -293,7 +289,6 @@
     n = lax.axis_size("space")
     tm_count = lax.axis_size("tm")
     freq_count = lax.axis_size("freq")
-    local = NF // freq_count
     blocks, local_times, columns = snapshots.shape
     rows = columns // n
     share = rows // freq_count
@@ -301,7 +296,7 @@
     tables = jnp.asarray(dft_blocks(n))
 
     last = n // 2
-    early_rows = share - share // 4
+    early_rows = share // 2
     parts = ((0, early_rows), (early_rows, share - early_rows))
     targets = n * tm_count * freq_count
 
@@ -315,23 +310,16 @@
     before = early(tables, n, 0, cut(snapshots, n, 0, rows, 0, share))
     for k, piece in zip(offsets, pieces):
         before = early(tables, n, k, piece, before)
-    own, other, grams = [], [], []
-    for (skip, _), piece in zip(parts, last_pieces):
-        if other:
-            other[-1] = partner(other[-1], "freq", freq_count, 1)
-            piece, other[-1] = lax.optimization_barrier((piece, other[-1]))
-        copies = targets if own else 2
-        mine, traded, *grams = late(
-            tables, n, last, skip, copies, before, piece, weights.reshape(1, rows), *grams
-        )
-        own.append(mine)
-        other.append(traded)
-    other[-1] = partner(other[-1], "freq", freq_count, 1)
-    grams = lax.all_to_all(
-        grams[0], ("space", "tm", "freq"), split_axis=0, concat_axis=0, tiled=True
-    )
+    weights = weights.reshape(1, rows)
+    first, gram, other, rest = late(tables, n, last, 0, 2, before, last_pieces[0], weights)
+    other, rest = partner(other, "freq", freq_count, 1), partner(rest, "freq", freq_count, 1)
+    raw, other, rest = lax.optimization_barrier((last_pieces[1], other, rest))
+    second, gram = late(tables, n, last, early_rows, targets, before, raw, weights, gram)
+    raw = partner(raw, "freq", freq_count, 1)
+    gram, raw = lax.optimization_barrier((gram, raw))
+    grams = lax.all_to_all(gram, ("space", "tm", "freq"), split_axis=0, concat_axis=0, tiled=True)
     total = rows * n * tm_count
-    return finish(grams, own, other, local, total)
+    return finish(tables, n, last, total, first, second, other, rest, raw, grams)
 
 
 def solution(mesh):

time: 75.1 us -> 68.5 us (0.912)
  waiting for transfers between devices: 49.6 us -> 35.2 us
  blocking collectives: 0 us -> 11.7 us
  starting transfers between devices: 11.5 us -> 8.83 us
  Pallas kernels: 12.7 us -> 11.5 us
    all_to_all x0 -> x1, blocking collectives: none -> 11.7 us  [on_device(): lax.all_to_all(gram, ('space', 'tm', 'freq'), split_axis=0, concat_axis=0...]
    ppermute x4, waiting for transfers between devices: 42 us -> 34.7 us  [send(): return lax.ppermute(sent, 'space', [(i, (i + k) % n) for i in range(n)])]
    all_to_all x1 -> x0, waiting for transfers between devices: 6.52 us -> none  [on_device(): lax.all_to_all(grams[0], ('space', 'tm', 'freq'), split_axis=0, concat_ax...]
    all_to_all x1 -> x0, starting transfers between devices: 4.5 us -> none  [on_device(): lax.all_to_all(grams[0], ('space', 'tm', 'freq'), split_axis=0, concat_ax...]
    ppermute x4, starting transfers between devices: 6.53 us -> 8.24 us  [send(): return lax.ppermute(sent, 'space', [(i, (i + k) % n) for i in range(n)])]
    pallas_call x3, Pallas kernels: 5.42 us -> 4.29 us  [the longest x1 2.25 us: finish(): pl.pallas_call(functools.partial(finish_kernel, n, k, total), out_shape=(...]
  transfers between devices with their start and end apart: 7 -> 7, of which waited for: 6 -> 5; matrix products, arithmetic and copies ran while one was open for 0% -> 0% of each run, Pallas kernels for 8% -> 12%
where the time goes in v8:
time: 68.5 us; the launch traced here: 68 us
  waiting for transfers between devices  35.2 us (51%)
  blocking collectives  11.7 us (17%)
  Pallas kernels  11.5 us (17%)
  starting transfers between devices  8.83 us (13%)
  between operations  0.74 us (1%)
    ppermute x4, waiting for transfers between devices, send(): return lax.ppermute(sent, 'space', [(i, (i + k) % n) for i in range(n)])  34.7 us
    all_to_all x1, blocking collectives, on_device(): lax.all_to_all(gram, ('space', 'tm', 'freq'), split_axis=0, concat_axis=0...  11.7 us
    ppermute x4, starting transfers between devices, send(): return lax.ppermute(sent, 'space', [(i, (i + k) % n) for i in range(n)])  8.24 us
    pallas_call x5, Pallas kernels, cut(): pl.pallas_call(functools.partial(cut_kernel, n, k, rows, skip), out_shape...  5.51 us
    pallas_call x1, Pallas kernels, finish(): pl.pallas_call(functools.partial(finish_kernel, n, k, total), out_shape=(...  2.25 us
    pallas_call x2, Pallas kernels, late(): pl.pallas_call(functools.partial(late_kernel, n, k, skip), out_shape=[jax...  2.03 us
    pallas_call x3, Pallas kernels, early(): pl.pallas_call(functools.partial(early_kernel, n, k), out_shape=jax.Shape...  1.73 us
  transfers between devices with their start and end apart: 7, of which 5 were waited for; matrix products, arithmetic and copies ran while one was open for 0% of the time, Pallas kernels for 12%

profile of v8, /device:TPU:0, one launch (start us, length us, event | category | flops | bytes accessed | tf_op | source)
XLA Modules:
  0.0 68.0 jit_solution(7543167243888409527)
XLA Ops:
  0.6 1.2 %shard_map.51 = f32[16,16,512]{2,1,0:T(8,128)S(1)} custom-call(f32[16,16,4096]{2,1,0:T(8,128)} %x_ref.9), custom_call_target="tpu_custom_call" | custom-call | flops 1 | bytes 1 | tf_op jit(solution)/shard_map/pallas_call | solution.py:81
  1.8 3.1 %collective-permute-start.1 = (f32[256,512]{1,0:T(8,128)S(1)}, f32[256,512]{1,0:T(8,128)S(1)}, u32[]{:S(2)}, u32[]{:S(2)}) collective-permute-start(f32[256,512]{1,0:T(8,128)S(1)} %bitcast.8), channel_id=1, source_target_pairs={{0,4},{4,8},{8,12},{12,0},{1,5},{5,9},{9,13},{13,1},{2,6},{6,10},{... | collective-permute-start | bytes 1572872 | tf_op jit(solution)/shard_map/ppermute | solution.py:305
  4.9 1.1 %shard_map.50 = f32[16,16,512]{2,1,0:T(8,128)S(1)} custom-call(f32[16,16,4096]{2,1,0:T(8,128)} %x_ref.9), custom_call_target="tpu_custom_call" | custom-call | flops 1 | bytes 1 | tf_op jit(solution)/shard_map/pallas_call | solution.py:81
  6.0 2.1 %collective-permute-start = (f32[256,512]{1,0:T(8,128)S(1)}, f32[256,512]{1,0:T(8,128)S(1)}, u32[]{:S(2)}, u32[]{:S(2)}) collective-permute-start(f32[256,512]{1,0:T(8,128)S(1)} %bitcast.7), channel_id=1, source_target_pairs={{0,12},{4,0},{8,4},{12,8},{1,13},{5,1},{9,5},{13,9},{2,14},{6,2},{... | collective-permute-start | bytes 1572872 | tf_op jit(solution)/shard_map/ppermute | solution.py:305
  8.1 1.0 %shard_map.56 = f32[16,16,256]{2,1,0:T(8,128)S(1)} custom-call(f32[16,16,4096]{2,1,0:T(8,128)} %x_ref.9), custom_call_target="tpu_custom_call" | custom-call | flops 1 | bytes 1 | tf_op jit(solution)/shard_map/pallas_call | solution.py:81
  9.2 0.0 copy-start
  9.2 1.0 %collective-permute-start.2 = (f32[256,256]{1,0:T(8,128)S(1)}, f32[256,256]{1,0:T(8,128)S(1)}, u32[]{:S(2)}, u32[]{:S(2)}) collective-permute-start(f32[256,256]{1,0:T(8,128)S(1)} %bitcast.10), channel_id=1, source_target_pairs={{0,8},{4,12},{8,0},{12,4},{1,9},{5,13},{9,1},{13,5},{2,10},{6,14},... | collective-permute-start | bytes 786440 | tf_op jit(solution)/shard_map/ppermute | solution.py:305
  10.2 1.0 %shard_map.58 = f32[16,16,256]{2,1,0:T(8,128)S(1)} custom-call(f32[16,16,4096]{2,1,0:T(8,128)} %x_ref.9), custom_call_target="tpu_custom_call" | custom-call | flops 1 | bytes 1 | tf_op jit(solution)/shard_map/pallas_call | solution.py:81
  11.3 2.0 %collective-permute-start.3 = (f32[256,256]{1,0:T(8,128)S(1)}, f32[256,256]{1,0:T(8,128)S(1)}, u32[]{:S(2)}, u32[]{:S(2)}) collective-permute-start(f32[256,256]{1,0:T(8,128)S(1)} %bitcast.9), channel_id=1, source_target_pairs={{0,8},{4,12},{8,0},{12,4},{1,9},{5,13},{9,1},{13,5},{2,10},{6,14},... | collective-permute-start | bytes 786440 | tf_op jit(solution)/shard_map/ppermute | solution.py:305
  13.3 1.1 %shard_map.52 = f32[16,16,512]{2,1,0:T(8,128)S(1)} custom-call(f32[16,16,4096]{2,1,0:T(8,128)} %x_ref.9), custom_call_target="tpu_custom_call" | custom-call | flops 1 | bytes 1 | tf_op jit(solution)/shard_map/pallas_call | solution.py:81
  14.4 0.0 copy-done
  14.4 0.6 shard_map.53.refs_0_
  15.0 4.7 %collective-permute-done.1.x_ref = f32[256,512]{1,0:T(8,128)S(1)} collective-permute-done((f32[256,512]{1,0:T(8,128)S(1)}, f32[256,512]{1,0:T(8,128)S(1)}, u32[]{:S(2)}, u32[]{:S(2)}) %collective-permute-start.1) | collective-permute-done | bytes 524320 | tf_op jit(solution)/shard_map/ppermute | solution.py:305
  19.7 0.6 shard_map.54.refs_0_
  20.3 0.0 copy-start.1
  20.3 9.8 %collective-permute-done.x_ref = f32[256,512]{1,0:T(8,128)S(1)} collective-permute-done((f32[256,512]{1,0:T(8,128)S(1)}, f32[256,512]{1,0:T(8,128)S(1)}, u32[]{:S(2)}, u32[]{:S(2)}) %collective-permute-start) | collective-permute-done | bytes 524320 | tf_op jit(solution)/shard_map/ppermute | solution.py:305
  30.1 0.6 shard_map.55.sum_ref
  30.6 16.4 %collective-permute-done.2.x_ref = f32[256,256]{1,0:T(8,128)S(1)} collective-permute-done((f32[256,256]{1,0:T(8,128)S(1)}, f32[256,256]{1,0:T(8,128)S(1)}, u32[]{:S(2)}, u32[]{:S(2)}) %collective-permute-start.2) | collective-permute-done | bytes 262176 | tf_op jit(solution)/shard_map/ppermute | solution.py:305
  47.0 0.0 copy-done.1
  47.0 1.0 %shard_map.57 = (f32[256,256]{1,0:T(8,128)S(1)}, f32[2,16,128]{2,1,0:T(8,128)S(1)}, f32[256,256]{1,0:T(8,128)S(1)}, f32[256,256]{1,0:T(8,128)S(1)}) custom-call(bf16[4,512,768]{2,1,0:T(8,128)(2,1)S(1)} %copy-done, f32[512,512]{1,0:T(8,128)S(1)} %shard_map.55.sum_ref, f32[256,256]{1,0:T(8,128)S(1)} %collective-permute-done.2.x_ref, f32[1,1024]{1,0:T(1,128)S(1)} %bitcast.11), custom_call_target="tpu_custom_call" | custom-call | flops 1 | bytes 1 | tf_op jit(solution)/shard_map/pallas_call | solution.py:160
  48.0 0.1 collective-permute-start.4
  48.1 0.5 collective-permute-start.5
  48.6 3.9 %collective-permute-done.3.x_ref = f32[256,256]{1,0:T(8,128)S(1)} collective-permute-done((f32[256,256]{1,0:T(8,128)S(1)}, f32[256,256]{1,0:T(8,128)S(1)}, u32[]{:S(2)}, u32[]{:S(2)}) %collective-permute-start.3) | collective-permute-done | bytes 262176 | tf_op jit(solution)/shard_map/ppermute | solution.py:305
  52.5 0.0 collective-permute-done.4.other_ref
  52.5 0.0 collective-permute-done.5.rest_ref
  52.5 0.0 collective-permute-start.6
  52.5 1.0 %shard_map.59 = (f32[256,256]{1,0:T(8,128)S(1)}, f32[16,16,128]{2,1,0:T(8,128)S(1)}) custom-call(bf16[4,512,768]{2,1,0:T(8,128)(2,1)S(1)} %copy-done, f32[512,512]{1,0:T(8,128)S(1)} %shard_map.55.sum_ref, f32[256,256]{1,0:T(8,128)S(1)} %collective-permute-done.3.x_ref, f32[1,1024]{1,0:T(1,128)S(1)} %bitcast.12, f32[2,16,128]{2,1,0:T(8,128)S(1)} %get-tuple-element.17.refs_0_), custom_call_target="tpu_custom_call" | custom-call | flops 1 | bytes 1 | tf_op jit(solution)/shard_map/pallas_call | solution.py:160
  53.6 0.5 collective-permute-done.6.raw_ref
  54.1 11.7 %all_to_all.5.grams_ref = f32[16,16,128]{2,1,0:T(8,128)S(1)} all-to-all(f32[16,16,128]{2,1,0:T(8,128)S(1)} %get-tuple-element.23), channel_id=1, replica_groups=mesh['groups'=2,'space'=4,'tm'=2,'freq'=2] {'space','tm','freq'}, dimensions={0} | all-to-all | bytes 262144 | tf_op jit(solution)/shard_map/all_to_all | solution.py:320
  65.7 2.3 %shard_map.60 = (f32[8,2,16,1024]{3,2,1,0:T(8,128)}, f32[2,8,16,16]{3,2,1,0:T(8,128)}) custom-call(bf16[4,512,768]{2,1,0:T(8,128)(2,1)S(1)} %copy-done, f32[256,256]{1,0:T(8,128)S(1)} %get-tuple-element.13.first_ref, f32[256,256]{1,0:T(8,128)S(1)} %get-tuple-element.18.second_ref, f32[256,256]{1,0:T(8,128)S(1)} %collective-permute-done.4.other_ref, ...), custom_call_target="tpu_custom_call" | custom-call | tf_op jit(solution)/shard_map/pallas_call | solution.py:274
Async XLA Ops:
  1.8 17.9 %collective-permute-start.1 = (f32[256,512]{1,0:T(8,128)S(1)}, f32[256,512]{1,0:T(8,128)S(1)}, u32[]{:S(2)}, u32[]{:S(2)}) collective-permute-start(f32[256,512]{1,0:T(8,128)S(1)} %bitcast.8), channel_id=1, source_target_pairs={{0,4},{4,8},{8,12},{12,0},{1,5},{5,9},{9,13},{13,1},{2,6},{6,10},{... | collective-permute-start | bytes 1572872 | tf_op jit(solution)/shard_map/ppermute | solution.py:305
  6.0 24.0 %collective-permute-start = (f32[256,512]{1,0:T(8,128)S(1)}, f32[256,512]{1,0:T(8,128)S(1)}, u32[]{:S(2)}, u32[]{:S(2)}) collective-permute-start(f32[256,512]{1,0:T(8,128)S(1)} %bitcast.7), channel_id=1, source_target_pairs={{0,12},{4,0},{8,4},{12,8},{1,13},{5,1},{9,5},{13,9},{2,14},{6,2},{... | collective-permute-start | bytes 1572872 | tf_op jit(solution)/shard_map/ppermute | solution.py:305
  9.2 5.3 %copy-start = (bf16[4,512,768]{2,1,0:T(8,128)(2,1)S(1)}, bf16[4,512,768]{2,1,0:T(8,128)(2,1)}, u32[]{:S(2)}) copy-start(bf16[4,512,768]{2,1,0:T(8,128)(2,1)} %constant.2.clone.t_ref) | copy-start | bytes 9437188
  9.2 37.8 %collective-permute-start.2 = (f32[256,256]{1,0:T(8,128)S(1)}, f32[256,256]{1,0:T(8,128)S(1)}, u32[]{:S(2)}, u32[]{:S(2)}) collective-permute-start(f32[256,256]{1,0:T(8,128)S(1)} %bitcast.10), channel_id=1, source_target_pairs={{0,8},{4,12},{8,0},{12,4},{1,9},{5,13},{9,1},{13,5},{2,10},{6,14},... | collective-permute-start | bytes 786440 | tf_op jit(solution)/shard_map/ppermute | solution.py:305
  11.3 41.2 %collective-permute-start.3 = (f32[256,256]{1,0:T(8,128)S(1)}, f32[256,256]{1,0:T(8,128)S(1)}, u32[]{:S(2)}, u32[]{:S(2)}) collective-permute-start(f32[256,256]{1,0:T(8,128)S(1)} %bitcast.9), channel_id=1, source_target_pairs={{0,8},{4,12},{8,0},{12,4},{1,9},{5,13},{9,1},{13,5},{2,10},{6,14},... | collective-permute-start | bytes 786440 | tf_op jit(solution)/shard_map/ppermute | solution.py:305
  20.3 26.7 %copy-start.1 = (f32[1024]{0:T(1024)S(1)}, f32[1024]{0:T(1024)}, u32[]{:S(2)}) copy-start(f32[1024]{0:T(1024)} %param.4) | copy-start | bytes 12292
  48.0 4.5 %collective-permute-start.4 = (f32[256,256]{1,0:T(8,128)S(1)}, f32[256,256]{1,0:T(8,128)S(1)}, u32[]{:S(2)}, u32[]{:S(2)}) collective-permute-start(f32[256,256]{1,0:T(8,128)S(1)} %get-tuple-element.14), channel_id=1, source_target_pairs={{0,1},{1,0},{2,3},{3,2},{4,5},{5,4},{6,7},{7,6},{8,9},{9,8},{10,11... | collective-permute-start | bytes 786440 | tf_op jit(solution)/shard_map/ppermute | solution.py:285
  48.1 4.4 %collective-permute-start.5 = (f32[256,256]{1,0:T(8,128)S(1)}, f32[256,256]{1,0:T(8,128)S(1)}, u32[]{:S(2)}, u32[]{:S(2)}) collective-permute-start(f32[256,256]{1,0:T(8,128)S(1)} %get-tuple-element.15), channel_id=1, source_target_pairs={{0,1},{1,0},{2,3},{3,2},{4,5},{5,4},{6,7},{7,6},{8,9},{9,8},{10,11... | collective-permute-start | bytes 786440 | tf_op jit(solution)/shard_map/ppermute | solution.py:285
  52.5 1.5 %collective-permute-start.6 = (f32[256,256]{1,0:T(8,128)S(1)}, f32[256,256]{1,0:T(8,128)S(1)}, u32[]{:S(2)}, u32[]{:S(2)}) collective-permute-start(f32[256,256]{1,0:T(8,128)S(1)} %collective-permute-done.3.x_ref), channel_id=1, source_target_pairs={{0,1},{1,0},{2,3},{3,2},{4,5},{5,4},{6,7},{7,6},{8,9},{9,8},{10,11... | collective-permute-start | bytes 786440 | tf_op jit(solution)/shard_map/ppermute | solution.py:285

commit v9 on v8

--- a/solution.py
+++ b/solution.py
@@ -12,6 +12,7 @@
 SEGMENT_FRAMES = 64
 NF = 16
 CUTS = 16
+TRADED = 128
 epsilon = 1e-05
 MIB = 1024 * 1024
 SMALL = pl.CostEstimate(flops=1, transcendentals=0, bytes_accessed=1)
@@ -57,7 +58,7 @@
 
 def cut_kernel(n, k, rows, skip, x_ref, o_ref, sem):
     size = o_ref.shape[2]
-    to = lax.rem(lax.axis_index("space") + k, n)
+    to = lax.bitwise_xor(lax.axis_index("space"), k)
     share = rows // 2
     start = pl.multiple_of(to * rows + lax.axis_index("freq") * share + skip, 128)
     part = NB // CUTS
@@ -88,14 +89,14 @@
             cost_estimate=SMALL,
         )(pltpu.with_memory_space_constraint(snapshots, pltpu.HBM))
     else:
-        to = lax.rem(lax.axis_index("space") + k, n)
+        to = lax.bitwise_xor(lax.axis_index("space"), k)
         start = to * rows + lax.axis_index("freq") * (rows // 2) + skip
         piece = lax.dynamic_slice_in_dim(snapshots, start, size, axis=2)
     return piece.reshape(blocks * local_times, size)
 
 
 def early_kernel(n, k, t_ref, x_ref, *refs):
-    src = lax.rem(lax.axis_index("space") - k + n, n)
+    src = lax.bitwise_xor(lax.axis_index("space"), k)
     part = times_split(t_ref[src], x_ref[...])
     refs[-1][...] = part if len(refs) == 1 else refs[0][...] + part
 
@@ -116,7 +117,7 @@
     cols = pl.ds(skip, size)
     at = lax.axis_index("freq") * share + skip
     weights = w_ref[:, pl.ds(pl.multiple_of(at, 128), size)]
-    src = lax.rem(lax.axis_index("space") - k + n, n)
+    src = lax.bitwise_xor(lax.axis_index("space"), k)
     spectra = sum_ref[:, cols] + times_split(t_ref[src], x_ref[...])
     half = spectra.shape[0] // 2
     width = half // 2
@@ -130,10 +131,11 @@
     if skip:
         before_ref, own_ref, gram_ref = refs
     else:
-        own_ref, gram_ref, other_ref, rest_ref = refs
-        rest = sum_ref[:, size:]
-        other_ref[...] = jnp.where(first, halves[1], halves[0])
-        rest_ref[...] = jnp.where(first, rest[half:], rest[:half])
+        own_ref, gram_ref, *other_refs = refs
+        both = jnp.concatenate([spectra, sum_ref[:, size:]], axis=1)
+        other = jnp.where(first, both[half:], both[:half])
+        for i, ref in enumerate(other_refs):
+            ref[...] = other[:, i * TRADED : (i + 1) * TRADED]
     own_ref[...] = jnp.where(first, halves[0], halves[1])
     packed = []
     for z in halves:
@@ -156,7 +158,7 @@
     half = tables.shape[1] // 2
     shapes = [(half, piece.shape[1]), (targets, NB, half // 2)]
     if not skip:
-        shapes += [(half, piece.shape[1]), (half, share - piece.shape[1])]
+        shapes += [(half, TRADED)] * (share // TRADED)
     return pl.pallas_call(
         functools.partial(late_kernel, n, k, skip),
         out_shape=[jax.ShapeDtypeStruct(shape, jnp.float32) for shape in shapes],
@@ -171,8 +173,9 @@
 
 
 def finish_kernel(
-    n, k, total, t_ref, first_ref, second_ref, other_ref, rest_ref, raw_ref, grams_ref, modes_ref, factor_ref
+    n, k, total, t_ref, first_ref, second_ref, raw_ref, grams_ref, *refs
 ):
+    *other_refs, modes_ref, factor_ref = refs
     local = modes_ref.shape[0]
     width = local * NB
     share = modes_ref.shape[3] // 2
@@ -248,11 +251,12 @@
     me = lax.axis_index("freq")
     high, low = split(mixing)
     mixing = jnp.concatenate([high, high, low], axis=1)
-    src = lax.rem(lax.axis_index("space") - k + n, n)
+    src = lax.bitwise_xor(lax.axis_index("space"), k)
     lines = pl.ds(pl.multiple_of(me * 2 * width, 128), 2 * width)
     own = [first_ref[...], second_ref[...]]
     added = times_split(t_ref[src, lines], raw_ref[...])
-    other = [other_ref[...], rest_ref[...] + added]
+    *other, rest = [ref[...] for ref in other_refs]
+    other.append(rest + added)
     for place, parts in ((me, own), (1 - me, other)):
         out = times_split(mixing, jnp.concatenate(parts, axis=1))
         cols = pl.ds(pl.multiple_of(place * share, 128), share)
@@ -268,9 +272,9 @@
         factor_ref[1, f] = -turned_im[f * NB : (f + 1) * NB, :NB]
 
 
-def finish(tables, n, k, total, first, second, other, rest, raw, grams):
+def finish(tables, n, k, total, first, second, raw, grams, others):
     local = tables.shape[1] // (4 * NB)
-    share = other.shape[1] + rest.shape[1]
+    share = first.shape[1] + second.shape[1]
     return pl.pallas_call(
         functools.partial(finish_kernel, n, k, total),
         out_shape=(
@@ -278,7 +282,7 @@
             jax.ShapeDtypeStruct((2, local, NB, NB), jnp.float32),
         ),
         compiler_params=pltpu.CompilerParams(vmem_limit_bytes=16 * MIB),
-    )(tables, first, second, other, rest, raw, grams)
+    )(tables, first, second, raw, grams, *others)
 
 
 def partner(value, axis, size, step):
@@ -296,30 +300,30 @@
     tables = jnp.asarray(dft_blocks(n))
 
     last = n // 2
-    early_rows = share // 2
+    early_rows = share - TRADED
     parts = ((0, early_rows), (early_rows, share - early_rows))
     targets = n * tm_count * freq_count
 
     def send(k, skip, size):
         sent = cut(snapshots, n, k, rows, skip, size)
-        return lax.ppermute(sent, "space", [(i, (i + k) % n) for i in range(n)])
-
-    offsets = [k for k in range(1, n) if k != last]
+        return partner(sent, "space", n, k)
+
+    offsets = [k for k in range(n - 1, 0, -1) if k != last]
     pieces = [send(k, 0, share) for k in offsets]
     last_pieces = [send(last, skip, size) for skip, size in parts]
     before = early(tables, n, 0, cut(snapshots, n, 0, rows, 0, share))
     for k, piece in zip(offsets, pieces):
         before = early(tables, n, k, piece, before)
     weights = weights.reshape(1, rows)
-    first, gram, other, rest = late(tables, n, last, 0, 2, before, last_pieces[0], weights)
-    other, rest = partner(other, "freq", freq_count, 1), partner(rest, "freq", freq_count, 1)
-    raw, other, rest = lax.optimization_barrier((last_pieces[1], other, rest))
+    first, gram, *others = late(tables, n, last, 0, 2, before, last_pieces[0], weights)
+    others = [partner(part, "freq", freq_count, 1) for part in others]
+    raw, others = lax.optimization_barrier((last_pieces[1], others))
     second, gram = late(tables, n, last, early_rows, targets, before, raw, weights, gram)
     raw = partner(raw, "freq", freq_count, 1)
     gram, raw = lax.optimization_barrier((gram, raw))
     grams = lax.all_to_all(gram, ("space", "tm", "freq"), split_axis=0, concat_axis=0, tiled=True)
     total = rows * n * tm_count
-    return finish(tables, n, last, total, first, second, other, rest, raw, grams)
+    return finish(tables, n, last, total, first, second, raw, grams, others)
 
 
 def solution(mesh):

time: 68.5 us -> 69.9 us (1.020)
  blocking collectives: 11.7 us -> 12.7 us
    ppermute x4 -> x0, waiting for transfers between devices: 34.7 us -> none  [send(): return lax.ppermute(sent, 'space', [(i, (i + k) % n) for i in range(n)])]
    ppermute x3 -> x9, waiting for transfers between devices: 0.51 us -> 34.9 us  [partner(): return lax.ppermute(value, axis, [(i, i ^ step) for i in range(size)])]
    ppermute x3 -> x9, starting transfers between devices: 0.59 us -> 9.35 us  [partner(): return lax.ppermute(value, axis, [(i, i ^ step) for i in range(size)])]
    ppermute x4 -> x0, starting transfers between devices: 8.24 us -> none  [send(): return lax.ppermute(sent, 'space', [(i, (i + k) % n) for i in range(n)])]
    all_to_all x1, blocking collectives: 11.7 us -> 12.7 us  [on_device(): lax.all_to_all(gram, ('space', 'tm', 'freq'), split_axis=0, concat_axis=0...]
  transfers between devices with their start and end apart: 7 -> 9, of which waited for: 5 -> 8; matrix products, arithmetic and copies ran while one was open for 0% -> 0% of each run, Pallas kernels for 12% -> 12%
where the time goes in v9:
time: 69.9 us; the launch traced here: 69.4 us
  waiting for transfers between devices  34.9 us (50%)
  blocking collectives  12.7 us (18%)
  Pallas kernels  11.7 us (17%)
  starting transfers between devices  9.35 us (13%)
  between operations  0.75 us (1%)
    ppermute x9, waiting for transfers between devices, partner(): return lax.ppermute(value, axis, [(i, i ^ step) for i in range(size)])  34.9 us
    all_to_all x1, blocking collectives, on_device(): lax.all_to_all(gram, ('space', 'tm', 'freq'), split_axis=0, concat_axis=0...  12.7 us
    ppermute x9, starting transfers between devices, partner(): return lax.ppermute(value, axis, [(i, i ^ step) for i in range(size)])  9.35 us
    pallas_call x5, Pallas kernels, cut(): pl.pallas_call(functools.partial(cut_kernel, n, k, rows, skip), out_shape...  5.81 us
    pallas_call x1, Pallas kernels, finish(): pl.pallas_call(functools.partial(finish_kernel, n, k, total), out_shape=(...  2.23 us
    pallas_call x2, Pallas kernels, late(): pl.pallas_call(functools.partial(late_kernel, n, k, skip), out_shape=[jax...  1.9 us
    pallas_call x3, Pallas kernels, early(): pl.pallas_call(functools.partial(early_kernel, n, k), out_shape=jax.Shape...  1.73 us
  transfers between devices with their start and end apart: 9, of which 8 were waited for; matrix products, arithmetic and copies ran while one was open for 0% of the time, Pallas kernels for 12%

profile of v9, /device:TPU:0, one launch (start us, length us, event | category | flops | bytes accessed | tf_op | source)
XLA Modules:
  0.0 69.4 jit_solution(1808550572056200380)
XLA Ops:
  0.6 1.2 %shard_map.51 = f32[16,16,512]{2,1,0:T(8,128)S(1)} custom-call(f32[16,16,4096]{2,1,0:T(8,128)} %x_ref.9), custom_call_target="tpu_custom_call" | custom-call | flops 1 | bytes 1 | tf_op jit(solution)/shard_map/pallas_call | solution.py:82
  1.8 5.1 %collective-permute-start.1 = (f32[256,512]{1,0:T(8,128)S(1)}, f32[256,512]{1,0:T(8,128)S(1)}, u32[]{:S(2)}, u32[]{:S(2)}) collective-permute-start(f32[256,512]{1,0:T(8,128)S(1)} %bitcast.8), channel_id=1, source_target_pairs={{0,12},{4,8},{8,4},{12,0},{1,13},{5,9},{9,5},{13,1},{2,14},{6,10},... | collective-permute-start | bytes 1572872 | tf_op jit(solution)/shard_map/ppermute | solution.py:289
  6.9 1.1 %shard_map.50 = f32[16,16,512]{2,1,0:T(8,128)S(1)} custom-call(f32[16,16,4096]{2,1,0:T(8,128)} %x_ref.9), custom_call_target="tpu_custom_call" | custom-call | flops 1 | bytes 1 | tf_op jit(solution)/shard_map/pallas_call | solution.py:82
  8.1 0.1 collective-permute-start
  8.1 1.1 %shard_map.56 = f32[16,16,384]{2,1,0:T(8,128)S(1)} custom-call(f32[16,16,4096]{2,1,0:T(8,128)} %x_ref.9), custom_call_target="tpu_custom_call" | custom-call | flops 1 | bytes 1 | tf_op jit(solution)/shard_map/pallas_call | solution.py:82
  9.2 0.0 copy-start
  9.2 0.6 collective-permute-start.2
  9.9 1.3 %shard_map.58 = f32[16,16,128]{2,1,0:T(8,128)S(1)} custom-call(f32[16,16,4096]{2,1,0:T(8,128)} %x_ref.9), custom_call_target="tpu_custom_call" | custom-call | flops 1 | bytes 1 | tf_op jit(solution)/shard_map/pallas_call | solution.py:82
  11.2 2.1 %collective-permute-start.3 = (f32[256,128]{1,0:T(8,128)S(1)}, f32[256,128]{1,0:T(8,128)S(1)}, u32[]{:S(2)}, u32[]{:S(2)}) collective-permute-start(f32[256,128]{1,0:T(8,128)S(1)} %bitcast.10), channel_id=1, source_target_pairs={{0,8},{4,12},{8,0},{12,4},{1,9},{5,13},{9,1},{13,5},{2,10},{6,14},... | collective-permute-start | bytes 393224 | tf_op jit(solution)/shard_map/ppermute | solution.py:289
  13.3 1.1 %shard_map.52 = f32[16,16,512]{2,1,0:T(8,128)S(1)} custom-call(f32[16,16,4096]{2,1,0:T(8,128)} %x_ref.9), custom_call_target="tpu_custom_call" | custom-call | flops 1 | bytes 1 | tf_op jit(solution)/shard_map/pallas_call | solution.py:82
  14.5 0.6 shard_map.53.refs_0_
  15.0 4.7 %collective-permute-done.1.x_ref = f32[256,512]{1,0:T(8,128)S(1)} collective-permute-done((f32[256,512]{1,0:T(8,128)S(1)}, f32[256,512]{1,0:T(8,128)S(1)}, u32[]{:S(2)}, u32[]{:S(2)}) %collective-permute-start.1) | collective-permute-done | bytes 524320 | tf_op jit(solution)/shard_map/ppermute | solution.py:289
  19.7 0.6 shard_map.54.refs_0_
  20.3 0.0 copy-start.1
  20.3 10.9 %collective-permute-done.x_ref = f32[256,512]{1,0:T(8,128)S(1)} collective-permute-done((f32[256,512]{1,0:T(8,128)S(1)}, f32[256,512]{1,0:T(8,128)S(1)}, u32[]{:S(2)}, u32[]{:S(2)}) %collective-permute-start) | collective-permute-done | bytes 524320 | tf_op jit(solution)/shard_map/ppermute | solution.py:289
  31.2 0.6 shard_map.55.sum_ref
  31.8 18.1 %collective-permute-done.2.x_ref = f32[256,384]{1,0:T(8,128)S(1)} collective-permute-done((f32[256,384]{1,0:T(8,128)S(1)}, f32[256,384]{1,0:T(8,128)S(1)}, u32[]{:S(2)}, u32[]{:S(2)}) %collective-permute-start.2) | collective-permute-done | bytes 393248 | tf_op jit(solution)/shard_map/ppermute | solution.py:289
  49.8 1.2 %shard_map.57 = (f32[256,384]{1,0:T(8,128)S(1)}, f32[2,16,128]{2,1,0:T(8,128)S(1)}, f32[256,128]{1,0:T(8,128)S(1)}, f32[256,128]{1,0:T(8,128)S(1)}, f32[256,128]{1,0:T(8,128)S(1)}, /*index=5*/f32[256,128]{1,0:T(8,128)S(1)}) custom-call(bf16[4,512,768]{2,1,0:T(8,128)(2,1)S(1)} %copy-done, f32[512,512]{1,0:T(8,128)S(1)} %shard_map.55.sum_ref, ...), custom_call_target="tpu_custom_call" | custom-call | flops 1 | bytes 1 | tf_op jit(solution)/shard_map/pallas_call | solution.py:162
  51.0 0.1 collective-permute-start.4
  51.1 0.5 collective-permute-start.5
  51.6 0.1 collective-permute-start.6
  51.7 0.4 collective-permute-start.7
  52.1 0.0 collective-permute-done.3.x_ref
  52.1 0.3 collective-permute-done.4.refs_0_
  52.5 0.2 collective-permute-done.5.refs_1_
  52.6 0.3 collective-permute-done.6.refs_2_
  53.0 0.2 collective-permute-done.7.refs_3_
  53.2 0.3 collective-permute-start.8
  53.5 0.7 %shard_map.59 = (f32[256,128]{1,0:T(8,128)S(1)}, f32[16,16,128]{2,1,0:T(8,128)S(1)}) custom-call(bf16[4,512,768]{2,1,0:T(8,128)(2,1)S(1)} %copy-done, f32[512,512]{1,0:T(8,128)S(1)} %shard_map.55.sum_ref, f32[256,128]{1,0:T(8,128)S(1)} %collective-permute-done.3.x_ref, f32[1,1024]{1,0:T(1,128)S(1)} %bitcast.12, f32[2,16,128]{2,1,0:T(8,128)S(1)} %get-tuple-element.23.refs_0_), custom_call_target="tpu_custom_call" | custom-call | flops 1 | bytes 1 | tf_op jit(solution)/shard_map/pallas_call | solution.py:162
  54.2 0.3 collective-permute-done.8.raw_ref
  54.5 12.7 %all_to_all.5.grams_ref = f32[16,16,128]{2,1,0:T(8,128)S(1)} all-to-all(f32[16,16,128]{2,1,0:T(8,128)S(1)} %get-tuple-element.27), channel_id=1, replica_groups=mesh['groups'=2,'space'=4,'tm'=2,'freq'=2] {'space','tm','freq'}, dimensions={0} | all-to-all | bytes 262144 | tf_op jit(solution)/shard_map/all_to_all | solution.py:324
  67.2 2.2 %shard_map.60 = (f32[8,2,16,1024]{3,2,1,0:T(8,128)}, f32[2,8,16,16]{3,2,1,0:T(8,128)}) custom-call(bf16[4,512,768]{2,1,0:T(8,128)(2,1)S(1)} %copy-done, f32[256,384]{1,0:T(8,128)S(1)} %get-tuple-element.17.first_ref, f32[256,128]{1,0:T(8,128)S(1)} %get-tuple-element.24.second_ref, f32[256,128]{1,0:T(8,128)S(1)} %collective-permute-done.8.raw_ref, ...), custom_call_target="tpu_custom_call" | custom-call | tf_op jit(solution)/shard_map/pallas_call | solution.py:278
  (2 shorter events, 0.0 us)
Async XLA Ops:
  1.8 18.0 %collective-permute-start.1 = (f32[256,512]{1,0:T(8,128)S(1)}, f32[256,512]{1,0:T(8,128)S(1)}, u32[]{:S(2)}, u32[]{:S(2)}) collective-permute-start(f32[256,512]{1,0:T(8,128)S(1)} %bitcast.8), channel_id=1, source_target_pairs={{0,12},{4,8},{8,4},{12,0},{1,13},{5,9},{9,5},{13,1},{2,14},{6,10},... | collective-permute-start | bytes 1572872 | tf_op jit(solution)/shard_map/ppermute | solution.py:289
  8.1 23.1 %collective-permute-start = (f32[256,512]{1,0:T(8,128)S(1)}, f32[256,512]{1,0:T(8,128)S(1)}, u32[]{:S(2)}, u32[]{:S(2)}) collective-permute-start(f32[256,512]{1,0:T(8,128)S(1)} %bitcast.7), channel_id=1, source_target_pairs={{0,4},{4,0},{8,12},{12,8},{1,5},{5,1},{9,13},{13,9},{2,6},{6,2},{1... | collective-permute-start | bytes 1572872 | tf_op jit(solution)/shard_map/ppermute | solution.py:289
  9.2 5.2 %copy-start = (bf16[4,512,768]{2,1,0:T(8,128)(2,1)S(1)}, bf16[4,512,768]{2,1,0:T(8,128)(2,1)}, u32[]{:S(2)}) copy-start(bf16[4,512,768]{2,1,0:T(8,128)(2,1)} %constant.2.clone.t_ref) | copy-start | bytes 9437188
  9.2 40.6 %collective-permute-start.2 = (f32[256,384]{1,0:T(8,128)S(1)}, f32[256,384]{1,0:T(8,128)S(1)}, u32[]{:S(2)}, u32[]{:S(2)}) collective-permute-start(f32[256,384]{1,0:T(8,128)S(1)} %bitcast.9), channel_id=1, source_target_pairs={{0,8},{4,12},{8,0},{12,4},{1,9},{5,13},{9,1},{13,5},{2,10},{6,14},... | collective-permute-start | bytes 1179656 | tf_op jit(solution)/shard_map/ppermute | solution.py:289
  11.2 41.0 %collective-permute-start.3 = (f32[256,128]{1,0:T(8,128)S(1)}, f32[256,128]{1,0:T(8,128)S(1)}, u32[]{:S(2)}, u32[]{:S(2)}) collective-permute-start(f32[256,128]{1,0:T(8,128)S(1)} %bitcast.10), channel_id=1, source_target_pairs={{0,8},{4,12},{8,0},{12,4},{1,9},{5,13},{9,1},{13,5},{2,10},{6,14},... | collective-permute-start | bytes 393224 | tf_op jit(solution)/shard_map/ppermute | solution.py:289
  20.3 29.5 %copy-start.1 = (f32[1024]{0:T(1024)S(1)}, f32[1024]{0:T(1024)}, u32[]{:S(2)}) copy-start(f32[1024]{0:T(1024)} %param.4) | copy-start | bytes 12292
  51.0 1.4 %collective-permute-start.4 = (f32[256,128]{1,0:T(8,128)S(1)}, f32[256,128]{1,0:T(8,128)S(1)}, u32[]{:S(2)}, u32[]{:S(2)}) collective-permute-start(f32[256,128]{1,0:T(8,128)S(1)} %get-tuple-element.18), channel_id=1, source_target_pairs={{0,1},{1,0},{2,3},{3,2},{4,5},{5,4},{6,7},{7,6},{8,9},{9,8},{10,11... | collective-permute-start | bytes 393224 | tf_op jit(solution)/shard_map/ppermute | solution.py:289
  51.1 1.5 %collective-permute-start.5 = (f32[256,128]{1,0:T(8,128)S(1)}, f32[256,128]{1,0:T(8,128)S(1)}, u32[]{:S(2)}, u32[]{:S(2)}) collective-permute-start(f32[256,128]{1,0:T(8,128)S(1)} %get-tuple-element.19), channel_id=1, source_target_pairs={{0,1},{1,0},{2,3},{3,2},{4,5},{5,4},{6,7},{7,6},{8,9},{9,8},{10,11... | collective-permute-start | bytes 393224 | tf_op jit(solution)/shard_map/ppermute | solution.py:289
  51.6 1.3 %collective-permute-start.6 = (f32[256,128]{1,0:T(8,128)S(1)}, f32[256,128]{1,0:T(8,128)S(1)}, u32[]{:S(2)}, u32[]{:S(2)}) collective-permute-start(f32[256,128]{1,0:T(8,128)S(1)} %get-tuple-element.20), channel_id=1, source_target_pairs={{0,1},{1,0},{2,3},{3,2},{4,5},{5,4},{6,7},{7,6},{8,9},{9,8},{10,11... | collective-permute-start | bytes 393224 | tf_op jit(solution)/shard_map/ppermute | solution.py:289
  51.7 1.5 %collective-permute-start.7 = (f32[256,128]{1,0:T(8,128)S(1)}, f32[256,128]{1,0:T(8,128)S(1)}, u32[]{:S(2)}, u32[]{:S(2)}) collective-permute-start(f32[256,128]{1,0:T(8,128)S(1)} %get-tuple-element.21), channel_id=1, source_target_pairs={{0,1},{1,0},{2,3},{3,2},{4,5},{5,4},{6,7},{7,6},{8,9},{9,8},{10,11... | collective-permute-start | bytes 393224 | tf_op jit(solution)/shard_map/ppermute | solution.py:289
  53.2 1.3 %collective-permute-start.8 = (f32[256,128]{1,0:T(8,128)S(1)}, f32[256,128]{1,0:T(8,128)S(1)}, u32[]{:S(2)}, u32[]{:S(2)}) collective-permute-start(f32[256,128]{1,0:T(8,128)S(1)} %collective-permute-done.3.x_ref), channel_id=1, source_target_pairs={{0,1},{1,0},{2,3},{3,2},{4,5},{5,4},{6,7},{7,6},{8,9},{9,8},{10,11... | collective-permute-start | bytes 393224 | tf_op jit(solution)/shard_map/ppermute | solution.py:289

commit v10 on v8

--- a/solution.py
+++ b/solution.py
@@ -148,7 +148,7 @@
     if skip:
         packed = [packed[h] + before_ref[h] for h in range(2)]
     for d in range(gram_ref.shape[0]):
-        gram_ref[d] = packed[d % 2]
+        gram_ref[d] = packed[(d + 1) % 2 if skip else d]
 
 
 def late(tables, n, k, skip, targets, partial_sum, piece, weights, *before):
@@ -317,7 +317,14 @@
     second, gram = late(tables, n, last, early_rows, targets, before, raw, weights, gram)
     raw = partner(raw, "freq", freq_count, 1)
     gram, raw = lax.optimization_barrier((gram, raw))
-    grams = lax.all_to_all(gram, ("space", "tm", "freq"), split_axis=0, concat_axis=0, tiled=True)
+    grams = lax.all_to_all(
+        gram,
+        ("space", "tm", "freq"),
+        split_axis=0,
+        concat_axis=0,
+        axis_index_groups=[list(range(targets - 1, -1, -1))],
+        tiled=True,
+    )
     total = rows * n * tm_count
     return finish(tables, n, last, total, first, second, other, rest, raw, grams)
 

time: 68.5 us -> 66.5 us (0.971)
  blocking collectives: 11.7 us -> 9.68 us
    all_to_all x1, blocking collectives: 11.7 us -> 9.68 us  [on_device(): lax.all_to_all(gram, ('space', 'tm', 'freq'), split_axis=0, concat_axis=0...]
where the time goes in v10:
time: 66.5 us; the launch traced here: 66 us
  waiting for transfers between devices  35.2 us (53%)
  Pallas kernels  11.5 us (17%)
  blocking collectives  9.68 us (15%)
  starting transfers between devices  8.83 us (13%)
  between operations  0.74 us (1%)
    ppermute x4, waiting for transfers between devices, send(): return lax.ppermute(sent, 'space', [(i, (i + k) % n) for i in range(n)])  34.7 us
    all_to_all x1, blocking collectives, on_device(): lax.all_to_all(gram, ('space', 'tm', 'freq'), split_axis=0, concat_axis=0...  9.68 us
    ppermute x4, starting transfers between devices, send(): return lax.ppermute(sent, 'space', [(i, (i + k) % n) for i in range(n)])  8.24 us
    pallas_call x5, Pallas kernels, cut(): pl.pallas_call(functools.partial(cut_kernel, n, k, rows, skip), out_shape...  5.51 us
    pallas_call x1, Pallas kernels, finish(): pl.pallas_call(functools.partial(finish_kernel, n, k, total), out_shape=(...  2.25 us
    pallas_call x2, Pallas kernels, late(): pl.pallas_call(functools.partial(late_kernel, n, k, skip), out_shape=[jax...  2.03 us
    pallas_call x3, Pallas kernels, early(): pl.pallas_call(functools.partial(early_kernel, n, k), out_shape=jax.Shape...  1.73 us
  transfers between devices with their start and end apart: 7, of which 5 were waited for; matrix products, arithmetic and copies ran while one was open for 0% of the time, Pallas kernels for 12%

profile of v10, /device:TPU:0, one launch (start us, length us, event | category | flops | bytes accessed | tf_op | source)
XLA Modules:
  0.0 66.0 jit_solution(5880542108535090231)
XLA Ops:
  0.6 1.2 %shard_map.51 = f32[16,16,512]{2,1,0:T(8,128)S(1)} custom-call(f32[16,16,4096]{2,1,0:T(8,128)} %x_ref.9), custom_call_target="tpu_custom_call" | custom-call | flops 1 | bytes 1 | tf_op jit(solution)/shard_map/pallas_call | solution.py:81
  1.8 3.1 %collective-permute-start.1 = (f32[256,512]{1,0:T(8,128)S(1)}, f32[256,512]{1,0:T(8,128)S(1)}, u32[]{:S(2)}, u32[]{:S(2)}) collective-permute-start(f32[256,512]{1,0:T(8,128)S(1)} %bitcast.8), channel_id=1, source_target_pairs={{0,4},{4,8},{8,12},{12,0},{1,5},{5,9},{9,13},{13,1},{2,6},{6,10},{... | collective-permute-start | bytes 1572872 | tf_op jit(solution)/shard_map/ppermute | solution.py:305
  4.9 1.1 %shard_map.50 = f32[16,16,512]{2,1,0:T(8,128)S(1)} custom-call(f32[16,16,4096]{2,1,0:T(8,128)} %x_ref.9), custom_call_target="tpu_custom_call" | custom-call | flops 1 | bytes 1 | tf_op jit(solution)/shard_map/pallas_call | solution.py:81
  6.0 2.1 %collective-permute-start = (f32[256,512]{1,0:T(8,128)S(1)}, f32[256,512]{1,0:T(8,128)S(1)}, u32[]{:S(2)}, u32[]{:S(2)}) collective-permute-start(f32[256,512]{1,0:T(8,128)S(1)} %bitcast.7), channel_id=1, source_target_pairs={{0,12},{4,0},{8,4},{12,8},{1,13},{5,1},{9,5},{13,9},{2,14},{6,2},{... | collective-permute-start | bytes 1572872 | tf_op jit(solution)/shard_map/ppermute | solution.py:305
  8.1 1.0 %shard_map.56 = f32[16,16,256]{2,1,0:T(8,128)S(1)} custom-call(f32[16,16,4096]{2,1,0:T(8,128)} %x_ref.9), custom_call_target="tpu_custom_call" | custom-call | flops 1 | bytes 1 | tf_op jit(solution)/shard_map/pallas_call | solution.py:81
  9.2 0.0 copy-start
  9.2 1.0 %collective-permute-start.2 = (f32[256,256]{1,0:T(8,128)S(1)}, f32[256,256]{1,0:T(8,128)S(1)}, u32[]{:S(2)}, u32[]{:S(2)}) collective-permute-start(f32[256,256]{1,0:T(8,128)S(1)} %bitcast.10), channel_id=1, source_target_pairs={{0,8},{4,12},{8,0},{12,4},{1,9},{5,13},{9,1},{13,5},{2,10},{6,14},... | collective-permute-start | bytes 786440 | tf_op jit(solution)/shard_map/ppermute | solution.py:305
  10.2 1.0 %shard_map.58 = f32[16,16,256]{2,1,0:T(8,128)S(1)} custom-call(f32[16,16,4096]{2,1,0:T(8,128)} %x_ref.9), custom_call_target="tpu_custom_call" | custom-call | flops 1 | bytes 1 | tf_op jit(solution)/shard_map/pallas_call | solution.py:81
  11.3 2.0 %collective-permute-start.3 = (f32[256,256]{1,0:T(8,128)S(1)}, f32[256,256]{1,0:T(8,128)S(1)}, u32[]{:S(2)}, u32[]{:S(2)}) collective-permute-start(f32[256,256]{1,0:T(8,128)S(1)} %bitcast.9), channel_id=1, source_target_pairs={{0,8},{4,12},{8,0},{12,4},{1,9},{5,13},{9,1},{13,5},{2,10},{6,14},... | collective-permute-start | bytes 786440 | tf_op jit(solution)/shard_map/ppermute | solution.py:305
  13.3 1.1 %shard_map.52 = f32[16,16,512]{2,1,0:T(8,128)S(1)} custom-call(f32[16,16,4096]{2,1,0:T(8,128)} %x_ref.9), custom_call_target="tpu_custom_call" | custom-call | flops 1 | bytes 1 | tf_op jit(solution)/shard_map/pallas_call | solution.py:81
  14.4 0.0 copy-done
  14.4 0.6 shard_map.53.refs_0_
  15.0 4.7 %collective-permute-done.1.x_ref = f32[256,512]{1,0:T(8,128)S(1)} collective-permute-done((f32[256,512]{1,0:T(8,128)S(1)}, f32[256,512]{1,0:T(8,128)S(1)}, u32[]{:S(2)}, u32[]{:S(2)}) %collective-permute-start.1) | collective-permute-done | bytes 524320 | tf_op jit(solution)/shard_map/ppermute | solution.py:305
  19.7 0.6 shard_map.54.refs_0_
  20.3 0.0 copy-start.1
  20.3 9.8 %collective-permute-done.x_ref = f32[256,512]{1,0:T(8,128)S(1)} collective-permute-done((f32[256,512]{1,0:T(8,128)S(1)}, f32[256,512]{1,0:T(8,128)S(1)}, u32[]{:S(2)}, u32[]{:S(2)}) %collective-permute-start) | collective-permute-done | bytes 524320 | tf_op jit(solution)/shard_map/ppermute | solution.py:305
  30.1 0.6 shard_map.55.sum_ref
  30.6 16.4 %collective-permute-done.2.x_ref = f32[256,256]{1,0:T(8,128)S(1)} collective-permute-done((f32[256,256]{1,0:T(8,128)S(1)}, f32[256,256]{1,0:T(8,128)S(1)}, u32[]{:S(2)}, u32[]{:S(2)}) %collective-permute-start.2) | collective-permute-done | bytes 262176 | tf_op jit(solution)/shard_map/ppermute | solution.py:305
  47.0 0.0 copy-done.1
  47.0 1.0 %shard_map.57 = (f32[256,256]{1,0:T(8,128)S(1)}, f32[2,16,128]{2,1,0:T(8,128)S(1)}, f32[256,256]{1,0:T(8,128)S(1)}, f32[256,256]{1,0:T(8,128)S(1)}) custom-call(bf16[4,512,768]{2,1,0:T(8,128)(2,1)S(1)} %copy-done, f32[512,512]{1,0:T(8,128)S(1)} %shard_map.55.sum_ref, f32[256,256]{1,0:T(8,128)S(1)} %collective-permute-done.2.x_ref, f32[1,1024]{1,0:T(1,128)S(1)} %bitcast.11), custom_call_target="tpu_custom_call" | custom-call | flops 1 | bytes 1 | tf_op jit(solution)/shard_map/pallas_call | solution.py:160
  48.0 0.1 collective-permute-start.4
  48.1 0.5 collective-permute-start.5
  48.6 3.9 %collective-permute-done.3.x_ref = f32[256,256]{1,0:T(8,128)S(1)} collective-permute-done((f32[256,256]{1,0:T(8,128)S(1)}, f32[256,256]{1,0:T(8,128)S(1)}, u32[]{:S(2)}, u32[]{:S(2)}) %collective-permute-start.3) | collective-permute-done | bytes 262176 | tf_op jit(solution)/shard_map/ppermute | solution.py:305
  52.5 0.0 collective-permute-done.4.other_ref
  52.5 0.0 collective-permute-done.5.rest_ref
  52.5 0.0 collective-permute-start.6
  52.5 1.0 %shard_map.59 = (f32[256,256]{1,0:T(8,128)S(1)}, f32[16,16,128]{2,1,0:T(8,128)S(1)}) custom-call(bf16[4,512,768]{2,1,0:T(8,128)(2,1)S(1)} %copy-done, f32[512,512]{1,0:T(8,128)S(1)} %shard_map.55.sum_ref, f32[256,256]{1,0:T(8,128)S(1)} %collective-permute-done.3.x_ref, f32[1,1024]{1,0:T(1,128)S(1)} %bitcast.12, f32[2,16,128]{2,1,0:T(8,128)S(1)} %get-tuple-element.17.refs_0_), custom_call_target="tpu_custom_call" | custom-call | flops 1 | bytes 1 | tf_op jit(solution)/shard_map/pallas_call | solution.py:160
  53.6 0.5 collective-permute-done.6.raw_ref
  54.1 9.7 %all_to_all.5.grams_ref = f32[16,16,128]{2,1,0:T(8,128)S(1)} all-to-all(f32[16,16,128]{2,1,0:T(8,128)S(1)} %get-tuple-element.23), channel_id=1, replica_groups={{15,14,13,12,11,10,9,8,7,6,5,4,3,2,1,0},{31,30,29,28,27,26,25,24,23,22,..., dimensions={0} | all-to-all | bytes 262144 | tf_op jit(solution)/shard_map/all_to_all | solution.py:320
  63.7 2.3 %shard_map.60 = (f32[8,2,16,1024]{3,2,1,0:T(8,128)}, f32[2,8,16,16]{3,2,1,0:T(8,128)}) custom-call(bf16[4,512,768]{2,1,0:T(8,128)(2,1)S(1)} %copy-done, f32[256,256]{1,0:T(8,128)S(1)} %get-tuple-element.13.first_ref, f32[256,256]{1,0:T(8,128)S(1)} %get-tuple-element.18.second_ref, f32[256,256]{1,0:T(8,128)S(1)} %collective-permute-done.4.other_ref, ...), custom_call_target="tpu_custom_call" | custom-call | tf_op jit(solution)/shard_map/pallas_call | solution.py:274
Async XLA Ops:
  1.8 17.9 %collective-permute-start.1 = (f32[256,512]{1,0:T(8,128)S(1)}, f32[256,512]{1,0:T(8,128)S(1)}, u32[]{:S(2)}, u32[]{:S(2)}) collective-permute-start(f32[256,512]{1,0:T(8,128)S(1)} %bitcast.8), channel_id=1, source_target_pairs={{0,4},{4,8},{8,12},{12,0},{1,5},{5,9},{9,13},{13,1},{2,6},{6,10},{... | collective-permute-start | bytes 1572872 | tf_op jit(solution)/shard_map/ppermute | solution.py:305
  6.0 24.0 %collective-permute-start = (f32[256,512]{1,0:T(8,128)S(1)}, f32[256,512]{1,0:T(8,128)S(1)}, u32[]{:S(2)}, u32[]{:S(2)}) collective-permute-start(f32[256,512]{1,0:T(8,128)S(1)} %bitcast.7), channel_id=1, source_target_pairs={{0,12},{4,0},{8,4},{12,8},{1,13},{5,1},{9,5},{13,9},{2,14},{6,2},{... | collective-permute-start | bytes 1572872 | tf_op jit(solution)/shard_map/ppermute | solution.py:305
  9.2 5.3 %copy-start = (bf16[4,512,768]{2,1,0:T(8,128)(2,1)S(1)}, bf16[4,512,768]{2,1,0:T(8,128)(2,1)}, u32[]{:S(2)}) copy-start(bf16[4,512,768]{2,1,0:T(8,128)(2,1)} %constant.2.clone.t_ref) | copy-start | bytes 9437188
  9.2 37.8 %collective-permute-start.2 = (f32[256,256]{1,0:T(8,128)S(1)}, f32[256,256]{1,0:T(8,128)S(1)}, u32[]{:S(2)}, u32[]{:S(2)}) collective-permute-start(f32[256,256]{1,0:T(8,128)S(1)} %bitcast.10), channel_id=1, source_target_pairs={{0,8},{4,12},{8,0},{12,4},{1,9},{5,13},{9,1},{13,5},{2,10},{6,14},... | collective-permute-start | bytes 786440 | tf_op jit(solution)/shard_map/ppermute | solution.py:305
  11.3 41.2 %collective-permute-start.3 = (f32[256,256]{1,0:T(8,128)S(1)}, f32[256,256]{1,0:T(8,128)S(1)}, u32[]{:S(2)}, u32[]{:S(2)}) collective-permute-start(f32[256,256]{1,0:T(8,128)S(1)} %bitcast.9), channel_id=1, source_target_pairs={{0,8},{4,12},{8,0},{12,4},{1,9},{5,13},{9,1},{13,5},{2,10},{6,14},... | collective-permute-start | bytes 786440 | tf_op jit(solution)/shard_map/ppermute | solution.py:305
  20.3 26.7 %copy-start.1 = (f32[1024]{0:T(1024)S(1)}, f32[1024]{0:T(1024)}, u32[]{:S(2)}) copy-start(f32[1024]{0:T(1024)} %param.4) | copy-start | bytes 12292
  48.0 4.5 %collective-permute-start.4 = (f32[256,256]{1,0:T(8,128)S(1)}, f32[256,256]{1,0:T(8,128)S(1)}, u32[]{:S(2)}, u32[]{:S(2)}) collective-permute-start(f32[256,256]{1,0:T(8,128)S(1)} %get-tuple-element.14), channel_id=1, source_target_pairs={{0,1},{1,0},{2,3},{3,2},{4,5},{5,4},{6,7},{7,6},{8,9},{9,8},{10,11... | collective-permute-start | bytes 786440 | tf_op jit(solution)/shard_map/ppermute | solution.py:285
  48.1 4.4 %collective-permute-start.5 = (f32[256,256]{1,0:T(8,128)S(1)}, f32[256,256]{1,0:T(8,128)S(1)}, u32[]{:S(2)}, u32[]{:S(2)}) collective-permute-start(f32[256,256]{1,0:T(8,128)S(1)} %get-tuple-element.15), channel_id=1, source_target_pairs={{0,1},{1,0},{2,3},{3,2},{4,5},{5,4},{6,7},{7,6},{8,9},{9,8},{10,11... | collective-permute-start | bytes 786440 | tf_op jit(solution)/shard_map/ppermute | solution.py:285
  52.5 1.5 %collective-permute-start.6 = (f32[256,256]{1,0:T(8,128)S(1)}, f32[256,256]{1,0:T(8,128)S(1)}, u32[]{:S(2)}, u32[]{:S(2)}) collective-permute-start(f32[256,256]{1,0:T(8,128)S(1)} %collective-permute-done.3.x_ref), channel_id=1, source_target_pairs={{0,1},{1,0},{2,3},{3,2},{4,5},{5,4},{6,7},{7,6},{8,9},{9,8},{10,11... | collective-permute-start | bytes 786440 | tf_op jit(solution)/shard_map/ppermute | solution.py:285

commit v11 on v10

--- a/solution.py
+++ b/solution.py
@@ -57,7 +57,7 @@
 
 def cut_kernel(n, k, rows, skip, x_ref, o_ref, sem):
     size = o_ref.shape[2]
-    to = lax.rem(lax.axis_index("space") + k, n)
+    to = lax.bitwise_xor(lax.axis_index("space"), k)
     share = rows // 2
     start = pl.multiple_of(to * rows + lax.axis_index("freq") * share + skip, 128)
     part = NB // CUTS
@@ -88,14 +88,14 @@
             cost_estimate=SMALL,
         )(pltpu.with_memory_space_constraint(snapshots, pltpu.HBM))
     else:
-        to = lax.rem(lax.axis_index("space") + k, n)
+        to = lax.bitwise_xor(lax.axis_index("space"), k)
         start = to * rows + lax.axis_index("freq") * (rows // 2) + skip
         piece = lax.dynamic_slice_in_dim(snapshots, start, size, axis=2)
     return piece.reshape(blocks * local_times, size)
 
 
 def early_kernel(n, k, t_ref, x_ref, *refs):
-    src = lax.rem(lax.axis_index("space") - k + n, n)
+    src = lax.bitwise_xor(lax.axis_index("space"), k)
     part = times_split(t_ref[src], x_ref[...])
     refs[-1][...] = part if len(refs) == 1 else refs[0][...] + part
 
@@ -116,7 +116,7 @@
     cols = pl.ds(skip, size)
     at = lax.axis_index("freq") * share + skip
     weights = w_ref[:, pl.ds(pl.multiple_of(at, 128), size)]
-    src = lax.rem(lax.axis_index("space") - k + n, n)
+    src = lax.bitwise_xor(lax.axis_index("space"), k)
     spectra = sum_ref[:, cols] + times_split(t_ref[src], x_ref[...])
     half = spectra.shape[0] // 2
     width = half // 2
@@ -248,7 +248,7 @@
     me = lax.axis_index("freq")
     high, low = split(mixing)
     mixing = jnp.concatenate([high, high, low], axis=1)
-    src = lax.rem(lax.axis_index("space") - k + n, n)
+    src = lax.bitwise_xor(lax.axis_index("space"), k)
     lines = pl.ds(pl.multiple_of(me * 2 * width, 128), 2 * width)
     own = [first_ref[...], second_ref[...]]
     added = times_split(t_ref[src, lines], raw_ref[...])
@@ -302,9 +302,9 @@
 
     def send(k, skip, size):
         sent = cut(snapshots, n, k, rows, skip, size)
-        return lax.ppermute(sent, "space", [(i, (i + k) % n) for i in range(n)])
-
-    offsets = [k for k in range(1, n) if k != last]
+        return partner(sent, "space", n, k)
+
+    offsets = [k for k in range(n - 1, 0, -1) if k != last]
     pieces = [send(k, 0, share) for k in offsets]
     last_pieces = [send(last, skip, size) for skip, size in parts]
     before = early(tables, n, 0, cut(snapshots, n, 0, rows, 0, share))

time: 66.5 us -> 65.8 us (0.989)
  waiting for transfers between devices: 35.2 us -> 34.4 us
    ppermute x4 -> x0, waiting for transfers between devices: 34.7 us -> none  [send(): return lax.ppermute(sent, 'space', [(i, (i + k) % n) for i in range(n)])]
    ppermute x3 -> x7, waiting for transfers between devices: 0.51 us -> 34.4 us  [partner(): return lax.ppermute(value, axis, [(i, i ^ step) for i in range(size)])]
    ppermute x4 -> x0, starting transfers between devices: 8.24 us -> none  [send(): return lax.ppermute(sent, 'space', [(i, (i + k) % n) for i in range(n)])]
    ppermute x3 -> x7, starting transfers between devices: 0.59 us -> 8.53 us  [partner(): return lax.ppermute(value, axis, [(i, i ^ step) for i in range(size)])]
  transfers between devices with their start and end apart: 7 -> 7, of which waited for: 5 -> 5; matrix products, arithmetic and copies ran while one was open for 0% -> 0% of each run, Pallas kernels for 12% -> 13%
where the time goes in v11:
time: 65.8 us; the launch traced here: 65.3 us
  waiting for transfers between devices  34.4 us (52%)
  Pallas kernels  11.8 us (18%)
  blocking collectives  9.8 us (15%)
  starting transfers between devices  8.53 us (13%)
  between operations  0.76 us (1%)
    ppermute x7, waiting for transfers between devices, partner(): return lax.ppermute(value, axis, [(i, i ^ step) for i in range(size)])  34.4 us
    all_to_all x1, blocking collectives, on_device(): lax.all_to_all(gram, ('space', 'tm', 'freq'), split_axis=0, concat_axis=0...  9.8 us
    ppermute x7, starting transfers between devices, partner(): return lax.ppermute(value, axis, [(i, i ^ step) for i in range(size)])  8.53 us
    pallas_call x5, Pallas kernels, cut(): pl.pallas_call(functools.partial(cut_kernel, n, k, rows, skip), out_shape...  5.8 us
    pallas_call x1, Pallas kernels, finish(): pl.pallas_call(functools.partial(finish_kernel, n, k, total), out_shape=(...  2.25 us
    pallas_call x2, Pallas kernels, late(): pl.pallas_call(functools.partial(late_kernel, n, k, skip), out_shape=[jax...  2.04 us
    pallas_call x3, Pallas kernels, early(): pl.pallas_call(functools.partial(early_kernel, n, k), out_shape=jax.Shape...  1.73 us
  transfers between devices with their start and end apart: 7, of which 5 were waited for; matrix products, arithmetic and copies ran while one was open for 0% of the time, Pallas kernels for 13%

profile of v11, /device:TPU:0, one launch (start us, length us, event | category | flops | bytes accessed | tf_op | source)
XLA Modules:
  0.0 65.3 jit_solution(9779342971220905102)
XLA Ops:
  0.6 1.2 %shard_map.51 = f32[16,16,512]{2,1,0:T(8,128)S(1)} custom-call(f32[16,16,4096]{2,1,0:T(8,128)} %x_ref.9), custom_call_target="tpu_custom_call" | custom-call | flops 1 | bytes 1 | tf_op jit(solution)/shard_map/pallas_call | solution.py:81
  1.8 5.1 %collective-permute-start.1 = (f32[256,512]{1,0:T(8,128)S(1)}, f32[256,512]{1,0:T(8,128)S(1)}, u32[]{:S(2)}, u32[]{:S(2)}) collective-permute-start(f32[256,512]{1,0:T(8,128)S(1)} %bitcast.8), channel_id=1, source_target_pairs={{0,12},{4,8},{8,4},{12,0},{1,13},{5,9},{9,5},{13,1},{2,14},{6,10},... | collective-permute-start | bytes 1572872 | tf_op jit(solution)/shard_map/ppermute | solution.py:285
  6.9 1.1 %shard_map.50 = f32[16,16,512]{2,1,0:T(8,128)S(1)} custom-call(f32[16,16,4096]{2,1,0:T(8,128)} %x_ref.9), custom_call_target="tpu_custom_call" | custom-call | flops 1 | bytes 1 | tf_op jit(solution)/shard_map/pallas_call | solution.py:81
  8.1 0.1 collective-permute-start
  8.1 1.1 %shard_map.56 = f32[16,16,256]{2,1,0:T(8,128)S(1)} custom-call(f32[16,16,4096]{2,1,0:T(8,128)} %x_ref.9), custom_call_target="tpu_custom_call" | custom-call | flops 1 | bytes 1 | tf_op jit(solution)/shard_map/pallas_call | solution.py:81
  9.2 0.0 copy-start
  9.2 0.6 collective-permute-start.2
  9.8 1.3 %shard_map.58 = f32[16,16,256]{2,1,0:T(8,128)S(1)} custom-call(f32[16,16,4096]{2,1,0:T(8,128)} %x_ref.9), custom_call_target="tpu_custom_call" | custom-call | flops 1 | bytes 1 | tf_op jit(solution)/shard_map/pallas_call | solution.py:81
  11.2 2.1 %collective-permute-start.3 = (f32[256,256]{1,0:T(8,128)S(1)}, f32[256,256]{1,0:T(8,128)S(1)}, u32[]{:S(2)}, u32[]{:S(2)}) collective-permute-start(f32[256,256]{1,0:T(8,128)S(1)} %bitcast.9), channel_id=1, source_target_pairs={{0,8},{4,12},{8,0},{12,4},{1,9},{5,13},{9,1},{13,5},{2,10},{6,14},... | collective-permute-start | bytes 786440 | tf_op jit(solution)/shard_map/ppermute | solution.py:285
  13.3 1.1 %shard_map.52 = f32[16,16,512]{2,1,0:T(8,128)S(1)} custom-call(f32[16,16,4096]{2,1,0:T(8,128)} %x_ref.9), custom_call_target="tpu_custom_call" | custom-call | flops 1 | bytes 1 | tf_op jit(solution)/shard_map/pallas_call | solution.py:81
  14.4 0.0 copy-done
  14.5 0.6 shard_map.53.refs_0_
  15.0 4.7 %collective-permute-done.1.x_ref = f32[256,512]{1,0:T(8,128)S(1)} collective-permute-done((f32[256,512]{1,0:T(8,128)S(1)}, f32[256,512]{1,0:T(8,128)S(1)}, u32[]{:S(2)}, u32[]{:S(2)}) %collective-permute-start.1) | collective-permute-done | bytes 524320 | tf_op jit(solution)/shard_map/ppermute | solution.py:285
  19.7 0.6 shard_map.54.refs_0_
  20.3 0.0 copy-start.1
  20.3 10.9 %collective-permute-done.x_ref = f32[256,512]{1,0:T(8,128)S(1)} collective-permute-done((f32[256,512]{1,0:T(8,128)S(1)}, f32[256,512]{1,0:T(8,128)S(1)}, u32[]{:S(2)}, u32[]{:S(2)}) %collective-permute-start) | collective-permute-done | bytes 524320 | tf_op jit(solution)/shard_map/ppermute | solution.py:285
  31.2 0.6 shard_map.55.sum_ref
  31.8 15.2 %collective-permute-done.2.x_ref = f32[256,256]{1,0:T(8,128)S(1)} collective-permute-done((f32[256,256]{1,0:T(8,128)S(1)}, f32[256,256]{1,0:T(8,128)S(1)}, u32[]{:S(2)}, u32[]{:S(2)}) %collective-permute-start.2) | collective-permute-done | bytes 262176 | tf_op jit(solution)/shard_map/ppermute | solution.py:285
  47.0 0.0 copy-done.1
  47.0 1.0 %shard_map.57 = (f32[256,256]{1,0:T(8,128)S(1)}, f32[2,16,128]{2,1,0:T(8,128)S(1)}, f32[256,256]{1,0:T(8,128)S(1)}, f32[256,256]{1,0:T(8,128)S(1)}) custom-call(bf16[4,512,768]{2,1,0:T(8,128)(2,1)S(1)} %copy-done, f32[512,512]{1,0:T(8,128)S(1)} %shard_map.55.sum_ref, f32[256,256]{1,0:T(8,128)S(1)} %collective-permute-done.2.x_ref, f32[1,1024]{1,0:T(1,128)S(1)} %bitcast.11), custom_call_target="tpu_custom_call" | custom-call | flops 1 | bytes 1 | tf_op jit(solution)/shard_map/pallas_call | solution.py:160
  48.1 0.1 collective-permute-start.4
  48.1 0.5 collective-permute-start.5
  48.6 3.0 %collective-permute-done.3.x_ref = f32[256,256]{1,0:T(8,128)S(1)} collective-permute-done((f32[256,256]{1,0:T(8,128)S(1)}, f32[256,256]{1,0:T(8,128)S(1)}, u32[]{:S(2)}, u32[]{:S(2)}) %collective-permute-start.3) | collective-permute-done | bytes 262176 | tf_op jit(solution)/shard_map/ppermute | solution.py:285
  51.7 0.0 collective-permute-done.4.other_ref
  51.7 0.0 collective-permute-done.5.rest_ref
  51.7 0.0 collective-permute-start.6
  51.7 1.0 %shard_map.59 = (f32[256,256]{1,0:T(8,128)S(1)}, f32[16,16,128]{2,1,0:T(8,128)S(1)}) custom-call(bf16[4,512,768]{2,1,0:T(8,128)(2,1)S(1)} %copy-done, f32[512,512]{1,0:T(8,128)S(1)} %shard_map.55.sum_ref, f32[256,256]{1,0:T(8,128)S(1)} %collective-permute-done.3.x_ref, f32[1,1024]{1,0:T(1,128)S(1)} %bitcast.12, f32[2,16,128]{2,1,0:T(8,128)S(1)} %get-tuple-element.17.refs_0_), custom_call_target="tpu_custom_call" | custom-call | flops 1 | bytes 1 | tf_op jit(solution)/shard_map/pallas_call | solution.py:160
  52.7 0.5 collective-permute-done.6.raw_ref
  53.2 9.8 %all_to_all.5.grams_ref = f32[16,16,128]{2,1,0:T(8,128)S(1)} all-to-all(f32[16,16,128]{2,1,0:T(8,128)S(1)} %get-tuple-element.23), channel_id=1, replica_groups={{15,14,13,12,11,10,9,8,7,6,5,4,3,2,1,0},{31,30,29,28,27,26,25,24,23,22,..., dimensions={0} | all-to-all | bytes 262144 | tf_op jit(solution)/shard_map/all_to_all | solution.py:320
  63.0 2.2 %shard_map.60 = (f32[8,2,16,1024]{3,2,1,0:T(8,128)}, f32[2,8,16,16]{3,2,1,0:T(8,128)}) custom-call(bf16[4,512,768]{2,1,0:T(8,128)(2,1)S(1)} %copy-done, f32[256,256]{1,0:T(8,128)S(1)} %get-tuple-element.13.first_ref, f32[256,256]{1,0:T(8,128)S(1)} %get-tuple-element.18.second_ref, f32[256,256]{1,0:T(8,128)S(1)} %collective-permute-done.4.other_ref, ...), custom_call_target="tpu_custom_call" | custom-call | tf_op jit(solution)/shard_map/pallas_call | solution.py:274
Async XLA Ops:
  1.8 18.0 %collective-permute-start.1 = (f32[256,512]{1,0:T(8,128)S(1)}, f32[256,512]{1,0:T(8,128)S(1)}, u32[]{:S(2)}, u32[]{:S(2)}) collective-permute-start(f32[256,512]{1,0:T(8,128)S(1)} %bitcast.8), channel_id=1, source_target_pairs={{0,12},{4,8},{8,4},{12,0},{1,13},{5,9},{9,5},{13,1},{2,14},{6,10},... | collective-permute-start | bytes 1572872 | tf_op jit(solution)/shard_map/ppermute | solution.py:285
  8.1 23.1 %collective-permute-start = (f32[256,512]{1,0:T(8,128)S(1)}, f32[256,512]{1,0:T(8,128)S(1)}, u32[]{:S(2)}, u32[]{:S(2)}) collective-permute-start(f32[256,512]{1,0:T(8,128)S(1)} %bitcast.7), channel_id=1, source_target_pairs={{0,4},{4,0},{8,12},{12,8},{1,5},{5,1},{9,13},{13,9},{2,6},{6,2},{1... | collective-permute-start | bytes 1572872 | tf_op jit(solution)/shard_map/ppermute | solution.py:285
  9.2 5.3 %copy-start = (bf16[4,512,768]{2,1,0:T(8,128)(2,1)S(1)}, bf16[4,512,768]{2,1,0:T(8,128)(2,1)}, u32[]{:S(2)}) copy-start(bf16[4,512,768]{2,1,0:T(8,128)(2,1)} %constant.2.clone.t_ref) | copy-start | bytes 9437188
  9.2 37.8 %collective-permute-start.2 = (f32[256,256]{1,0:T(8,128)S(1)}, f32[256,256]{1,0:T(8,128)S(1)}, u32[]{:S(2)}, u32[]{:S(2)}) collective-permute-start(f32[256,256]{1,0:T(8,128)S(1)} %bitcast.10), channel_id=1, source_target_pairs={{0,8},{4,12},{8,0},{12,4},{1,9},{5,13},{9,1},{13,5},{2,10},{6,14},... | collective-permute-start | bytes 786440 | tf_op jit(solution)/shard_map/ppermute | solution.py:285
  11.2 40.5 %collective-permute-start.3 = (f32[256,256]{1,0:T(8,128)S(1)}, f32[256,256]{1,0:T(8,128)S(1)}, u32[]{:S(2)}, u32[]{:S(2)}) collective-permute-start(f32[256,256]{1,0:T(8,128)S(1)} %bitcast.9), channel_id=1, source_target_pairs={{0,8},{4,12},{8,0},{12,4},{1,9},{5,13},{9,1},{13,5},{2,10},{6,14},... | collective-permute-start | bytes 786440 | tf_op jit(solution)/shard_map/ppermute | solution.py:285
  20.3 26.7 %copy-start.1 = (f32[1024]{0:T(1024)S(1)}, f32[1024]{0:T(1024)}, u32[]{:S(2)}) copy-start(f32[1024]{0:T(1024)} %param.4) | copy-start | bytes 12292
  48.1 3.6 %collective-permute-start.4 = (f32[256,256]{1,0:T(8,128)S(1)}, f32[256,256]{1,0:T(8,128)S(1)}, u32[]{:S(2)}, u32[]{:S(2)}) collective-permute-start(f32[256,256]{1,0:T(8,128)S(1)} %get-tuple-element.14), channel_id=1, source_target_pairs={{0,1},{1,0},{2,3},{3,2},{4,5},{5,4},{6,7},{7,6},{8,9},{9,8},{10,11... | collective-permute-start | bytes 786440 | tf_op jit(solution)/shard_map/ppermute | solution.py:285
  48.1 3.6 %collective-permute-start.5 = (f32[256,256]{1,0:T(8,128)S(1)}, f32[256,256]{1,0:T(8,128)S(1)}, u32[]{:S(2)}, u32[]{:S(2)}) collective-permute-start(f32[256,256]{1,0:T(8,128)S(1)} %get-tuple-element.15), channel_id=1, source_target_pairs={{0,1},{1,0},{2,3},{3,2},{4,5},{5,4},{6,7},{7,6},{8,9},{9,8},{10,11... | collective-permute-start | bytes 786440 | tf_op jit(solution)/shard_map/ppermute | solution.py:285
  51.7 1.5 %collective-permute-start.6 = (f32[256,256]{1,0:T(8,128)S(1)}, f32[256,256]{1,0:T(8,128)S(1)}, u32[]{:S(2)}, u32[]{:S(2)}) collective-permute-start(f32[256,256]{1,0:T(8,128)S(1)} %collective-permute-done.3.x_ref), channel_id=1, source_target_pairs={{0,1},{1,0},{2,3},{3,2},{4,5},{5,4},{6,7},{7,6},{8,9},{9,8},{10,11... | collective-permute-start | bytes 786440 | tf_op jit(solution)/shard_map/ppermute | solution.py:285

commit v12 on v11

--- a/solution.py
+++ b/solution.py
@@ -11,7 +11,7 @@
 NB = 16
 SEGMENT_FRAMES = 64
 NF = 16
-CUTS = 16
+CUTS = 4
 epsilon = 1e-05
 MIB = 1024 * 1024
 SMALL = pl.CostEstimate(flops=1, transcendentals=0, bytes_accessed=1)
@@ -48,7 +48,7 @@
     a_high, a_low = split(a)
     b_high, b_low = split(b)
     total = 0.0
-    for x, y in ((a_high, b_high), (a_high, b_low), (a_low, b_high)):
+    for x, y in ((a_low, b_low), (a_low, b_high), (a_high, b_low), (a_high, b_high)):
         total = total + lax.dot_general(
             x, y, (((1,), (1,)), ((), ())), preferred_element_type=jnp.float32
         )
@@ -128,7 +128,7 @@
     first = lax.axis_index("freq") == 0
     halves = [spectra[:half], spectra[half:]]
     if skip:
-        before_ref, own_ref, gram_ref = refs
+        before_ref, own_ref, gram_ref, lent_ref = refs
     else:
         own_ref, gram_ref, other_ref, rest_ref = refs
         rest = sum_ref[:, size:]
@@ -147,16 +147,23 @@
         packed.append(jnp.where(row >= col, both[0], both[1]))
     if skip:
         packed = [packed[h] + before_ref[h] for h in range(2)]
-    for d in range(gram_ref.shape[0]):
-        gram_ref[d] = packed[(d + 1) % 2 if skip else d]
-
-
-def late(tables, n, k, skip, targets, partial_sum, piece, weights, *before):
+    if skip:
+        gram_ref[...] = jnp.where(first, packed[0], packed[1])
+        lent_ref[...] = jnp.where(first, packed[1], packed[0])
+    else:
+        for h in range(2):
+            gram_ref[h] = packed[h]
+
+
+def late(tables, n, k, skip, partial_sum, piece, weights, *before):
     share = partial_sum.shape[1]
     half = tables.shape[1] // 2
-    shapes = [(half, piece.shape[1]), (targets, NB, half // 2)]
-    if not skip:
-        shapes += [(half, piece.shape[1]), (half, share - piece.shape[1])]
+    gram = (NB, half // 2)
+    shapes = [(half, piece.shape[1])]
+    if skip:
+        shapes += [gram, gram]
+    else:
+        shapes += [(2, *gram), (half, piece.shape[1]), (half, share - piece.shape[1])]
     return pl.pallas_call(
         functools.partial(late_kernel, n, k, skip),
         out_shape=[jax.ShapeDtypeStruct(shape, jnp.float32) for shape in shapes],
@@ -298,7 +305,7 @@
     last = n // 2
     early_rows = share // 2
     parts = ((0, early_rows), (early_rows, share - early_rows))
-    targets = n * tm_count * freq_count
+    targets = n * tm_count
 
     def send(k, skip, size):
         sent = cut(snapshots, n, k, rows, skip, size)
@@ -311,21 +318,23 @@
     for k, piece in zip(offsets, pieces):
         before = early(tables, n, k, piece, before)
     weights = weights.reshape(1, rows)
-    first, gram, other, rest = late(tables, n, last, 0, 2, before, last_pieces[0], weights)
+    first, gram, other, rest = late(tables, n, last, 0, before, last_pieces[0], weights)
     other, rest = partner(other, "freq", freq_count, 1), partner(rest, "freq", freq_count, 1)
     raw, other, rest = lax.optimization_barrier((last_pieces[1], other, rest))
-    second, gram = late(tables, n, last, early_rows, targets, before, raw, weights, gram)
+    second, gram, lent = late(tables, n, last, early_rows, before, raw, weights, gram)
     raw = partner(raw, "freq", freq_count, 1)
-    gram, raw = lax.optimization_barrier((gram, raw))
+    gram = gram + partner(lent, "freq", freq_count, 1)
+    repeated = jnp.broadcast_to(gram, (targets,) + gram.shape)
+    repeated, raw = lax.optimization_barrier((repeated, raw))
     grams = lax.all_to_all(
-        gram,
-        ("space", "tm", "freq"),
+        repeated,
+        ("space", "tm"),
         split_axis=0,
         concat_axis=0,
         axis_index_groups=[list(range(targets - 1, -1, -1))],
         tiled=True,
     )
-    total = rows * n * tm_count
+    total = rows * targets
     return finish(tables, n, last, total, first, second, other, rest, raw, grams)
 
 

time: 65.8 us -> 65.6 us (level)
  blocking collectives: 9.8 us -> 8.85 us
    all_to_all x1, blocking collectives: 9.8 us -> 8.85 us  [on_device(): lax.all_to_all(repeated, ('space', 'tm'), split_axis=0, concat_axis=0, ax...]
    ppermute x7 -> x8, starting transfers between devices: 8.53 us -> 9.07 us  [partner(): return lax.ppermute(value, axis, [(i, i ^ step) for i in range(size)])]
    ppermute x7 -> x8, waiting for transfers between devices: 34.4 us -> 34.8 us  [partner(): return lax.ppermute(value, axis, [(i, i ^ step) for i in range(size)])]
  transfers between devices with their start and end apart: 7 -> 8, of which waited for: 5 -> 5; matrix products, arithmetic and copies ran while one was open for 0% -> 0% of each run, Pallas kernels for 13% -> 13%
where the time goes in v12:
time: 65.6 us; the launch traced here: 65.3 us
  waiting for transfers between devices  34.8 us (53%)
  Pallas kernels  11.8 us (18%)
  starting transfers between devices  9.07 us (14%)
  blocking collectives  8.85 us (13%)
  between operations  0.76 us (1%)
    ppermute x8, waiting for transfers between devices, partner(): return lax.ppermute(value, axis, [(i, i ^ step) for i in range(size)])  34.8 us
    ppermute x8, starting transfers between devices, partner(): return lax.ppermute(value, axis, [(i, i ^ step) for i in range(size)])  9.07 us
    all_to_all x1, blocking collectives, on_device(): lax.all_to_all(repeated, ('space', 'tm'), split_axis=0, concat_axis=0, ax...  8.85 us
    pallas_call x5, Pallas kernels, cut(): pl.pallas_call(functools.partial(cut_kernel, n, k, rows, skip), out_shape...  5.66 us
    pallas_call x1, Pallas kernels, finish(): pl.pallas_call(functools.partial(finish_kernel, n, k, total), out_shape=(...  2.23 us
    pallas_call x2, Pallas kernels, late(): pl.pallas_call(functools.partial(late_kernel, n, k, skip), out_shape=[jax...  2.21 us
    pallas_call x3, Pallas kernels, early(): pl.pallas_call(functools.partial(early_kernel, n, k), out_shape=jax.Shape...  1.74 us
  transfers between devices with their start and end apart: 8, of which 5 were waited for; matrix products, arithmetic and copies ran while one was open for 0% of the time, Pallas kernels for 13%

profile of v12, /device:TPU:0, one launch (start us, length us, event | category | flops | bytes accessed | tf_op | source)
XLA Modules:
  0.0 65.3 jit_solution(9543666400741373846)
XLA Ops:
  0.6 1.1 %shard_map.51 = f32[16,16,512]{2,1,0:T(8,128)S(1)} custom-call(f32[16,16,4096]{2,1,0:T(8,128)} %x_ref.9), custom_call_target="tpu_custom_call" | custom-call | flops 1 | bytes 1 | tf_op jit(solution)/shard_map/pallas_call | solution.py:81
  1.8 5.1 %collective-permute-start.1 = (f32[256,512]{1,0:T(8,128)S(1)}, f32[256,512]{1,0:T(8,128)S(1)}, u32[]{:S(2)}, u32[]{:S(2)}) collective-permute-start(f32[256,512]{1,0:T(8,128)S(1)} %bitcast.8), channel_id=1, source_target_pairs={{0,12},{4,8},{8,4},{12,0},{1,13},{5,9},{9,5},{13,1},{2,14},{6,10},... | collective-permute-start | bytes 1572872 | tf_op jit(solution)/shard_map/ppermute | solution.py:292
  6.9 1.1 %shard_map.50 = f32[16,16,512]{2,1,0:T(8,128)S(1)} custom-call(f32[16,16,4096]{2,1,0:T(8,128)} %x_ref.9), custom_call_target="tpu_custom_call" | custom-call | flops 1 | bytes 1 | tf_op jit(solution)/shard_map/pallas_call | solution.py:81
  8.0 0.1 collective-permute-start
  8.1 1.0 %shard_map.56 = f32[16,16,256]{2,1,0:T(8,128)S(1)} custom-call(f32[16,16,4096]{2,1,0:T(8,128)} %x_ref.9), custom_call_target="tpu_custom_call" | custom-call | flops 1 | bytes 1 | tf_op jit(solution)/shard_map/pallas_call | solution.py:81
  9.1 0.0 copy-start
  9.1 0.6 collective-permute-start.2
  9.7 1.3 %shard_map.58 = f32[16,16,256]{2,1,0:T(8,128)S(1)} custom-call(f32[16,16,4096]{2,1,0:T(8,128)} %x_ref.9), custom_call_target="tpu_custom_call" | custom-call | flops 1 | bytes 1 | tf_op jit(solution)/shard_map/pallas_call | solution.py:81
  11.0 2.1 %collective-permute-start.3 = (f32[256,256]{1,0:T(8,128)S(1)}, f32[256,256]{1,0:T(8,128)S(1)}, u32[]{:S(2)}, u32[]{:S(2)}) collective-permute-start(f32[256,256]{1,0:T(8,128)S(1)} %bitcast.9), channel_id=1, source_target_pairs={{0,8},{4,12},{8,0},{12,4},{1,9},{5,13},{9,1},{13,5},{2,10},{6,14},... | collective-permute-start | bytes 786440 | tf_op jit(solution)/shard_map/ppermute | solution.py:292
  13.1 1.1 %shard_map.52 = f32[16,16,512]{2,1,0:T(8,128)S(1)} custom-call(f32[16,16,4096]{2,1,0:T(8,128)} %x_ref.9), custom_call_target="tpu_custom_call" | custom-call | flops 1 | bytes 1 | tf_op jit(solution)/shard_map/pallas_call | solution.py:81
  14.3 0.0 copy-done
  14.3 0.6 shard_map.53.refs_0_
  14.9 4.9 %collective-permute-done.1.x_ref = f32[256,512]{1,0:T(8,128)S(1)} collective-permute-done((f32[256,512]{1,0:T(8,128)S(1)}, f32[256,512]{1,0:T(8,128)S(1)}, u32[]{:S(2)}, u32[]{:S(2)}) %collective-permute-start.1) | collective-permute-done | bytes 524320 | tf_op jit(solution)/shard_map/ppermute | solution.py:292
  19.7 0.6 shard_map.54.refs_0_
  20.3 0.0 copy-start.1
  20.3 10.9 %collective-permute-done.x_ref = f32[256,512]{1,0:T(8,128)S(1)} collective-permute-done((f32[256,512]{1,0:T(8,128)S(1)}, f32[256,512]{1,0:T(8,128)S(1)}, u32[]{:S(2)}, u32[]{:S(2)}) %collective-permute-start) | collective-permute-done | bytes 524320 | tf_op jit(solution)/shard_map/ppermute | solution.py:292
  31.2 0.6 shard_map.55.sum_ref
  31.8 15.2 %collective-permute-done.2.x_ref = f32[256,256]{1,0:T(8,128)S(1)} collective-permute-done((f32[256,256]{1,0:T(8,128)S(1)}, f32[256,256]{1,0:T(8,128)S(1)}, u32[]{:S(2)}, u32[]{:S(2)}) %collective-permute-start.2) | collective-permute-done | bytes 262176 | tf_op jit(solution)/shard_map/ppermute | solution.py:292
  47.0 0.0 copy-done.1
  47.0 1.1 %shard_map.57 = (f32[256,256]{1,0:T(8,128)S(1)}, f32[2,16,128]{2,1,0:T(8,128)S(1)}, f32[256,256]{1,0:T(8,128)S(1)}, f32[256,256]{1,0:T(8,128)S(1)}) custom-call(bf16[4,512,768]{2,1,0:T(8,128)(2,1)S(1)} %copy-done, f32[512,512]{1,0:T(8,128)S(1)} %shard_map.55.sum_ref, f32[256,256]{1,0:T(8,128)S(1)} %collective-permute-done.2.x_ref, f32[1,1024]{1,0:T(1,128)S(1)} %bitcast.11), custom_call_target="tpu_custom_call" | custom-call | flops 1 | bytes 1 | tf_op jit(solution)/shard_map/pallas_call | solution.py:167
  48.1 0.1 collective-permute-start.4
  48.2 0.5 collective-permute-start.5
  48.7 3.0 %collective-permute-done.3.x_ref = f32[256,256]{1,0:T(8,128)S(1)} collective-permute-done((f32[256,256]{1,0:T(8,128)S(1)}, f32[256,256]{1,0:T(8,128)S(1)}, u32[]{:S(2)}, u32[]{:S(2)}) %collective-permute-start.3) | collective-permute-done | bytes 262176 | tf_op jit(solution)/shard_map/ppermute | solution.py:292
  51.7 0.0 collective-permute-done.4.other_ref
  51.7 0.0 collective-permute-done.5.rest_ref
  51.7 0.0 collective-permute-start.7
  51.7 1.1 %shard_map.59 = (f32[256,256]{1,0:T(8,128)S(1)}, f32[16,128]{1,0:T(8,128)S(1)}, f32[16,128]{1,0:T(8,128)S(1)}) custom-call(bf16[4,512,768]{2,1,0:T(8,128)(2,1)S(1)} %copy-done, f32[512,512]{1,0:T(8,128)S(1)} %shard_map.55.sum_ref, f32[256,256]{1,0:T(8,128)S(1)} %collective-permute-done.3.x_ref, f32[1,1024]{1,0:T(1,128)S(1)} %bitcast.12, ...), custom_call_target="tpu_custom_call" | custom-call | flops 1 | bytes 1 | tf_op jit(solution)/shard_map/pallas_call | solution.py:167
  52.8 0.6 collective-permute-start.6
  53.4 0.8 %collective-permute-done.6 = f32[16,128]{1,0:T(8,128)S(1)} collective-permute-done((f32[16,128]{1,0:T(8,128)S(1)}, f32[16,128]{1,0:T(8,128)S(1)}, u32[]{:S(2)}, u32[]{:S(2)}) %collective-permute-start.6) | collective-permute-done | bytes 8224 | tf_op jit(solution)/shard_map/ppermute | solution.py:292
  54.2 0.0 collective-permute-done.7.raw_ref
  54.2 8.9 %all_to_all.5.grams_ref = f32[8,16,128]{2,1,0:T(8,128)S(1)} all-to-all(f32[8,16,128]{2,1,0:T(8,128)S(1)} %broadcast_in_dim.3), channel_id=1, replica_groups={{14,12,10,8,6,4,2,0},{15,13,11,9,7,5,3,1},{30,28,26,24,22,20,18,16},{31..., dimensions={0} | all-to-all | bytes 131072 | tf_op jit(solution)/shard_map/all_to_all | solution.py:329
  63.1 2.2 %shard_map.60 = (f32[8,2,16,1024]{3,2,1,0:T(8,128)}, f32[2,8,16,16]{3,2,1,0:T(8,128)}) custom-call(bf16[4,512,768]{2,1,0:T(8,128)(2,1)S(1)} %copy-done, f32[256,256]{1,0:T(8,128)S(1)} %get-tuple-element.14.first_ref, f32[256,256]{1,0:T(8,128)S(1)} %get-tuple-element.19.second_ref, f32[256,256]{1,0:T(8,128)S(1)} %collective-permute-done.4.other_ref, ...), custom_call_target="tpu_custom_call" | custom-call | tf_op jit(solution)/shard_map/pallas_call | solution.py:281
  (2 shorter events, 0.0 us)
Async XLA Ops:
  1.8 18.0 %collective-permute-start.1 = (f32[256,512]{1,0:T(8,128)S(1)}, f32[256,512]{1,0:T(8,128)S(1)}, u32[]{:S(2)}, u32[]{:S(2)}) collective-permute-start(f32[256,512]{1,0:T(8,128)S(1)} %bitcast.8), channel_id=1, source_target_pairs={{0,12},{4,8},{8,4},{12,0},{1,13},{5,9},{9,5},{13,1},{2,14},{6,10},... | collective-permute-start | bytes 1572872 | tf_op jit(solution)/shard_map/ppermute | solution.py:292
  8.0 23.2 %collective-permute-start = (f32[256,512]{1,0:T(8,128)S(1)}, f32[256,512]{1,0:T(8,128)S(1)}, u32[]{:S(2)}, u32[]{:S(2)}) collective-permute-start(f32[256,512]{1,0:T(8,128)S(1)} %bitcast.7), channel_id=1, source_target_pairs={{0,4},{4,0},{8,12},{12,8},{1,5},{5,1},{9,13},{13,9},{2,6},{6,2},{1... | collective-permute-start | bytes 1572872 | tf_op jit(solution)/shard_map/ppermute | solution.py:292
  9.1 5.2 %copy-start = (bf16[4,512,768]{2,1,0:T(8,128)(2,1)S(1)}, bf16[4,512,768]{2,1,0:T(8,128)(2,1)}, u32[]{:S(2)}) copy-start(bf16[4,512,768]{2,1,0:T(8,128)(2,1)} %constant.2.clone.t_ref) | copy-start | bytes 9437188
  9.1 37.9 %collective-permute-start.2 = (f32[256,256]{1,0:T(8,128)S(1)}, f32[256,256]{1,0:T(8,128)S(1)}, u32[]{:S(2)}, u32[]{:S(2)}) collective-permute-start(f32[256,256]{1,0:T(8,128)S(1)} %bitcast.10), channel_id=1, source_target_pairs={{0,8},{4,12},{8,0},{12,4},{1,9},{5,13},{9,1},{13,5},{2,10},{6,14},... | collective-permute-start | bytes 786440 | tf_op jit(solution)/shard_map/ppermute | solution.py:292
  11.0 40.6 %collective-permute-start.3 = (f32[256,256]{1,0:T(8,128)S(1)}, f32[256,256]{1,0:T(8,128)S(1)}, u32[]{:S(2)}, u32[]{:S(2)}) collective-permute-start(f32[256,256]{1,0:T(8,128)S(1)} %bitcast.9), channel_id=1, source_target_pairs={{0,8},{4,12},{8,0},{12,4},{1,9},{5,13},{9,1},{13,5},{2,10},{6,14},... | collective-permute-start | bytes 786440 | tf_op jit(solution)/shard_map/ppermute | solution.py:292
  20.3 26.7 %copy-start.1 = (f32[1024]{0:T(1024)S(1)}, f32[1024]{0:T(1024)}, u32[]{:S(2)}) copy-start(f32[1024]{0:T(1024)} %param.4) | copy-start | bytes 12292
  48.1 3.5 %collective-permute-start.4 = (f32[256,256]{1,0:T(8,128)S(1)}, f32[256,256]{1,0:T(8,128)S(1)}, u32[]{:S(2)}, u32[]{:S(2)}) collective-permute-start(f32[256,256]{1,0:T(8,128)S(1)} %get-tuple-element.15), channel_id=1, source_target_pairs={{0,1},{1,0},{2,3},{3,2},{4,5},{5,4},{6,7},{7,6},{8,9},{9,8},{10,11... | collective-permute-start | bytes 786440 | tf_op jit(solution)/shard_map/ppermute | solution.py:292
  48.2 3.5 %collective-permute-start.5 = (f32[256,256]{1,0:T(8,128)S(1)}, f32[256,256]{1,0:T(8,128)S(1)}, u32[]{:S(2)}, u32[]{:S(2)}) collective-permute-start(f32[256,256]{1,0:T(8,128)S(1)} %get-tuple-element.16), channel_id=1, source_target_pairs={{0,1},{1,0},{2,3},{3,2},{4,5},{5,4},{6,7},{7,6},{8,9},{9,8},{10,11... | collective-permute-start | bytes 786440 | tf_op jit(solution)/shard_map/ppermute | solution.py:292
  51.7 2.5 %collective-permute-start.7 = (f32[256,256]{1,0:T(8,128)S(1)}, f32[256,256]{1,0:T(8,128)S(1)}, u32[]{:S(2)}, u32[]{:S(2)}) collective-permute-start(f32[256,256]{1,0:T(8,128)S(1)} %collective-permute-done.3.x_ref), channel_id=1, source_target_pairs={{0,1},{1,0},{2,3},{3,2},{4,5},{5,4},{6,7},{7,6},{8,9},{9,8},{10,11... | collective-permute-start | bytes 786440 | tf_op jit(solution)/shard_map/ppermute | solution.py:292
  52.8 1.4 %collective-permute-start.6 = (f32[16,128]{1,0:T(8,128)S(1)}, f32[16,128]{1,0:T(8,128)S(1)}, u32[]{:S(2)}, u32[]{:S(2)}) collective-permute-start(f32[16,128]{1,0:T(8,128)S(1)} %get-tuple-element.23), channel_id=1, source_target_pairs={{0,1},{1,0},{2,3},{3,2},{4,5},{5,4},{6,7},{7,6},{8,9},{9,8},{10,11... | collective-permute-start | bytes 24584 | tf_op jit(solution)/shard_map/ppermute | solution.py:292

commit v13 on v12

--- a/solution.py
+++ b/solution.py
@@ -110,62 +110,85 @@
     )(tables, piece, *before)
 
 
-def late_kernel(n, k, skip, t_ref, sum_ref, x_ref, w_ref, *refs):
-    size = x_ref.shape[1]
-    share = sum_ref.shape[1]
-    cols = pl.ds(skip, size)
-    at = lax.axis_index("freq") * share + skip
-    weights = w_ref[:, pl.ds(pl.multiple_of(at, 128), size)]
-    src = lax.bitwise_xor(lax.axis_index("space"), k)
-    spectra = sum_ref[:, cols] + times_split(t_ref[src], x_ref[...])
-    half = spectra.shape[0] // 2
-    width = half // 2
+def gram_of(z, weights):
+    width = z.shape[0] // 2
     local = width // NB
     line = lax.broadcasted_iota(jnp.int32, (width, width), 0) // NB
     lane = lax.broadcasted_iota(jnp.int32, (width, width), 1) // NB
     row = lax.broadcasted_iota(jnp.int32, (NB, width), 0)
     col = lax.broadcasted_iota(jnp.int32, (NB, width), 1) % NB
-    first = lax.axis_index("freq") == 0
-    halves = [spectra[:half], spectra[half:]]
-    if skip:
-        before_ref, own_ref, gram_ref, lent_ref = refs
-    else:
-        own_ref, gram_ref, other_ref, rest_ref = refs
-        rest = sum_ref[:, size:]
-        other_ref[...] = jnp.where(first, halves[1], halves[0])
-        rest_ref[...] = jnp.where(first, rest[half:], rest[:half])
-    own_ref[...] = jnp.where(first, halves[0], halves[1])
-    packed = []
-    for z in halves:
-        full = rows_product(z * weights, z)
-        gram_re = full[:width, :width] + full[width:, width:]
-        gram_im = full[:width, width:] - full[width:, :width]
-        both = []
-        for part in (gram_re, gram_im):
-            kept = jnp.where(line == lane, part, 0.0)
-            both.append(jnp.sum(kept.reshape(local, NB, width), axis=0))
-        packed.append(jnp.where(row >= col, both[0], both[1]))
-    if skip:
-        packed = [packed[h] + before_ref[h] for h in range(2)]
-    if skip:
-        gram_ref[...] = jnp.where(first, packed[0], packed[1])
-        lent_ref[...] = jnp.where(first, packed[1], packed[0])
-    else:
-        for h in range(2):
-            gram_ref[h] = packed[h]
-
-
-def late(tables, n, k, skip, partial_sum, piece, weights, *before):
+    full = rows_product(z * weights, z)
+    gram_re = full[:width, :width] + full[width:, width:]
+    gram_im = full[:width, width:] - full[width:, :width]
+    both = []
+    for part in (gram_re, gram_im):
+        kept = jnp.where(line == lane, part, 0.0)
+        both.append(jnp.sum(kept.reshape(local, NB, width), axis=0))
+    return jnp.where(row >= col, both[0], both[1])
+
+
+def weights_at(w_ref, place, share, skip, size):
+    return w_ref[:, pl.ds(pl.multiple_of(place * share + skip, 128), size)]
+
+
+def first_part_kernel(
+    n, k, t_ref, sum_ref, x_ref, w_ref, own_ref, rest_ref, other_ref, later_ref, gram_ref, lent_ref
+):
+    size = x_ref.shape[1]
+    me = lax.axis_index("freq")
+    src = lax.bitwise_xor(lax.axis_index("space"), k)
+    spectra = sum_ref[:, :size] + times_split(t_ref[src], x_ref[...])
+    weights = weights_at(w_ref, me, sum_ref.shape[1], 0, size)
+    rest = sum_ref[:, size:]
+    half = spectra.shape[0] // 2
+    first = me == 0
+    own_ref[...] = jnp.where(first, spectra[:half], spectra[half:])
+    other_ref[...] = jnp.where(first, spectra[half:], spectra[:half])
+    rest_ref[...] = jnp.where(first, rest[:half], rest[half:])
+    later_ref[...] = jnp.where(first, rest[half:], rest[:half])
+    grams = [gram_of(z, weights) for z in (spectra[:half], spectra[half:])]
+    gram_ref[...] = jnp.where(first, grams[0], grams[1])
+    lent_ref[...] = jnp.where(first, grams[1], grams[0])
+
+
+def first_part(tables, n, k, partial_sum, piece, weights):
     share = partial_sum.shape[1]
     half = tables.shape[1] // 2
+    size = piece.shape[1]
     gram = (NB, half // 2)
-    shapes = [(half, piece.shape[1])]
-    if skip:
-        shapes += [gram, gram]
+    shapes = [(half, size), (half, share - size), (half, size), (half, share - size), gram, gram]
+    return pl.pallas_call(
+        functools.partial(first_part_kernel, n, k),
+        out_shape=[jax.ShapeDtypeStruct(shape, jnp.float32) for shape in shapes],
+        compiler_params=pltpu.CompilerParams(vmem_limit_bytes=16 * MIB),
+        cost_estimate=SMALL,
+    )(tables, partial_sum, piece, weights)
+
+
+def last_part_kernel(n, k, swapped, skip, t_ref, sum_ref, x_ref, w_ref, *refs):
+    *before, own_ref, gram_ref = refs
+    half, size = sum_ref.shape
+    me = lax.axis_index("freq")
+    src = lax.bitwise_xor(lax.axis_index("space"), k)
+    lines = pl.ds(pl.multiple_of(me * half, 128), half)
+    spectra = sum_ref[...] + times_split(t_ref[src, lines], x_ref[...])
+    own_ref[...] = spectra
+    place = 1 - me if swapped else me
+    gram = gram_of(spectra, weights_at(w_ref, place, skip + size, skip, size))
+    for ref in before:
+        gram = gram + ref[...]
+    if len(gram_ref.shape) == 2:
+        gram_ref[...] = gram
     else:
-        shapes += [(2, *gram), (half, piece.shape[1]), (half, share - piece.shape[1])]
+        for d in range(gram_ref.shape[0]):
+            gram_ref[d] = gram
+
+
+def last_part(tables, n, k, swapped, skip, copies, partial_sum, piece, weights, *before):
+    gram = (NB, partial_sum.shape[0] // 2)
+    shapes = [partial_sum.shape, (copies, *gram) if copies else gram]
     return pl.pallas_call(
-        functools.partial(late_kernel, n, k, skip),
+        functools.partial(last_part_kernel, n, k, swapped, skip),
         out_shape=[jax.ShapeDtypeStruct(shape, jnp.float32) for shape in shapes],
         compiler_params=pltpu.CompilerParams(vmem_limit_bytes=16 * MIB),
         cost_estimate=SMALL,
@@ -178,7 +201,7 @@
 
 
 def finish_kernel(
-    n, k, total, t_ref, first_ref, second_ref, other_ref, rest_ref, raw_ref, grams_ref, modes_ref, factor_ref
+    total, own_ref, own_last_ref, other_ref, other_last_ref, grams_ref, modes_ref, factor_ref
 ):
     local = modes_ref.shape[0]
     width = local * NB
@@ -217,31 +240,36 @@
     def pick(halves, i):
         return jnp.broadcast_to(halves[i // 8][i % 8 : i % 8 + 1, :], (8, width))
 
+    pivots = [pick(col_re[j], j) + epsilon for j in range(NB)]
+    scales = [jnp.zeros((8, width), jnp.float32) for h in (0, 1)]
     for p in range(NB):
-        pivot = pick(col_re[p], p) + epsilon
-        scale = inv_sqrt(pivot)
-        coef_re, coef_im = [None, None], [None, None]
+        scale = inv_sqrt(pivots[p])
+        inverse = scale * scale
         for h in range(p // 8, 2):
             below = rows[h] > p
-            coef_re[h] = jnp.where(below, col_re[p][h] * scale, 0.0)
-            coef_im[h] = jnp.where(below, col_im[p][h] * scale, 0.0)
             here = lanes == p
-            diag = jnp.where(rows[h] == p, pivot * scale, coef_re[h])
-            low_re[h] = jnp.where(here, diag, low_re[h])
-            low_im[h] = jnp.where(here, coef_im[h], low_im[h])
+            scales[h] = jnp.where(rows[h] == p, scale, scales[h])
+            col_re[p][h] = jnp.where(below, col_re[p][h], 0.0)
+            col_im[p][h] = jnp.where(below, col_im[p][h], 0.0)
+            diag = jnp.where(rows[h] == p, pivots[p], col_re[p][h])
+            low_re[h] = jnp.where(here, diag * scale, low_re[h])
+            low_im[h] = jnp.where(here, col_im[p][h] * scale, low_im[h])
         for j in range(p + 1, NB):
-            a_re, a_im = pick(coef_re, j), pick(coef_im, j)
+            a_re, a_im = pick(col_re[p], j), pick(col_im[p], j)
+            u_re, u_im = a_re * inverse, a_im * inverse
+            pivots[j] = pivots[j] - (a_re * u_re + a_im * u_im)
             for h in range(j // 8, 2):
-                col_re[j][h] = col_re[j][h] - (coef_re[h] * a_re + coef_im[h] * a_im)
-                col_im[j][h] = col_im[j][h] - (coef_im[h] * a_re - coef_re[h] * a_im)
-        line_re = pick(inv_re, p) * scale
-        line_im = pick(inv_im, p) * scale
+                c_re, c_im = col_re[p][h], col_im[p][h]
+                col_re[j][h] = col_re[j][h] - (c_re * u_re + c_im * u_im)
+                col_im[j][h] = col_im[j][h] - (c_im * u_re - c_re * u_im)
+        line_re = pick(inv_re, p) * inverse
+        line_im = pick(inv_im, p) * inverse
         for h in range(p // 8, 2):
-            at = rows[h] == p
-            new_re = inv_re[h] - (coef_re[h] * line_re - coef_im[h] * line_im)
-            new_im = inv_im[h] - (coef_re[h] * line_im + coef_im[h] * line_re)
-            inv_re[h] = jnp.where(at, line_re, new_re)
-            inv_im[h] = jnp.where(at, line_im, new_im)
+            c_re, c_im = col_re[p][h], col_im[p][h]
+            inv_re[h] = inv_re[h] - (c_re * line_re - c_im * line_im)
+            inv_im[h] = inv_im[h] - (c_re * line_im + c_im * line_re)
+    inv_re = [inv_re[h] * scales[h] for h in (0, 1)]
+    inv_im = [inv_im[h] * scales[h] for h in (0, 1)]
 
     block_re = jnp.where(same, jnp.concatenate(inv_re * local, axis=0), 0.0)
     block_im = jnp.where(same, jnp.concatenate(inv_im * local, axis=0), 0.0)
@@ -255,11 +283,8 @@
     me = lax.axis_index("freq")
     high, low = split(mixing)
     mixing = jnp.concatenate([high, high, low], axis=1)
-    src = lax.bitwise_xor(lax.axis_index("space"), k)
-    lines = pl.ds(pl.multiple_of(me * 2 * width, 128), 2 * width)
-    own = [first_ref[...], second_ref[...]]
-    added = times_split(t_ref[src, lines], raw_ref[...])
-    other = [other_ref[...], rest_ref[...] + added]
+    own = [own_ref[...], own_last_ref[...]]
+    other = [other_ref[...], other_last_ref[...]]
     for place, parts in ((me, own), (1 - me, other)):
         out = times_split(mixing, jnp.concatenate(parts, axis=1))
         cols = pl.ds(pl.multiple_of(place * share, 128), share)
@@ -275,17 +300,18 @@
         factor_ref[1, f] = -turned_im[f * NB : (f + 1) * NB, :NB]
 
 
-def finish(tables, n, k, total, first, second, other, rest, raw, grams):
-    local = tables.shape[1] // (4 * NB)
-    share = other.shape[1] + rest.shape[1]
+def finish(total, own, own_last, other, other_last, grams):
+    half, size = own.shape
+    local = half // (2 * NB)
+    share = size + own_last.shape[1]
     return pl.pallas_call(
-        functools.partial(finish_kernel, n, k, total),
+        functools.partial(finish_kernel, total),
         out_shape=(
             jax.ShapeDtypeStruct((local, 2, NB, 2 * share), jnp.float32),
             jax.ShapeDtypeStruct((2, local, NB, NB), jnp.float32),
         ),
         compiler_params=pltpu.CompilerParams(vmem_limit_bytes=16 * MIB),
-    )(tables, first, second, other, rest, raw, grams)
+    )(own, own_last, other, other_last, grams)
 
 
 def partner(value, axis, size, step):
@@ -318,16 +344,20 @@
     for k, piece in zip(offsets, pieces):
         before = early(tables, n, k, piece, before)
     weights = weights.reshape(1, rows)
-    first, gram, other, rest = late(tables, n, last, 0, before, last_pieces[0], weights)
-    other, rest = partner(other, "freq", freq_count, 1), partner(rest, "freq", freq_count, 1)
-    raw, other, rest = lax.optimization_barrier((last_pieces[1], other, rest))
-    second, gram, lent = late(tables, n, last, early_rows, before, raw, weights, gram)
-    raw = partner(raw, "freq", freq_count, 1)
-    gram = gram + partner(lent, "freq", freq_count, 1)
-    repeated = jnp.broadcast_to(gram, (targets,) + gram.shape)
-    repeated, raw = lax.optimization_barrier((repeated, raw))
+    own, rest, other, later, gram, lent = first_part(
+        tables, n, last, before, last_pieces[0], weights
+    )
+    traded = [partner(part, "freq", freq_count, 1) for part in (other, later, lent)]
+    piece, (other, later, lent) = lax.optimization_barrier((last_pieces[1], traded))
+    raw = partner(piece, "freq", freq_count, 1)
+    own_last, gram = last_part(
+        tables, n, last, False, early_rows, 0, rest, piece, weights, gram, lent
+    )
+    other_last, gram = last_part(
+        tables, n, last, True, early_rows, targets, later, raw, weights, gram
+    )
     grams = lax.all_to_all(
-        repeated,
+        gram,
         ("space", "tm"),
         split_axis=0,
         concat_axis=0,
@@ -335,7 +365,7 @@
         tiled=True,
     )
     total = rows * targets
-    return finish(tables, n, last, total, first, second, other, rest, raw, grams)
+    return finish(total, own, own_last, other, other_last, grams)
 
 
 def solution(mesh):

time: 65.6 us -> 65.3 us (level)
    pallas_call x3 -> x4, Pallas kernels: 4.44 us -> 4.75 us  [the longest x1 2.2 us: finish(): pl.pallas_call(functools.partial(finish_kernel, total), out_shape=(jax.Sh...]
  transfers between devices with their start and end apart: 8 -> 8, of which waited for: 5 -> 5; matrix products, arithmetic and copies ran while one was open for 0% -> 0% of each run, Pallas kernels for 13% -> 12%
where the time goes in v13:
time: 65.3 us; the launch traced here: 65 us
  waiting for transfers between devices  34.6 us (53%)
  Pallas kernels  12.1 us (19%)
  blocking collectives  8.83 us (14%)
  starting transfers between devices  8.65 us (13%)
  between operations  0.77 us (1%)
    ppermute x8, waiting for transfers between devices, partner(): return lax.ppermute(value, axis, [(i, i ^ step) for i in range(size)])  34.6 us
    all_to_all x1, blocking collectives, on_device(): lax.all_to_all(gram, ('space', 'tm'), split_axis=0, concat_axis=0, axis_i...  8.83 us
    ppermute x8, starting transfers between devices, partner(): return lax.ppermute(value, axis, [(i, i ^ step) for i in range(size)])  8.65 us
    pallas_call x5, Pallas kernels, cut(): pl.pallas_call(functools.partial(cut_kernel, n, k, rows, skip), out_shape...  5.66 us
    pallas_call x1, Pallas kernels, finish(): pl.pallas_call(functools.partial(finish_kernel, total), out_shape=(jax.Sh...  2.2 us
    pallas_call x3, Pallas kernels, early(): pl.pallas_call(functools.partial(early_kernel, n, k), out_shape=jax.Shape...  1.74 us
    pallas_call x2, Pallas kernels, last_part(): pl.pallas_call(functools.partial(last_part_kernel, n, k, swapped, skip),...  1.42 us
  transfers between devices with their start and end apart: 8, of which 5 were waited for; matrix products, arithmetic and copies ran while one was open for 0% of the time, Pallas kernels for 12%

profile of v13, /device:TPU:0, one launch (start us, length us, event | category | flops | bytes accessed | tf_op | source)
XLA Modules:
  0.0 65.0 jit_solution(2019932151531711557)
XLA Ops:
  0.6 1.1 %shard_map.51 = f32[16,16,512]{2,1,0:T(8,128)S(1)} custom-call(f32[16,16,4096]{2,1,0:T(8,128)} %x_ref.9), custom_call_target="tpu_custom_call" | custom-call | flops 1 | bytes 1 | tf_op jit(solution)/shard_map/pallas_call | solution.py:81
  1.8 5.1 %collective-permute-start.1 = (f32[256,512]{1,0:T(8,128)S(1)}, f32[256,512]{1,0:T(8,128)S(1)}, u32[]{:S(2)}, u32[]{:S(2)}) collective-permute-start(f32[256,512]{1,0:T(8,128)S(1)} %bitcast.8), channel_id=1, source_target_pairs={{0,12},{4,8},{8,4},{12,0},{1,13},{5,9},{9,5},{13,1},{2,14},{6,10},... | collective-permute-start | bytes 1572872 | tf_op jit(solution)/shard_map/ppermute | solution.py:318
  6.9 1.1 %shard_map.50 = f32[16,16,512]{2,1,0:T(8,128)S(1)} custom-call(f32[16,16,4096]{2,1,0:T(8,128)} %x_ref.9), custom_call_target="tpu_custom_call" | custom-call | flops 1 | bytes 1 | tf_op jit(solution)/shard_map/pallas_call | solution.py:81
  8.0 0.1 collective-permute-start
  8.1 1.0 %shard_map.56 = f32[16,16,256]{2,1,0:T(8,128)S(1)} custom-call(f32[16,16,4096]{2,1,0:T(8,128)} %x_ref.9), custom_call_target="tpu_custom_call" | custom-call | flops 1 | bytes 1 | tf_op jit(solution)/shard_map/pallas_call | solution.py:81
  9.1 0.0 copy-start
  9.1 0.6 collective-permute-start.2
  9.7 1.3 %shard_map.58 = f32[16,16,256]{2,1,0:T(8,128)S(1)} custom-call(f32[16,16,4096]{2,1,0:T(8,128)} %x_ref.9), custom_call_target="tpu_custom_call" | custom-call | flops 1 | bytes 1 | tf_op jit(solution)/shard_map/pallas_call | solution.py:81
  11.0 2.1 %collective-permute-start.3 = (f32[256,256]{1,0:T(8,128)S(1)}, f32[256,256]{1,0:T(8,128)S(1)}, u32[]{:S(2)}, u32[]{:S(2)}) collective-permute-start(f32[256,256]{1,0:T(8,128)S(1)} %bitcast.9), channel_id=1, source_target_pairs={{0,8},{4,12},{8,0},{12,4},{1,9},{5,13},{9,1},{13,5},{2,10},{6,14},... | collective-permute-start | bytes 786440 | tf_op jit(solution)/shard_map/ppermute | solution.py:318
  13.1 1.1 %shard_map.52 = f32[16,16,512]{2,1,0:T(8,128)S(1)} custom-call(f32[16,16,4096]{2,1,0:T(8,128)} %x_ref.9), custom_call_target="tpu_custom_call" | custom-call | flops 1 | bytes 1 | tf_op jit(solution)/shard_map/pallas_call | solution.py:81
  14.3 0.0 copy-done
  14.3 0.6 shard_map.53.refs_0_
  14.9 4.9 %collective-permute-done.1.x_ref = f32[256,512]{1,0:T(8,128)S(1)} collective-permute-done((f32[256,512]{1,0:T(8,128)S(1)}, f32[256,512]{1,0:T(8,128)S(1)}, u32[]{:S(2)}, u32[]{:S(2)}) %collective-permute-start.1) | collective-permute-done | bytes 524320 | tf_op jit(solution)/shard_map/ppermute | solution.py:318
  19.7 0.6 shard_map.54.refs_0_
  20.3 0.0 copy-start.1
  20.3 10.9 %collective-permute-done.x_ref = f32[256,512]{1,0:T(8,128)S(1)} collective-permute-done((f32[256,512]{1,0:T(8,128)S(1)}, f32[256,512]{1,0:T(8,128)S(1)}, u32[]{:S(2)}, u32[]{:S(2)}) %collective-permute-start) | collective-permute-done | bytes 524320 | tf_op jit(solution)/shard_map/ppermute | solution.py:318
  31.2 0.6 shard_map.55.sum_ref
  31.8 15.2 %collective-permute-done.2.x_ref = f32[256,256]{1,0:T(8,128)S(1)} collective-permute-done((f32[256,256]{1,0:T(8,128)S(1)}, f32[256,256]{1,0:T(8,128)S(1)}, u32[]{:S(2)}, u32[]{:S(2)}) %collective-permute-start.2) | collective-permute-done | bytes 262176 | tf_op jit(solution)/shard_map/ppermute | solution.py:318
  47.0 1.1 %shard_map.57 = (f32[256,256]{1,0:T(8,128)S(1)}, f32[256,256]{1,0:T(8,128)S(1)}, f32[256,256]{1,0:T(8,128)S(1)}, f32[256,256]{1,0:T(8,128)S(1)}, f32[16,128]{1,0:T(8,128)S(1)}, /*index=5*/f32[16,128]{1,0:T(8,128)S(1)}) custom-call(bf16[4,512,768]{2,1,0:T(8,128)(2,1)S(1)} %copy-done, f32[512,512]{1,0:T(8,128)S(1)} %shard_map.55.sum_ref, ...), custom_call_target="tpu_custom_call" | custom-call | flops 1 | bytes 1 | tf_op jit(solution)/shard_map/pallas_call | solution.py:160
  48.2 0.1 collective-permute-start.4
  48.2 0.5 collective-permute-start.5
  48.7 0.1 collective-permute-start.6
  48.8 2.9 %collective-permute-done.3.x_ref = f32[256,256]{1,0:T(8,128)S(1)} collective-permute-done((f32[256,256]{1,0:T(8,128)S(1)}, f32[256,256]{1,0:T(8,128)S(1)}, u32[]{:S(2)}, u32[]{:S(2)}) %collective-permute-start.3) | collective-permute-done | bytes 262176 | tf_op jit(solution)/shard_map/ppermute | solution.py:318
  51.7 0.0 collective-permute-done.6.refs_1_
  51.7 0.0 collective-permute-done.4.other_ref
  51.7 0.0 collective-permute-done.5.sum_ref
  51.7 0.1 collective-permute-start.7
  51.8 0.7 %shard_map.59 = (f32[256,256]{1,0:T(8,128)S(1)}, f32[16,128]{1,0:T(8,128)S(1)}) custom-call(bf16[4,512,768]{2,1,0:T(8,128)(2,1)S(1)} %copy-done, f32[256,256]{1,0:T(8,128)S(1)} %get-tuple-element.17.sum_ref, f32[256,256]{1,0:T(8,128)S(1)} %collective-permute-done.3.x_ref, f32[1,1024]{1,0:T(1,128)S(1)} %bitcast.12, f32[16,128]{1,0:T(8,128)S(1)} %get-tuple-element.22.refs_0_, ...), custom_call_target="tpu_custom_call" | custom-call | flops 1 | bytes 1 | tf_op jit(solution)/shard_map/pallas_call | solution.py:190
  52.5 0.8 %collective-permute-done.7.x_ref = f32[256,256]{1,0:T(8,128)S(1)} collective-permute-done((f32[256,256]{1,0:T(8,128)S(1)}, f32[256,256]{1,0:T(8,128)S(1)}, u32[]{:S(2)}, u32[]{:S(2)}) %collective-permute-start.7) | collective-permute-done | bytes 262176 | tf_op jit(solution)/shard_map/ppermute | solution.py:318
  53.3 0.7 %shard_map.60 = (f32[256,256]{1,0:T(8,128)S(1)}, f32[8,16,128]{2,1,0:T(8,128)S(1)}) custom-call(bf16[4,512,768]{2,1,0:T(8,128)(2,1)S(1)} %copy-done, f32[256,256]{1,0:T(8,128)S(1)} %collective-permute-done.5.sum_ref, f32[256,256]{1,0:T(8,128)S(1)} %collective-permute-done.7.x_ref, f32[1,1024]{1,0:T(1,128)S(1)} %bitcast.13, ...), custom_call_target="tpu_custom_call" | custom-call | flops 1 | bytes 1 | tf_op jit(solution)/shard_map/pallas_call | solution.py:190
  54.0 8.8 %all_to_all.5.grams_ref = f32[8,16,128]{2,1,0:T(8,128)S(1)} all-to-all(f32[8,16,128]{2,1,0:T(8,128)S(1)} %get-tuple-element.29), channel_id=1, replica_groups={{14,12,10,8,6,4,2,0},{15,13,11,9,7,5,3,1},{30,28,26,24,22,20,18,16},{31..., dimensions={0} | all-to-all | bytes 131072 | tf_op jit(solution)/shard_map/all_to_all | solution.py:359
  62.8 2.2 %shard_map.61 = (f32[8,2,16,1024]{3,2,1,0:T(8,128)}, f32[2,8,16,16]{3,2,1,0:T(8,128)}) custom-call(f32[256,256]{1,0:T(8,128)S(1)} %get-tuple-element.16.own_ref, f32[256,256]{1,0:T(8,128)S(1)} %get-tuple-element.24.own_last_ref, f32[256,256]{1,0:T(8,128)S(1)} %collective-permute-done.4.other_ref, f32[256,256]{1,0:T(8,128)S(1)} %get-tuple-element.28.other_last_ref, ...), custom_call_target="tpu_custom_call" | custom-call | tf_op jit(solution)/shard_map/pallas_call | solution.py:307
  (1 shorter events, 0.0 us)
Async XLA Ops:
  1.8 18.0 %collective-permute-start.1 = (f32[256,512]{1,0:T(8,128)S(1)}, f32[256,512]{1,0:T(8,128)S(1)}, u32[]{:S(2)}, u32[]{:S(2)}) collective-permute-start(f32[256,512]{1,0:T(8,128)S(1)} %bitcast.8), channel_id=1, source_target_pairs={{0,12},{4,8},{8,4},{12,0},{1,13},{5,9},{9,5},{13,1},{2,14},{6,10},... | collective-permute-start | bytes 1572872 | tf_op jit(solution)/shard_map/ppermute | solution.py:318
  8.0 23.2 %collective-permute-start = (f32[256,512]{1,0:T(8,128)S(1)}, f32[256,512]{1,0:T(8,128)S(1)}, u32[]{:S(2)}, u32[]{:S(2)}) collective-permute-start(f32[256,512]{1,0:T(8,128)S(1)} %bitcast.7), channel_id=1, source_target_pairs={{0,4},{4,0},{8,12},{12,8},{1,5},{5,1},{9,13},{13,9},{2,6},{6,2},{1... | collective-permute-start | bytes 1572872 | tf_op jit(solution)/shard_map/ppermute | solution.py:318
  9.1 5.2 %copy-start = (bf16[4,512,768]{2,1,0:T(8,128)(2,1)S(1)}, bf16[4,512,768]{2,1,0:T(8,128)(2,1)}, u32[]{:S(2)}) copy-start(bf16[4,512,768]{2,1,0:T(8,128)(2,1)} %constant.2.clone.t_ref) | copy-start | bytes 9437188
  9.1 37.9 %collective-permute-start.2 = (f32[256,256]{1,0:T(8,128)S(1)}, f32[256,256]{1,0:T(8,128)S(1)}, u32[]{:S(2)}, u32[]{:S(2)}) collective-permute-start(f32[256,256]{1,0:T(8,128)S(1)} %bitcast.10), channel_id=1, source_target_pairs={{0,8},{4,12},{8,0},{12,4},{1,9},{5,13},{9,1},{13,5},{2,10},{6,14},... | collective-permute-start | bytes 786440 | tf_op jit(solution)/shard_map/ppermute | solution.py:318
  11.0 40.6 %collective-permute-start.3 = (f32[256,256]{1,0:T(8,128)S(1)}, f32[256,256]{1,0:T(8,128)S(1)}, u32[]{:S(2)}, u32[]{:S(2)}) collective-permute-start(f32[256,256]{1,0:T(8,128)S(1)} %bitcast.9), channel_id=1, source_target_pairs={{0,8},{4,12},{8,0},{12,4},{1,9},{5,13},{9,1},{13,5},{2,10},{6,14},... | collective-permute-start | bytes 786440 | tf_op jit(solution)/shard_map/ppermute | solution.py:318
  20.3 26.7 %copy-start.1 = (f32[1024]{0:T(1024)S(1)}, f32[1024]{0:T(1024)}, u32[]{:S(2)}) copy-start(f32[1024]{0:T(1024)} %param.4) | copy-start | bytes 12292
  48.2 3.5 %collective-permute-start.4 = (f32[256,256]{1,0:T(8,128)S(1)}, f32[256,256]{1,0:T(8,128)S(1)}, u32[]{:S(2)}, u32[]{:S(2)}) collective-permute-start(f32[256,256]{1,0:T(8,128)S(1)} %get-tuple-element.18), channel_id=1, source_target_pairs={{0,1},{1,0},{2,3},{3,2},{4,5},{5,4},{6,7},{7,6},{8,9},{9,8},{10,11... | collective-permute-start | bytes 786440 | tf_op jit(solution)/shard_map/ppermute | solution.py:318
  48.2 3.4 %collective-permute-start.5 = (f32[256,256]{1,0:T(8,128)S(1)}, f32[256,256]{1,0:T(8,128)S(1)}, u32[]{:S(2)}, u32[]{:S(2)}) collective-permute-start(f32[256,256]{1,0:T(8,128)S(1)} %get-tuple-element.19), channel_id=1, source_target_pairs={{0,1},{1,0},{2,3},{3,2},{4,5},{5,4},{6,7},{7,6},{8,9},{9,8},{10,11... | collective-permute-start | bytes 786440 | tf_op jit(solution)/shard_map/ppermute | solution.py:318
  48.7 2.9 %collective-permute-start.6 = (f32[16,128]{1,0:T(8,128)S(1)}, f32[16,128]{1,0:T(8,128)S(1)}, u32[]{:S(2)}, u32[]{:S(2)}) collective-permute-start(f32[16,128]{1,0:T(8,128)S(1)} %get-tuple-element.20), channel_id=1, source_target_pairs={{0,1},{1,0},{2,3},{3,2},{4,5},{5,4},{6,7},{7,6},{8,9},{9,8},{10,11... | collective-permute-start | bytes 24584 | tf_op jit(solution)/shard_map/ppermute | solution.py:318
  51.7 1.6 %collective-permute-start.7 = (f32[256,256]{1,0:T(8,128)S(1)}, f32[256,256]{1,0:T(8,128)S(1)}, u32[]{:S(2)}, u32[]{:S(2)}) collective-permute-start(f32[256,256]{1,0:T(8,128)S(1)} %collective-permute-done.3.x_ref), channel_id=1, source_target_pairs={{0,1},{1,0},{2,3},{3,2},{4,5},{5,4},{6,7},{7,6},{8,9},{9,8},{10,11... | collective-permute-start | bytes 786440 | tf_op jit(solution)/shard_map/ppermute | solution.py:318

commit v14 on v13

--- a/solution.py
+++ b/solution.py
@@ -328,7 +328,7 @@
 
     tables = jnp.asarray(dft_blocks(n))
 
-    last = n // 2
+    last = n - 1
     early_rows = share // 2
     parts = ((0, early_rows), (early_rows, share - early_rows))
     targets = n * tm_count

time: 65.3 us -> 65.5 us (level)
  waiting for transfers between devices: 34.6 us -> 26.9 us
  blocking collectives: 8.83 us -> 15.2 us
  starting transfers between devices: 8.65 us -> 10.3 us
    ppermute x8, waiting for transfers between devices: 34.6 us -> 26.9 us  [partner(): return lax.ppermute(value, axis, [(i, i ^ step) for i in range(size)])]
    all_to_all x1, blocking collectives: 8.83 us -> 15.2 us  [on_device(): lax.all_to_all(gram, ('space', 'tm'), split_axis=0, concat_axis=0, axis_i...]
    ppermute x8, starting transfers between devices: 8.65 us -> 10.3 us  [partner(): return lax.ppermute(value, axis, [(i, i ^ step) for i in range(size)])]
  transfers between devices with their start and end apart: 8 -> 8, of which waited for: 5 -> 4; matrix products, arithmetic and copies ran while one was open for 0% -> 0% of each run, Pallas kernels for 12% -> 12%
where the time goes in v14:
time: 65.5 us; the launch traced here: 65.2 us
  waiting for transfers between devices  26.9 us (41%)
  blocking collectives  15.2 us (23%)
  Pallas kernels  12 us (18%)
  starting transfers between devices  10.3 us (16%)
  between operations  0.77 us (1%)
    ppermute x8, waiting for transfers between devices, partner(): return lax.ppermute(value, axis, [(i, i ^ step) for i in range(size)])  26.9 us
    all_to_all x1, blocking collectives, on_device(): lax.all_to_all(gram, ('space', 'tm'), split_axis=0, concat_axis=0, axis_i...  15.2 us
    ppermute x8, starting transfers between devices, partner(): return lax.ppermute(value, axis, [(i, i ^ step) for i in range(size)])  10.3 us
    pallas_call x5, Pallas kernels, cut(): pl.pallas_call(functools.partial(cut_kernel, n, k, rows, skip), out_shape...  5.5 us
    pallas_call x1, Pallas kernels, finish(): pl.pallas_call(functools.partial(finish_kernel, total), out_shape=(jax.Sh...  2.19 us
    pallas_call x3, Pallas kernels, early(): pl.pallas_call(functools.partial(early_kernel, n, k), out_shape=jax.Shape...  1.74 us
    pallas_call x2, Pallas kernels, last_part(): pl.pallas_call(functools.partial(last_part_kernel, n, k, swapped, skip),...  1.42 us
  transfers between devices with their start and end apart: 8, of which 4 were waited for; matrix products, arithmetic and copies ran while one was open for 0% of the time, Pallas kernels for 12%

profile of v14, /device:TPU:0, one launch (start us, length us, event | category | flops | bytes accessed | tf_op | source)
XLA Modules:
  0.0 65.2 jit_solution(10809649218213878844)
XLA Ops:
  0.6 1.1 %shard_map.51 = f32[16,16,512]{2,1,0:T(8,128)S(1)} custom-call(f32[16,16,4096]{2,1,0:T(8,128)} %x_ref.9), custom_call_target="tpu_custom_call" | custom-call | flops 1 | bytes 1 | tf_op jit(solution)/shard_map/pallas_call | solution.py:81
  1.8 4.1 %collective-permute-start.1 = (f32[256,512]{1,0:T(8,128)S(1)}, f32[256,512]{1,0:T(8,128)S(1)}, u32[]{:S(2)}, u32[]{:S(2)}) collective-permute-start(f32[256,512]{1,0:T(8,128)S(1)} %bitcast.8), channel_id=1, source_target_pairs={{0,8},{4,12},{8,0},{12,4},{1,9},{5,13},{9,1},{13,5},{2,10},{6,14},... | collective-permute-start | bytes 1572872 | tf_op jit(solution)/shard_map/ppermute | solution.py:318
  5.9 1.1 %shard_map.50 = f32[16,16,512]{2,1,0:T(8,128)S(1)} custom-call(f32[16,16,4096]{2,1,0:T(8,128)} %x_ref.9), custom_call_target="tpu_custom_call" | custom-call | flops 1 | bytes 1 | tf_op jit(solution)/shard_map/pallas_call | solution.py:81
  7.0 1.6 %collective-permute-start = (f32[256,512]{1,0:T(8,128)S(1)}, f32[256,512]{1,0:T(8,128)S(1)}, u32[]{:S(2)}, u32[]{:S(2)}) collective-permute-start(f32[256,512]{1,0:T(8,128)S(1)} %bitcast.7), channel_id=1, source_target_pairs={{0,4},{4,0},{8,12},{12,8},{1,5},{5,1},{9,13},{13,9},{2,6},{6,2},{1... | collective-permute-start | bytes 1572872 | tf_op jit(solution)/shard_map/ppermute | solution.py:318
  8.7 1.0 %shard_map.56 = f32[16,16,256]{2,1,0:T(8,128)S(1)} custom-call(f32[16,16,4096]{2,1,0:T(8,128)} %x_ref.9), custom_call_target="tpu_custom_call" | custom-call | flops 1 | bytes 1 | tf_op jit(solution)/shard_map/pallas_call | solution.py:81
  9.6 0.0 copy-start
  9.6 0.1 collective-permute-start.2
  9.7 1.1 %shard_map.58 = f32[16,16,256]{2,1,0:T(8,128)S(1)} custom-call(f32[16,16,4096]{2,1,0:T(8,128)} %x_ref.9), custom_call_target="tpu_custom_call" | custom-call | flops 1 | bytes 1 | tf_op jit(solution)/shard_map/pallas_call | solution.py:81
  10.9 3.7 %collective-permute-start.3 = (f32[256,256]{1,0:T(8,128)S(1)}, f32[256,256]{1,0:T(8,128)S(1)}, u32[]{:S(2)}, u32[]{:S(2)}) collective-permute-start(f32[256,256]{1,0:T(8,128)S(1)} %bitcast.9), channel_id=1, source_target_pairs={{0,12},{4,8},{8,4},{12,0},{1,13},{5,9},{9,5},{13,1},{2,14},{6,10},... | collective-permute-start | bytes 786440 | tf_op jit(solution)/shard_map/ppermute | solution.py:318
  14.6 1.1 %shard_map.52 = f32[16,16,512]{2,1,0:T(8,128)S(1)} custom-call(f32[16,16,4096]{2,1,0:T(8,128)} %x_ref.9), custom_call_target="tpu_custom_call" | custom-call | flops 1 | bytes 1 | tf_op jit(solution)/shard_map/pallas_call | solution.py:81
  15.7 0.0 copy-done
  15.7 0.6 shard_map.53.refs_0_
  16.3 14.5 %collective-permute-done.1.x_ref = f32[256,512]{1,0:T(8,128)S(1)} collective-permute-done((f32[256,512]{1,0:T(8,128)S(1)}, f32[256,512]{1,0:T(8,128)S(1)}, u32[]{:S(2)}, u32[]{:S(2)}) %collective-permute-start.1) | collective-permute-done | bytes 524320 | tf_op jit(solution)/shard_map/ppermute | solution.py:318
  30.8 0.6 shard_map.54.refs_0_
  31.4 0.0 copy-start.1
  31.4 10.4 %collective-permute-done.x_ref = f32[256,512]{1,0:T(8,128)S(1)} collective-permute-done((f32[256,512]{1,0:T(8,128)S(1)}, f32[256,512]{1,0:T(8,128)S(1)}, u32[]{:S(2)}, u32[]{:S(2)}) %collective-permute-start) | collective-permute-done | bytes 524320 | tf_op jit(solution)/shard_map/ppermute | solution.py:318
  41.8 0.6 shard_map.55.sum_ref
  42.4 0.0 collective-permute-done.2.x_ref
  42.4 1.1 %shard_map.57 = (f32[256,256]{1,0:T(8,128)S(1)}, f32[256,256]{1,0:T(8,128)S(1)}, f32[256,256]{1,0:T(8,128)S(1)}, f32[256,256]{1,0:T(8,128)S(1)}, f32[16,128]{1,0:T(8,128)S(1)}, /*index=5*/f32[16,128]{1,0:T(8,128)S(1)}) custom-call(bf16[4,512,768]{2,1,0:T(8,128)(2,1)S(1)} %copy-done, f32[512,512]{1,0:T(8,128)S(1)} %shard_map.55.sum_ref, ...), custom_call_target="tpu_custom_call" | custom-call | flops 1 | bytes 1 | tf_op jit(solution)/shard_map/pallas_call | solution.py:160
  43.5 0.1 collective-permute-start.4
  43.6 0.5 collective-permute-start.5
  44.1 0.1 collective-permute-start.6
  44.2 0.0 collective-permute-done.3.x_ref
  44.2 1.3 %collective-permute-done.6.refs_1_ = f32[16,128]{1,0:T(8,128)S(1)} collective-permute-done((f32[16,128]{1,0:T(8,128)S(1)}, f32[16,128]{1,0:T(8,128)S(1)}, u32[]{:S(2)}, u32[]{:S(2)}) %collective-permute-start.6) | collective-permute-done | bytes 8224 | tf_op jit(solution)/shard_map/ppermute | solution.py:318
  45.5 0.0 collective-permute-done.4.other_ref
  45.5 0.0 collective-permute-done.5.sum_ref
  45.5 0.1 collective-permute-start.7
  45.7 0.7 %shard_map.59 = (f32[256,256]{1,0:T(8,128)S(1)}, f32[16,128]{1,0:T(8,128)S(1)}) custom-call(bf16[4,512,768]{2,1,0:T(8,128)(2,1)S(1)} %copy-done, f32[256,256]{1,0:T(8,128)S(1)} %get-tuple-element.17.sum_ref, f32[256,256]{1,0:T(8,128)S(1)} %collective-permute-done.3.x_ref, f32[1,1024]{1,0:T(1,128)S(1)} %bitcast.12, f32[16,128]{1,0:T(8,128)S(1)} %get-tuple-element.22.refs_0_, ...), custom_call_target="tpu_custom_call" | custom-call | flops 1 | bytes 1 | tf_op jit(solution)/shard_map/pallas_call | solution.py:190
  46.4 0.7 %collective-permute-done.7.x_ref = f32[256,256]{1,0:T(8,128)S(1)} collective-permute-done((f32[256,256]{1,0:T(8,128)S(1)}, f32[256,256]{1,0:T(8,128)S(1)}, u32[]{:S(2)}, u32[]{:S(2)}) %collective-permute-start.7) | collective-permute-done | bytes 262176 | tf_op jit(solution)/shard_map/ppermute | solution.py:318
  47.1 0.7 %shard_map.60 = (f32[256,256]{1,0:T(8,128)S(1)}, f32[8,16,128]{2,1,0:T(8,128)S(1)}) custom-call(bf16[4,512,768]{2,1,0:T(8,128)(2,1)S(1)} %copy-done, f32[256,256]{1,0:T(8,128)S(1)} %collective-permute-done.5.sum_ref, f32[256,256]{1,0:T(8,128)S(1)} %collective-permute-done.7.x_ref, f32[1,1024]{1,0:T(1,128)S(1)} %bitcast.13, ...), custom_call_target="tpu_custom_call" | custom-call | flops 1 | bytes 1 | tf_op jit(solution)/shard_map/pallas_call | solution.py:190
  47.8 15.2 %all_to_all.5.grams_ref = f32[8,16,128]{2,1,0:T(8,128)S(1)} all-to-all(f32[8,16,128]{2,1,0:T(8,128)S(1)} %get-tuple-element.29), channel_id=1, replica_groups={{14,12,10,8,6,4,2,0},{15,13,11,9,7,5,3,1},{30,28,26,24,22,20,18,16},{31..., dimensions={0} | all-to-all | bytes 131072 | tf_op jit(solution)/shard_map/all_to_all | solution.py:359
  63.0 2.2 %shard_map.61 = (f32[8,2,16,1024]{3,2,1,0:T(8,128)}, f32[2,8,16,16]{3,2,1,0:T(8,128)}) custom-call(f32[256,256]{1,0:T(8,128)S(1)} %get-tuple-element.16.own_ref, f32[256,256]{1,0:T(8,128)S(1)} %get-tuple-element.24.own_last_ref, f32[256,256]{1,0:T(8,128)S(1)} %collective-permute-done.4.other_ref, f32[256,256]{1,0:T(8,128)S(1)} %get-tuple-element.28.other_last_ref, ...), custom_call_target="tpu_custom_call" | custom-call | tf_op jit(solution)/shard_map/pallas_call | solution.py:307
  (1 shorter events, 0.0 us)
Async XLA Ops:
  1.8 29.0 %collective-permute-start.1 = (f32[256,512]{1,0:T(8,128)S(1)}, f32[256,512]{1,0:T(8,128)S(1)}, u32[]{:S(2)}, u32[]{:S(2)}) collective-permute-start(f32[256,512]{1,0:T(8,128)S(1)} %bitcast.8), channel_id=1, source_target_pairs={{0,8},{4,12},{8,0},{12,4},{1,9},{5,13},{9,1},{13,5},{2,10},{6,14},... | collective-permute-start | bytes 1572872 | tf_op jit(solution)/shard_map/ppermute | solution.py:318
  7.0 34.8 %collective-permute-start = (f32[256,512]{1,0:T(8,128)S(1)}, f32[256,512]{1,0:T(8,128)S(1)}, u32[]{:S(2)}, u32[]{:S(2)}) collective-permute-start(f32[256,512]{1,0:T(8,128)S(1)} %bitcast.7), channel_id=1, source_target_pairs={{0,4},{4,0},{8,12},{12,8},{1,5},{5,1},{9,13},{13,9},{2,6},{6,2},{1... | collective-permute-start | bytes 1572872 | tf_op jit(solution)/shard_map/ppermute | solution.py:318
  9.6 6.1 %copy-start = (bf16[4,512,768]{2,1,0:T(8,128)(2,1)S(1)}, bf16[4,512,768]{2,1,0:T(8,128)(2,1)}, u32[]{:S(2)}) copy-start(bf16[4,512,768]{2,1,0:T(8,128)(2,1)} %constant.2.clone.t_ref) | copy-start | bytes 9437188
  9.6 32.7 %collective-permute-start.2 = (f32[256,256]{1,0:T(8,128)S(1)}, f32[256,256]{1,0:T(8,128)S(1)}, u32[]{:S(2)}, u32[]{:S(2)}) collective-permute-start(f32[256,256]{1,0:T(8,128)S(1)} %bitcast.10), channel_id=1, source_target_pairs={{0,12},{4,8},{8,4},{12,0},{1,13},{5,9},{9,5},{13,1},{2,14},{6,10},... | collective-permute-start | bytes 786440 | tf_op jit(solution)/shard_map/ppermute | solution.py:318
  10.9 33.3 %collective-permute-start.3 = (f32[256,256]{1,0:T(8,128)S(1)}, f32[256,256]{1,0:T(8,128)S(1)}, u32[]{:S(2)}, u32[]{:S(2)}) collective-permute-start(f32[256,256]{1,0:T(8,128)S(1)} %bitcast.9), channel_id=1, source_target_pairs={{0,12},{4,8},{8,4},{12,0},{1,13},{5,9},{9,5},{13,1},{2,14},{6,10},... | collective-permute-start | bytes 786440 | tf_op jit(solution)/shard_map/ppermute | solution.py:318
  31.4 11.0 %copy-start.1 = (f32[1024]{0:T(1024)S(1)}, f32[1024]{0:T(1024)}, u32[]{:S(2)}) copy-start(f32[1024]{0:T(1024)} %param.4) | copy-start | bytes 12292
  43.5 2.0 %collective-permute-start.4 = (f32[256,256]{1,0:T(8,128)S(1)}, f32[256,256]{1,0:T(8,128)S(1)}, u32[]{:S(2)}, u32[]{:S(2)}) collective-permute-start(f32[256,256]{1,0:T(8,128)S(1)} %get-tuple-element.18), channel_id=1, source_target_pairs={{0,1},{1,0},{2,3},{3,2},{4,5},{5,4},{6,7},{7,6},{8,9},{9,8},{10,11... | collective-permute-start | bytes 786440 | tf_op jit(solution)/shard_map/ppermute | solution.py:318
  43.6 1.9 %collective-permute-start.5 = (f32[256,256]{1,0:T(8,128)S(1)}, f32[256,256]{1,0:T(8,128)S(1)}, u32[]{:S(2)}, u32[]{:S(2)}) collective-permute-start(f32[256,256]{1,0:T(8,128)S(1)} %get-tuple-element.19), channel_id=1, source_target_pairs={{0,1},{1,0},{2,3},{3,2},{4,5},{5,4},{6,7},{7,6},{8,9},{9,8},{10,11... | collective-permute-start | bytes 786440 | tf_op jit(solution)/shard_map/ppermute | solution.py:318
  44.1 1.4 %collective-permute-start.6 = (f32[16,128]{1,0:T(8,128)S(1)}, f32[16,128]{1,0:T(8,128)S(1)}, u32[]{:S(2)}, u32[]{:S(2)}) collective-permute-start(f32[16,128]{1,0:T(8,128)S(1)} %get-tuple-element.20), channel_id=1, source_target_pairs={{0,1},{1,0},{2,3},{3,2},{4,5},{5,4},{6,7},{7,6},{8,9},{9,8},{10,11... | collective-permute-start | bytes 24584 | tf_op jit(solution)/shard_map/ppermute | solution.py:318
  45.5 1.5 %collective-permute-start.7 = (f32[256,256]{1,0:T(8,128)S(1)}, f32[256,256]{1,0:T(8,128)S(1)}, u32[]{:S(2)}, u32[]{:S(2)}) collective-permute-start(f32[256,256]{1,0:T(8,128)S(1)} %collective-permute-done.3.x_ref), channel_id=1, source_target_pairs={{0,1},{1,0},{2,3},{3,2},{4,5},{5,4},{6,7},{7,6},{8,9},{9,8},{10,11... | collective-permute-start | bytes 786440 | tf_op jit(solution)/shard_map/ppermute | solution.py:318

commit v15 on v14

--- a/solution.py
+++ b/solution.py
@@ -165,31 +165,41 @@
     )(tables, partial_sum, piece, weights)
 
 
-def last_part_kernel(n, k, swapped, skip, t_ref, sum_ref, x_ref, w_ref, *refs):
-    *before, own_ref, gram_ref = refs
+def last_part_kernel(n, k, swapped, t_ref, sum_ref, x_ref, w_ref, *refs):
     half, size = sum_ref.shape
     me = lax.axis_index("freq")
     src = lax.bitwise_xor(lax.axis_index("space"), k)
     lines = pl.ds(pl.multiple_of(me * half, 128), half)
     spectra = sum_ref[...] + times_split(t_ref[src, lines], x_ref[...])
-    own_ref[...] = spectra
+    share = w_ref.shape[1] // 2
+    skip = share - size
     place = 1 - me if swapped else me
-    gram = gram_of(spectra, weights_at(w_ref, place, skip + size, skip, size))
-    for ref in before:
-        gram = gram + ref[...]
-    if len(gram_ref.shape) == 2:
-        gram_ref[...] = gram
-    else:
+    gram = gram_of(spectra, weights_at(w_ref, place, share, skip, size))
+    if swapped:
+        before_ref, high_ref, low_ref, gram_ref = refs
+        gram = gram + before_ref[...]
+        high_ref[...], low_ref[...] = split(spectra)
         for d in range(gram_ref.shape[0]):
             gram_ref[d] = gram
-
-
-def last_part(tables, n, k, swapped, skip, copies, partial_sum, piece, weights, *before):
-    gram = (NB, partial_sum.shape[0] // 2)
-    shapes = [partial_sum.shape, (copies, *gram) if copies else gram]
+        return
+    gram_own_ref, gram_lent_ref, own_ref, other_ref, *refs = refs
+    high_ref, low_ref, other_high_ref, other_low_ref, gram_ref = refs
+    gram_ref[...] = gram + gram_own_ref[...] + gram_lent_ref[...]
+    high_ref[:, :skip], low_ref[:, :skip] = split(own_ref[...])
+    high_ref[:, skip:], low_ref[:, skip:] = split(spectra)
+    other_high_ref[...], other_low_ref[...] = split(other_ref[...])
+
+
+def last_part(tables, n, k, copies, partial_sum, piece, weights, *before):
+    half, size = partial_sum.shape
+    share = weights.shape[1] // 2
+    gram = (NB, half // 2)
+    widths = [size, size] if copies else [share, share, share - size, share - size]
+    parts = [jax.ShapeDtypeStruct((half, width), jnp.bfloat16) for width in widths]
+    gram = jax.ShapeDtypeStruct((copies, *gram) if copies else gram, jnp.float32)
     return pl.pallas_call(
-        functools.partial(last_part_kernel, n, k, swapped, skip),
-        out_shape=[jax.ShapeDtypeStruct(shape, jnp.float32) for shape in shapes],
+        functools.partial(last_part_kernel, n, k, bool(copies)),
+        out_shape=[*parts, gram],
         compiler_params=pltpu.CompilerParams(vmem_limit_bytes=16 * MIB),
         cost_estimate=SMALL,
     )(tables, partial_sum, piece, weights, *before)
@@ -201,7 +211,18 @@
 
 
 def finish_kernel(
-    total, own_ref, own_last_ref, other_ref, other_last_ref, grams_ref, modes_ref, factor_ref
+    total,
+    own_high_ref,
+    own_low_ref,
+    first_high_ref,
+    first_low_ref,
+    last_high_ref,
+    last_low_ref,
+    grams_ref,
+    modes_ref,
+    factor_ref,
+    slots,
+    sems,
 ):
     local = modes_ref.shape[0]
     width = local * NB
@@ -271,47 +292,76 @@
     inv_re = [inv_re[h] * scales[h] for h in (0, 1)]
     inv_im = [inv_im[h] * scales[h] for h in (0, 1)]
 
-    block_re = jnp.where(same, jnp.concatenate(inv_re * local, axis=0), 0.0)
-    block_im = jnp.where(same, jnp.concatenate(inv_im * local, axis=0), 0.0)
-    mixing = jnp.concatenate(
-        [
-            jnp.concatenate([block_re, block_im], axis=1),
-            jnp.concatenate([-block_im, block_re], axis=1),
-        ],
-        axis=0,
-    )
     me = lax.axis_index("freq")
-    high, low = split(mixing)
-    mixing = jnp.concatenate([high, high, low], axis=1)
-    own = [own_ref[...], own_last_ref[...]]
-    other = [other_ref[...], other_last_ref[...]]
-    for place, parts in ((me, own), (1 - me, other)):
-        out = times_split(mixing, jnp.concatenate(parts, axis=1))
-        cols = pl.ds(pl.multiple_of(place * share, 128), share)
-        for part in range(2):
-            for f in range(local):
-                at = part * width + f * NB
-                modes_ref[f, part, :, cols] = out[at : at + NB]
+    own = own_high_ref[...], own_low_ref[...]
+    other = [
+        jnp.concatenate([a[...], b[...]], axis=1)
+        for a, b in ((first_high_ref, last_high_ref), (first_low_ref, last_low_ref))
+    ]
+    part = width // 2
+    lane = lax.broadcasted_iota(jnp.int32, (NB, width), 1)
+    left_half = lane < part
+    line = lax.broadcasted_iota(jnp.int32, (width, width), 0) % part // NB
+    block = lax.broadcasted_iota(jnp.int32, (width, width), 1) % part // NB
+    inv_re, inv_im = jnp.concatenate(inv_re, axis=0), jnp.concatenate(inv_im, axis=0)
+    turned_re, turned_im = pltpu.roll(inv_re, part, 1), pltpu.roll(inv_im, part, 1)
+    moves = []
+    for h in range(2):
+        stay = left_half if h == 0 else jnp.logical_not(left_half)
+        twice_re = jnp.where(stay, inv_re, turned_re)
+        twice_im = jnp.where(stay, inv_im, turned_im)
+        top = jnp.where(left_half, twice_re, twice_im)
+        bottom = jnp.where(left_half, -twice_im, twice_re)
+        count = part // NB
+        mixing = jnp.concatenate([top] * count + [bottom] * count, axis=0)
+        high, low = split(jnp.where(line == block, mixing, 0.0))
+        left = jnp.concatenate([high, high, low], axis=1)
+        lines = [slice(r * width + h * part, r * width + (h + 1) * part) for r in range(2)]
+        for place, (x_high, x_low) in ((me, own), (1 - me, other)):
+            right = [x[at] for x in (x_high, x_low, x_high) for at in lines]
+            out = jnp.dot(
+                left, jnp.concatenate(right, axis=0), preferred_element_type=jnp.float32
+            )
+            cols = pl.ds(pl.multiple_of(place * share, 128), share)
+            for r in range(2):
+                for f in range(count):
+                    at = r * part + f * NB
+                    slots[h, f, r, :, cols] = out[at : at + NB]
+        moves.append(
+            pltpu.make_async_copy(
+                slots.at[h], modes_ref.at[pl.ds(h * count, count)], sems.at[h]
+            )
+        )
+        moves[-1].start()
     pad = jnp.zeros((width - NB, width), jnp.float32)
     turned_re = jnp.transpose(jnp.concatenate(low_re + [pad], axis=0))
     turned_im = jnp.transpose(jnp.concatenate(low_im + [pad], axis=0))
     for f in range(local):
         factor_ref[0, f] = turned_re[f * NB : (f + 1) * NB, :NB]
         factor_ref[1, f] = -turned_im[f * NB : (f + 1) * NB, :NB]
-
-
-def finish(total, own, own_last, other, other_last, grams):
-    half, size = own.shape
+    for move in moves:
+        move.wait()
+
+
+def finish(total, own, others, grams):
+    half, share = own[0].shape
     local = half // (2 * NB)
-    share = size + own_last.shape[1]
     return pl.pallas_call(
         functools.partial(finish_kernel, total),
         out_shape=(
             jax.ShapeDtypeStruct((local, 2, NB, 2 * share), jnp.float32),
             jax.ShapeDtypeStruct((2, local, NB, NB), jnp.float32),
         ),
+        out_specs=(
+            pl.BlockSpec(memory_space=pltpu.HBM),
+            pl.BlockSpec(memory_space=pltpu.VMEM),
+        ),
+        scratch_shapes=[
+            pltpu.VMEM((2, local // 2, 2, NB, 2 * share), jnp.float32),
+            pltpu.SemaphoreType.DMA((2,)),
+        ],
         compiler_params=pltpu.CompilerParams(vmem_limit_bytes=16 * MIB),
-    )(own, own_last, other, other_last, grams)
+    )(*own, *others, grams)
 
 
 def partner(value, axis, size, step):
@@ -350,12 +400,10 @@
     traded = [partner(part, "freq", freq_count, 1) for part in (other, later, lent)]
     piece, (other, later, lent) = lax.optimization_barrier((last_pieces[1], traded))
     raw = partner(piece, "freq", freq_count, 1)
-    own_last, gram = last_part(
-        tables, n, last, False, early_rows, 0, rest, piece, weights, gram, lent
+    *parts, gram = last_part(
+        tables, n, last, 0, rest, piece, weights, gram, lent, own, other
     )
-    other_last, gram = last_part(
-        tables, n, last, True, early_rows, targets, later, raw, weights, gram
-    )
+    *last_parts, gram = last_part(tables, n, last, targets, later, raw, weights, gram)
     grams = lax.all_to_all(
         gram,
         ("space", "tm"),
@@ -365,7 +413,7 @@
         tiled=True,
     )
     total = rows * targets
-    return finish(total, own, own_last, other, other_last, grams)
+    return finish(total, parts[:2], [*parts[2:], *last_parts], grams)
 
 
 def solution(mesh):

time: 65.5 us -> 66 us (level)
  no operation moved by 1% of the time
where the time goes in v15:
time: 66 us; the launch traced here: 65.7 us
  waiting for transfers between devices  26.8 us (41%)
  blocking collectives  15.2 us (23%)
  Pallas kernels  12.6 us (19%)
  starting transfers between devices  10.3 us (16%)
  between operations  0.77 us (1%)
    ppermute x8, waiting for transfers between devices, partner(): return lax.ppermute(value, axis, [(i, i ^ step) for i in range(size)])  26.8 us
    all_to_all x1, blocking collectives, on_device(): lax.all_to_all(gram, ('space', 'tm'), split_axis=0, concat_axis=0, axis_i...  15.2 us
    ppermute x8, starting transfers between devices, partner(): return lax.ppermute(value, axis, [(i, i ^ step) for i in range(size)])  10.3 us
    pallas_call x5, Pallas kernels, cut(): pl.pallas_call(functools.partial(cut_kernel, n, k, rows, skip), out_shape...  5.5 us
    pallas_call x1, Pallas kernels, finish(): pl.pallas_call(functools.partial(finish_kernel, total), out_shape=(jax.Sh...  2.71 us
    pallas_call x3, Pallas kernels, early(): pl.pallas_call(functools.partial(early_kernel, n, k), out_shape=jax.Shape...  1.74 us
    pallas_call x2, Pallas kernels, last_part(): pl.pallas_call(functools.partial(last_part_kernel, n, k, bool(copies)), o...  1.48 us
  transfers between devices with their start and end apart: 8, of which 4 were waited for; matrix products, arithmetic and copies ran while one was open for 0% of the time, Pallas kernels for 12%

profile of v15, /device:TPU:0, one launch (start us, length us, event | category | flops | bytes accessed | tf_op | source)
XLA Modules:
  0.0 65.7 jit_solution(9394262503495286618)
XLA Ops:
  0.6 1.1 %shard_map.51 = f32[16,16,512]{2,1,0:T(8,128)S(1)} custom-call(f32[16,16,4096]{2,1,0:T(8,128)} %x_ref.9), custom_call_target="tpu_custom_call" | custom-call | flops 1 | bytes 1 | tf_op jit(solution)/shard_map/pallas_call | solution.py:81
  1.8 4.1 %collective-permute-start.1 = (f32[256,512]{1,0:T(8,128)S(1)}, f32[256,512]{1,0:T(8,128)S(1)}, u32[]{:S(2)}, u32[]{:S(2)}) collective-permute-start(f32[256,512]{1,0:T(8,128)S(1)} %bitcast.8), channel_id=1, source_target_pairs={{0,8},{4,12},{8,0},{12,4},{1,9},{5,13},{9,1},{13,5},{2,10},{6,14},... | collective-permute-start | bytes 1572872 | tf_op jit(solution)/shard_map/ppermute | solution.py:368
  5.9 1.1 %shard_map.50 = f32[16,16,512]{2,1,0:T(8,128)S(1)} custom-call(f32[16,16,4096]{2,1,0:T(8,128)} %x_ref.9), custom_call_target="tpu_custom_call" | custom-call | flops 1 | bytes 1 | tf_op jit(solution)/shard_map/pallas_call | solution.py:81
  7.0 1.6 %collective-permute-start = (f32[256,512]{1,0:T(8,128)S(1)}, f32[256,512]{1,0:T(8,128)S(1)}, u32[]{:S(2)}, u32[]{:S(2)}) collective-permute-start(f32[256,512]{1,0:T(8,128)S(1)} %bitcast.7), channel_id=1, source_target_pairs={{0,4},{4,0},{8,12},{12,8},{1,5},{5,1},{9,13},{13,9},{2,6},{6,2},{1... | collective-permute-start | bytes 1572872 | tf_op jit(solution)/shard_map/ppermute | solution.py:368
  8.7 1.0 %shard_map.56 = f32[16,16,256]{2,1,0:T(8,128)S(1)} custom-call(f32[16,16,4096]{2,1,0:T(8,128)} %x_ref.9), custom_call_target="tpu_custom_call" | custom-call | flops 1 | bytes 1 | tf_op jit(solution)/shard_map/pallas_call | solution.py:81
  9.6 0.0 copy-start
  9.6 0.1 collective-permute-start.2
  9.7 1.1 %shard_map.58 = f32[16,16,256]{2,1,0:T(8,128)S(1)} custom-call(f32[16,16,4096]{2,1,0:T(8,128)} %x_ref.9), custom_call_target="tpu_custom_call" | custom-call | flops 1 | bytes 1 | tf_op jit(solution)/shard_map/pallas_call | solution.py:81
  10.9 3.7 %collective-permute-start.3 = (f32[256,256]{1,0:T(8,128)S(1)}, f32[256,256]{1,0:T(8,128)S(1)}, u32[]{:S(2)}, u32[]{:S(2)}) collective-permute-start(f32[256,256]{1,0:T(8,128)S(1)} %bitcast.9), channel_id=1, source_target_pairs={{0,12},{4,8},{8,4},{12,0},{1,13},{5,9},{9,5},{13,1},{2,14},{6,10},... | collective-permute-start | bytes 786440 | tf_op jit(solution)/shard_map/ppermute | solution.py:368
  14.6 1.1 %shard_map.52 = f32[16,16,512]{2,1,0:T(8,128)S(1)} custom-call(f32[16,16,4096]{2,1,0:T(8,128)} %x_ref.9), custom_call_target="tpu_custom_call" | custom-call | flops 1 | bytes 1 | tf_op jit(solution)/shard_map/pallas_call | solution.py:81
  15.7 0.6 shard_map.53.refs_0_
  16.3 14.5 %collective-permute-done.1.x_ref = f32[256,512]{1,0:T(8,128)S(1)} collective-permute-done((f32[256,512]{1,0:T(8,128)S(1)}, f32[256,512]{1,0:T(8,128)S(1)}, u32[]{:S(2)}, u32[]{:S(2)}) %collective-permute-start.1) | collective-permute-done | bytes 524320 | tf_op jit(solution)/shard_map/ppermute | solution.py:368
  30.8 0.6 shard_map.54.refs_0_
  31.4 0.0 copy-start.1
  31.4 10.4 %collective-permute-done.x_ref = f32[256,512]{1,0:T(8,128)S(1)} collective-permute-done((f32[256,512]{1,0:T(8,128)S(1)}, f32[256,512]{1,0:T(8,128)S(1)}, u32[]{:S(2)}, u32[]{:S(2)}) %collective-permute-start) | collective-permute-done | bytes 524320 | tf_op jit(solution)/shard_map/ppermute | solution.py:368
  41.8 0.6 shard_map.55.sum_ref
  42.4 0.0 collective-permute-done.2.x_ref
  42.4 0.0 copy-done.1
  42.4 1.1 %shard_map.57 = (f32[256,256]{1,0:T(8,128)S(1)}, f32[256,256]{1,0:T(8,128)S(1)}, f32[256,256]{1,0:T(8,128)S(1)}, f32[256,256]{1,0:T(8,128)S(1)}, f32[16,128]{1,0:T(8,128)S(1)}, /*index=5*/f32[16,128]{1,0:T(8,128)S(1)}) custom-call(bf16[4,512,768]{2,1,0:T(8,128)(2,1)S(1)} %copy-done, f32[512,512]{1,0:T(8,128)S(1)} %shard_map.55.sum_ref, ...), custom_call_target="tpu_custom_call" | custom-call | flops 1 | bytes 1 | tf_op jit(solution)/shard_map/pallas_call | solution.py:160
  43.5 0.1 collective-permute-start.4
  43.6 0.5 collective-permute-start.5
  44.1 0.1 collective-permute-start.6
  44.2 0.0 collective-permute-done.3.x_ref
  44.2 1.3 %collective-permute-done.6.refs_1_ = f32[16,128]{1,0:T(8,128)S(1)} collective-permute-done((f32[16,128]{1,0:T(8,128)S(1)}, f32[16,128]{1,0:T(8,128)S(1)}, u32[]{:S(2)}, u32[]{:S(2)}) %collective-permute-start.6) | collective-permute-done | bytes 8224 | tf_op jit(solution)/shard_map/ppermute | solution.py:368
  45.5 0.0 collective-permute-done.4.refs_3_
  45.5 0.0 collective-permute-done.5.sum_ref
  45.5 0.1 collective-permute-start.7
  45.7 0.8 %shard_map.59 = (bf16[256,512]{1,0:T(8,128)(2,1)S(1)}, bf16[256,512]{1,0:T(8,128)(2,1)S(1)}, bf16[256,256]{1,0:T(8,128)(2,1)S(1)}, bf16[256,256]{1,0:T(8,128)(2,1)S(1)}, f32[16,128]{1,0:T(8,128)S(1)}) custom-call(bf16[4,512,768]{2,1,0:T(8,128)(2,1)S(1)} %copy-done, f32[256,256]{1,0:T(8,128)S(1)} %get-tuple-element.20.sum_ref, ...), custom_call_target="tpu_custom_call" | custom-call | flops 1 | bytes 1 | tf_op jit(solution)/shard_map/pallas_call | solution.py:200
  46.4 0.6 collective-permute-done.7.x_ref
  47.1 0.7 %shard_map.60 = (bf16[256,256]{1,0:T(8,128)(2,1)S(1)}, bf16[256,256]{1,0:T(8,128)(2,1)S(1)}, f32[8,16,128]{2,1,0:T(8,128)S(1)}) custom-call(bf16[4,512,768]{2,1,0:T(8,128)(2,1)S(1)} %copy-done, f32[256,256]{1,0:T(8,128)S(1)} %collective-permute-done.5.sum_ref, f32[256,256]{1,0:T(8,128)S(1)} %collective-permute-done.7.x_ref, f32[1,1024]{1,0:T(1,128)S(1)} %bitcast.13, ...), custom_call_target="tpu_custom_call" | custom-call | flops 1 | bytes 1 | tf_op jit(solution)/shard_map/pallas_call | solution.py:200
  47.8 15.2 %all_to_all.5.grams_ref = f32[8,16,128]{2,1,0:T(8,128)S(1)} all-to-all(f32[8,16,128]{2,1,0:T(8,128)S(1)} %get-tuple-element.37), channel_id=1, replica_groups={{14,12,10,8,6,4,2,0},{15,13,11,9,7,5,3,1},{30,28,26,24,22,20,18,16},{31..., dimensions={0} | all-to-all | bytes 131072 | tf_op jit(solution)/shard_map/all_to_all | solution.py:407
  63.0 2.7 %shard_map.61 = (f32[8,2,16,1024]{3,2,1,0:T(8,128)}, f32[2,8,16,16]{3,2,1,0:T(8,128)}) custom-call(bf16[256,512]{1,0:T(8,128)(2,1)S(1)} %get-tuple-element.29.own_high_ref, bf16[256,512]{1,0:T(8,128)(2,1)S(1)} %get-tuple-element.30.own_low_ref, bf16[256,256]{1,0:T(8,128)(2,1)S(1)} %get-tuple-element.31.first_high_ref, ...), custom_call_target="tpu_custom_call" | custom-call | tf_op jit(solution)/shard_map/pallas_call | solution.py:349
  (1 shorter events, 0.0 us)
Async XLA Ops:
  1.8 29.0 %collective-permute-start.1 = (f32[256,512]{1,0:T(8,128)S(1)}, f32[256,512]{1,0:T(8,128)S(1)}, u32[]{:S(2)}, u32[]{:S(2)}) collective-permute-start(f32[256,512]{1,0:T(8,128)S(1)} %bitcast.8), channel_id=1, source_target_pairs={{0,8},{4,12},{8,0},{12,4},{1,9},{5,13},{9,1},{13,5},{2,10},{6,14},... | collective-permute-start | bytes 1572872 | tf_op jit(solution)/shard_map/ppermute | solution.py:368
  7.0 34.8 %collective-permute-start = (f32[256,512]{1,0:T(8,128)S(1)}, f32[256,512]{1,0:T(8,128)S(1)}, u32[]{:S(2)}, u32[]{:S(2)}) collective-permute-start(f32[256,512]{1,0:T(8,128)S(1)} %bitcast.7), channel_id=1, source_target_pairs={{0,4},{4,0},{8,12},{12,8},{1,5},{5,1},{9,13},{13,9},{2,6},{6,2},{1... | collective-permute-start | bytes 1572872 | tf_op jit(solution)/shard_map/ppermute | solution.py:368
  9.6 6.1 %copy-start = (bf16[4,512,768]{2,1,0:T(8,128)(2,1)S(1)}, bf16[4,512,768]{2,1,0:T(8,128)(2,1)}, u32[]{:S(2)}) copy-start(bf16[4,512,768]{2,1,0:T(8,128)(2,1)} %constant.2.clone.t_ref) | copy-start | bytes 9437188
  9.6 32.7 %collective-permute-start.2 = (f32[256,256]{1,0:T(8,128)S(1)}, f32[256,256]{1,0:T(8,128)S(1)}, u32[]{:S(2)}, u32[]{:S(2)}) collective-permute-start(f32[256,256]{1,0:T(8,128)S(1)} %bitcast.10), channel_id=1, source_target_pairs={{0,12},{4,8},{8,4},{12,0},{1,13},{5,9},{9,5},{13,1},{2,14},{6,10},... | collective-permute-start | bytes 786440 | tf_op jit(solution)/shard_map/ppermute | solution.py:368
  10.9 33.3 %collective-permute-start.3 = (f32[256,256]{1,0:T(8,128)S(1)}, f32[256,256]{1,0:T(8,128)S(1)}, u32[]{:S(2)}, u32[]{:S(2)}) collective-permute-start(f32[256,256]{1,0:T(8,128)S(1)} %bitcast.9), channel_id=1, source_target_pairs={{0,12},{4,8},{8,4},{12,0},{1,13},{5,9},{9,5},{13,1},{2,14},{6,10},... | collective-permute-start | bytes 786440 | tf_op jit(solution)/shard_map/ppermute | solution.py:368
  31.4 11.0 %copy-start.1 = (f32[1024]{0:T(1024)S(1)}, f32[1024]{0:T(1024)}, u32[]{:S(2)}) copy-start(f32[1024]{0:T(1024)} %param.4) | copy-start | bytes 12292
  43.5 2.0 %collective-permute-start.4 = (f32[256,256]{1,0:T(8,128)S(1)}, f32[256,256]{1,0:T(8,128)S(1)}, u32[]{:S(2)}, u32[]{:S(2)}) collective-permute-start(f32[256,256]{1,0:T(8,128)S(1)} %get-tuple-element.21), channel_id=1, source_target_pairs={{0,1},{1,0},{2,3},{3,2},{4,5},{5,4},{6,7},{7,6},{8,9},{9,8},{10,11... | collective-permute-start | bytes 786440 | tf_op jit(solution)/shard_map/ppermute | solution.py:368
  43.6 1.9 %collective-permute-start.5 = (f32[256,256]{1,0:T(8,128)S(1)}, f32[256,256]{1,0:T(8,128)S(1)}, u32[]{:S(2)}, u32[]{:S(2)}) collective-permute-start(f32[256,256]{1,0:T(8,128)S(1)} %get-tuple-element.22), channel_id=1, source_target_pairs={{0,1},{1,0},{2,3},{3,2},{4,5},{5,4},{6,7},{7,6},{8,9},{9,8},{10,11... | collective-permute-start | bytes 786440 | tf_op jit(solution)/shard_map/ppermute | solution.py:368
  44.1 1.4 %collective-permute-start.6 = (f32[16,128]{1,0:T(8,128)S(1)}, f32[16,128]{1,0:T(8,128)S(1)}, u32[]{:S(2)}, u32[]{:S(2)}) collective-permute-start(f32[16,128]{1,0:T(8,128)S(1)} %get-tuple-element.23), channel_id=1, source_target_pairs={{0,1},{1,0},{2,3},{3,2},{4,5},{5,4},{6,7},{7,6},{8,9},{9,8},{10,11... | collective-permute-start | bytes 24584 | tf_op jit(solution)/shard_map/ppermute | solution.py:368
  45.5 1.5 %collective-permute-start.7 = (f32[256,256]{1,0:T(8,128)S(1)}, f32[256,256]{1,0:T(8,128)S(1)}, u32[]{:S(2)}, u32[]{:S(2)}) collective-permute-start(f32[256,256]{1,0:T(8,128)S(1)} %collective-permute-done.3.x_ref), channel_id=1, source_target_pairs={{0,1},{1,0},{2,3},{3,2},{4,5},{5,4},{6,7},{7,6},{8,9},{9,8},{10,11... | collective-permute-start | bytes 786440 | tf_op jit(solution)/shard_map/ppermute | solution.py:368

commit v16 on v15

--- a/solution.py
+++ b/solution.py
@@ -221,8 +221,6 @@
     grams_ref,
     modes_ref,
     factor_ref,
-    slots,
-    sems,
 ):
     local = modes_ref.shape[0]
     width = local * NB
@@ -305,7 +303,6 @@
     block = lax.broadcasted_iota(jnp.int32, (width, width), 1) % part // NB
     inv_re, inv_im = jnp.concatenate(inv_re, axis=0), jnp.concatenate(inv_im, axis=0)
     turned_re, turned_im = pltpu.roll(inv_re, part, 1), pltpu.roll(inv_im, part, 1)
-    moves = []
     for h in range(2):
         stay = left_half if h == 0 else jnp.logical_not(left_half)
         twice_re = jnp.where(stay, inv_re, turned_re)
@@ -326,21 +323,13 @@
             for r in range(2):
                 for f in range(count):
                     at = r * part + f * NB
-                    slots[h, f, r, :, cols] = out[at : at + NB]
-        moves.append(
-            pltpu.make_async_copy(
-                slots.at[h], modes_ref.at[pl.ds(h * count, count)], sems.at[h]
-            )
-        )
-        moves[-1].start()
+                    modes_ref[h * count + f, r, :, cols] = out[at : at + NB]
     pad = jnp.zeros((width - NB, width), jnp.float32)
     turned_re = jnp.transpose(jnp.concatenate(low_re + [pad], axis=0))
     turned_im = jnp.transpose(jnp.concatenate(low_im + [pad], axis=0))
     for f in range(local):
         factor_ref[0, f] = turned_re[f * NB : (f + 1) * NB, :NB]
         factor_ref[1, f] = -turned_im[f * NB : (f + 1) * NB, :NB]
-    for move in moves:
-        move.wait()
 
 
 def finish(total, own, others, grams):
@@ -352,14 +341,6 @@
             jax.ShapeDtypeStruct((local, 2, NB, 2 * share), jnp.float32),
             jax.ShapeDtypeStruct((2, local, NB, NB), jnp.float32),
         ),
-        out_specs=(
-            pl.BlockSpec(memory_space=pltpu.HBM),
-            pl.BlockSpec(memory_space=pltpu.VMEM),
-        ),
-        scratch_shapes=[
-            pltpu.VMEM((2, local // 2, 2, NB, 2 * share), jnp.float32),
-            pltpu.SemaphoreType.DMA((2,)),
-        ],
         compiler_params=pltpu.CompilerParams(vmem_limit_bytes=16 * MIB),
     )(*own, *others, grams)
 

time: 66 us -> 65.5 us (level)
  no operation moved by 1% of the time
where the time goes in v16:
time: 65.5 us; the launch traced here: 65.2 us
  waiting for transfers between devices  26.8 us (41%)
  blocking collectives  15.2 us (23%)
  Pallas kernels  12 us (18%)
  starting transfers between devices  10.3 us (16%)
  between operations  0.77 us (1%)
    ppermute x8, waiting for transfers between devices, partner(): return lax.ppermute(value, axis, [(i, i ^ step) for i in range(size)])  26.8 us
    all_to_all x1, blocking collectives, on_device(): lax.all_to_all(gram, ('space', 'tm'), split_axis=0, concat_axis=0, axis_i...  15.2 us
    ppermute x8, starting transfers between devices, partner(): return lax.ppermute(value, axis, [(i, i ^ step) for i in range(size)])  10.3 us
    pallas_call x5, Pallas kernels, cut(): pl.pallas_call(functools.partial(cut_kernel, n, k, rows, skip), out_shape...  5.5 us
    pallas_call x1, Pallas kernels, finish(): pl.pallas_call(functools.partial(finish_kernel, total), out_shape=(jax.Sh...  2.19 us
    pallas_call x3, Pallas kernels, early(): pl.pallas_call(functools.partial(early_kernel, n, k), out_shape=jax.Shape...  1.74 us
    pallas_call x2, Pallas kernels, last_part(): pl.pallas_call(functools.partial(last_part_kernel, n, k, bool(copies)), o...  1.48 us
  transfers between devices with their start and end apart: 8, of which 4 were waited for; matrix products, arithmetic and copies ran while one was open for 0% of the time, Pallas kernels for 12%

profile of v16, /device:TPU:0, one launch (start us, length us, event | category | flops | bytes accessed | tf_op | source)
XLA Modules:
  0.0 65.2 jit_solution(2055837213728168069)
XLA Ops:
  0.6 1.1 %shard_map.51 = f32[16,16,512]{2,1,0:T(8,128)S(1)} custom-call(f32[16,16,4096]{2,1,0:T(8,128)} %x_ref.9), custom_call_target="tpu_custom_call" | custom-call | flops 1 | bytes 1 | tf_op jit(solution)/shard_map/pallas_call | solution.py:81
  1.8 4.1 %collective-permute-start.1 = (f32[256,512]{1,0:T(8,128)S(1)}, f32[256,512]{1,0:T(8,128)S(1)}, u32[]{:S(2)}, u32[]{:S(2)}) collective-permute-start(f32[256,512]{1,0:T(8,128)S(1)} %bitcast.8), channel_id=1, source_target_pairs={{0,8},{4,12},{8,0},{12,4},{1,9},{5,13},{9,1},{13,5},{2,10},{6,14},... | collective-permute-start | bytes 1572872 | tf_op jit(solution)/shard_map/ppermute | solution.py:349
  5.9 1.1 %shard_map.50 = f32[16,16,512]{2,1,0:T(8,128)S(1)} custom-call(f32[16,16,4096]{2,1,0:T(8,128)} %x_ref.9), custom_call_target="tpu_custom_call" | custom-call | flops 1 | bytes 1 | tf_op jit(solution)/shard_map/pallas_call | solution.py:81
  7.0 1.6 %collective-permute-start = (f32[256,512]{1,0:T(8,128)S(1)}, f32[256,512]{1,0:T(8,128)S(1)}, u32[]{:S(2)}, u32[]{:S(2)}) collective-permute-start(f32[256,512]{1,0:T(8,128)S(1)} %bitcast.7), channel_id=1, source_target_pairs={{0,4},{4,0},{8,12},{12,8},{1,5},{5,1},{9,13},{13,9},{2,6},{6,2},{1... | collective-permute-start | bytes 1572872 | tf_op jit(solution)/shard_map/ppermute | solution.py:349
  8.7 1.0 %shard_map.56 = f32[16,16,256]{2,1,0:T(8,128)S(1)} custom-call(f32[16,16,4096]{2,1,0:T(8,128)} %x_ref.9), custom_call_target="tpu_custom_call" | custom-call | flops 1 | bytes 1 | tf_op jit(solution)/shard_map/pallas_call | solution.py:81
  9.6 0.0 copy-start
  9.6 0.1 collective-permute-start.2
  9.7 1.1 %shard_map.58 = f32[16,16,256]{2,1,0:T(8,128)S(1)} custom-call(f32[16,16,4096]{2,1,0:T(8,128)} %x_ref.9), custom_call_target="tpu_custom_call" | custom-call | flops 1 | bytes 1 | tf_op jit(solution)/shard_map/pallas_call | solution.py:81
  10.9 3.7 %collective-permute-start.3 = (f32[256,256]{1,0:T(8,128)S(1)}, f32[256,256]{1,0:T(8,128)S(1)}, u32[]{:S(2)}, u32[]{:S(2)}) collective-permute-start(f32[256,256]{1,0:T(8,128)S(1)} %bitcast.9), channel_id=1, source_target_pairs={{0,12},{4,8},{8,4},{12,0},{1,13},{5,9},{9,5},{13,1},{2,14},{6,10},... | collective-permute-start | bytes 786440 | tf_op jit(solution)/shard_map/ppermute | solution.py:349
  14.6 1.1 %shard_map.52 = f32[16,16,512]{2,1,0:T(8,128)S(1)} custom-call(f32[16,16,4096]{2,1,0:T(8,128)} %x_ref.9), custom_call_target="tpu_custom_call" | custom-call | flops 1 | bytes 1 | tf_op jit(solution)/shard_map/pallas_call | solution.py:81
  15.7 0.6 shard_map.53.refs_0_
  16.3 14.5 %collective-permute-done.1.x_ref = f32[256,512]{1,0:T(8,128)S(1)} collective-permute-done((f32[256,512]{1,0:T(8,128)S(1)}, f32[256,512]{1,0:T(8,128)S(1)}, u32[]{:S(2)}, u32[]{:S(2)}) %collective-permute-start.1) | collective-permute-done | bytes 524320 | tf_op jit(solution)/shard_map/ppermute | solution.py:349
  30.8 0.6 shard_map.54.refs_0_
  31.4 0.0 copy-start.1
  31.4 10.4 %collective-permute-done.x_ref = f32[256,512]{1,0:T(8,128)S(1)} collective-permute-done((f32[256,512]{1,0:T(8,128)S(1)}, f32[256,512]{1,0:T(8,128)S(1)}, u32[]{:S(2)}, u32[]{:S(2)}) %collective-permute-start) | collective-permute-done | bytes 524320 | tf_op jit(solution)/shard_map/ppermute | solution.py:349
  41.8 0.6 shard_map.55.sum_ref
  42.4 0.0 collective-permute-done.2.x_ref
  42.4 0.0 copy-done.1
  42.4 1.1 %shard_map.57 = (f32[256,256]{1,0:T(8,128)S(1)}, f32[256,256]{1,0:T(8,128)S(1)}, f32[256,256]{1,0:T(8,128)S(1)}, f32[256,256]{1,0:T(8,128)S(1)}, f32[16,128]{1,0:T(8,128)S(1)}, /*index=5*/f32[16,128]{1,0:T(8,128)S(1)}) custom-call(bf16[4,512,768]{2,1,0:T(8,128)(2,1)S(1)} %copy-done, f32[512,512]{1,0:T(8,128)S(1)} %shard_map.55.sum_ref, ...), custom_call_target="tpu_custom_call" | custom-call | flops 1 | bytes 1 | tf_op jit(solution)/shard_map/pallas_call | solution.py:160
  43.5 0.1 collective-permute-start.4
  43.6 0.5 collective-permute-start.5
  44.1 0.1 collective-permute-start.6
  44.2 0.0 collective-permute-done.3.x_ref
  44.2 1.3 %collective-permute-done.6.refs_1_ = f32[16,128]{1,0:T(8,128)S(1)} collective-permute-done((f32[16,128]{1,0:T(8,128)S(1)}, f32[16,128]{1,0:T(8,128)S(1)}, u32[]{:S(2)}, u32[]{:S(2)}) %collective-permute-start.6) | collective-permute-done | bytes 8224 | tf_op jit(solution)/shard_map/ppermute | solution.py:349
  45.5 0.0 collective-permute-done.4.refs_3_
  45.5 0.0 collective-permute-done.5.sum_ref
  45.5 0.1 collective-permute-start.7
  45.7 0.8 %shard_map.59 = (bf16[256,512]{1,0:T(8,128)(2,1)S(1)}, bf16[256,512]{1,0:T(8,128)(2,1)S(1)}, bf16[256,256]{1,0:T(8,128)(2,1)S(1)}, bf16[256,256]{1,0:T(8,128)(2,1)S(1)}, f32[16,128]{1,0:T(8,128)S(1)}) custom-call(bf16[4,512,768]{2,1,0:T(8,128)(2,1)S(1)} %copy-done, f32[256,256]{1,0:T(8,128)S(1)} %get-tuple-element.20.sum_ref, ...), custom_call_target="tpu_custom_call" | custom-call | flops 1 | bytes 1 | tf_op jit(solution)/shard_map/pallas_call | solution.py:200
  46.4 0.6 collective-permute-done.7.x_ref
  47.1 0.7 %shard_map.60 = (bf16[256,256]{1,0:T(8,128)(2,1)S(1)}, bf16[256,256]{1,0:T(8,128)(2,1)S(1)}, f32[8,16,128]{2,1,0:T(8,128)S(1)}) custom-call(bf16[4,512,768]{2,1,0:T(8,128)(2,1)S(1)} %copy-done, f32[256,256]{1,0:T(8,128)S(1)} %collective-permute-done.5.sum_ref, f32[256,256]{1,0:T(8,128)S(1)} %collective-permute-done.7.x_ref, f32[1,1024]{1,0:T(1,128)S(1)} %bitcast.13, ...), custom_call_target="tpu_custom_call" | custom-call | flops 1 | bytes 1 | tf_op jit(solution)/shard_map/pallas_call | solution.py:200
  47.8 15.2 %all_to_all.5.grams_ref = f32[8,16,128]{2,1,0:T(8,128)S(1)} all-to-all(f32[8,16,128]{2,1,0:T(8,128)S(1)} %get-tuple-element.37), channel_id=1, replica_groups={{14,12,10,8,6,4,2,0},{15,13,11,9,7,5,3,1},{30,28,26,24,22,20,18,16},{31..., dimensions={0} | all-to-all | bytes 131072 | tf_op jit(solution)/shard_map/all_to_all | solution.py:388
  63.0 2.2 %shard_map.61 = (f32[8,2,16,1024]{3,2,1,0:T(8,128)}, f32[2,8,16,16]{3,2,1,0:T(8,128)}) custom-call(bf16[256,512]{1,0:T(8,128)(2,1)S(1)} %get-tuple-element.29.own_high_ref, bf16[256,512]{1,0:T(8,128)(2,1)S(1)} %get-tuple-element.30.own_low_ref, bf16[256,256]{1,0:T(8,128)(2,1)S(1)} %get-tuple-element.31.first_high_ref, ...), custom_call_target="tpu_custom_call" | custom-call | tf_op jit(solution)/shard_map/pallas_call | solution.py:338
  (1 shorter events, 0.0 us)
Async XLA Ops:
  1.8 29.0 %collective-permute-start.1 = (f32[256,512]{1,0:T(8,128)S(1)}, f32[256,512]{1,0:T(8,128)S(1)}, u32[]{:S(2)}, u32[]{:S(2)}) collective-permute-start(f32[256,512]{1,0:T(8,128)S(1)} %bitcast.8), channel_id=1, source_target_pairs={{0,8},{4,12},{8,0},{12,4},{1,9},{5,13},{9,1},{13,5},{2,10},{6,14},... | collective-permute-start | bytes 1572872 | tf_op jit(solution)/shard_map/ppermute | solution.py:349
  7.0 34.8 %collective-permute-start = (f32[256,512]{1,0:T(8,128)S(1)}, f32[256,512]{1,0:T(8,128)S(1)}, u32[]{:S(2)}, u32[]{:S(2)}) collective-permute-start(f32[256,512]{1,0:T(8,128)S(1)} %bitcast.7), channel_id=1, source_target_pairs={{0,4},{4,0},{8,12},{12,8},{1,5},{5,1},{9,13},{13,9},{2,6},{6,2},{1... | collective-permute-start | bytes 1572872 | tf_op jit(solution)/shard_map/ppermute | solution.py:349
  9.6 6.1 %copy-start = (bf16[4,512,768]{2,1,0:T(8,128)(2,1)S(1)}, bf16[4,512,768]{2,1,0:T(8,128)(2,1)}, u32[]{:S(2)}) copy-start(bf16[4,512,768]{2,1,0:T(8,128)(2,1)} %constant.2.clone.t_ref) | copy-start | bytes 9437188
  9.6 32.7 %collective-permute-start.2 = (f32[256,256]{1,0:T(8,128)S(1)}, f32[256,256]{1,0:T(8,128)S(1)}, u32[]{:S(2)}, u32[]{:S(2)}) collective-permute-start(f32[256,256]{1,0:T(8,128)S(1)} %bitcast.10), channel_id=1, source_target_pairs={{0,12},{4,8},{8,4},{12,0},{1,13},{5,9},{9,5},{13,1},{2,14},{6,10},... | collective-permute-start | bytes 786440 | tf_op jit(solution)/shard_map/ppermute | solution.py:349
  10.9 33.3 %collective-permute-start.3 = (f32[256,256]{1,0:T(8,128)S(1)}, f32[256,256]{1,0:T(8,128)S(1)}, u32[]{:S(2)}, u32[]{:S(2)}) collective-permute-start(f32[256,256]{1,0:T(8,128)S(1)} %bitcast.9), channel_id=1, source_target_pairs={{0,12},{4,8},{8,4},{12,0},{1,13},{5,9},{9,5},{13,1},{2,14},{6,10},... | collective-permute-start | bytes 786440 | tf_op jit(solution)/shard_map/ppermute | solution.py:349
  31.4 11.0 %copy-start.1 = (f32[1024]{0:T(1024)S(1)}, f32[1024]{0:T(1024)}, u32[]{:S(2)}) copy-start(f32[1024]{0:T(1024)} %param.4) | copy-start | bytes 12292
  43.5 2.0 %collective-permute-start.4 = (f32[256,256]{1,0:T(8,128)S(1)}, f32[256,256]{1,0:T(8,128)S(1)}, u32[]{:S(2)}, u32[]{:S(2)}) collective-permute-start(f32[256,256]{1,0:T(8,128)S(1)} %get-tuple-element.21), channel_id=1, source_target_pairs={{0,1},{1,0},{2,3},{3,2},{4,5},{5,4},{6,7},{7,6},{8,9},{9,8},{10,11... | collective-permute-start | bytes 786440 | tf_op jit(solution)/shard_map/ppermute | solution.py:349
  43.6 1.9 %collective-permute-start.5 = (f32[256,256]{1,0:T(8,128)S(1)}, f32[256,256]{1,0:T(8,128)S(1)}, u32[]{:S(2)}, u32[]{:S(2)}) collective-permute-start(f32[256,256]{1,0:T(8,128)S(1)} %get-tuple-element.22), channel_id=1, source_target_pairs={{0,1},{1,0},{2,3},{3,2},{4,5},{5,4},{6,7},{7,6},{8,9},{9,8},{10,11... | collective-permute-start | bytes 786440 | tf_op jit(solution)/shard_map/ppermute | solution.py:349
  44.1 1.4 %collective-permute-start.6 = (f32[16,128]{1,0:T(8,128)S(1)}, f32[16,128]{1,0:T(8,128)S(1)}, u32[]{:S(2)}, u32[]{:S(2)}) collective-permute-start(f32[16,128]{1,0:T(8,128)S(1)} %get-tuple-element.23), channel_id=1, source_target_pairs={{0,1},{1,0},{2,3},{3,2},{4,5},{5,4},{6,7},{7,6},{8,9},{9,8},{10,11... | collective-permute-start | bytes 24584 | tf_op jit(solution)/shard_map/ppermute | solution.py:349
  45.5 1.5 %collective-permute-start.7 = (f32[256,256]{1,0:T(8,128)S(1)}, f32[256,256]{1,0:T(8,128)S(1)}, u32[]{:S(2)}, u32[]{:S(2)}) collective-permute-start(f32[256,256]{1,0:T(8,128)S(1)} %collective-permute-done.3.x_ref), channel_id=1, source_target_pairs={{0,1},{1,0},{2,3},{3,2},{4,5},{5,4},{6,7},{7,6},{8,9},{9,8},{10,11... | collective-permute-start | bytes 786440 | tf_op jit(solution)/shard_map/ppermute | solution.py:349

commit v17 on v16

--- a/solution.py
+++ b/solution.py
@@ -385,12 +385,14 @@
         tables, n, last, 0, rest, piece, weights, gram, lent, own, other
     )
     *last_parts, gram = last_part(tables, n, last, targets, later, raw, weights, gram)
+    order = sorted(range(n), key=lambda z: abs(2 * z - n))
+    order = [z * tm_count + x for z in order for x in range(tm_count - 1, -1, -1)]
     grams = lax.all_to_all(
         gram,
         ("space", "tm"),
         split_axis=0,
         concat_axis=0,
-        axis_index_groups=[list(range(targets - 1, -1, -1))],
+        axis_index_groups=[order],
         tiled=True,
     )
     total = rows * targets

time: 65.5 us -> 65.8 us (level)
  no operation moved by 1% of the time
where the time goes in v17:
time: 65.8 us; the launch traced here: 65.5 us
  waiting for transfers between devices  26.8 us (41%)
  blocking collectives  15.5 us (24%)
  Pallas kernels  12 us (18%)
  starting transfers between devices  10.3 us (16%)
  between operations  0.77 us (1%)
    ppermute x8, waiting for transfers between devices, partner(): return lax.ppermute(value, axis, [(i, i ^ step) for i in range(size)])  26.8 us
    all_to_all x1, blocking collectives, on_device(): lax.all_to_all(gram, ('space', 'tm'), split_axis=0, concat_axis=0, axis_i...  15.5 us
    ppermute x8, starting transfers between devices, partner(): return lax.ppermute(value, axis, [(i, i ^ step) for i in range(size)])  10.3 us
    pallas_call x5, Pallas kernels, cut(): pl.pallas_call(functools.partial(cut_kernel, n, k, rows, skip), out_shape...  5.5 us
    pallas_call x1, Pallas kernels, finish(): pl.pallas_call(functools.partial(finish_kernel, total), out_shape=(jax.Sh...  2.19 us
    pallas_call x3, Pallas kernels, early(): pl.pallas_call(functools.partial(early_kernel, n, k), out_shape=jax.Shape...  1.74 us
    pallas_call x2, Pallas kernels, last_part(): pl.pallas_call(functools.partial(last_part_kernel, n, k, bool(copies)), o...  1.48 us
  transfers between devices with their start and end apart: 8, of which 4 were waited for; matrix products, arithmetic and copies ran while one was open for 0% of the time, Pallas kernels for 12%

profile of v17, /device:TPU:0, one launch (start us, length us, event | category | flops | bytes accessed | tf_op | source)
XLA Modules:
  0.0 65.5 jit_solution(12817921169512844292)
XLA Ops:
  0.6 1.1 %shard_map.51 = f32[16,16,512]{2,1,0:T(8,128)S(1)} custom-call(f32[16,16,4096]{2,1,0:T(8,128)} %x_ref.9), custom_call_target="tpu_custom_call" | custom-call | flops 1 | bytes 1 | tf_op jit(solution)/shard_map/pallas_call | solution.py:81
  1.8 4.1 %collective-permute-start.1 = (f32[256,512]{1,0:T(8,128)S(1)}, f32[256,512]{1,0:T(8,128)S(1)}, u32[]{:S(2)}, u32[]{:S(2)}) collective-permute-start(f32[256,512]{1,0:T(8,128)S(1)} %bitcast.8), channel_id=1, source_target_pairs={{0,8},{4,12},{8,0},{12,4},{1,9},{5,13},{9,1},{13,5},{2,10},{6,14},... | collective-permute-start | bytes 1572872 | tf_op jit(solution)/shard_map/ppermute | solution.py:349
  5.9 1.1 %shard_map.50 = f32[16,16,512]{2,1,0:T(8,128)S(1)} custom-call(f32[16,16,4096]{2,1,0:T(8,128)} %x_ref.9), custom_call_target="tpu_custom_call" | custom-call | flops 1 | bytes 1 | tf_op jit(solution)/shard_map/pallas_call | solution.py:81
  7.0 1.6 %collective-permute-start = (f32[256,512]{1,0:T(8,128)S(1)}, f32[256,512]{1,0:T(8,128)S(1)}, u32[]{:S(2)}, u32[]{:S(2)}) collective-permute-start(f32[256,512]{1,0:T(8,128)S(1)} %bitcast.7), channel_id=1, source_target_pairs={{0,4},{4,0},{8,12},{12,8},{1,5},{5,1},{9,13},{13,9},{2,6},{6,2},{1... | collective-permute-start | bytes 1572872 | tf_op jit(solution)/shard_map/ppermute | solution.py:349
  8.7 1.0 %shard_map.56 = f32[16,16,256]{2,1,0:T(8,128)S(1)} custom-call(f32[16,16,4096]{2,1,0:T(8,128)} %x_ref.9), custom_call_target="tpu_custom_call" | custom-call | flops 1 | bytes 1 | tf_op jit(solution)/shard_map/pallas_call | solution.py:81
  9.6 0.0 copy-start
  9.6 0.1 collective-permute-start.2
  9.7 1.1 %shard_map.58 = f32[16,16,256]{2,1,0:T(8,128)S(1)} custom-call(f32[16,16,4096]{2,1,0:T(8,128)} %x_ref.9), custom_call_target="tpu_custom_call" | custom-call | flops 1 | bytes 1 | tf_op jit(solution)/shard_map/pallas_call | solution.py:81
  10.9 3.7 %collective-permute-start.3 = (f32[256,256]{1,0:T(8,128)S(1)}, f32[256,256]{1,0:T(8,128)S(1)}, u32[]{:S(2)}, u32[]{:S(2)}) collective-permute-start(f32[256,256]{1,0:T(8,128)S(1)} %bitcast.9), channel_id=1, source_target_pairs={{0,12},{4,8},{8,4},{12,0},{1,13},{5,9},{9,5},{13,1},{2,14},{6,10},... | collective-permute-start | bytes 786440 | tf_op jit(solution)/shard_map/ppermute | solution.py:349
  14.6 1.1 %shard_map.52 = f32[16,16,512]{2,1,0:T(8,128)S(1)} custom-call(f32[16,16,4096]{2,1,0:T(8,128)} %x_ref.9), custom_call_target="tpu_custom_call" | custom-call | flops 1 | bytes 1 | tf_op jit(solution)/shard_map/pallas_call | solution.py:81
  15.7 0.0 copy-done
  15.7 0.6 shard_map.53.refs_0_
  16.3 14.5 %collective-permute-done.1.x_ref = f32[256,512]{1,0:T(8,128)S(1)} collective-permute-done((f32[256,512]{1,0:T(8,128)S(1)}, f32[256,512]{1,0:T(8,128)S(1)}, u32[]{:S(2)}, u32[]{:S(2)}) %collective-permute-start.1) | collective-permute-done | bytes 524320 | tf_op jit(solution)/shard_map/ppermute | solution.py:349
  30.8 0.6 shard_map.54.refs_0_
  31.4 0.0 copy-start.1
  31.4 10.4 %collective-permute-done.x_ref = f32[256,512]{1,0:T(8,128)S(1)} collective-permute-done((f32[256,512]{1,0:T(8,128)S(1)}, f32[256,512]{1,0:T(8,128)S(1)}, u32[]{:S(2)}, u32[]{:S(2)}) %collective-permute-start) | collective-permute-done | bytes 524320 | tf_op jit(solution)/shard_map/ppermute | solution.py:349
  41.8 0.6 shard_map.55.sum_ref
  42.4 0.0 collective-permute-done.2.x_ref
  42.4 1.1 %shard_map.57 = (f32[256,256]{1,0:T(8,128)S(1)}, f32[256,256]{1,0:T(8,128)S(1)}, f32[256,256]{1,0:T(8,128)S(1)}, f32[256,256]{1,0:T(8,128)S(1)}, f32[16,128]{1,0:T(8,128)S(1)}, /*index=5*/f32[16,128]{1,0:T(8,128)S(1)}) custom-call(bf16[4,512,768]{2,1,0:T(8,128)(2,1)S(1)} %copy-done, f32[512,512]{1,0:T(8,128)S(1)} %shard_map.55.sum_ref, ...), custom_call_target="tpu_custom_call" | custom-call | flops 1 | bytes 1 | tf_op jit(solution)/shard_map/pallas_call | solution.py:160
  43.5 0.1 collective-permute-start.4
  43.6 0.5 collective-permute-start.5
  44.1 0.1 collective-permute-start.6
  44.2 0.0 collective-permute-done.3.x_ref
  44.2 1.3 %collective-permute-done.6.refs_1_ = f32[16,128]{1,0:T(8,128)S(1)} collective-permute-done((f32[16,128]{1,0:T(8,128)S(1)}, f32[16,128]{1,0:T(8,128)S(1)}, u32[]{:S(2)}, u32[]{:S(2)}) %collective-permute-start.6) | collective-permute-done | bytes 8224 | tf_op jit(solution)/shard_map/ppermute | solution.py:349
  45.5 0.0 collective-permute-done.4.refs_3_
  45.5 0.0 collective-permute-done.5.sum_ref
  45.5 0.1 collective-permute-start.7
  45.7 0.8 %shard_map.59 = (bf16[256,512]{1,0:T(8,128)(2,1)S(1)}, bf16[256,512]{1,0:T(8,128)(2,1)S(1)}, bf16[256,256]{1,0:T(8,128)(2,1)S(1)}, bf16[256,256]{1,0:T(8,128)(2,1)S(1)}, f32[16,128]{1,0:T(8,128)S(1)}) custom-call(bf16[4,512,768]{2,1,0:T(8,128)(2,1)S(1)} %copy-done, f32[256,256]{1,0:T(8,128)S(1)} %get-tuple-element.20.sum_ref, ...), custom_call_target="tpu_custom_call" | custom-call | flops 1 | bytes 1 | tf_op jit(solution)/shard_map/pallas_call | solution.py:200
  46.4 0.6 collective-permute-done.7.x_ref
  47.1 0.7 %shard_map.60 = (bf16[256,256]{1,0:T(8,128)(2,1)S(1)}, bf16[256,256]{1,0:T(8,128)(2,1)S(1)}, f32[8,16,128]{2,1,0:T(8,128)S(1)}) custom-call(bf16[4,512,768]{2,1,0:T(8,128)(2,1)S(1)} %copy-done, f32[256,256]{1,0:T(8,128)S(1)} %collective-permute-done.5.sum_ref, f32[256,256]{1,0:T(8,128)S(1)} %collective-permute-done.7.x_ref, f32[1,1024]{1,0:T(1,128)S(1)} %bitcast.13, ...), custom_call_target="tpu_custom_call" | custom-call | flops 1 | bytes 1 | tf_op jit(solution)/shard_map/pallas_call | solution.py:200
  47.8 15.5 %all_to_all.5.grams_ref = f32[8,16,128]{2,1,0:T(8,128)S(1)} all-to-all(f32[8,16,128]{2,1,0:T(8,128)S(1)} %get-tuple-element.37), channel_id=1, replica_groups={{10,8,6,4,14,12,2,0},{11,9,7,5,15,13,3,1},{26,24,22,20,30,28,18,16},{27..., dimensions={0} | all-to-all | bytes 131072 | tf_op jit(solution)/shard_map/all_to_all | solution.py:390
  63.3 2.2 %shard_map.61 = (f32[8,2,16,1024]{3,2,1,0:T(8,128)}, f32[2,8,16,16]{3,2,1,0:T(8,128)}) custom-call(bf16[256,512]{1,0:T(8,128)(2,1)S(1)} %get-tuple-element.29.own_high_ref, bf16[256,512]{1,0:T(8,128)(2,1)S(1)} %get-tuple-element.30.own_low_ref, bf16[256,256]{1,0:T(8,128)(2,1)S(1)} %get-tuple-element.31.first_high_ref, ...), custom_call_target="tpu_custom_call" | custom-call | tf_op jit(solution)/shard_map/pallas_call | solution.py:338
  (1 shorter events, 0.0 us)
Async XLA Ops:
  1.8 29.0 %collective-permute-start.1 = (f32[256,512]{1,0:T(8,128)S(1)}, f32[256,512]{1,0:T(8,128)S(1)}, u32[]{:S(2)}, u32[]{:S(2)}) collective-permute-start(f32[256,512]{1,0:T(8,128)S(1)} %bitcast.8), channel_id=1, source_target_pairs={{0,8},{4,12},{8,0},{12,4},{1,9},{5,13},{9,1},{13,5},{2,10},{6,14},... | collective-permute-start | bytes 1572872 | tf_op jit(solution)/shard_map/ppermute | solution.py:349
  7.0 34.8 %collective-permute-start = (f32[256,512]{1,0:T(8,128)S(1)}, f32[256,512]{1,0:T(8,128)S(1)}, u32[]{:S(2)}, u32[]{:S(2)}) collective-permute-start(f32[256,512]{1,0:T(8,128)S(1)} %bitcast.7), channel_id=1, source_target_pairs={{0,4},{4,0},{8,12},{12,8},{1,5},{5,1},{9,13},{13,9},{2,6},{6,2},{1... | collective-permute-start | bytes 1572872 | tf_op jit(solution)/shard_map/ppermute | solution.py:349
  9.6 6.1 %copy-start = (bf16[4,512,768]{2,1,0:T(8,128)(2,1)S(1)}, bf16[4,512,768]{2,1,0:T(8,128)(2,1)}, u32[]{:S(2)}) copy-start(bf16[4,512,768]{2,1,0:T(8,128)(2,1)} %constant.2.clone.t_ref) | copy-start | bytes 9437188
  9.6 32.7 %collective-permute-start.2 = (f32[256,256]{1,0:T(8,128)S(1)}, f32[256,256]{1,0:T(8,128)S(1)}, u32[]{:S(2)}, u32[]{:S(2)}) collective-permute-start(f32[256,256]{1,0:T(8,128)S(1)} %bitcast.10), channel_id=1, source_target_pairs={{0,12},{4,8},{8,4},{12,0},{1,13},{5,9},{9,5},{13,1},{2,14},{6,10},... | collective-permute-start | bytes 786440 | tf_op jit(solution)/shard_map/ppermute | solution.py:349
  10.9 33.3 %collective-permute-start.3 = (f32[256,256]{1,0:T(8,128)S(1)}, f32[256,256]{1,0:T(8,128)S(1)}, u32[]{:S(2)}, u32[]{:S(2)}) collective-permute-start(f32[256,256]{1,0:T(8,128)S(1)} %bitcast.9), channel_id=1, source_target_pairs={{0,12},{4,8},{8,4},{12,0},{1,13},{5,9},{9,5},{13,1},{2,14},{6,10},... | collective-permute-start | bytes 786440 | tf_op jit(solution)/shard_map/ppermute | solution.py:349
  31.4 11.0 %copy-start.1 = (f32[1024]{0:T(1024)S(1)}, f32[1024]{0:T(1024)}, u32[]{:S(2)}) copy-start(f32[1024]{0:T(1024)} %param.4) | copy-start | bytes 12292
  43.5 2.0 %collective-permute-start.4 = (f32[256,256]{1,0:T(8,128)S(1)}, f32[256,256]{1,0:T(8,128)S(1)}, u32[]{:S(2)}, u32[]{:S(2)}) collective-permute-start(f32[256,256]{1,0:T(8,128)S(1)} %get-tuple-element.21), channel_id=1, source_target_pairs={{0,1},{1,0},{2,3},{3,2},{4,5},{5,4},{6,7},{7,6},{8,9},{9,8},{10,11... | collective-permute-start | bytes 786440 | tf_op jit(solution)/shard_map/ppermute | solution.py:349
  43.6 1.9 %collective-permute-start.5 = (f32[256,256]{1,0:T(8,128)S(1)}, f32[256,256]{1,0:T(8,128)S(1)}, u32[]{:S(2)}, u32[]{:S(2)}) collective-permute-start(f32[256,256]{1,0:T(8,128)S(1)} %get-tuple-element.22), channel_id=1, source_target_pairs={{0,1},{1,0},{2,3},{3,2},{4,5},{5,4},{6,7},{7,6},{8,9},{9,8},{10,11... | collective-permute-start | bytes 786440 | tf_op jit(solution)/shard_map/ppermute | solution.py:349
  44.1 1.4 %collective-permute-start.6 = (f32[16,128]{1,0:T(8,128)S(1)}, f32[16,128]{1,0:T(8,128)S(1)}, u32[]{:S(2)}, u32[]{:S(2)}) collective-permute-start(f32[16,128]{1,0:T(8,128)S(1)} %get-tuple-element.23), channel_id=1, source_target_pairs={{0,1},{1,0},{2,3},{3,2},{4,5},{5,4},{6,7},{7,6},{8,9},{9,8},{10,11... | collective-permute-start | bytes 24584 | tf_op jit(solution)/shard_map/ppermute | solution.py:349
  45.5 1.5 %collective-permute-start.7 = (f32[256,256]{1,0:T(8,128)S(1)}, f32[256,256]{1,0:T(8,128)S(1)}, u32[]{:S(2)}, u32[]{:S(2)}) collective-permute-start(f32[256,256]{1,0:T(8,128)S(1)} %collective-permute-done.3.x_ref), channel_id=1, source_target_pairs={{0,1},{1,0},{2,3},{3,2},{4,5},{5,4},{6,7},{7,6},{8,9},{9,8},{10,11... | collective-permute-start | bytes 786440 | tf_op jit(solution)/shard_map/ppermute | solution.py:349

commit v18 on v17

--- a/solution.py
+++ b/solution.py
@@ -94,16 +94,25 @@
     return piece.reshape(blocks * local_times, size)
 
 
-def early_kernel(n, k, t_ref, x_ref, *refs):
+def early_kernel(n, k, skip, t_ref, x_ref, *refs):
     src = lax.bitwise_xor(lax.axis_index("space"), k)
     part = times_split(t_ref[src], x_ref[...])
-    refs[-1][...] = part if len(refs) == 1 else refs[0][...] + part
-
-
-def early(tables, n, k, piece, *before):
-    share = piece.shape[1]
+    if len(refs) == 1:
+        refs[0][...] = part
+        return
+    before_ref, out_ref = refs
+    end = skip + x_ref.shape[1]
+    out_ref[:, skip:end] = before_ref[:, skip:end] + part
+    if skip:
+        out_ref[:, :skip] = before_ref[:, :skip]
+    if end < out_ref.shape[1]:
+        out_ref[:, end:] = before_ref[:, end:]
+
+
+def early(tables, n, k, skip, piece, *before):
+    share = before[0].shape[1] if before else piece.shape[1]
     return pl.pallas_call(
-        functools.partial(early_kernel, n, k),
+        functools.partial(early_kernel, n, k, skip),
         out_shape=jax.ShapeDtypeStruct((tables.shape[1], share), jnp.float32),
         compiler_params=pltpu.CompilerParams(vmem_limit_bytes=16 * MIB),
         cost_estimate=SMALL,
@@ -132,12 +141,11 @@
 
 
 def first_part_kernel(
-    n, k, t_ref, sum_ref, x_ref, w_ref, own_ref, rest_ref, other_ref, later_ref, gram_ref, lent_ref
+    sum_ref, w_ref, own_ref, rest_ref, other_ref, later_ref, gram_ref, lent_ref
 ):
-    size = x_ref.shape[1]
+    size = own_ref.shape[1]
     me = lax.axis_index("freq")
-    src = lax.bitwise_xor(lax.axis_index("space"), k)
-    spectra = sum_ref[:, :size] + times_split(t_ref[src], x_ref[...])
+    spectra = sum_ref[:, :size]
     weights = weights_at(w_ref, me, sum_ref.shape[1], 0, size)
     rest = sum_ref[:, size:]
     half = spectra.shape[0] // 2
@@ -151,18 +159,17 @@
     lent_ref[...] = jnp.where(first, grams[1], grams[0])
 
 
-def first_part(tables, n, k, partial_sum, piece, weights):
+def first_part(size, partial_sum, weights):
     share = partial_sum.shape[1]
-    half = tables.shape[1] // 2
-    size = piece.shape[1]
+    half = partial_sum.shape[0] // 2
     gram = (NB, half // 2)
     shapes = [(half, size), (half, share - size), (half, size), (half, share - size), gram, gram]
     return pl.pallas_call(
-        functools.partial(first_part_kernel, n, k),
+        first_part_kernel,
         out_shape=[jax.ShapeDtypeStruct(shape, jnp.float32) for shape in shapes],
         compiler_params=pltpu.CompilerParams(vmem_limit_bytes=16 * MIB),
         cost_estimate=SMALL,
-    )(tables, partial_sum, piece, weights)
+    )(partial_sum, weights)
 
 
 def last_part_kernel(n, k, swapped, t_ref, sum_ref, x_ref, w_ref, *refs):
@@ -361,31 +368,30 @@
 
     last = n - 1
     early_rows = share // 2
-    parts = ((0, early_rows), (early_rows, share - early_rows))
     targets = n * tm_count
 
     def send(k, skip, size):
         sent = cut(snapshots, n, k, rows, skip, size)
         return partner(sent, "space", n, k)
 
-    offsets = [k for k in range(n - 1, 0, -1) if k != last]
-    pieces = [send(k, 0, share) for k in offsets]
-    last_pieces = [send(last, skip, size) for skip, size in parts]
-    before = early(tables, n, 0, cut(snapshots, n, 0, rows, 0, share))
-    for k, piece in zip(offsets, pieces):
-        before = early(tables, n, k, piece, before)
+    halves = ((0, early_rows), (early_rows, share - early_rows))
+    sends = [(last, *halves[0])]
+    sends += [(k, *half) for k in range(n - 2, 0, -1) for half in halves]
+    pieces = [(k, skip, send(k, skip, size)) for k, skip, size in sends]
+    last_piece = send(last, *halves[1])
+    before = early(tables, n, 0, 0, cut(snapshots, n, 0, rows, 0, share))
+    for k, skip, piece in pieces:
+        before = early(tables, n, k, skip, piece, before)
     weights = weights.reshape(1, rows)
-    own, rest, other, later, gram, lent = first_part(
-        tables, n, last, before, last_pieces[0], weights
-    )
+    own, rest, other, later, gram, lent = first_part(early_rows, before, weights)
     traded = [partner(part, "freq", freq_count, 1) for part in (other, later, lent)]
-    piece, (other, later, lent) = lax.optimization_barrier((last_pieces[1], traded))
+    piece, (other, later, lent) = lax.optimization_barrier((last_piece, traded))
     raw = partner(piece, "freq", freq_count, 1)
     *parts, gram = last_part(
         tables, n, last, 0, rest, piece, weights, gram, lent, own, other
     )
     *last_parts, gram = last_part(tables, n, last, targets, later, raw, weights, gram)
-    order = sorted(range(n), key=lambda z: abs(2 * z - n))
+    order = sorted(range(n), key=lambda z: abs(4 * z - (2 * n - 3)))
     order = [z * tm_count + x for z in order for x in range(tm_count - 1, -1, -1)]
     grams = lax.all_to_all(
         gram,

time: 65.8 us -> 65 us (0.988)
  blocking collectives: 15.5 us -> 9.51 us
  waiting for transfers between devices: 26.8 us -> 29.1 us
  Pallas kernels: 12 us -> 13.7 us
  starting transfers between devices: 10.3 us -> 11.5 us
    all_to_all x1, blocking collectives: 15.5 us -> 9.51 us  [on_device(): lax.all_to_all(gram, ('space', 'tm'), split_axis=0, concat_axis=0, axis_i...]
    ppermute x8 -> x10, waiting for transfers between devices: 26.8 us -> 29.1 us  [partner(): return lax.ppermute(value, axis, [(i, i ^ step) for i in range(size)])]
    pallas_call x5 -> x7, Pallas kernels: 5.5 us -> 7 us  [cut(): pl.pallas_call(functools.partial(cut_kernel, n, k, rows, skip), out_shape...]
    ppermute x8 -> x10, starting transfers between devices: 10.3 us -> 11.5 us  [partner(): return lax.ppermute(value, axis, [(i, i ^ step) for i in range(size)])]
    pallas_call x4 -> x7, Pallas kernels: 2.87 us -> 3 us  [the longest x6 2.43 us: early(): pl.pallas_call(functools.partial(early_kernel, n, k, skip), out_shape=jax...]
  transfers between devices with their start and end apart: 8 -> 10, of which waited for: 4 -> 4; matrix products, arithmetic and copies ran while one was open for 0% -> 0% of each run, Pallas kernels for 12% -> 15%
where the time goes in v18:
time: 65 us; the launch traced here: 64.6 us
  waiting for transfers between devices  29.1 us (45%)
  Pallas kernels  13.7 us (21%)
  starting transfers between devices  11.5 us (18%)
  blocking collectives  9.51 us (15%)
  between operations  0.84 us (1%)
    ppermute x10, waiting for transfers between devices, partner(): return lax.ppermute(value, axis, [(i, i ^ step) for i in range(size)])  29.1 us
    ppermute x10, starting transfers between devices, partner(): return lax.ppermute(value, axis, [(i, i ^ step) for i in range(size)])  11.5 us
    all_to_all x1, blocking collectives, on_device(): lax.all_to_all(gram, ('space', 'tm'), split_axis=0, concat_axis=0, axis_i...  9.51 us
    pallas_call x7, Pallas kernels, cut(): pl.pallas_call(functools.partial(cut_kernel, n, k, rows, skip), out_shape...  7 us
    pallas_call x6, Pallas kernels, early(): pl.pallas_call(functools.partial(early_kernel, n, k, skip), out_shape=jax...  2.43 us
    pallas_call x1, Pallas kernels, finish(): pl.pallas_call(functools.partial(finish_kernel, total), out_shape=(jax.Sh...  2.19 us
    pallas_call x2, Pallas kernels, last_part(): pl.pallas_call(functools.partial(last_part_kernel, n, k, bool(copies)), o...  1.49 us
  transfers between devices with their start and end apart: 10, of which 4 were waited for; matrix products, arithmetic and copies ran while one was open for 0% of the time, Pallas kernels for 15%

profile of v18, /device:TPU:0, one launch (start us, length us, event | category | flops | bytes accessed | tf_op | source)
XLA Modules:
  0.0 64.6 jit_solution(14019629315957116499)
XLA Ops:
  0.6 1.0 %shard_map.54 = f32[16,16,256]{2,1,0:T(8,128)S(1)} custom-call(f32[16,16,4096]{2,1,0:T(8,128)} %x_ref.13), custom_call_target="tpu_custom_call" | custom-call | flops 1 | bytes 1 | tf_op jit(solution)/shard_map/pallas_call | solution.py:81
  1.6 5.1 %collective-permute-start.4 = (f32[256,256]{1,0:T(8,128)S(1)}, f32[256,256]{1,0:T(8,128)S(1)}, u32[]{:S(2)}, u32[]{:S(2)}) collective-permute-start(f32[256,256]{1,0:T(8,128)S(1)} %bitcast.14), channel_id=1, source_target_pairs={{0,12},{4,8},{8,4},{12,0},{1,13},{5,9},{9,5},{13,1},{2,14},{6,10},... | collective-permute-start | bytes 786440 | tf_op jit(solution)/shard_map/ppermute | solution.py:356
  6.7 1.0 %shard_map.53 = f32[16,16,256]{2,1,0:T(8,128)S(1)} custom-call(f32[16,16,4096]{2,1,0:T(8,128)} %x_ref.13), custom_call_target="tpu_custom_call" | custom-call | flops 1 | bytes 1 | tf_op jit(solution)/shard_map/pallas_call | solution.py:81
  7.7 0.1 collective-permute-start.3
  7.8 1.0 %shard_map.52 = f32[16,16,256]{2,1,0:T(8,128)S(1)} custom-call(f32[16,16,4096]{2,1,0:T(8,128)} %x_ref.13), custom_call_target="tpu_custom_call" | custom-call | flops 1 | bytes 1 | tf_op jit(solution)/shard_map/pallas_call | solution.py:81
  8.8 3.0 %collective-permute-start.2 = (f32[256,256]{1,0:T(8,128)S(1)}, f32[256,256]{1,0:T(8,128)S(1)}, u32[]{:S(2)}, u32[]{:S(2)}) collective-permute-start(f32[256,256]{1,0:T(8,128)S(1)} %bitcast.12), channel_id=1, source_target_pairs={{0,8},{4,12},{8,0},{12,4},{1,9},{5,13},{9,1},{13,5},{2,10},{6,14},... | collective-permute-start | bytes 786440 | tf_op jit(solution)/shard_map/ppermute | solution.py:356
  11.7 1.0 %shard_map.51 = f32[16,16,256]{2,1,0:T(8,128)S(1)} custom-call(f32[16,16,4096]{2,1,0:T(8,128)} %x_ref.13), custom_call_target="tpu_custom_call" | custom-call | flops 1 | bytes 1 | tf_op jit(solution)/shard_map/pallas_call | solution.py:81
  12.7 0.1 collective-permute-start.1
  12.8 1.0 %shard_map.50 = f32[16,16,256]{2,1,0:T(8,128)S(1)} custom-call(f32[16,16,4096]{2,1,0:T(8,128)} %x_ref.13), custom_call_target="tpu_custom_call" | custom-call | flops 1 | bytes 1 | tf_op jit(solution)/shard_map/pallas_call | solution.py:81
  13.8 2.1 %collective-permute-start = (f32[256,256]{1,0:T(8,128)S(1)}, f32[256,256]{1,0:T(8,128)S(1)}, u32[]{:S(2)}, u32[]{:S(2)}) collective-permute-start(f32[256,256]{1,0:T(8,128)S(1)} %bitcast.10), channel_id=1, source_target_pairs={{0,4},{4,0},{8,12},{12,8},{1,5},{5,1},{9,13},{13,9},{2,6},{6,2},{1... | collective-permute-start | bytes 786440 | tf_op jit(solution)/shard_map/ppermute | solution.py:356
  15.9 1.1 %shard_map.55 = f32[16,16,512]{2,1,0:T(8,128)S(1)} custom-call(f32[16,16,4096]{2,1,0:T(8,128)} %x_ref.13), custom_call_target="tpu_custom_call" | custom-call | flops 1 | bytes 1 | tf_op jit(solution)/shard_map/pallas_call | solution.py:81
  17.0 1.0 %shard_map.63 = f32[16,16,256]{2,1,0:T(8,128)S(1)} custom-call(f32[16,16,4096]{2,1,0:T(8,128)} %x_ref.13), custom_call_target="tpu_custom_call" | custom-call | flops 1 | bytes 1 | tf_op jit(solution)/shard_map/pallas_call | solution.py:81
  18.0 0.6 shard_map.56.refs_0_
  18.6 0.4 collective-permute-start.5
  19.0 0.4 shard_map.57.refs_0_
  19.4 17.1 %collective-permute-done.3.x_ref = f32[256,256]{1,0:T(8,128)S(1)} collective-permute-done((f32[256,256]{1,0:T(8,128)S(1)}, f32[256,256]{1,0:T(8,128)S(1)}, u32[]{:S(2)}, u32[]{:S(2)}) %collective-permute-start.3) | collective-permute-done | bytes 262176 | tf_op jit(solution)/shard_map/ppermute | solution.py:356
  36.5 0.4 shard_map.58.refs_0_
  36.8 10.0 %collective-permute-done.2.x_ref = f32[256,256]{1,0:T(8,128)S(1)} collective-permute-done((f32[256,256]{1,0:T(8,128)S(1)}, f32[256,256]{1,0:T(8,128)S(1)}, u32[]{:S(2)}, u32[]{:S(2)}) %collective-permute-start.2) | collective-permute-done | bytes 262176 | tf_op jit(solution)/shard_map/ppermute | solution.py:356
  46.9 0.4 shard_map.59.refs_0_
  47.3 0.4 shard_map.60.refs_0_
  47.6 0.4 shard_map.61.sum_ref
  48.0 0.6 shard_map.62
  48.6 0.1 collective-permute-start.6
  48.7 0.5 collective-permute-start.7
  49.2 0.1 collective-permute-start.8
  49.3 1.3 %collective-permute-done.8.refs_1_ = f32[16,128]{1,0:T(8,128)S(1)} collective-permute-done((f32[16,128]{1,0:T(8,128)S(1)}, f32[16,128]{1,0:T(8,128)S(1)}, u32[]{:S(2)}, u32[]{:S(2)}) %collective-permute-start.8) | collective-permute-done | bytes 8224 | tf_op jit(solution)/shard_map/ppermute | solution.py:356
  50.6 0.1 collective-permute-start.9
  50.7 0.8 %shard_map.64 = (bf16[256,512]{1,0:T(8,128)(2,1)S(1)}, bf16[256,512]{1,0:T(8,128)(2,1)S(1)}, bf16[256,256]{1,0:T(8,128)(2,1)S(1)}, bf16[256,256]{1,0:T(8,128)(2,1)S(1)}, f32[16,128]{1,0:T(8,128)S(1)}) custom-call(bf16[4,512,768]{2,1,0:T(8,128)(2,1)S(1)} %copy-done, f32[256,256]{1,0:T(8,128)S(1)} %get-tuple-element.20.sum_ref, ...), custom_call_target="tpu_custom_call" | custom-call | flops 1 | bytes 1 | tf_op jit(solution)/shard_map/pallas_call | solution.py:207
  51.5 0.6 collective-permute-done.9.x_ref
  52.1 0.7 %shard_map.65 = (bf16[256,256]{1,0:T(8,128)(2,1)S(1)}, bf16[256,256]{1,0:T(8,128)(2,1)S(1)}, f32[8,16,128]{2,1,0:T(8,128)S(1)}) custom-call(bf16[4,512,768]{2,1,0:T(8,128)(2,1)S(1)} %copy-done, f32[256,256]{1,0:T(8,128)S(1)} %collective-permute-done.7.sum_ref, f32[256,256]{1,0:T(8,128)S(1)} %collective-permute-done.9.x_ref, f32[1,1024]{1,0:T(1,128)S(1)} %bitcast.17, ...), custom_call_target="tpu_custom_call" | custom-call | flops 1 | bytes 1 | tf_op jit(solution)/shard_map/pallas_call | solution.py:207
  52.9 9.5 %all_to_all.5.grams_ref = f32[8,16,128]{2,1,0:T(8,128)S(1)} all-to-all(f32[8,16,128]{2,1,0:T(8,128)S(1)} %get-tuple-element.37), channel_id=1, replica_groups={{6,4,10,8,2,0,14,12},{7,5,11,9,3,1,15,13},{22,20,26,24,18,16,30,28},{23..., dimensions={0} | all-to-all | bytes 131072 | tf_op jit(solution)/shard_map/all_to_all | solution.py:396
  62.4 2.2 %shard_map.66 = (f32[8,2,16,1024]{3,2,1,0:T(8,128)}, f32[2,8,16,16]{3,2,1,0:T(8,128)}) custom-call(bf16[256,512]{1,0:T(8,128)(2,1)S(1)} %get-tuple-element.29.own_high_ref, bf16[256,512]{1,0:T(8,128)(2,1)S(1)} %get-tuple-element.30.own_low_ref, bf16[256,256]{1,0:T(8,128)(2,1)S(1)} %get-tuple-element.31.first_high_ref, ...), custom_call_target="tpu_custom_call" | custom-call | tf_op jit(solution)/shard_map/pallas_call | solution.py:345
  (10 shorter events, 0.0 us)
Async XLA Ops:
  1.6 17.0 %collective-permute-start.4 = (f32[256,256]{1,0:T(8,128)S(1)}, f32[256,256]{1,0:T(8,128)S(1)}, u32[]{:S(2)}, u32[]{:S(2)}) collective-permute-start(f32[256,256]{1,0:T(8,128)S(1)} %bitcast.14), channel_id=1, source_target_pairs={{0,12},{4,8},{8,4},{12,0},{1,13},{5,9},{9,5},{13,1},{2,14},{6,10},... | collective-permute-start | bytes 786440 | tf_op jit(solution)/shard_map/ppermute | solution.py:356
  7.7 28.8 %collective-permute-start.3 = (f32[256,256]{1,0:T(8,128)S(1)}, f32[256,256]{1,0:T(8,128)S(1)}, u32[]{:S(2)}, u32[]{:S(2)}) collective-permute-start(f32[256,256]{1,0:T(8,128)S(1)} %bitcast.13), channel_id=1, source_target_pairs={{0,8},{4,12},{8,0},{12,4},{1,9},{5,13},{9,1},{13,5},{2,10},{6,14},... | collective-permute-start | bytes 786440 | tf_op jit(solution)/shard_map/ppermute | solution.py:356
  8.8 38.1 %collective-permute-start.2 = (f32[256,256]{1,0:T(8,128)S(1)}, f32[256,256]{1,0:T(8,128)S(1)}, u32[]{:S(2)}, u32[]{:S(2)}) collective-permute-start(f32[256,256]{1,0:T(8,128)S(1)} %bitcast.12), channel_id=1, source_target_pairs={{0,8},{4,12},{8,0},{12,4},{1,9},{5,13},{9,1},{13,5},{2,10},{6,14},... | collective-permute-start | bytes 786440 | tf_op jit(solution)/shard_map/ppermute | solution.py:356
  12.7 34.5 %collective-permute-start.1 = (f32[256,256]{1,0:T(8,128)S(1)}, f32[256,256]{1,0:T(8,128)S(1)}, u32[]{:S(2)}, u32[]{:S(2)}) collective-permute-start(f32[256,256]{1,0:T(8,128)S(1)} %bitcast.11), channel_id=1, source_target_pairs={{0,4},{4,0},{8,12},{12,8},{1,5},{5,1},{9,13},{13,9},{2,6},{6,2},{1... | collective-permute-start | bytes 786440 | tf_op jit(solution)/shard_map/ppermute | solution.py:356
  13.8 4.2 %copy-start = (bf16[4,512,768]{2,1,0:T(8,128)(2,1)S(1)}, bf16[4,512,768]{2,1,0:T(8,128)(2,1)}, u32[]{:S(2)}) copy-start(bf16[4,512,768]{2,1,0:T(8,128)(2,1)} %constant.2.clone.t_ref) | copy-start | bytes 9437188
  13.8 33.8 %collective-permute-start = (f32[256,256]{1,0:T(8,128)S(1)}, f32[256,256]{1,0:T(8,128)S(1)}, u32[]{:S(2)}, u32[]{:S(2)}) collective-permute-start(f32[256,256]{1,0:T(8,128)S(1)} %bitcast.10), channel_id=1, source_target_pairs={{0,4},{4,0},{8,12},{12,8},{1,5},{5,1},{9,13},{13,9},{2,6},{6,2},{1... | collective-permute-start | bytes 786440 | tf_op jit(solution)/shard_map/ppermute | solution.py:356
  18.6 30.7 %collective-permute-start.5 = (f32[256,256]{1,0:T(8,128)S(1)}, f32[256,256]{1,0:T(8,128)S(1)}, u32[]{:S(2)}, u32[]{:S(2)}) collective-permute-start(f32[256,256]{1,0:T(8,128)S(1)} %bitcast.9), channel_id=1, source_target_pairs={{0,12},{4,8},{8,4},{12,0},{1,13},{5,9},{9,5},{13,1},{2,14},{6,10},... | collective-permute-start | bytes 786440 | tf_op jit(solution)/shard_map/ppermute | solution.py:356
  47.2 0.8 %copy-start.1 = (f32[1024]{0:T(1024)S(1)}, f32[1024]{0:T(1024)}, u32[]{:S(2)}) copy-start(f32[1024]{0:T(1024)} %param.4) | copy-start | bytes 12292
  48.6 2.0 %collective-permute-start.6 = (f32[256,256]{1,0:T(8,128)S(1)}, f32[256,256]{1,0:T(8,128)S(1)}, u32[]{:S(2)}, u32[]{:S(2)}) collective-permute-start(f32[256,256]{1,0:T(8,128)S(1)} %get-tuple-element.21), channel_id=1, source_target_pairs={{0,1},{1,0},{2,3},{3,2},{4,5},{5,4},{6,7},{7,6},{8,9},{9,8},{10,11... | collective-permute-start | bytes 786440 | tf_op jit(solution)/shard_map/ppermute | solution.py:356
  48.7 1.9 %collective-permute-start.7 = (f32[256,256]{1,0:T(8,128)S(1)}, f32[256,256]{1,0:T(8,128)S(1)}, u32[]{:S(2)}, u32[]{:S(2)}) collective-permute-start(f32[256,256]{1,0:T(8,128)S(1)} %get-tuple-element.22), channel_id=1, source_target_pairs={{0,1},{1,0},{2,3},{3,2},{4,5},{5,4},{6,7},{7,6},{8,9},{9,8},{10,11... | collective-permute-start | bytes 786440 | tf_op jit(solution)/shard_map/ppermute | solution.py:356
  49.2 1.4 %collective-permute-start.8 = (f32[16,128]{1,0:T(8,128)S(1)}, f32[16,128]{1,0:T(8,128)S(1)}, u32[]{:S(2)}, u32[]{:S(2)}) collective-permute-start(f32[16,128]{1,0:T(8,128)S(1)} %get-tuple-element.23), channel_id=1, source_target_pairs={{0,1},{1,0},{2,3},{3,2},{4,5},{5,4},{6,7},{7,6},{8,9},{9,8},{10,11... | collective-permute-start | bytes 24584 | tf_op jit(solution)/shard_map/ppermute | solution.py:356
  50.6 1.5 %collective-permute-start.9 = (f32[256,256]{1,0:T(8,128)S(1)}, f32[256,256]{1,0:T(8,128)S(1)}, u32[]{:S(2)}, u32[]{:S(2)}) collective-permute-start(f32[256,256]{1,0:T(8,128)S(1)} %collective-permute-done.5.x_ref), channel_id=1, source_target_pairs={{0,1},{1,0},{2,3},{3,2},{4,5},{5,4},{6,7},{7,6},{8,9},{9,8},{10,11... | collective-permute-start | bytes 786440 | tf_op jit(solution)/shard_map/ppermute | solution.py:356

commit v19 on v18

--- a/solution.py
+++ b/solution.py
@@ -12,6 +12,7 @@
 SEGMENT_FRAMES = 64
 NF = 16
 CUTS = 4
+TRADED = 128
 epsilon = 1e-05
 MIB = 1024 * 1024
 SMALL = pl.CostEstimate(flops=1, transcendentals=0, bytes_accessed=1)
@@ -140,20 +141,20 @@
     return w_ref[:, pl.ds(pl.multiple_of(place * share + skip, 128), size)]
 
 
-def first_part_kernel(
-    sum_ref, w_ref, own_ref, rest_ref, other_ref, later_ref, gram_ref, lent_ref
-):
+def first_part_kernel(sum_ref, w_ref, own_ref, rest_ref, gram_ref, lent_ref, *traded_refs):
     size = own_ref.shape[1]
     me = lax.axis_index("freq")
-    spectra = sum_ref[:, :size]
+    total = sum_ref[...]
+    spectra = total[:, :size]
     weights = weights_at(w_ref, me, sum_ref.shape[1], 0, size)
-    rest = sum_ref[:, size:]
-    half = spectra.shape[0] // 2
+    half = total.shape[0] // 2
     first = me == 0
-    own_ref[...] = jnp.where(first, spectra[:half], spectra[half:])
-    other_ref[...] = jnp.where(first, spectra[half:], spectra[:half])
-    rest_ref[...] = jnp.where(first, rest[:half], rest[half:])
-    later_ref[...] = jnp.where(first, rest[half:], rest[:half])
+    mine = jnp.where(first, total[:half], total[half:])
+    own_ref[...] = mine[:, :size]
+    rest_ref[...] = mine[:, size:]
+    other = jnp.where(first, total[half:], total[:half])
+    for i, ref in enumerate(traded_refs):
+        ref[...] = other[:, i * TRADED : (i + 1) * TRADED]
     grams = [gram_of(z, weights) for z in (spectra[:half], spectra[half:])]
     gram_ref[...] = jnp.where(first, grams[0], grams[1])
     lent_ref[...] = jnp.where(first, grams[1], grams[0])
@@ -163,7 +164,8 @@
     share = partial_sum.shape[1]
     half = partial_sum.shape[0] // 2
     gram = (NB, half // 2)
-    shapes = [(half, size), (half, share - size), (half, size), (half, share - size), gram, gram]
+    shapes = [(half, size), (half, share - size), gram, gram]
+    shapes += [(half, TRADED)] * (share // TRADED)
     return pl.pallas_call(
         first_part_kernel,
         out_shape=[jax.ShapeDtypeStruct(shape, jnp.float32) for shape in shapes],
@@ -183,18 +185,19 @@
     place = 1 - me if swapped else me
     gram = gram_of(spectra, weights_at(w_ref, place, share, skip, size))
     if swapped:
-        before_ref, high_ref, low_ref, gram_ref = refs
-        gram = gram + before_ref[...]
+        before_ref, lent_ref, high_ref, low_ref, gram_ref = refs
+        gram = gram + before_ref[...] + lent_ref[...]
         high_ref[...], low_ref[...] = split(spectra)
         for d in range(gram_ref.shape[0]):
             gram_ref[d] = gram
         return
-    gram_own_ref, gram_lent_ref, own_ref, other_ref, *refs = refs
-    high_ref, low_ref, other_high_ref, other_low_ref, gram_ref = refs
-    gram_ref[...] = gram + gram_own_ref[...] + gram_lent_ref[...]
+    before_ref, own_ref, *other_refs = refs[:-5]
+    high_ref, low_ref, other_high_ref, other_low_ref, gram_ref = refs[-5:]
+    gram_ref[...] = gram + before_ref[...]
     high_ref[:, :skip], low_ref[:, :skip] = split(own_ref[...])
     high_ref[:, skip:], low_ref[:, skip:] = split(spectra)
-    other_high_ref[...], other_low_ref[...] = split(other_ref[...])
+    other = jnp.concatenate([ref[...] for ref in other_refs], axis=1)
+    other_high_ref[...], other_low_ref[...] = split(other)
 
 
 def last_part(tables, n, k, copies, partial_sum, piece, weights, *before):
@@ -367,30 +370,29 @@
     tables = jnp.asarray(dft_blocks(n))
 
     last = n - 1
-    early_rows = share // 2
+    early_rows = share - TRADED
     targets = n * tm_count
 
     def send(k, skip, size):
         sent = cut(snapshots, n, k, rows, skip, size)
         return partner(sent, "space", n, k)
 
-    halves = ((0, early_rows), (early_rows, share - early_rows))
-    sends = [(last, *halves[0])]
-    sends += [(k, *half) for k in range(n - 2, 0, -1) for half in halves]
+    half = share // 2
+    sends = [(last, 0, early_rows)]
+    sends += [(k, skip, half) for k in range(n - 2, 0, -1) for skip in (0, half)]
     pieces = [(k, skip, send(k, skip, size)) for k, skip, size in sends]
-    last_piece = send(last, *halves[1])
+    last_piece = send(last, early_rows, share - early_rows)
     before = early(tables, n, 0, 0, cut(snapshots, n, 0, rows, 0, share))
     for k, skip, piece in pieces:
         before = early(tables, n, k, skip, piece, before)
     weights = weights.reshape(1, rows)
-    own, rest, other, later, gram, lent = first_part(early_rows, before, weights)
-    traded = [partner(part, "freq", freq_count, 1) for part in (other, later, lent)]
-    piece, (other, later, lent) = lax.optimization_barrier((last_piece, traded))
+    own, rest, gram, lent, *traded = first_part(early_rows, before, weights)
+    lent = partner(lent, "freq", freq_count, 1)
+    traded = [partner(part, "freq", freq_count, 1) for part in traded]
+    piece, (*others, later) = lax.optimization_barrier((last_piece, traded))
     raw = partner(piece, "freq", freq_count, 1)
-    *parts, gram = last_part(
-        tables, n, last, 0, rest, piece, weights, gram, lent, own, other
-    )
-    *last_parts, gram = last_part(tables, n, last, targets, later, raw, weights, gram)
+    *parts, gram = last_part(tables, n, last, 0, rest, piece, weights, gram, own, *others)
+    *last_parts, gram = last_part(tables, n, last, targets, later, raw, weights, gram, lent)
     order = sorted(range(n), key=lambda z: abs(4 * z - (2 * n - 3)))
     order = [z * tm_count + x for z in order for x in range(tm_count - 1, -1, -1)]
     grams = lax.all_to_all(

time: 65 us -> 68.2 us (1.049)
  starting transfers between devices: 11.5 us -> 14 us
    ppermute x10 -> x12, starting transfers between devices: 11.5 us -> 14 us  [partner(): return lax.ppermute(value, axis, [(i, i ^ step) for i in range(size)])]
    ppermute x10 -> x12, waiting for transfers between devices: 29.1 us -> 29.3 us  [partner(): return lax.ppermute(value, axis, [(i, i ^ step) for i in range(size)])]
  transfers between devices with their start and end apart: 10 -> 12, of which waited for: 4 -> 7; matrix products, arithmetic and copies ran while one was open for 0% -> 0% of each run, Pallas kernels for 15% -> 15%
where the time goes in v19:
time: 68.2 us; the launch traced here: 67.7 us
  waiting for transfers between devices  29.3 us (43%)
  Pallas kernels  14.1 us (21%)
  starting transfers between devices  14 us (21%)
  blocking collectives  9.51 us (14%)
  between operations  0.84 us (1%)
    ppermute x12, waiting for transfers between devices, partner(): return lax.ppermute(value, axis, [(i, i ^ step) for i in range(size)])  29.3 us
    ppermute x12, starting transfers between devices, partner(): return lax.ppermute(value, axis, [(i, i ^ step) for i in range(size)])  14 us
    all_to_all x1, blocking collectives, on_device(): lax.all_to_all(gram, ('space', 'tm'), split_axis=0, concat_axis=0, axis_i...  9.51 us
    pallas_call x7, Pallas kernels, cut(): pl.pallas_call(functools.partial(cut_kernel, n, k, rows, skip), out_shape...  6.97 us
    pallas_call x6, Pallas kernels, early(): pl.pallas_call(functools.partial(early_kernel, n, k, skip), out_shape=jax...  2.63 us
    pallas_call x1, Pallas kernels, finish(): pl.pallas_call(functools.partial(finish_kernel, total), out_shape=(jax.Sh...  2.18 us
    pallas_call x2, Pallas kernels, last_part(): pl.pallas_call(functools.partial(last_part_kernel, n, k, bool(copies)), o...  1.47 us
  transfers between devices with their start and end apart: 12, of which 7 were waited for; matrix products, arithmetic and copies ran while one was open for 0% of the time, Pallas kernels for 15%

profile of v19, /device:TPU:0, one launch (start us, length us, event | category | flops | bytes accessed | tf_op | source)
XLA Modules:
  0.0 67.7 jit_solution(979253492680078630)
XLA Ops:
  0.6 1.1 %shard_map.54 = f32[16,16,384]{2,1,0:T(8,128)S(1)} custom-call(f32[16,16,4096]{2,1,0:T(8,128)} %x_ref.13), custom_call_target="tpu_custom_call" | custom-call | flops 1 | bytes 1 | tf_op jit(solution)/shard_map/pallas_call | solution.py:82
  1.7 5.1 %collective-permute-start.4 = (f32[256,384]{1,0:T(8,128)S(1)}, f32[256,384]{1,0:T(8,128)S(1)}, u32[]{:S(2)}, u32[]{:S(2)}) collective-permute-start(f32[256,384]{1,0:T(8,128)S(1)} %bitcast.9), channel_id=1, source_target_pairs={{0,12},{4,8},{8,4},{12,0},{1,13},{5,9},{9,5},{13,1},{2,14},{6,10},... | collective-permute-start | bytes 1179656 | tf_op jit(solution)/shard_map/ppermute | solution.py:359
  6.8 1.0 %shard_map.53 = f32[16,16,256]{2,1,0:T(8,128)S(1)} custom-call(f32[16,16,4096]{2,1,0:T(8,128)} %x_ref.13), custom_call_target="tpu_custom_call" | custom-call | flops 1 | bytes 1 | tf_op jit(solution)/shard_map/pallas_call | solution.py:82
  7.9 1.0 %shard_map.52 = f32[16,16,256]{2,1,0:T(8,128)S(1)} custom-call(f32[16,16,4096]{2,1,0:T(8,128)} %x_ref.13), custom_call_target="tpu_custom_call" | custom-call | flops 1 | bytes 1 | tf_op jit(solution)/shard_map/pallas_call | solution.py:82
  8.9 3.0 %collective-permute-start.2 = (f32[256,256]{1,0:T(8,128)S(1)}, f32[256,256]{1,0:T(8,128)S(1)}, u32[]{:S(2)}, u32[]{:S(2)}) collective-permute-start(f32[256,256]{1,0:T(8,128)S(1)} %bitcast.12), channel_id=1, source_target_pairs={{0,8},{4,12},{8,0},{12,4},{1,9},{5,13},{9,1},{13,5},{2,10},{6,14},... | collective-permute-start | bytes 786440 | tf_op jit(solution)/shard_map/ppermute | solution.py:359
  11.8 1.0 %shard_map.51 = f32[16,16,256]{2,1,0:T(8,128)S(1)} custom-call(f32[16,16,4096]{2,1,0:T(8,128)} %x_ref.13), custom_call_target="tpu_custom_call" | custom-call | flops 1 | bytes 1 | tf_op jit(solution)/shard_map/pallas_call | solution.py:82
  12.9 1.0 %shard_map.50 = f32[16,16,256]{2,1,0:T(8,128)S(1)} custom-call(f32[16,16,4096]{2,1,0:T(8,128)} %x_ref.13), custom_call_target="tpu_custom_call" | custom-call | flops 1 | bytes 1 | tf_op jit(solution)/shard_map/pallas_call | solution.py:82
  13.9 2.1 %collective-permute-start = (f32[256,256]{1,0:T(8,128)S(1)}, f32[256,256]{1,0:T(8,128)S(1)}, u32[]{:S(2)}, u32[]{:S(2)}) collective-permute-start(f32[256,256]{1,0:T(8,128)S(1)} %bitcast.10), channel_id=1, source_target_pairs={{0,4},{4,0},{8,12},{12,8},{1,5},{5,1},{9,13},{13,9},{2,6},{6,2},{1... | collective-permute-start | bytes 786440 | tf_op jit(solution)/shard_map/ppermute | solution.py:359
  16.0 1.1 %shard_map.55 = f32[16,16,512]{2,1,0:T(8,128)S(1)} custom-call(f32[16,16,4096]{2,1,0:T(8,128)} %x_ref.13), custom_call_target="tpu_custom_call" | custom-call | flops 1 | bytes 1 | tf_op jit(solution)/shard_map/pallas_call | solution.py:82
  17.1 0.9 %shard_map.63 = f32[16,16,128]{2,1,0:T(8,128)S(1)} custom-call(f32[16,16,4096]{2,1,0:T(8,128)} %x_ref.13), custom_call_target="tpu_custom_call" | custom-call | flops 1 | bytes 1 | tf_op jit(solution)/shard_map/pallas_call | solution.py:82
  18.0 0.6 shard_map.56.refs_0_
  18.6 2.2 %collective-permute-start.5 = (f32[256,128]{1,0:T(8,128)S(1)}, f32[256,128]{1,0:T(8,128)S(1)}, u32[]{:S(2)}, u32[]{:S(2)}) collective-permute-start(f32[256,128]{1,0:T(8,128)S(1)} %bitcast.14), channel_id=1, source_target_pairs={{0,12},{4,8},{8,4},{12,0},{1,13},{5,9},{9,5},{13,1},{2,14},{6,10},... | collective-permute-start | bytes 393224 | tf_op jit(solution)/shard_map/ppermute | solution.py:359
  20.7 0.6 shard_map.57.refs_0_
  21.3 22.8 %collective-permute-done.3.x_ref = f32[256,256]{1,0:T(8,128)S(1)} collective-permute-done((f32[256,256]{1,0:T(8,128)S(1)}, f32[256,256]{1,0:T(8,128)S(1)}, u32[]{:S(2)}, u32[]{:S(2)}) %collective-permute-start.3) | collective-permute-done | bytes 262176 | tf_op jit(solution)/shard_map/ppermute | solution.py:359
  44.1 0.4 shard_map.58.refs_0_
  44.5 5.2 %collective-permute-done.2.x_ref = f32[256,256]{1,0:T(8,128)S(1)} collective-permute-done((f32[256,256]{1,0:T(8,128)S(1)}, f32[256,256]{1,0:T(8,128)S(1)}, u32[]{:S(2)}, u32[]{:S(2)}) %collective-permute-start.2) | collective-permute-done | bytes 262176 | tf_op jit(solution)/shard_map/ppermute | solution.py:359
  49.8 0.4 shard_map.59.refs_0_
  50.2 0.4 shard_map.60.refs_0_
  50.6 0.4 shard_map.61.sum_ref
  50.9 0.8 %shard_map.62 = (f32[256,384]{1,0:T(8,128)S(1)}, f32[256,128]{1,0:T(8,128)S(1)}, f32[16,128]{1,0:T(8,128)S(1)}, f32[16,128]{1,0:T(8,128)S(1)}, f32[256,128]{1,0:...) custom-call(f32[512,512]{1,0:T(8,128)S(1)} %shard_map.61.sum_ref, ...), custom_call_target="tpu_custom_call" | custom-call | flops 1 | bytes 1 | tf_op jit(solution)/shard_map/pallas_call | solution.py:169
  51.9 0.5 collective-permute-start.7
  52.4 0.4 collective-permute-start.9
  52.9 0.3 collective-permute-done.6.refs_2_
  53.2 0.2 collective-permute-done.7.refs_3_
  53.4 0.3 collective-permute-done.8.refs_4_
  53.7 0.2 collective-permute-done.9.sum_ref
  53.9 0.3 collective-permute-start.10
  54.2 0.2 collective-permute-start.11
  54.4 0.8 %shard_map.64 = (bf16[256,512]{1,0:T(8,128)(2,1)S(1)}, bf16[256,512]{1,0:T(8,128)(2,1)S(1)}, bf16[256,384]{1,0:T(8,128)(2,1)S(1)}, bf16[256,384]{1,0:T(8,128)(2,1)S(1)}, f32[16,128]{1,0:T(8,128)S(1)}) custom-call(bf16[4,512,768]{2,1,0:T(8,128)(2,1)S(1)} %copy-done, f32[256,128]{1,0:T(8,128)S(1)} %get-tuple-element.23.sum_ref, ...), custom_call_target="tpu_custom_call" | custom-call | flops 1 | bytes 1 | tf_op jit(solution)/shard_map/pallas_call | solution.py:210
  55.4 0.7 shard_map.65
  56.1 9.5 %all_to_all.5.grams_ref = f32[8,16,128]{2,1,0:T(8,128)S(1)} all-to-all(f32[8,16,128]{2,1,0:T(8,128)S(1)} %get-tuple-element.43), channel_id=1, replica_groups={{6,4,10,8,2,0,14,12},{7,5,11,9,3,1,15,13},{22,20,26,24,18,16,30,28},{23..., dimensions={0} | all-to-all | bytes 131072 | tf_op jit(solution)/shard_map/all_to_all | solution.py:398
  65.6 2.2 %shard_map.66 = (f32[8,2,16,1024]{3,2,1,0:T(8,128)}, f32[2,8,16,16]{3,2,1,0:T(8,128)}) custom-call(bf16[256,512]{1,0:T(8,128)(2,1)S(1)} %get-tuple-element.34.own_high_ref, bf16[256,512]{1,0:T(8,128)(2,1)S(1)} %get-tuple-element.35.own_low_ref, bf16[256,384]{1,0:T(8,128)(2,1)S(1)} %get-tuple-element.36.first_high_ref, ...), custom_call_target="tpu_custom_call" | custom-call | tf_op jit(solution)/shard_map/pallas_call | solution.py:348
  (14 shorter events, 0.5 us)
Async XLA Ops:
  1.7 16.8 %collective-permute-start.4 = (f32[256,384]{1,0:T(8,128)S(1)}, f32[256,384]{1,0:T(8,128)S(1)}, u32[]{:S(2)}, u32[]{:S(2)}) collective-permute-start(f32[256,384]{1,0:T(8,128)S(1)} %bitcast.9), channel_id=1, source_target_pairs={{0,12},{4,8},{8,4},{12,0},{1,13},{5,9},{9,5},{13,1},{2,14},{6,10},... | collective-permute-start | bytes 1179656 | tf_op jit(solution)/shard_map/ppermute | solution.py:359
  7.8 36.3 %collective-permute-start.3 = (f32[256,256]{1,0:T(8,128)S(1)}, f32[256,256]{1,0:T(8,128)S(1)}, u32[]{:S(2)}, u32[]{:S(2)}) collective-permute-start(f32[256,256]{1,0:T(8,128)S(1)} %bitcast.13), channel_id=1, source_target_pairs={{0,8},{4,12},{8,0},{12,4},{1,9},{5,13},{9,1},{13,5},{2,10},{6,14},... | collective-permute-start | bytes 786440 | tf_op jit(solution)/shard_map/ppermute | solution.py:359
  8.9 40.9 %collective-permute-start.2 = (f32[256,256]{1,0:T(8,128)S(1)}, f32[256,256]{1,0:T(8,128)S(1)}, u32[]{:S(2)}, u32[]{:S(2)}) collective-permute-start(f32[256,256]{1,0:T(8,128)S(1)} %bitcast.12), channel_id=1, source_target_pairs={{0,8},{4,12},{8,0},{12,4},{1,9},{5,13},{9,1},{13,5},{2,10},{6,14},... | collective-permute-start | bytes 786440 | tf_op jit(solution)/shard_map/ppermute | solution.py:359
  12.8 37.3 %collective-permute-start.1 = (f32[256,256]{1,0:T(8,128)S(1)}, f32[256,256]{1,0:T(8,128)S(1)}, u32[]{:S(2)}, u32[]{:S(2)}) collective-permute-start(f32[256,256]{1,0:T(8,128)S(1)} %bitcast.11), channel_id=1, source_target_pairs={{0,4},{4,0},{8,12},{12,8},{1,5},{5,1},{9,13},{13,9},{2,6},{6,2},{1... | collective-permute-start | bytes 786440 | tf_op jit(solution)/shard_map/ppermute | solution.py:359
  13.9 4.1 %copy-start = (bf16[4,512,768]{2,1,0:T(8,128)(2,1)S(1)}, bf16[4,512,768]{2,1,0:T(8,128)(2,1)}, u32[]{:S(2)}) copy-start(bf16[4,512,768]{2,1,0:T(8,128)(2,1)} %constant.2.clone.t_ref) | copy-start | bytes 9437188
  13.9 36.6 %collective-permute-start = (f32[256,256]{1,0:T(8,128)S(1)}, f32[256,256]{1,0:T(8,128)S(1)}, u32[]{:S(2)}, u32[]{:S(2)}) collective-permute-start(f32[256,256]{1,0:T(8,128)S(1)} %bitcast.10), channel_id=1, source_target_pairs={{0,4},{4,0},{8,12},{12,8},{1,5},{5,1},{9,13},{13,9},{2,6},{6,2},{1... | collective-permute-start | bytes 786440 | tf_op jit(solution)/shard_map/ppermute | solution.py:359
  18.6 34.3 %collective-permute-start.5 = (f32[256,128]{1,0:T(8,128)S(1)}, f32[256,128]{1,0:T(8,128)S(1)}, u32[]{:S(2)}, u32[]{:S(2)}) collective-permute-start(f32[256,128]{1,0:T(8,128)S(1)} %bitcast.14), channel_id=1, source_target_pairs={{0,12},{4,8},{8,4},{12,0},{1,13},{5,9},{9,5},{13,1},{2,14},{6,10},... | collective-permute-start | bytes 393224 | tf_op jit(solution)/shard_map/ppermute | solution.py:359
  50.1 0.8 %copy-start.1 = (f32[1024]{0:T(1024)S(1)}, f32[1024]{0:T(1024)}, u32[]{:S(2)}) copy-start(f32[1024]{0:T(1024)} %param.4) | copy-start | bytes 12292
  51.8 1.4 %collective-permute-start.6 = (f32[256,128]{1,0:T(8,128)S(1)}, f32[256,128]{1,0:T(8,128)S(1)}, u32[]{:S(2)}, u32[]{:S(2)}) collective-permute-start(f32[256,128]{1,0:T(8,128)S(1)} %get-tuple-element.24), channel_id=1, source_target_pairs={{0,1},{1,0},{2,3},{3,2},{4,5},{5,4},{6,7},{7,6},{8,9},{9,8},{10,11... | collective-permute-start | bytes 393224 | tf_op jit(solution)/shard_map/ppermute | solution.py:359
  51.9 1.5 %collective-permute-start.7 = (f32[256,128]{1,0:T(8,128)S(1)}, f32[256,128]{1,0:T(8,128)S(1)}, u32[]{:S(2)}, u32[]{:S(2)}) collective-permute-start(f32[256,128]{1,0:T(8,128)S(1)} %get-tuple-element.25), channel_id=1, source_target_pairs={{0,1},{1,0},{2,3},{3,2},{4,5},{5,4},{6,7},{7,6},{8,9},{9,8},{10,11... | collective-permute-start | bytes 393224 | tf_op jit(solution)/shard_map/ppermute | solution.py:359
  52.4 1.3 %collective-permute-start.8 = (f32[256,128]{1,0:T(8,128)S(1)}, f32[256,128]{1,0:T(8,128)S(1)}, u32[]{:S(2)}, u32[]{:S(2)}) collective-permute-start(f32[256,128]{1,0:T(8,128)S(1)} %get-tuple-element.26), channel_id=1, source_target_pairs={{0,1},{1,0},{2,3},{3,2},{4,5},{5,4},{6,7},{7,6},{8,9},{9,8},{10,11... | collective-permute-start | bytes 393224 | tf_op jit(solution)/shard_map/ppermute | solution.py:359
  52.4 1.5 %collective-permute-start.9 = (f32[256,128]{1,0:T(8,128)S(1)}, f32[256,128]{1,0:T(8,128)S(1)}, u32[]{:S(2)}, u32[]{:S(2)}) collective-permute-start(f32[256,128]{1,0:T(8,128)S(1)} %get-tuple-element.27), channel_id=1, source_target_pairs={{0,1},{1,0},{2,3},{3,2},{4,5},{5,4},{6,7},{7,6},{8,9},{9,8},{10,11... | collective-permute-start | bytes 393224 | tf_op jit(solution)/shard_map/ppermute | solution.py:359
  53.9 1.5 %collective-permute-start.10 = (f32[256,128]{1,0:T(8,128)S(1)}, f32[256,128]{1,0:T(8,128)S(1)}, u32[]{:S(2)}, u32[]{:S(2)}) collective-permute-start(f32[256,128]{1,0:T(8,128)S(1)} %collective-permute-done.5.x_ref), channel_id=1, source_target_pairs={{0,1},{1,0},{2,3},{3,2},{4,5},{5,4},{6,7},{7,6},{8,9},{9,8},{10,11... | collective-permute-start | bytes 393224 | tf_op jit(solution)/shard_map/ppermute | solution.py:359
  54.2 1.2 %collective-permute-start.11 = (f32[16,128]{1,0:T(8,128)S(1)}, f32[16,128]{1,0:T(8,128)S(1)}, u32[]{:S(2)}, u32[]{:S(2)}) collective-permute-start(f32[16,128]{1,0:T(8,128)S(1)} %get-tuple-element.40), channel_id=1, source_target_pairs={{0,1},{1,0},{2,3},{3,2},{4,5},{5,4},{6,7},{7,6},{8,9},{9,8},{10,11... | collective-permute-start | bytes 24584 | tf_op jit(solution)/shard_map/ppermute | solution.py:359

commit v20 on v18

--- a/solution.py
+++ b/solution.py
@@ -297,6 +297,12 @@
     inv_re = [inv_re[h] * scales[h] for h in (0, 1)]
     inv_im = [inv_im[h] * scales[h] for h in (0, 1)]
 
+    pad = jnp.zeros((width - NB, width), jnp.float32)
+    upper_re = jnp.transpose(jnp.concatenate(low_re + [pad], axis=0))
+    upper_im = jnp.transpose(jnp.concatenate(low_im + [pad], axis=0))
+    for f in range(local):
+        factor_ref[0, f] = upper_re[f * NB : (f + 1) * NB, :NB]
+        factor_ref[1, f] = -upper_im[f * NB : (f + 1) * NB, :NB]
     me = lax.axis_index("freq")
     own = own_high_ref[...], own_low_ref[...]
     other = [
@@ -331,12 +337,6 @@
                 for f in range(count):
                     at = r * part + f * NB
                     modes_ref[h * count + f, r, :, cols] = out[at : at + NB]
-    pad = jnp.zeros((width - NB, width), jnp.float32)
-    turned_re = jnp.transpose(jnp.concatenate(low_re + [pad], axis=0))
-    turned_im = jnp.transpose(jnp.concatenate(low_im + [pad], axis=0))
-    for f in range(local):
-        factor_ref[0, f] = turned_re[f * NB : (f + 1) * NB, :NB]
-        factor_ref[1, f] = -turned_im[f * NB : (f + 1) * NB, :NB]
 
 
 def finish(total, own, others, grams):
@@ -391,8 +391,7 @@
         tables, n, last, 0, rest, piece, weights, gram, lent, own, other
     )
     *last_parts, gram = last_part(tables, n, last, targets, later, raw, weights, gram)
-    order = sorted(range(n), key=lambda z: abs(4 * z - (2 * n - 3)))
-    order = [z * tm_count + x for z in order for x in range(tm_count - 1, -1, -1)]
+    order = [(z + 1) % n * tm_count + x for z in range(n) for x in range(tm_count - 1, -1, -1)]
     grams = lax.all_to_all(
         gram,
         ("space", "tm"),

time: 65 us -> 65.1 us (level)
  no operation moved by 1% of the time
where the time goes in v20:
time: 65.1 us; the launch traced here: 64.6 us
  waiting for transfers between devices  29.1 us (45%)
  Pallas kernels  13.6 us (21%)
  starting transfers between devices  11.5 us (18%)
  blocking collectives  9.59 us (15%)
  between operations  0.84 us (1%)
    ppermute x10, waiting for transfers between devices, partner(): return lax.ppermute(value, axis, [(i, i ^ step) for i in range(size)])  29.1 us
    ppermute x10, starting transfers between devices, partner(): return lax.ppermute(value, axis, [(i, i ^ step) for i in range(size)])  11.5 us
    all_to_all x1, blocking collectives, on_device(): lax.all_to_all(gram, ('space', 'tm'), split_axis=0, concat_axis=0, axis_i...  9.59 us
    pallas_call x7, Pallas kernels, cut(): pl.pallas_call(functools.partial(cut_kernel, n, k, rows, skip), out_shape...  7 us
    pallas_call x6, Pallas kernels, early(): pl.pallas_call(functools.partial(early_kernel, n, k, skip), out_shape=jax...  2.43 us
    pallas_call x1, Pallas kernels, finish(): pl.pallas_call(functools.partial(finish_kernel, total), out_shape=(jax.Sh...  2.16 us
    pallas_call x2, Pallas kernels, last_part(): pl.pallas_call(functools.partial(last_part_kernel, n, k, bool(copies)), o...  1.49 us
  transfers between devices with their start and end apart: 10, of which 4 were waited for; matrix products, arithmetic and copies ran while one was open for 0% of the time, Pallas kernels for 15%

profile of v20, /device:TPU:0, one launch (start us, length us, event | category | flops | bytes accessed | tf_op | source)
XLA Modules:
  0.0 64.6 jit_solution(11169857928537498085)
XLA Ops:
  0.6 1.0 %shard_map.54 = f32[16,16,256]{2,1,0:T(8,128)S(1)} custom-call(f32[16,16,4096]{2,1,0:T(8,128)} %x_ref.13), custom_call_target="tpu_custom_call" | custom-call | flops 1 | bytes 1 | tf_op jit(solution)/shard_map/pallas_call | solution.py:81
  1.6 5.1 %collective-permute-start.4 = (f32[256,256]{1,0:T(8,128)S(1)}, f32[256,256]{1,0:T(8,128)S(1)}, u32[]{:S(2)}, u32[]{:S(2)}) collective-permute-start(f32[256,256]{1,0:T(8,128)S(1)} %bitcast.14), channel_id=1, source_target_pairs={{0,12},{4,8},{8,4},{12,0},{1,13},{5,9},{9,5},{13,1},{2,14},{6,10},... | collective-permute-start | bytes 786440 | tf_op jit(solution)/shard_map/ppermute | solution.py:356
  6.7 1.0 %shard_map.53 = f32[16,16,256]{2,1,0:T(8,128)S(1)} custom-call(f32[16,16,4096]{2,1,0:T(8,128)} %x_ref.13), custom_call_target="tpu_custom_call" | custom-call | flops 1 | bytes 1 | tf_op jit(solution)/shard_map/pallas_call | solution.py:81
  7.7 0.1 collective-permute-start.3
  7.8 1.0 %shard_map.52 = f32[16,16,256]{2,1,0:T(8,128)S(1)} custom-call(f32[16,16,4096]{2,1,0:T(8,128)} %x_ref.13), custom_call_target="tpu_custom_call" | custom-call | flops 1 | bytes 1 | tf_op jit(solution)/shard_map/pallas_call | solution.py:81
  8.8 3.0 %collective-permute-start.2 = (f32[256,256]{1,0:T(8,128)S(1)}, f32[256,256]{1,0:T(8,128)S(1)}, u32[]{:S(2)}, u32[]{:S(2)}) collective-permute-start(f32[256,256]{1,0:T(8,128)S(1)} %bitcast.12), channel_id=1, source_target_pairs={{0,8},{4,12},{8,0},{12,4},{1,9},{5,13},{9,1},{13,5},{2,10},{6,14},... | collective-permute-start | bytes 786440 | tf_op jit(solution)/shard_map/ppermute | solution.py:356
  11.7 1.0 %shard_map.51 = f32[16,16,256]{2,1,0:T(8,128)S(1)} custom-call(f32[16,16,4096]{2,1,0:T(8,128)} %x_ref.13), custom_call_target="tpu_custom_call" | custom-call | flops 1 | bytes 1 | tf_op jit(solution)/shard_map/pallas_call | solution.py:81
  12.7 0.1 collective-permute-start.1
  12.8 1.0 %shard_map.50 = f32[16,16,256]{2,1,0:T(8,128)S(1)} custom-call(f32[16,16,4096]{2,1,0:T(8,128)} %x_ref.13), custom_call_target="tpu_custom_call" | custom-call | flops 1 | bytes 1 | tf_op jit(solution)/shard_map/pallas_call | solution.py:81
  13.8 2.1 %collective-permute-start = (f32[256,256]{1,0:T(8,128)S(1)}, f32[256,256]{1,0:T(8,128)S(1)}, u32[]{:S(2)}, u32[]{:S(2)}) collective-permute-start(f32[256,256]{1,0:T(8,128)S(1)} %bitcast.10), channel_id=1, source_target_pairs={{0,4},{4,0},{8,12},{12,8},{1,5},{5,1},{9,13},{13,9},{2,6},{6,2},{1... | collective-permute-start | bytes 786440 | tf_op jit(solution)/shard_map/ppermute | solution.py:356
  15.9 1.1 %shard_map.55 = f32[16,16,512]{2,1,0:T(8,128)S(1)} custom-call(f32[16,16,4096]{2,1,0:T(8,128)} %x_ref.13), custom_call_target="tpu_custom_call" | custom-call | flops 1 | bytes 1 | tf_op jit(solution)/shard_map/pallas_call | solution.py:81
  17.0 1.0 %shard_map.63 = f32[16,16,256]{2,1,0:T(8,128)S(1)} custom-call(f32[16,16,4096]{2,1,0:T(8,128)} %x_ref.13), custom_call_target="tpu_custom_call" | custom-call | flops 1 | bytes 1 | tf_op jit(solution)/shard_map/pallas_call | solution.py:81
  18.0 0.6 shard_map.56.refs_0_
  18.6 0.4 collective-permute-start.5
  19.0 0.4 shard_map.57.refs_0_
  19.4 17.1 %collective-permute-done.3.x_ref = f32[256,256]{1,0:T(8,128)S(1)} collective-permute-done((f32[256,256]{1,0:T(8,128)S(1)}, f32[256,256]{1,0:T(8,128)S(1)}, u32[]{:S(2)}, u32[]{:S(2)}) %collective-permute-start.3) | collective-permute-done | bytes 262176 | tf_op jit(solution)/shard_map/ppermute | solution.py:356
  36.5 0.4 shard_map.58.refs_0_
  36.8 10.0 %collective-permute-done.2.x_ref = f32[256,256]{1,0:T(8,128)S(1)} collective-permute-done((f32[256,256]{1,0:T(8,128)S(1)}, f32[256,256]{1,0:T(8,128)S(1)}, u32[]{:S(2)}, u32[]{:S(2)}) %collective-permute-start.2) | collective-permute-done | bytes 262176 | tf_op jit(solution)/shard_map/ppermute | solution.py:356
  46.9 0.4 shard_map.59.refs_0_
  47.3 0.4 shard_map.60.refs_0_
  47.6 0.4 shard_map.61.sum_ref
  48.0 0.6 shard_map.62
  48.6 0.1 collective-permute-start.6
  48.7 0.5 collective-permute-start.7
  49.2 0.1 collective-permute-start.8
  49.3 1.3 %collective-permute-done.8.refs_1_ = f32[16,128]{1,0:T(8,128)S(1)} collective-permute-done((f32[16,128]{1,0:T(8,128)S(1)}, f32[16,128]{1,0:T(8,128)S(1)}, u32[]{:S(2)}, u32[]{:S(2)}) %collective-permute-start.8) | collective-permute-done | bytes 8224 | tf_op jit(solution)/shard_map/ppermute | solution.py:356
  50.6 0.1 collective-permute-start.9
  50.7 0.8 %shard_map.64 = (bf16[256,512]{1,0:T(8,128)(2,1)S(1)}, bf16[256,512]{1,0:T(8,128)(2,1)S(1)}, bf16[256,256]{1,0:T(8,128)(2,1)S(1)}, bf16[256,256]{1,0:T(8,128)(2,1)S(1)}, f32[16,128]{1,0:T(8,128)S(1)}) custom-call(bf16[4,512,768]{2,1,0:T(8,128)(2,1)S(1)} %copy-done, f32[256,256]{1,0:T(8,128)S(1)} %get-tuple-element.20.sum_ref, ...), custom_call_target="tpu_custom_call" | custom-call | flops 1 | bytes 1 | tf_op jit(solution)/shard_map/pallas_call | solution.py:207
  51.5 0.6 collective-permute-done.9.x_ref
  52.1 0.7 %shard_map.65 = (bf16[256,256]{1,0:T(8,128)(2,1)S(1)}, bf16[256,256]{1,0:T(8,128)(2,1)S(1)}, f32[8,16,128]{2,1,0:T(8,128)S(1)}) custom-call(bf16[4,512,768]{2,1,0:T(8,128)(2,1)S(1)} %copy-done, f32[256,256]{1,0:T(8,128)S(1)} %collective-permute-done.7.sum_ref, f32[256,256]{1,0:T(8,128)S(1)} %collective-permute-done.9.x_ref, f32[1,1024]{1,0:T(1,128)S(1)} %bitcast.17, ...), custom_call_target="tpu_custom_call" | custom-call | flops 1 | bytes 1 | tf_op jit(solution)/shard_map/pallas_call | solution.py:207
  52.9 9.6 %all_to_all.5.grams_ref = f32[8,16,128]{2,1,0:T(8,128)S(1)} all-to-all(f32[8,16,128]{2,1,0:T(8,128)S(1)} %get-tuple-element.37), channel_id=1, replica_groups={{6,4,10,8,14,12,2,0},{7,5,11,9,15,13,3,1},{22,20,26,24,30,28,18,16},{23..., dimensions={0} | all-to-all | bytes 131072 | tf_op jit(solution)/shard_map/all_to_all | solution.py:395
  62.5 2.2 %shard_map.66 = (f32[8,2,16,1024]{3,2,1,0:T(8,128)}, f32[2,8,16,16]{3,2,1,0:T(8,128)}) custom-call(bf16[256,512]{1,0:T(8,128)(2,1)S(1)} %get-tuple-element.29.own_high_ref, bf16[256,512]{1,0:T(8,128)(2,1)S(1)} %get-tuple-element.30.own_low_ref, bf16[256,256]{1,0:T(8,128)(2,1)S(1)} %get-tuple-element.31.first_high_ref, ...), custom_call_target="tpu_custom_call" | custom-call | tf_op jit(solution)/shard_map/pallas_call | solution.py:345
  (10 shorter events, 0.0 us)
Async XLA Ops:
  1.6 17.0 %collective-permute-start.4 = (f32[256,256]{1,0:T(8,128)S(1)}, f32[256,256]{1,0:T(8,128)S(1)}, u32[]{:S(2)}, u32[]{:S(2)}) collective-permute-start(f32[256,256]{1,0:T(8,128)S(1)} %bitcast.14), channel_id=1, source_target_pairs={{0,12},{4,8},{8,4},{12,0},{1,13},{5,9},{9,5},{13,1},{2,14},{6,10},... | collective-permute-start | bytes 786440 | tf_op jit(solution)/shard_map/ppermute | solution.py:356
  7.7 28.8 %collective-permute-start.3 = (f32[256,256]{1,0:T(8,128)S(1)}, f32[256,256]{1,0:T(8,128)S(1)}, u32[]{:S(2)}, u32[]{:S(2)}) collective-permute-start(f32[256,256]{1,0:T(8,128)S(1)} %bitcast.13), channel_id=1, source_target_pairs={{0,8},{4,12},{8,0},{12,4},{1,9},{5,13},{9,1},{13,5},{2,10},{6,14},... | collective-permute-start | bytes 786440 | tf_op jit(solution)/shard_map/ppermute | solution.py:356
  8.8 38.1 %collective-permute-start.2 = (f32[256,256]{1,0:T(8,128)S(1)}, f32[256,256]{1,0:T(8,128)S(1)}, u32[]{:S(2)}, u32[]{:S(2)}) collective-permute-start(f32[256,256]{1,0:T(8,128)S(1)} %bitcast.12), channel_id=1, source_target_pairs={{0,8},{4,12},{8,0},{12,4},{1,9},{5,13},{9,1},{13,5},{2,10},{6,14},... | collective-permute-start | bytes 786440 | tf_op jit(solution)/shard_map/ppermute | solution.py:356
  12.7 34.5 %collective-permute-start.1 = (f32[256,256]{1,0:T(8,128)S(1)}, f32[256,256]{1,0:T(8,128)S(1)}, u32[]{:S(2)}, u32[]{:S(2)}) collective-permute-start(f32[256,256]{1,0:T(8,128)S(1)} %bitcast.11), channel_id=1, source_target_pairs={{0,4},{4,0},{8,12},{12,8},{1,5},{5,1},{9,13},{13,9},{2,6},{6,2},{1... | collective-permute-start | bytes 786440 | tf_op jit(solution)/shard_map/ppermute | solution.py:356
  13.8 4.2 %copy-start = (bf16[4,512,768]{2,1,0:T(8,128)(2,1)S(1)}, bf16[4,512,768]{2,1,0:T(8,128)(2,1)}, u32[]{:S(2)}) copy-start(bf16[4,512,768]{2,1,0:T(8,128)(2,1)} %constant.2.clone.t_ref) | copy-start | bytes 9437188
  13.8 33.8 %collective-permute-start = (f32[256,256]{1,0:T(8,128)S(1)}, f32[256,256]{1,0:T(8,128)S(1)}, u32[]{:S(2)}, u32[]{:S(2)}) collective-permute-start(f32[256,256]{1,0:T(8,128)S(1)} %bitcast.10), channel_id=1, source_target_pairs={{0,4},{4,0},{8,12},{12,8},{1,5},{5,1},{9,13},{13,9},{2,6},{6,2},{1... | collective-permute-start | bytes 786440 | tf_op jit(solution)/shard_map/ppermute | solution.py:356
  18.6 30.7 %collective-permute-start.5 = (f32[256,256]{1,0:T(8,128)S(1)}, f32[256,256]{1,0:T(8,128)S(1)}, u32[]{:S(2)}, u32[]{:S(2)}) collective-permute-start(f32[256,256]{1,0:T(8,128)S(1)} %bitcast.9), channel_id=1, source_target_pairs={{0,12},{4,8},{8,4},{12,0},{1,13},{5,9},{9,5},{13,1},{2,14},{6,10},... | collective-permute-start | bytes 786440 | tf_op jit(solution)/shard_map/ppermute | solution.py:356
  47.2 0.8 %copy-start.1 = (f32[1024]{0:T(1024)S(1)}, f32[1024]{0:T(1024)}, u32[]{:S(2)}) copy-start(f32[1024]{0:T(1024)} %param.4) | copy-start | bytes 12292
  48.6 2.0 %collective-permute-start.6 = (f32[256,256]{1,0:T(8,128)S(1)}, f32[256,256]{1,0:T(8,128)S(1)}, u32[]{:S(2)}, u32[]{:S(2)}) collective-permute-start(f32[256,256]{1,0:T(8,128)S(1)} %get-tuple-element.21), channel_id=1, source_target_pairs={{0,1},{1,0},{2,3},{3,2},{4,5},{5,4},{6,7},{7,6},{8,9},{9,8},{10,11... | collective-permute-start | bytes 786440 | tf_op jit(solution)/shard_map/ppermute | solution.py:356
  48.7 1.9 %collective-permute-start.7 = (f32[256,256]{1,0:T(8,128)S(1)}, f32[256,256]{1,0:T(8,128)S(1)}, u32[]{:S(2)}, u32[]{:S(2)}) collective-permute-start(f32[256,256]{1,0:T(8,128)S(1)} %get-tuple-element.22), channel_id=1, source_target_pairs={{0,1},{1,0},{2,3},{3,2},{4,5},{5,4},{6,7},{7,6},{8,9},{9,8},{10,11... | collective-permute-start | bytes 786440 | tf_op jit(solution)/shard_map/ppermute | solution.py:356
  49.2 1.4 %collective-permute-start.8 = (f32[16,128]{1,0:T(8,128)S(1)}, f32[16,128]{1,0:T(8,128)S(1)}, u32[]{:S(2)}, u32[]{:S(2)}) collective-permute-start(f32[16,128]{1,0:T(8,128)S(1)} %get-tuple-element.23), channel_id=1, source_target_pairs={{0,1},{1,0},{2,3},{3,2},{4,5},{5,4},{6,7},{7,6},{8,9},{9,8},{10,11... | collective-permute-start | bytes 24584 | tf_op jit(solution)/shard_map/ppermute | solution.py:356
  50.6 1.5 %collective-permute-start.9 = (f32[256,256]{1,0:T(8,128)S(1)}, f32[256,256]{1,0:T(8,128)S(1)}, u32[]{:S(2)}, u32[]{:S(2)}) collective-permute-start(f32[256,256]{1,0:T(8,128)S(1)} %collective-permute-done.5.x_ref), channel_id=1, source_target_pairs={{0,1},{1,0},{2,3},{3,2},{4,5},{5,4},{6,7},{7,6},{8,9},{9,8},{10,11... | collective-permute-start | bytes 786440 | tf_op jit(solution)/shard_map/ppermute | solution.py:356

commit v21 on v20

--- a/solution.py
+++ b/solution.py
@@ -391,7 +391,7 @@
         tables, n, last, 0, rest, piece, weights, gram, lent, own, other
     )
     *last_parts, gram = last_part(tables, n, last, targets, later, raw, weights, gram)
-    order = [(z + 1) % n * tm_count + x for z in range(n) for x in range(tm_count - 1, -1, -1)]
+    order = list(range(targets - 1, -1, -1))
     grams = lax.all_to_all(
         gram,
         ("space", "tm"),

time: 65.1 us -> 64.5 us (level)
  no operation moved by 1% of the time
where the time goes in v21:
time: 64.5 us; the launch traced here: 64.1 us
  waiting for transfers between devices  29.1 us (45%)
  Pallas kernels  13.6 us (21%)
  starting transfers between devices  11.5 us (18%)
  blocking collectives  9.03 us (14%)
  between operations  0.84 us (1%)
    ppermute x10, waiting for transfers between devices, partner(): return lax.ppermute(value, axis, [(i, i ^ step) for i in range(size)])  29.1 us
    ppermute x10, starting transfers between devices, partner(): return lax.ppermute(value, axis, [(i, i ^ step) for i in range(size)])  11.5 us
    all_to_all x1, blocking collectives, on_device(): lax.all_to_all(gram, ('space', 'tm'), split_axis=0, concat_axis=0, axis_i...  9.03 us
    pallas_call x7, Pallas kernels, cut(): pl.pallas_call(functools.partial(cut_kernel, n, k, rows, skip), out_shape...  7 us
    pallas_call x6, Pallas kernels, early(): pl.pallas_call(functools.partial(early_kernel, n, k, skip), out_shape=jax...  2.43 us
    pallas_call x1, Pallas kernels, finish(): pl.pallas_call(functools.partial(finish_kernel, total), out_shape=(jax.Sh...  2.16 us
    pallas_call x2, Pallas kernels, last_part(): pl.pallas_call(functools.partial(last_part_kernel, n, k, bool(copies)), o...  1.49 us
  transfers between devices with their start and end apart: 10, of which 4 were waited for; matrix products, arithmetic and copies ran while one was open for 0% of the time, Pallas kernels for 15%

profile of v21, /device:TPU:0, one launch (start us, length us, event | category | flops | bytes accessed | tf_op | source)
XLA Modules:
  0.0 64.1 jit_solution(2573294278914349831)
XLA Ops:
  0.6 1.0 %shard_map.54 = f32[16,16,256]{2,1,0:T(8,128)S(1)} custom-call(f32[16,16,4096]{2,1,0:T(8,128)} %x_ref.13), custom_call_target="tpu_custom_call" | custom-call | flops 1 | bytes 1 | tf_op jit(solution)/shard_map/pallas_call | solution.py:81
  1.6 5.1 %collective-permute-start.4 = (f32[256,256]{1,0:T(8,128)S(1)}, f32[256,256]{1,0:T(8,128)S(1)}, u32[]{:S(2)}, u32[]{:S(2)}) collective-permute-start(f32[256,256]{1,0:T(8,128)S(1)} %bitcast.14), channel_id=1, source_target_pairs={{0,12},{4,8},{8,4},{12,0},{1,13},{5,9},{9,5},{13,1},{2,14},{6,10},... | collective-permute-start | bytes 786440 | tf_op jit(solution)/shard_map/ppermute | solution.py:356
  6.7 1.0 %shard_map.53 = f32[16,16,256]{2,1,0:T(8,128)S(1)} custom-call(f32[16,16,4096]{2,1,0:T(8,128)} %x_ref.13), custom_call_target="tpu_custom_call" | custom-call | flops 1 | bytes 1 | tf_op jit(solution)/shard_map/pallas_call | solution.py:81
  7.7 0.1 collective-permute-start.3
  7.8 1.0 %shard_map.52 = f32[16,16,256]{2,1,0:T(8,128)S(1)} custom-call(f32[16,16,4096]{2,1,0:T(8,128)} %x_ref.13), custom_call_target="tpu_custom_call" | custom-call | flops 1 | bytes 1 | tf_op jit(solution)/shard_map/pallas_call | solution.py:81
  8.8 3.0 %collective-permute-start.2 = (f32[256,256]{1,0:T(8,128)S(1)}, f32[256,256]{1,0:T(8,128)S(1)}, u32[]{:S(2)}, u32[]{:S(2)}) collective-permute-start(f32[256,256]{1,0:T(8,128)S(1)} %bitcast.12), channel_id=1, source_target_pairs={{0,8},{4,12},{8,0},{12,4},{1,9},{5,13},{9,1},{13,5},{2,10},{6,14},... | collective-permute-start | bytes 786440 | tf_op jit(solution)/shard_map/ppermute | solution.py:356
  11.7 1.0 %shard_map.51 = f32[16,16,256]{2,1,0:T(8,128)S(1)} custom-call(f32[16,16,4096]{2,1,0:T(8,128)} %x_ref.13), custom_call_target="tpu_custom_call" | custom-call | flops 1 | bytes 1 | tf_op jit(solution)/shard_map/pallas_call | solution.py:81
  12.7 0.1 collective-permute-start.1
  12.8 1.0 %shard_map.50 = f32[16,16,256]{2,1,0:T(8,128)S(1)} custom-call(f32[16,16,4096]{2,1,0:T(8,128)} %x_ref.13), custom_call_target="tpu_custom_call" | custom-call | flops 1 | bytes 1 | tf_op jit(solution)/shard_map/pallas_call | solution.py:81
  13.8 2.1 %collective-permute-start = (f32[256,256]{1,0:T(8,128)S(1)}, f32[256,256]{1,0:T(8,128)S(1)}, u32[]{:S(2)}, u32[]{:S(2)}) collective-permute-start(f32[256,256]{1,0:T(8,128)S(1)} %bitcast.10), channel_id=1, source_target_pairs={{0,4},{4,0},{8,12},{12,8},{1,5},{5,1},{9,13},{13,9},{2,6},{6,2},{1... | collective-permute-start | bytes 786440 | tf_op jit(solution)/shard_map/ppermute | solution.py:356
  15.9 1.1 %shard_map.55 = f32[16,16,512]{2,1,0:T(8,128)S(1)} custom-call(f32[16,16,4096]{2,1,0:T(8,128)} %x_ref.13), custom_call_target="tpu_custom_call" | custom-call | flops 1 | bytes 1 | tf_op jit(solution)/shard_map/pallas_call | solution.py:81
  17.0 1.0 %shard_map.63 = f32[16,16,256]{2,1,0:T(8,128)S(1)} custom-call(f32[16,16,4096]{2,1,0:T(8,128)} %x_ref.13), custom_call_target="tpu_custom_call" | custom-call | flops 1 | bytes 1 | tf_op jit(solution)/shard_map/pallas_call | solution.py:81
  18.0 0.6 shard_map.56.refs_0_
  18.6 0.4 collective-permute-start.5
  19.0 0.4 shard_map.57.refs_0_
  19.4 17.1 %collective-permute-done.3.x_ref = f32[256,256]{1,0:T(8,128)S(1)} collective-permute-done((f32[256,256]{1,0:T(8,128)S(1)}, f32[256,256]{1,0:T(8,128)S(1)}, u32[]{:S(2)}, u32[]{:S(2)}) %collective-permute-start.3) | collective-permute-done | bytes 262176 | tf_op jit(solution)/shard_map/ppermute | solution.py:356
  36.5 0.4 shard_map.58.refs_0_
  36.8 10.0 %collective-permute-done.2.x_ref = f32[256,256]{1,0:T(8,128)S(1)} collective-permute-done((f32[256,256]{1,0:T(8,128)S(1)}, f32[256,256]{1,0:T(8,128)S(1)}, u32[]{:S(2)}, u32[]{:S(2)}) %collective-permute-start.2) | collective-permute-done | bytes 262176 | tf_op jit(solution)/shard_map/ppermute | solution.py:356
  46.9 0.4 shard_map.59.refs_0_
  47.3 0.4 shard_map.60.refs_0_
  47.6 0.4 shard_map.61.sum_ref
  48.0 0.6 shard_map.62
  48.6 0.1 collective-permute-start.6
  48.7 0.5 collective-permute-start.7
  49.2 0.1 collective-permute-start.8
  49.3 1.3 %collective-permute-done.8.refs_1_ = f32[16,128]{1,0:T(8,128)S(1)} collective-permute-done((f32[16,128]{1,0:T(8,128)S(1)}, f32[16,128]{1,0:T(8,128)S(1)}, u32[]{:S(2)}, u32[]{:S(2)}) %collective-permute-start.8) | collective-permute-done | bytes 8224 | tf_op jit(solution)/shard_map/ppermute | solution.py:356
  50.6 0.1 collective-permute-start.9
  50.7 0.8 %shard_map.64 = (bf16[256,512]{1,0:T(8,128)(2,1)S(1)}, bf16[256,512]{1,0:T(8,128)(2,1)S(1)}, bf16[256,256]{1,0:T(8,128)(2,1)S(1)}, bf16[256,256]{1,0:T(8,128)(2,1)S(1)}, f32[16,128]{1,0:T(8,128)S(1)}) custom-call(bf16[4,512,768]{2,1,0:T(8,128)(2,1)S(1)} %copy-done, f32[256,256]{1,0:T(8,128)S(1)} %get-tuple-element.20.sum_ref, ...), custom_call_target="tpu_custom_call" | custom-call | flops 1 | bytes 1 | tf_op jit(solution)/shard_map/pallas_call | solution.py:207
  51.5 0.6 collective-permute-done.9.x_ref
  52.1 0.7 %shard_map.65 = (bf16[256,256]{1,0:T(8,128)(2,1)S(1)}, bf16[256,256]{1,0:T(8,128)(2,1)S(1)}, f32[8,16,128]{2,1,0:T(8,128)S(1)}) custom-call(bf16[4,512,768]{2,1,0:T(8,128)(2,1)S(1)} %copy-done, f32[256,256]{1,0:T(8,128)S(1)} %collective-permute-done.7.sum_ref, f32[256,256]{1,0:T(8,128)S(1)} %collective-permute-done.9.x_ref, f32[1,1024]{1,0:T(1,128)S(1)} %bitcast.17, ...), custom_call_target="tpu_custom_call" | custom-call | flops 1 | bytes 1 | tf_op jit(solution)/shard_map/pallas_call | solution.py:207
  52.9 9.0 %all_to_all.5.grams_ref = f32[8,16,128]{2,1,0:T(8,128)S(1)} all-to-all(f32[8,16,128]{2,1,0:T(8,128)S(1)} %get-tuple-element.37), channel_id=1, replica_groups={{14,12,10,8,6,4,2,0},{15,13,11,9,7,5,3,1},{30,28,26,24,22,20,18,16},{31..., dimensions={0} | all-to-all | bytes 131072 | tf_op jit(solution)/shard_map/all_to_all | solution.py:395
  61.9 2.2 %shard_map.66 = (f32[8,2,16,1024]{3,2,1,0:T(8,128)}, f32[2,8,16,16]{3,2,1,0:T(8,128)}) custom-call(bf16[256,512]{1,0:T(8,128)(2,1)S(1)} %get-tuple-element.29.own_high_ref, bf16[256,512]{1,0:T(8,128)(2,1)S(1)} %get-tuple-element.30.own_low_ref, bf16[256,256]{1,0:T(8,128)(2,1)S(1)} %get-tuple-element.31.first_high_ref, ...), custom_call_target="tpu_custom_call" | custom-call | tf_op jit(solution)/shard_map/pallas_call | solution.py:345
  (10 shorter events, 0.0 us)
Async XLA Ops:
  1.6 17.0 %collective-permute-start.4 = (f32[256,256]{1,0:T(8,128)S(1)}, f32[256,256]{1,0:T(8,128)S(1)}, u32[]{:S(2)}, u32[]{:S(2)}) collective-permute-start(f32[256,256]{1,0:T(8,128)S(1)} %bitcast.14), channel_id=1, source_target_pairs={{0,12},{4,8},{8,4},{12,0},{1,13},{5,9},{9,5},{13,1},{2,14},{6,10},... | collective-permute-start | bytes 786440 | tf_op jit(solution)/shard_map/ppermute | solution.py:356
  7.7 28.8 %collective-permute-start.3 = (f32[256,256]{1,0:T(8,128)S(1)}, f32[256,256]{1,0:T(8,128)S(1)}, u32[]{:S(2)}, u32[]{:S(2)}) collective-permute-start(f32[256,256]{1,0:T(8,128)S(1)} %bitcast.13), channel_id=1, source_target_pairs={{0,8},{4,12},{8,0},{12,4},{1,9},{5,13},{9,1},{13,5},{2,10},{6,14},... | collective-permute-start | bytes 786440 | tf_op jit(solution)/shard_map/ppermute | solution.py:356
  8.8 38.1 %collective-permute-start.2 = (f32[256,256]{1,0:T(8,128)S(1)}, f32[256,256]{1,0:T(8,128)S(1)}, u32[]{:S(2)}, u32[]{:S(2)}) collective-permute-start(f32[256,256]{1,0:T(8,128)S(1)} %bitcast.12), channel_id=1, source_target_pairs={{0,8},{4,12},{8,0},{12,4},{1,9},{5,13},{9,1},{13,5},{2,10},{6,14},... | collective-permute-start | bytes 786440 | tf_op jit(solution)/shard_map/ppermute | solution.py:356
  12.7 34.5 %collective-permute-start.1 = (f32[256,256]{1,0:T(8,128)S(1)}, f32[256,256]{1,0:T(8,128)S(1)}, u32[]{:S(2)}, u32[]{:S(2)}) collective-permute-start(f32[256,256]{1,0:T(8,128)S(1)} %bitcast.11), channel_id=1, source_target_pairs={{0,4},{4,0},{8,12},{12,8},{1,5},{5,1},{9,13},{13,9},{2,6},{6,2},{1... | collective-permute-start | bytes 786440 | tf_op jit(solution)/shard_map/ppermute | solution.py:356
  13.8 4.2 %copy-start = (bf16[4,512,768]{2,1,0:T(8,128)(2,1)S(1)}, bf16[4,512,768]{2,1,0:T(8,128)(2,1)}, u32[]{:S(2)}) copy-start(bf16[4,512,768]{2,1,0:T(8,128)(2,1)} %constant.2.clone.t_ref) | copy-start | bytes 9437188
  13.8 33.8 %collective-permute-start = (f32[256,256]{1,0:T(8,128)S(1)}, f32[256,256]{1,0:T(8,128)S(1)}, u32[]{:S(2)}, u32[]{:S(2)}) collective-permute-start(f32[256,256]{1,0:T(8,128)S(1)} %bitcast.10), channel_id=1, source_target_pairs={{0,4},{4,0},{8,12},{12,8},{1,5},{5,1},{9,13},{13,9},{2,6},{6,2},{1... | collective-permute-start | bytes 786440 | tf_op jit(solution)/shard_map/ppermute | solution.py:356
  18.6 30.7 %collective-permute-start.5 = (f32[256,256]{1,0:T(8,128)S(1)}, f32[256,256]{1,0:T(8,128)S(1)}, u32[]{:S(2)}, u32[]{:S(2)}) collective-permute-start(f32[256,256]{1,0:T(8,128)S(1)} %bitcast.9), channel_id=1, source_target_pairs={{0,12},{4,8},{8,4},{12,0},{1,13},{5,9},{9,5},{13,1},{2,14},{6,10},... | collective-permute-start | bytes 786440 | tf_op jit(solution)/shard_map/ppermute | solution.py:356
  47.2 0.8 %copy-start.1 = (f32[1024]{0:T(1024)S(1)}, f32[1024]{0:T(1024)}, u32[]{:S(2)}) copy-start(f32[1024]{0:T(1024)} %param.4) | copy-start | bytes 12292
  48.6 2.0 %collective-permute-start.6 = (f32[256,256]{1,0:T(8,128)S(1)}, f32[256,256]{1,0:T(8,128)S(1)}, u32[]{:S(2)}, u32[]{:S(2)}) collective-permute-start(f32[256,256]{1,0:T(8,128)S(1)} %get-tuple-element.21), channel_id=1, source_target_pairs={{0,1},{1,0},{2,3},{3,2},{4,5},{5,4},{6,7},{7,6},{8,9},{9,8},{10,11... | collective-permute-start | bytes 786440 | tf_op jit(solution)/shard_map/ppermute | solution.py:356
  48.7 1.9 %collective-permute-start.7 = (f32[256,256]{1,0:T(8,128)S(1)}, f32[256,256]{1,0:T(8,128)S(1)}, u32[]{:S(2)}, u32[]{:S(2)}) collective-permute-start(f32[256,256]{1,0:T(8,128)S(1)} %get-tuple-element.22), channel_id=1, source_target_pairs={{0,1},{1,0},{2,3},{3,2},{4,5},{5,4},{6,7},{7,6},{8,9},{9,8},{10,11... | collective-permute-start | bytes 786440 | tf_op jit(solution)/shard_map/ppermute | solution.py:356
  49.2 1.4 %collective-permute-start.8 = (f32[16,128]{1,0:T(8,128)S(1)}, f32[16,128]{1,0:T(8,128)S(1)}, u32[]{:S(2)}, u32[]{:S(2)}) collective-permute-start(f32[16,128]{1,0:T(8,128)S(1)} %get-tuple-element.23), channel_id=1, source_target_pairs={{0,1},{1,0},{2,3},{3,2},{4,5},{5,4},{6,7},{7,6},{8,9},{9,8},{10,11... | collective-permute-start | bytes 24584 | tf_op jit(solution)/shard_map/ppermute | solution.py:356
  50.6 1.5 %collective-permute-start.9 = (f32[256,256]{1,0:T(8,128)S(1)}, f32[256,256]{1,0:T(8,128)S(1)}, u32[]{:S(2)}, u32[]{:S(2)}) collective-permute-start(f32[256,256]{1,0:T(8,128)S(1)} %collective-permute-done.5.x_ref), channel_id=1, source_target_pairs={{0,1},{1,0},{2,3},{3,2},{4,5},{5,4},{6,7},{7,6},{8,9},{9,8},{10,11... | collective-permute-start | bytes 786440 | tf_op jit(solution)/shard_map/ppermute | solution.py:356

commit v22 on v21

--- a/solution.py
+++ b/solution.py
@@ -45,14 +45,15 @@
 
 
 def rows_product(a, b):
-    a_high, a_low = split(a)
-    b_high, b_low = split(b)
-    total = 0.0
-    for x, y in ((a_low, b_low), (a_low, b_high), (a_high, b_low), (a_high, b_high)):
-        total = total + lax.dot_general(
-            x, y, (((1,), (1,)), ((), ())), preferred_element_type=jnp.float32
-        )
-    return total
+    lines, columns = a.shape[0], b.shape[0]
+    full = lax.dot_general(
+        jnp.concatenate(split(a), axis=0),
+        jnp.concatenate(split(b), axis=0),
+        (((1,), (1,)), ((), ())),
+        preferred_element_type=jnp.float32,
+    )
+    small = full[lines:, columns:] + full[lines:, :columns] + full[:lines, columns:]
+    return small + full[:lines, :columns]
 
 
 def cut_kernel(n, k, rows, skip, x_ref, o_ref, sem):

time: 64.5 us -> 64.6 us (level)
  no operation moved by 1% of the time
where the time goes in v22:
time: 64.6 us; the launch traced here: 64.1 us
  waiting for transfers between devices  29.1 us (45%)
  Pallas kernels  13.6 us (21%)
  starting transfers between devices  11.5 us (18%)
  blocking collectives  9.05 us (14%)
  between operations  0.84 us (1%)
    ppermute x10, waiting for transfers between devices, partner(): return lax.ppermute(value, axis, [(i, i ^ step) for i in range(size)])  29.1 us
    ppermute x10, starting transfers between devices, partner(): return lax.ppermute(value, axis, [(i, i ^ step) for i in range(size)])  11.5 us
    all_to_all x1, blocking collectives, on_device(): lax.all_to_all(gram, ('space', 'tm'), split_axis=0, concat_axis=0, axis_i...  9.05 us
    pallas_call x7, Pallas kernels, cut(): pl.pallas_call(functools.partial(cut_kernel, n, k, rows, skip), out_shape...  7 us
    pallas_call x6, Pallas kernels, early(): pl.pallas_call(functools.partial(early_kernel, n, k, skip), out_shape=jax...  2.43 us
    pallas_call x1, Pallas kernels, finish(): pl.pallas_call(functools.partial(finish_kernel, total), out_shape=(jax.Sh...  2.17 us
    pallas_call x2, Pallas kernels, last_part(): pl.pallas_call(functools.partial(last_part_kernel, n, k, bool(copies)), o...  1.49 us
  transfers between devices with their start and end apart: 10, of which 4 were waited for; matrix products, arithmetic and copies ran while one was open for 0% of the time, Pallas kernels for 15%

profile of v22, /device:TPU:0, one launch (start us, length us, event | category | flops | bytes accessed | tf_op | source)
XLA Modules:
  0.0 64.1 jit_solution(745675555681862692)
XLA Ops:
  0.6 1.0 %shard_map.54 = f32[16,16,256]{2,1,0:T(8,128)S(1)} custom-call(f32[16,16,4096]{2,1,0:T(8,128)} %x_ref.13), custom_call_target="tpu_custom_call" | custom-call | flops 1 | bytes 1 | tf_op jit(solution)/shard_map/pallas_call | solution.py:82
  1.6 5.1 %collective-permute-start.4 = (f32[256,256]{1,0:T(8,128)S(1)}, f32[256,256]{1,0:T(8,128)S(1)}, u32[]{:S(2)}, u32[]{:S(2)}) collective-permute-start(f32[256,256]{1,0:T(8,128)S(1)} %bitcast.14), channel_id=1, source_target_pairs={{0,12},{4,8},{8,4},{12,0},{1,13},{5,9},{9,5},{13,1},{2,14},{6,10},... | collective-permute-start | bytes 786440 | tf_op jit(solution)/shard_map/ppermute | solution.py:357
  6.7 1.0 %shard_map.53 = f32[16,16,256]{2,1,0:T(8,128)S(1)} custom-call(f32[16,16,4096]{2,1,0:T(8,128)} %x_ref.13), custom_call_target="tpu_custom_call" | custom-call | flops 1 | bytes 1 | tf_op jit(solution)/shard_map/pallas_call | solution.py:82
  7.7 0.1 collective-permute-start.3
  7.8 1.0 %shard_map.52 = f32[16,16,256]{2,1,0:T(8,128)S(1)} custom-call(f32[16,16,4096]{2,1,0:T(8,128)} %x_ref.13), custom_call_target="tpu_custom_call" | custom-call | flops 1 | bytes 1 | tf_op jit(solution)/shard_map/pallas_call | solution.py:82
  8.8 3.0 %collective-permute-start.2 = (f32[256,256]{1,0:T(8,128)S(1)}, f32[256,256]{1,0:T(8,128)S(1)}, u32[]{:S(2)}, u32[]{:S(2)}) collective-permute-start(f32[256,256]{1,0:T(8,128)S(1)} %bitcast.12), channel_id=1, source_target_pairs={{0,8},{4,12},{8,0},{12,4},{1,9},{5,13},{9,1},{13,5},{2,10},{6,14},... | collective-permute-start | bytes 786440 | tf_op jit(solution)/shard_map/ppermute | solution.py:357
  11.7 1.0 %shard_map.51 = f32[16,16,256]{2,1,0:T(8,128)S(1)} custom-call(f32[16,16,4096]{2,1,0:T(8,128)} %x_ref.13), custom_call_target="tpu_custom_call" | custom-call | flops 1 | bytes 1 | tf_op jit(solution)/shard_map/pallas_call | solution.py:82
  12.7 0.1 collective-permute-start.1
  12.8 1.0 %shard_map.50 = f32[16,16,256]{2,1,0:T(8,128)S(1)} custom-call(f32[16,16,4096]{2,1,0:T(8,128)} %x_ref.13), custom_call_target="tpu_custom_call" | custom-call | flops 1 | bytes 1 | tf_op jit(solution)/shard_map/pallas_call | solution.py:82
  13.8 2.1 %collective-permute-start = (f32[256,256]{1,0:T(8,128)S(1)}, f32[256,256]{1,0:T(8,128)S(1)}, u32[]{:S(2)}, u32[]{:S(2)}) collective-permute-start(f32[256,256]{1,0:T(8,128)S(1)} %bitcast.10), channel_id=1, source_target_pairs={{0,4},{4,0},{8,12},{12,8},{1,5},{5,1},{9,13},{13,9},{2,6},{6,2},{1... | collective-permute-start | bytes 786440 | tf_op jit(solution)/shard_map/ppermute | solution.py:357
  15.9 1.1 %shard_map.55 = f32[16,16,512]{2,1,0:T(8,128)S(1)} custom-call(f32[16,16,4096]{2,1,0:T(8,128)} %x_ref.13), custom_call_target="tpu_custom_call" | custom-call | flops 1 | bytes 1 | tf_op jit(solution)/shard_map/pallas_call | solution.py:82
  17.0 1.0 %shard_map.63 = f32[16,16,256]{2,1,0:T(8,128)S(1)} custom-call(f32[16,16,4096]{2,1,0:T(8,128)} %x_ref.13), custom_call_target="tpu_custom_call" | custom-call | flops 1 | bytes 1 | tf_op jit(solution)/shard_map/pallas_call | solution.py:82
  18.0 0.6 shard_map.56.refs_0_
  18.6 0.4 collective-permute-start.5
  19.0 0.4 shard_map.57.refs_0_
  19.4 17.1 %collective-permute-done.3.x_ref = f32[256,256]{1,0:T(8,128)S(1)} collective-permute-done((f32[256,256]{1,0:T(8,128)S(1)}, f32[256,256]{1,0:T(8,128)S(1)}, u32[]{:S(2)}, u32[]{:S(2)}) %collective-permute-start.3) | collective-permute-done | bytes 262176 | tf_op jit(solution)/shard_map/ppermute | solution.py:357
  36.5 0.4 shard_map.58.refs_0_
  36.8 10.0 %collective-permute-done.2.x_ref = f32[256,256]{1,0:T(8,128)S(1)} collective-permute-done((f32[256,256]{1,0:T(8,128)S(1)}, f32[256,256]{1,0:T(8,128)S(1)}, u32[]{:S(2)}, u32[]{:S(2)}) %collective-permute-start.2) | collective-permute-done | bytes 262176 | tf_op jit(solution)/shard_map/ppermute | solution.py:357
  46.9 0.4 shard_map.59.refs_0_
  47.3 0.4 shard_map.60.refs_0_
  47.6 0.4 shard_map.61.sum_ref
  48.0 0.5 shard_map.62
  48.6 0.1 collective-permute-start.6
  48.7 0.5 collective-permute-start.7
  49.2 0.1 collective-permute-start.8
  49.2 1.3 %collective-permute-done.8.refs_1_ = f32[16,128]{1,0:T(8,128)S(1)} collective-permute-done((f32[16,128]{1,0:T(8,128)S(1)}, f32[16,128]{1,0:T(8,128)S(1)}, u32[]{:S(2)}, u32[]{:S(2)}) %collective-permute-start.8) | collective-permute-done | bytes 8224 | tf_op jit(solution)/shard_map/ppermute | solution.py:357
  50.6 0.1 collective-permute-start.9
  50.7 0.8 %shard_map.64 = (bf16[256,512]{1,0:T(8,128)(2,1)S(1)}, bf16[256,512]{1,0:T(8,128)(2,1)S(1)}, bf16[256,256]{1,0:T(8,128)(2,1)S(1)}, bf16[256,256]{1,0:T(8,128)(2,1)S(1)}, f32[16,128]{1,0:T(8,128)S(1)}) custom-call(bf16[4,512,768]{2,1,0:T(8,128)(2,1)S(1)} %copy-done, f32[256,256]{1,0:T(8,128)S(1)} %get-tuple-element.20.sum_ref, ...), custom_call_target="tpu_custom_call" | custom-call | flops 1 | bytes 1 | tf_op jit(solution)/shard_map/pallas_call | solution.py:208
  51.5 0.6 collective-permute-done.9.x_ref
  52.1 0.7 %shard_map.65 = (bf16[256,256]{1,0:T(8,128)(2,1)S(1)}, bf16[256,256]{1,0:T(8,128)(2,1)S(1)}, f32[8,16,128]{2,1,0:T(8,128)S(1)}) custom-call(bf16[4,512,768]{2,1,0:T(8,128)(2,1)S(1)} %copy-done, f32[256,256]{1,0:T(8,128)S(1)} %collective-permute-done.7.sum_ref, f32[256,256]{1,0:T(8,128)S(1)} %collective-permute-done.9.x_ref, f32[1,1024]{1,0:T(1,128)S(1)} %bitcast.17, ...), custom_call_target="tpu_custom_call" | custom-call | flops 1 | bytes 1 | tf_op jit(solution)/shard_map/pallas_call | solution.py:208
  52.8 9.1 %all_to_all.5.grams_ref = f32[8,16,128]{2,1,0:T(8,128)S(1)} all-to-all(f32[8,16,128]{2,1,0:T(8,128)S(1)} %get-tuple-element.37), channel_id=1, replica_groups={{14,12,10,8,6,4,2,0},{15,13,11,9,7,5,3,1},{30,28,26,24,22,20,18,16},{31..., dimensions={0} | all-to-all | bytes 131072 | tf_op jit(solution)/shard_map/all_to_all | solution.py:396
  61.9 2.2 %shard_map.66 = (f32[8,2,16,1024]{3,2,1,0:T(8,128)}, f32[2,8,16,16]{3,2,1,0:T(8,128)}) custom-call(bf16[256,512]{1,0:T(8,128)(2,1)S(1)} %get-tuple-element.29.own_high_ref, bf16[256,512]{1,0:T(8,128)(2,1)S(1)} %get-tuple-element.30.own_low_ref, bf16[256,256]{1,0:T(8,128)(2,1)S(1)} %get-tuple-element.31.first_high_ref, ...), custom_call_target="tpu_custom_call" | custom-call | tf_op jit(solution)/shard_map/pallas_call | solution.py:346
  (10 shorter events, 0.0 us)
Async XLA Ops:
  1.6 17.0 %collective-permute-start.4 = (f32[256,256]{1,0:T(8,128)S(1)}, f32[256,256]{1,0:T(8,128)S(1)}, u32[]{:S(2)}, u32[]{:S(2)}) collective-permute-start(f32[256,256]{1,0:T(8,128)S(1)} %bitcast.14), channel_id=1, source_target_pairs={{0,12},{4,8},{8,4},{12,0},{1,13},{5,9},{9,5},{13,1},{2,14},{6,10},... | collective-permute-start | bytes 786440 | tf_op jit(solution)/shard_map/ppermute | solution.py:357
  7.7 28.8 %collective-permute-start.3 = (f32[256,256]{1,0:T(8,128)S(1)}, f32[256,256]{1,0:T(8,128)S(1)}, u32[]{:S(2)}, u32[]{:S(2)}) collective-permute-start(f32[256,256]{1,0:T(8,128)S(1)} %bitcast.13), channel_id=1, source_target_pairs={{0,8},{4,12},{8,0},{12,4},{1,9},{5,13},{9,1},{13,5},{2,10},{6,14},... | collective-permute-start | bytes 786440 | tf_op jit(solution)/shard_map/ppermute | solution.py:357
  8.8 38.1 %collective-permute-start.2 = (f32[256,256]{1,0:T(8,128)S(1)}, f32[256,256]{1,0:T(8,128)S(1)}, u32[]{:S(2)}, u32[]{:S(2)}) collective-permute-start(f32[256,256]{1,0:T(8,128)S(1)} %bitcast.12), channel_id=1, source_target_pairs={{0,8},{4,12},{8,0},{12,4},{1,9},{5,13},{9,1},{13,5},{2,10},{6,14},... | collective-permute-start | bytes 786440 | tf_op jit(solution)/shard_map/ppermute | solution.py:357
  12.7 34.5 %collective-permute-start.1 = (f32[256,256]{1,0:T(8,128)S(1)}, f32[256,256]{1,0:T(8,128)S(1)}, u32[]{:S(2)}, u32[]{:S(2)}) collective-permute-start(f32[256,256]{1,0:T(8,128)S(1)} %bitcast.11), channel_id=1, source_target_pairs={{0,4},{4,0},{8,12},{12,8},{1,5},{5,1},{9,13},{13,9},{2,6},{6,2},{1... | collective-permute-start | bytes 786440 | tf_op jit(solution)/shard_map/ppermute | solution.py:357
  13.8 4.2 %copy-start = (bf16[4,512,768]{2,1,0:T(8,128)(2,1)S(1)}, bf16[4,512,768]{2,1,0:T(8,128)(2,1)}, u32[]{:S(2)}) copy-start(bf16[4,512,768]{2,1,0:T(8,128)(2,1)} %constant.2.clone.t_ref) | copy-start | bytes 9437188
  13.8 33.8 %collective-permute-start = (f32[256,256]{1,0:T(8,128)S(1)}, f32[256,256]{1,0:T(8,128)S(1)}, u32[]{:S(2)}, u32[]{:S(2)}) collective-permute-start(f32[256,256]{1,0:T(8,128)S(1)} %bitcast.10), channel_id=1, source_target_pairs={{0,4},{4,0},{8,12},{12,8},{1,5},{5,1},{9,13},{13,9},{2,6},{6,2},{1... | collective-permute-start | bytes 786440 | tf_op jit(solution)/shard_map/ppermute | solution.py:357
  18.6 30.7 %collective-permute-start.5 = (f32[256,256]{1,0:T(8,128)S(1)}, f32[256,256]{1,0:T(8,128)S(1)}, u32[]{:S(2)}, u32[]{:S(2)}) collective-permute-start(f32[256,256]{1,0:T(8,128)S(1)} %bitcast.9), channel_id=1, source_target_pairs={{0,12},{4,8},{8,4},{12,0},{1,13},{5,9},{9,5},{13,1},{2,14},{6,10},... | collective-permute-start | bytes 786440 | tf_op jit(solution)/shard_map/ppermute | solution.py:357
  47.2 0.8 %copy-start.1 = (f32[1024]{0:T(1024)S(1)}, f32[1024]{0:T(1024)}, u32[]{:S(2)}) copy-start(f32[1024]{0:T(1024)} %param.4) | copy-start | bytes 12292
  48.6 2.0 %collective-permute-start.6 = (f32[256,256]{1,0:T(8,128)S(1)}, f32[256,256]{1,0:T(8,128)S(1)}, u32[]{:S(2)}, u32[]{:S(2)}) collective-permute-start(f32[256,256]{1,0:T(8,128)S(1)} %get-tuple-element.21), channel_id=1, source_target_pairs={{0,1},{1,0},{2,3},{3,2},{4,5},{5,4},{6,7},{7,6},{8,9},{9,8},{10,11... | collective-permute-start | bytes 786440 | tf_op jit(solution)/shard_map/ppermute | solution.py:357
  48.7 1.9 %collective-permute-start.7 = (f32[256,256]{1,0:T(8,128)S(1)}, f32[256,256]{1,0:T(8,128)S(1)}, u32[]{:S(2)}, u32[]{:S(2)}) collective-permute-start(f32[256,256]{1,0:T(8,128)S(1)} %get-tuple-element.22), channel_id=1, source_target_pairs={{0,1},{1,0},{2,3},{3,2},{4,5},{5,4},{6,7},{7,6},{8,9},{9,8},{10,11... | collective-permute-start | bytes 786440 | tf_op jit(solution)/shard_map/ppermute | solution.py:357
  49.2 1.4 %collective-permute-start.8 = (f32[16,128]{1,0:T(8,128)S(1)}, f32[16,128]{1,0:T(8,128)S(1)}, u32[]{:S(2)}, u32[]{:S(2)}) collective-permute-start(f32[16,128]{1,0:T(8,128)S(1)} %get-tuple-element.23), channel_id=1, source_target_pairs={{0,1},{1,0},{2,3},{3,2},{4,5},{5,4},{6,7},{7,6},{8,9},{9,8},{10,11... | collective-permute-start | bytes 24584 | tf_op jit(solution)/shard_map/ppermute | solution.py:357
  50.6 1.5 %collective-permute-start.9 = (f32[256,256]{1,0:T(8,128)S(1)}, f32[256,256]{1,0:T(8,128)S(1)}, u32[]{:S(2)}, u32[]{:S(2)}) collective-permute-start(f32[256,256]{1,0:T(8,128)S(1)} %collective-permute-done.5.x_ref), channel_id=1, source_target_pairs={{0,1},{1,0},{2,3},{3,2},{4,5},{5,4},{6,7},{7,6},{8,9},{9,8},{10,11... | collective-permute-start | bytes 786440 | tf_op jit(solution)/shard_map/ppermute | solution.py:357

commit v23 on v22

--- a/solution.py
+++ b/solution.py
@@ -377,7 +377,8 @@
 
     halves = ((0, early_rows), (early_rows, share - early_rows))
     sends = [(last, *halves[0])]
-    sends += [(k, *half) for k in range(n - 2, 0, -1) for half in halves]
+    sends += [(k, *halves[0]) for k in range(n - 2, 0, -1)]
+    sends += [(k, *halves[1]) for k in range(1, n - 1)]
     pieces = [(k, skip, send(k, skip, size)) for k, skip, size in sends]
     last_piece = send(last, *halves[1])
     before = early(tables, n, 0, 0, cut(snapshots, n, 0, rows, 0, share))

time: 64.6 us -> 64.6 us (level)
  waiting for transfers between devices: 29.1 us -> 28.3 us
  blocking collectives: 9.05 us -> 9.84 us
    all_to_all x1, blocking collectives: 9.05 us -> 9.84 us  [on_device(): lax.all_to_all(gram, ('space', 'tm'), split_axis=0, concat_axis=0, axis_i...]
    ppermute x10, waiting for transfers between devices: 29.1 us -> 28.3 us  [partner(): return lax.ppermute(value, axis, [(i, i ^ step) for i in range(size)])]
where the time goes in v23:
time: 64.6 us; the launch traced here: 64.1 us
  waiting for transfers between devices  28.3 us (44%)
  Pallas kernels  13.6 us (21%)
  starting transfers between devices  11.5 us (18%)
  blocking collectives  9.84 us (15%)
  between operations  0.83 us (1%)
    ppermute x10, waiting for transfers between devices, partner(): return lax.ppermute(value, axis, [(i, i ^ step) for i in range(size)])  28.3 us
    ppermute x10, starting transfers between devices, partner(): return lax.ppermute(value, axis, [(i, i ^ step) for i in range(size)])  11.5 us
    all_to_all x1, blocking collectives, on_device(): lax.all_to_all(gram, ('space', 'tm'), split_axis=0, concat_axis=0, axis_i...  9.84 us
    pallas_call x7, Pallas kernels, cut(): pl.pallas_call(functools.partial(cut_kernel, n, k, rows, skip), out_shape...  6.98 us
    pallas_call x6, Pallas kernels, early(): pl.pallas_call(functools.partial(early_kernel, n, k, skip), out_shape=jax...  2.44 us
    pallas_call x1, Pallas kernels, finish(): pl.pallas_call(functools.partial(finish_kernel, total), out_shape=(jax.Sh...  2.18 us
    pallas_call x2, Pallas kernels, last_part(): pl.pallas_call(functools.partial(last_part_kernel, n, k, bool(copies)), o...  1.49 us
  transfers between devices with their start and end apart: 10, of which 4 were waited for; matrix products, arithmetic and copies ran while one was open for 0% of the time, Pallas kernels for 15%

profile of v23, /device:TPU:0, one launch (start us, length us, event | category | flops | bytes accessed | tf_op | source)
XLA Modules:
  0.0 64.1 jit_solution(18423933286352949430)
XLA Ops:
  0.6 1.0 %shard_map.54 = f32[16,16,256]{2,1,0:T(8,128)S(1)} custom-call(f32[16,16,4096]{2,1,0:T(8,128)} %x_ref.13), custom_call_target="tpu_custom_call" | custom-call | flops 1 | bytes 1 | tf_op jit(solution)/shard_map/pallas_call | solution.py:82
  1.6 5.1 %collective-permute-start.4 = (f32[256,256]{1,0:T(8,128)S(1)}, f32[256,256]{1,0:T(8,128)S(1)}, u32[]{:S(2)}, u32[]{:S(2)}) collective-permute-start(f32[256,256]{1,0:T(8,128)S(1)} %bitcast.14), channel_id=1, source_target_pairs={{0,12},{4,8},{8,4},{12,0},{1,13},{5,9},{9,5},{13,1},{2,14},{6,10},... | collective-permute-start | bytes 786440 | tf_op jit(solution)/shard_map/ppermute | solution.py:357
  6.7 1.0 %shard_map.53 = f32[16,16,256]{2,1,0:T(8,128)S(1)} custom-call(f32[16,16,4096]{2,1,0:T(8,128)} %x_ref.13), custom_call_target="tpu_custom_call" | custom-call | flops 1 | bytes 1 | tf_op jit(solution)/shard_map/pallas_call | solution.py:82
  7.7 0.1 collective-permute-start.3
  7.8 1.0 %shard_map.52 = f32[16,16,256]{2,1,0:T(8,128)S(1)} custom-call(f32[16,16,4096]{2,1,0:T(8,128)} %x_ref.13), custom_call_target="tpu_custom_call" | custom-call | flops 1 | bytes 1 | tf_op jit(solution)/shard_map/pallas_call | solution.py:82
  8.8 0.6 collective-permute-start.2
  9.4 1.0 %shard_map.51 = f32[16,16,256]{2,1,0:T(8,128)S(1)} custom-call(f32[16,16,4096]{2,1,0:T(8,128)} %x_ref.13), custom_call_target="tpu_custom_call" | custom-call | flops 1 | bytes 1 | tf_op jit(solution)/shard_map/pallas_call | solution.py:82
  10.4 1.5 %collective-permute-start.1 = (f32[256,256]{1,0:T(8,128)S(1)}, f32[256,256]{1,0:T(8,128)S(1)}, u32[]{:S(2)}, u32[]{:S(2)}) collective-permute-start(f32[256,256]{1,0:T(8,128)S(1)} %bitcast.11), channel_id=1, source_target_pairs={{0,4},{4,0},{8,12},{12,8},{1,5},{5,1},{9,13},{13,9},{2,6},{6,2},{1... | collective-permute-start | bytes 786440 | tf_op jit(solution)/shard_map/ppermute | solution.py:357
  11.9 1.0 %shard_map.50 = f32[16,16,256]{2,1,0:T(8,128)S(1)} custom-call(f32[16,16,4096]{2,1,0:T(8,128)} %x_ref.13), custom_call_target="tpu_custom_call" | custom-call | flops 1 | bytes 1 | tf_op jit(solution)/shard_map/pallas_call | solution.py:82
  12.9 3.0 %collective-permute-start = (f32[256,256]{1,0:T(8,128)S(1)}, f32[256,256]{1,0:T(8,128)S(1)}, u32[]{:S(2)}, u32[]{:S(2)}) collective-permute-start(f32[256,256]{1,0:T(8,128)S(1)} %bitcast.10), channel_id=1, source_target_pairs={{0,8},{4,12},{8,0},{12,4},{1,9},{5,13},{9,1},{13,5},{2,10},{6,14},... | collective-permute-start | bytes 786440 | tf_op jit(solution)/shard_map/ppermute | solution.py:357
  15.9 1.1 %shard_map.55 = f32[16,16,512]{2,1,0:T(8,128)S(1)} custom-call(f32[16,16,4096]{2,1,0:T(8,128)} %x_ref.13), custom_call_target="tpu_custom_call" | custom-call | flops 1 | bytes 1 | tf_op jit(solution)/shard_map/pallas_call | solution.py:82
  17.0 1.0 %shard_map.63 = f32[16,16,256]{2,1,0:T(8,128)S(1)} custom-call(f32[16,16,4096]{2,1,0:T(8,128)} %x_ref.13), custom_call_target="tpu_custom_call" | custom-call | flops 1 | bytes 1 | tf_op jit(solution)/shard_map/pallas_call | solution.py:82
  18.0 0.6 shard_map.56.refs_0_
  18.6 0.4 collective-permute-start.5
  19.0 0.4 shard_map.57.refs_0_
  19.4 21.9 %collective-permute-done.3.x_ref = f32[256,256]{1,0:T(8,128)S(1)} collective-permute-done((f32[256,256]{1,0:T(8,128)S(1)}, f32[256,256]{1,0:T(8,128)S(1)}, u32[]{:S(2)}, u32[]{:S(2)}) %collective-permute-start.3) | collective-permute-done | bytes 262176 | tf_op jit(solution)/shard_map/ppermute | solution.py:357
  41.3 0.4 shard_map.58.refs_0_
  41.7 0.4 shard_map.59.refs_0_
  42.1 0.4 shard_map.60.refs_0_
  42.5 4.4 %collective-permute-done.x_ref = f32[256,256]{1,0:T(8,128)S(1)} collective-permute-done((f32[256,256]{1,0:T(8,128)S(1)}, f32[256,256]{1,0:T(8,128)S(1)}, u32[]{:S(2)}, u32[]{:S(2)}) %collective-permute-start) | collective-permute-done | bytes 262176 | tf_op jit(solution)/shard_map/ppermute | solution.py:357
  46.9 0.4 shard_map.61.sum_ref
  47.3 0.5 shard_map.62
  47.8 0.1 collective-permute-start.6
  47.9 0.5 collective-permute-start.7
  48.4 0.1 collective-permute-start.8
  48.5 1.3 %collective-permute-done.8.refs_1_ = f32[16,128]{1,0:T(8,128)S(1)} collective-permute-done((f32[16,128]{1,0:T(8,128)S(1)}, f32[16,128]{1,0:T(8,128)S(1)}, u32[]{:S(2)}, u32[]{:S(2)}) %collective-permute-start.8) | collective-permute-done | bytes 8224 | tf_op jit(solution)/shard_map/ppermute | solution.py:357
  49.8 0.1 collective-permute-start.9
  50.0 0.8 %shard_map.64 = (bf16[256,512]{1,0:T(8,128)(2,1)S(1)}, bf16[256,512]{1,0:T(8,128)(2,1)S(1)}, bf16[256,256]{1,0:T(8,128)(2,1)S(1)}, bf16[256,256]{1,0:T(8,128)(2,1)S(1)}, f32[16,128]{1,0:T(8,128)S(1)}) custom-call(bf16[4,512,768]{2,1,0:T(8,128)(2,1)S(1)} %copy-done, f32[256,256]{1,0:T(8,128)S(1)} %get-tuple-element.20.sum_ref, ...), custom_call_target="tpu_custom_call" | custom-call | flops 1 | bytes 1 | tf_op jit(solution)/shard_map/pallas_call | solution.py:208
  50.8 0.6 collective-permute-done.9.x_ref
  51.4 0.7 %shard_map.65 = (bf16[256,256]{1,0:T(8,128)(2,1)S(1)}, bf16[256,256]{1,0:T(8,128)(2,1)S(1)}, f32[8,16,128]{2,1,0:T(8,128)S(1)}) custom-call(bf16[4,512,768]{2,1,0:T(8,128)(2,1)S(1)} %copy-done, f32[256,256]{1,0:T(8,128)S(1)} %collective-permute-done.7.sum_ref, f32[256,256]{1,0:T(8,128)S(1)} %collective-permute-done.9.x_ref, f32[1,1024]{1,0:T(1,128)S(1)} %bitcast.17, ...), custom_call_target="tpu_custom_call" | custom-call | flops 1 | bytes 1 | tf_op jit(solution)/shard_map/pallas_call | solution.py:208
  52.1 9.8 %all_to_all.5.grams_ref = f32[8,16,128]{2,1,0:T(8,128)S(1)} all-to-all(f32[8,16,128]{2,1,0:T(8,128)S(1)} %get-tuple-element.37), channel_id=1, replica_groups={{14,12,10,8,6,4,2,0},{15,13,11,9,7,5,3,1},{30,28,26,24,22,20,18,16},{31..., dimensions={0} | all-to-all | bytes 131072 | tf_op jit(solution)/shard_map/all_to_all | solution.py:397
  61.9 2.2 %shard_map.66 = (f32[8,2,16,1024]{3,2,1,0:T(8,128)}, f32[2,8,16,16]{3,2,1,0:T(8,128)}) custom-call(bf16[256,512]{1,0:T(8,128)(2,1)S(1)} %get-tuple-element.29.own_high_ref, bf16[256,512]{1,0:T(8,128)(2,1)S(1)} %get-tuple-element.30.own_low_ref, bf16[256,256]{1,0:T(8,128)(2,1)S(1)} %get-tuple-element.31.first_high_ref, ...), custom_call_target="tpu_custom_call" | custom-call | tf_op jit(solution)/shard_map/pallas_call | solution.py:346
  (10 shorter events, 0.0 us)
Async XLA Ops:
  1.6 17.0 %collective-permute-start.4 = (f32[256,256]{1,0:T(8,128)S(1)}, f32[256,256]{1,0:T(8,128)S(1)}, u32[]{:S(2)}, u32[]{:S(2)}) collective-permute-start(f32[256,256]{1,0:T(8,128)S(1)} %bitcast.14), channel_id=1, source_target_pairs={{0,12},{4,8},{8,4},{12,0},{1,13},{5,9},{9,5},{13,1},{2,14},{6,10},... | collective-permute-start | bytes 786440 | tf_op jit(solution)/shard_map/ppermute | solution.py:357
  7.7 33.6 %collective-permute-start.3 = (f32[256,256]{1,0:T(8,128)S(1)}, f32[256,256]{1,0:T(8,128)S(1)}, u32[]{:S(2)}, u32[]{:S(2)}) collective-permute-start(f32[256,256]{1,0:T(8,128)S(1)} %bitcast.13), channel_id=1, source_target_pairs={{0,8},{4,12},{8,0},{12,4},{1,9},{5,13},{9,1},{13,5},{2,10},{6,14},... | collective-permute-start | bytes 786440 | tf_op jit(solution)/shard_map/ppermute | solution.py:357
  8.8 32.9 %collective-permute-start.2 = (f32[256,256]{1,0:T(8,128)S(1)}, f32[256,256]{1,0:T(8,128)S(1)}, u32[]{:S(2)}, u32[]{:S(2)}) collective-permute-start(f32[256,256]{1,0:T(8,128)S(1)} %bitcast.12), channel_id=1, source_target_pairs={{0,4},{4,0},{8,12},{12,8},{1,5},{5,1},{9,13},{13,9},{2,6},{6,2},{1... | collective-permute-start | bytes 786440 | tf_op jit(solution)/shard_map/ppermute | solution.py:357
  10.4 31.7 %collective-permute-start.1 = (f32[256,256]{1,0:T(8,128)S(1)}, f32[256,256]{1,0:T(8,128)S(1)}, u32[]{:S(2)}, u32[]{:S(2)}) collective-permute-start(f32[256,256]{1,0:T(8,128)S(1)} %bitcast.11), channel_id=1, source_target_pairs={{0,4},{4,0},{8,12},{12,8},{1,5},{5,1},{9,13},{13,9},{2,6},{6,2},{1... | collective-permute-start | bytes 786440 | tf_op jit(solution)/shard_map/ppermute | solution.py:357
  12.9 5.1 %copy-start = (bf16[4,512,768]{2,1,0:T(8,128)(2,1)S(1)}, bf16[4,512,768]{2,1,0:T(8,128)(2,1)}, u32[]{:S(2)}) copy-start(bf16[4,512,768]{2,1,0:T(8,128)(2,1)} %constant.2.clone.t_ref) | copy-start | bytes 9437188
  12.9 34.0 %collective-permute-start = (f32[256,256]{1,0:T(8,128)S(1)}, f32[256,256]{1,0:T(8,128)S(1)}, u32[]{:S(2)}, u32[]{:S(2)}) collective-permute-start(f32[256,256]{1,0:T(8,128)S(1)} %bitcast.10), channel_id=1, source_target_pairs={{0,8},{4,12},{8,0},{12,4},{1,9},{5,13},{9,1},{13,5},{2,10},{6,14},... | collective-permute-start | bytes 786440 | tf_op jit(solution)/shard_map/ppermute | solution.py:357
  18.6 29.9 %collective-permute-start.5 = (f32[256,256]{1,0:T(8,128)S(1)}, f32[256,256]{1,0:T(8,128)S(1)}, u32[]{:S(2)}, u32[]{:S(2)}) collective-permute-start(f32[256,256]{1,0:T(8,128)S(1)} %bitcast.9), channel_id=1, source_target_pairs={{0,12},{4,8},{8,4},{12,0},{1,13},{5,9},{9,5},{13,1},{2,14},{6,10},... | collective-permute-start | bytes 786440 | tf_op jit(solution)/shard_map/ppermute | solution.py:357
  42.1 5.2 %copy-start.1 = (f32[1024]{0:T(1024)S(1)}, f32[1024]{0:T(1024)}, u32[]{:S(2)}) copy-start(f32[1024]{0:T(1024)} %param.4) | copy-start | bytes 12292
  47.8 2.0 %collective-permute-start.6 = (f32[256,256]{1,0:T(8,128)S(1)}, f32[256,256]{1,0:T(8,128)S(1)}, u32[]{:S(2)}, u32[]{:S(2)}) collective-permute-start(f32[256,256]{1,0:T(8,128)S(1)} %get-tuple-element.21), channel_id=1, source_target_pairs={{0,1},{1,0},{2,3},{3,2},{4,5},{5,4},{6,7},{7,6},{8,9},{9,8},{10,11... | collective-permute-start | bytes 786440 | tf_op jit(solution)/shard_map/ppermute | solution.py:357
  47.9 1.9 %collective-permute-start.7 = (f32[256,256]{1,0:T(8,128)S(1)}, f32[256,256]{1,0:T(8,128)S(1)}, u32[]{:S(2)}, u32[]{:S(2)}) collective-permute-start(f32[256,256]{1,0:T(8,128)S(1)} %get-tuple-element.22), channel_id=1, source_target_pairs={{0,1},{1,0},{2,3},{3,2},{4,5},{5,4},{6,7},{7,6},{8,9},{9,8},{10,11... | collective-permute-start | bytes 786440 | tf_op jit(solution)/shard_map/ppermute | solution.py:357
  48.4 1.4 %collective-permute-start.8 = (f32[16,128]{1,0:T(8,128)S(1)}, f32[16,128]{1,0:T(8,128)S(1)}, u32[]{:S(2)}, u32[]{:S(2)}) collective-permute-start(f32[16,128]{1,0:T(8,128)S(1)} %get-tuple-element.23), channel_id=1, source_target_pairs={{0,1},{1,0},{2,3},{3,2},{4,5},{5,4},{6,7},{7,6},{8,9},{9,8},{10,11... | collective-permute-start | bytes 24584 | tf_op jit(solution)/shard_map/ppermute | solution.py:357
  49.8 1.5 %collective-permute-start.9 = (f32[256,256]{1,0:T(8,128)S(1)}, f32[256,256]{1,0:T(8,128)S(1)}, u32[]{:S(2)}, u32[]{:S(2)}) collective-permute-start(f32[256,256]{1,0:T(8,128)S(1)} %collective-permute-done.5.x_ref), channel_id=1, source_target_pairs={{0,1},{1,0},{2,3},{3,2},{4,5},{5,4},{6,7},{7,6},{8,9},{9,8},{10,11... | collective-permute-start | bytes 786440 | tf_op jit(solution)/shard_map/ppermute | solution.py:357

commit v24 on v23

--- a/solution.py
+++ b/solution.py
@@ -393,7 +393,7 @@
         tables, n, last, 0, rest, piece, weights, gram, lent, own, other
     )
     *last_parts, gram = last_part(tables, n, last, targets, later, raw, weights, gram)
-    order = list(range(targets - 1, -1, -1))
+    order = [z * tm_count + x for z in range(n - 1, -1, -1) for x in range(tm_count)]
     grams = lax.all_to_all(
         gram,
         ("space", "tm"),

time: 64.6 us -> 65.2 us (level)
  blocking collectives: 9.84 us -> 10.5 us
where the time goes in v24:
time: 65.2 us; the launch traced here: 64.7 us
  waiting for transfers between devices  28.3 us (43%)
  Pallas kernels  13.6 us (21%)
  starting transfers between devices  11.5 us (18%)
  blocking collectives  10.5 us (16%)
  between operations  0.83 us (1%)
    ppermute x10, waiting for transfers between devices, partner(): return lax.ppermute(value, axis, [(i, i ^ step) for i in range(size)])  28.3 us
    ppermute x10, starting transfers between devices, partner(): return lax.ppermute(value, axis, [(i, i ^ step) for i in range(size)])  11.5 us
    all_to_all x1, blocking collectives, on_device(): lax.all_to_all(gram, ('space', 'tm'), split_axis=0, concat_axis=0, axis_i...  10.5 us
    pallas_call x7, Pallas kernels, cut(): pl.pallas_call(functools.partial(cut_kernel, n, k, rows, skip), out_shape...  6.98 us
    pallas_call x6, Pallas kernels, early(): pl.pallas_call(functools.partial(early_kernel, n, k, skip), out_shape=jax...  2.44 us
    pallas_call x1, Pallas kernels, finish(): pl.pallas_call(functools.partial(finish_kernel, total), out_shape=(jax.Sh...  2.17 us
    pallas_call x2, Pallas kernels, last_part(): pl.pallas_call(functools.partial(last_part_kernel, n, k, bool(copies)), o...  1.49 us
  transfers between devices with their start and end apart: 10, of which 4 were waited for; matrix products, arithmetic and copies ran while one was open for 0% of the time, Pallas kernels for 15%

profile of v24, /device:TPU:0, one launch (start us, length us, event | category | flops | bytes accessed | tf_op | source)
XLA Modules:
  0.0 64.7 jit_solution(10527425129113008555)
XLA Ops:
  0.6 1.0 %shard_map.54 = f32[16,16,256]{2,1,0:T(8,128)S(1)} custom-call(f32[16,16,4096]{2,1,0:T(8,128)} %x_ref.13), custom_call_target="tpu_custom_call" | custom-call | flops 1 | bytes 1 | tf_op jit(solution)/shard_map/pallas_call | solution.py:82
  1.6 5.1 %collective-permute-start.4 = (f32[256,256]{1,0:T(8,128)S(1)}, f32[256,256]{1,0:T(8,128)S(1)}, u32[]{:S(2)}, u32[]{:S(2)}) collective-permute-start(f32[256,256]{1,0:T(8,128)S(1)} %bitcast.14), channel_id=1, source_target_pairs={{0,12},{4,8},{8,4},{12,0},{1,13},{5,9},{9,5},{13,1},{2,14},{6,10},... | collective-permute-start | bytes 786440 | tf_op jit(solution)/shard_map/ppermute | solution.py:357
  6.7 1.0 %shard_map.53 = f32[16,16,256]{2,1,0:T(8,128)S(1)} custom-call(f32[16,16,4096]{2,1,0:T(8,128)} %x_ref.13), custom_call_target="tpu_custom_call" | custom-call | flops 1 | bytes 1 | tf_op jit(solution)/shard_map/pallas_call | solution.py:82
  7.7 0.1 collective-permute-start.3
  7.8 1.0 %shard_map.52 = f32[16,16,256]{2,1,0:T(8,128)S(1)} custom-call(f32[16,16,4096]{2,1,0:T(8,128)} %x_ref.13), custom_call_target="tpu_custom_call" | custom-call | flops 1 | bytes 1 | tf_op jit(solution)/shard_map/pallas_call | solution.py:82
  8.8 0.6 collective-permute-start.2
  9.4 1.0 %shard_map.51 = f32[16,16,256]{2,1,0:T(8,128)S(1)} custom-call(f32[16,16,4096]{2,1,0:T(8,128)} %x_ref.13), custom_call_target="tpu_custom_call" | custom-call | flops 1 | bytes 1 | tf_op jit(solution)/shard_map/pallas_call | solution.py:82
  10.4 1.5 %collective-permute-start.1 = (f32[256,256]{1,0:T(8,128)S(1)}, f32[256,256]{1,0:T(8,128)S(1)}, u32[]{:S(2)}, u32[]{:S(2)}) collective-permute-start(f32[256,256]{1,0:T(8,128)S(1)} %bitcast.11), channel_id=1, source_target_pairs={{0,4},{4,0},{8,12},{12,8},{1,5},{5,1},{9,13},{13,9},{2,6},{6,2},{1... | collective-permute-start | bytes 786440 | tf_op jit(solution)/shard_map/ppermute | solution.py:357
  11.9 1.0 %shard_map.50 = f32[16,16,256]{2,1,0:T(8,128)S(1)} custom-call(f32[16,16,4096]{2,1,0:T(8,128)} %x_ref.13), custom_call_target="tpu_custom_call" | custom-call | flops 1 | bytes 1 | tf_op jit(solution)/shard_map/pallas_call | solution.py:82
  12.9 3.0 %collective-permute-start = (f32[256,256]{1,0:T(8,128)S(1)}, f32[256,256]{1,0:T(8,128)S(1)}, u32[]{:S(2)}, u32[]{:S(2)}) collective-permute-start(f32[256,256]{1,0:T(8,128)S(1)} %bitcast.10), channel_id=1, source_target_pairs={{0,8},{4,12},{8,0},{12,4},{1,9},{5,13},{9,1},{13,5},{2,10},{6,14},... | collective-permute-start | bytes 786440 | tf_op jit(solution)/shard_map/ppermute | solution.py:357
  15.9 1.1 %shard_map.55 = f32[16,16,512]{2,1,0:T(8,128)S(1)} custom-call(f32[16,16,4096]{2,1,0:T(8,128)} %x_ref.13), custom_call_target="tpu_custom_call" | custom-call | flops 1 | bytes 1 | tf_op jit(solution)/shard_map/pallas_call | solution.py:82
  17.0 1.0 %shard_map.63 = f32[16,16,256]{2,1,0:T(8,128)S(1)} custom-call(f32[16,16,4096]{2,1,0:T(8,128)} %x_ref.13), custom_call_target="tpu_custom_call" | custom-call | flops 1 | bytes 1 | tf_op jit(solution)/shard_map/pallas_call | solution.py:82
  18.0 0.6 shard_map.56.refs_0_
  18.6 0.4 collective-permute-start.5
  19.0 0.4 shard_map.57.refs_0_
  19.4 21.9 %collective-permute-done.3.x_ref = f32[256,256]{1,0:T(8,128)S(1)} collective-permute-done((f32[256,256]{1,0:T(8,128)S(1)}, f32[256,256]{1,0:T(8,128)S(1)}, u32[]{:S(2)}, u32[]{:S(2)}) %collective-permute-start.3) | collective-permute-done | bytes 262176 | tf_op jit(solution)/shard_map/ppermute | solution.py:357
  41.3 0.4 shard_map.58.refs_0_
  41.7 0.4 shard_map.59.refs_0_
  42.1 0.4 shard_map.60.refs_0_
  42.5 4.4 %collective-permute-done.x_ref = f32[256,256]{1,0:T(8,128)S(1)} collective-permute-done((f32[256,256]{1,0:T(8,128)S(1)}, f32[256,256]{1,0:T(8,128)S(1)}, u32[]{:S(2)}, u32[]{:S(2)}) %collective-permute-start) | collective-permute-done | bytes 262176 | tf_op jit(solution)/shard_map/ppermute | solution.py:357
  46.9 0.4 shard_map.61.sum_ref
  47.3 0.5 shard_map.62
  47.8 0.1 collective-permute-start.6
  47.9 0.5 collective-permute-start.7
  48.4 0.1 collective-permute-start.8
  48.5 1.3 %collective-permute-done.8.refs_1_ = f32[16,128]{1,0:T(8,128)S(1)} collective-permute-done((f32[16,128]{1,0:T(8,128)S(1)}, f32[16,128]{1,0:T(8,128)S(1)}, u32[]{:S(2)}, u32[]{:S(2)}) %collective-permute-start.8) | collective-permute-done | bytes 8224 | tf_op jit(solution)/shard_map/ppermute | solution.py:357
  49.8 0.1 collective-permute-start.9
  50.0 0.8 %shard_map.64 = (bf16[256,512]{1,0:T(8,128)(2,1)S(1)}, bf16[256,512]{1,0:T(8,128)(2,1)S(1)}, bf16[256,256]{1,0:T(8,128)(2,1)S(1)}, bf16[256,256]{1,0:T(8,128)(2,1)S(1)}, f32[16,128]{1,0:T(8,128)S(1)}) custom-call(bf16[4,512,768]{2,1,0:T(8,128)(2,1)S(1)} %copy-done, f32[256,256]{1,0:T(8,128)S(1)} %get-tuple-element.20.sum_ref, ...), custom_call_target="tpu_custom_call" | custom-call | flops 1 | bytes 1 | tf_op jit(solution)/shard_map/pallas_call | solution.py:208
  50.8 0.6 collective-permute-done.9.x_ref
  51.4 0.7 %shard_map.65 = (bf16[256,256]{1,0:T(8,128)(2,1)S(1)}, bf16[256,256]{1,0:T(8,128)(2,1)S(1)}, f32[8,16,128]{2,1,0:T(8,128)S(1)}) custom-call(bf16[4,512,768]{2,1,0:T(8,128)(2,1)S(1)} %copy-done, f32[256,256]{1,0:T(8,128)S(1)} %collective-permute-done.7.sum_ref, f32[256,256]{1,0:T(8,128)S(1)} %collective-permute-done.9.x_ref, f32[1,1024]{1,0:T(1,128)S(1)} %bitcast.17, ...), custom_call_target="tpu_custom_call" | custom-call | flops 1 | bytes 1 | tf_op jit(solution)/shard_map/pallas_call | solution.py:208
  52.1 10.5 %all_to_all.5.grams_ref = f32[8,16,128]{2,1,0:T(8,128)S(1)} all-to-all(f32[8,16,128]{2,1,0:T(8,128)S(1)} %get-tuple-element.37), channel_id=1, replica_groups={{12,14,8,10,4,6,0,2},{13,15,9,11,5,7,1,3},{28,30,24,26,20,22,16,18},{29..., dimensions={0} | all-to-all | bytes 131072 | tf_op jit(solution)/shard_map/all_to_all | solution.py:397
  62.6 2.2 %shard_map.66 = (f32[8,2,16,1024]{3,2,1,0:T(8,128)}, f32[2,8,16,16]{3,2,1,0:T(8,128)}) custom-call(bf16[256,512]{1,0:T(8,128)(2,1)S(1)} %get-tuple-element.29.own_high_ref, bf16[256,512]{1,0:T(8,128)(2,1)S(1)} %get-tuple-element.30.own_low_ref, bf16[256,256]{1,0:T(8,128)(2,1)S(1)} %get-tuple-element.31.first_high_ref, ...), custom_call_target="tpu_custom_call" | custom-call | tf_op jit(solution)/shard_map/pallas_call | solution.py:346
  (10 shorter events, 0.0 us)
Async XLA Ops:
  1.6 17.0 %collective-permute-start.4 = (f32[256,256]{1,0:T(8,128)S(1)}, f32[256,256]{1,0:T(8,128)S(1)}, u32[]{:S(2)}, u32[]{:S(2)}) collective-permute-start(f32[256,256]{1,0:T(8,128)S(1)} %bitcast.14), channel_id=1, source_target_pairs={{0,12},{4,8},{8,4},{12,0},{1,13},{5,9},{9,5},{13,1},{2,14},{6,10},... | collective-permute-start | bytes 786440 | tf_op jit(solution)/shard_map/ppermute | solution.py:357
  7.7 33.6 %collective-permute-start.3 = (f32[256,256]{1,0:T(8,128)S(1)}, f32[256,256]{1,0:T(8,128)S(1)}, u32[]{:S(2)}, u32[]{:S(2)}) collective-permute-start(f32[256,256]{1,0:T(8,128)S(1)} %bitcast.13), channel_id=1, source_target_pairs={{0,8},{4,12},{8,0},{12,4},{1,9},{5,13},{9,1},{13,5},{2,10},{6,14},... | collective-permute-start | bytes 786440 | tf_op jit(solution)/shard_map/ppermute | solution.py:357
  8.8 32.9 %collective-permute-start.2 = (f32[256,256]{1,0:T(8,128)S(1)}, f32[256,256]{1,0:T(8,128)S(1)}, u32[]{:S(2)}, u32[]{:S(2)}) collective-permute-start(f32[256,256]{1,0:T(8,128)S(1)} %bitcast.12), channel_id=1, source_target_pairs={{0,4},{4,0},{8,12},{12,8},{1,5},{5,1},{9,13},{13,9},{2,6},{6,2},{1... | collective-permute-start | bytes 786440 | tf_op jit(solution)/shard_map/ppermute | solution.py:357
  10.4 31.7 %collective-permute-start.1 = (f32[256,256]{1,0:T(8,128)S(1)}, f32[256,256]{1,0:T(8,128)S(1)}, u32[]{:S(2)}, u32[]{:S(2)}) collective-permute-start(f32[256,256]{1,0:T(8,128)S(1)} %bitcast.11), channel_id=1, source_target_pairs={{0,4},{4,0},{8,12},{12,8},{1,5},{5,1},{9,13},{13,9},{2,6},{6,2},{1... | collective-permute-start | bytes 786440 | tf_op jit(solution)/shard_map/ppermute | solution.py:357
  12.9 5.1 %copy-start = (bf16[4,512,768]{2,1,0:T(8,128)(2,1)S(1)}, bf16[4,512,768]{2,1,0:T(8,128)(2,1)}, u32[]{:S(2)}) copy-start(bf16[4,512,768]{2,1,0:T(8,128)(2,1)} %constant.2.clone.t_ref) | copy-start | bytes 9437188
  12.9 34.0 %collective-permute-start = (f32[256,256]{1,0:T(8,128)S(1)}, f32[256,256]{1,0:T(8,128)S(1)}, u32[]{:S(2)}, u32[]{:S(2)}) collective-permute-start(f32[256,256]{1,0:T(8,128)S(1)} %bitcast.10), channel_id=1, source_target_pairs={{0,8},{4,12},{8,0},{12,4},{1,9},{5,13},{9,1},{13,5},{2,10},{6,14},... | collective-permute-start | bytes 786440 | tf_op jit(solution)/shard_map/ppermute | solution.py:357
  18.6 29.9 %collective-permute-start.5 = (f32[256,256]{1,0:T(8,128)S(1)}, f32[256,256]{1,0:T(8,128)S(1)}, u32[]{:S(2)}, u32[]{:S(2)}) collective-permute-start(f32[256,256]{1,0:T(8,128)S(1)} %bitcast.9), channel_id=1, source_target_pairs={{0,12},{4,8},{8,4},{12,0},{1,13},{5,9},{9,5},{13,1},{2,14},{6,10},... | collective-permute-start | bytes 786440 | tf_op jit(solution)/shard_map/ppermute | solution.py:357
  42.1 5.2 %copy-start.1 = (f32[1024]{0:T(1024)S(1)}, f32[1024]{0:T(1024)}, u32[]{:S(2)}) copy-start(f32[1024]{0:T(1024)} %param.4) | copy-start | bytes 12292
  47.8 2.0 %collective-permute-start.6 = (f32[256,256]{1,0:T(8,128)S(1)}, f32[256,256]{1,0:T(8,128)S(1)}, u32[]{:S(2)}, u32[]{:S(2)}) collective-permute-start(f32[256,256]{1,0:T(8,128)S(1)} %get-tuple-element.21), channel_id=1, source_target_pairs={{0,1},{1,0},{2,3},{3,2},{4,5},{5,4},{6,7},{7,6},{8,9},{9,8},{10,11... | collective-permute-start | bytes 786440 | tf_op jit(solution)/shard_map/ppermute | solution.py:357
  47.9 1.9 %collective-permute-start.7 = (f32[256,256]{1,0:T(8,128)S(1)}, f32[256,256]{1,0:T(8,128)S(1)}, u32[]{:S(2)}, u32[]{:S(2)}) collective-permute-start(f32[256,256]{1,0:T(8,128)S(1)} %get-tuple-element.22), channel_id=1, source_target_pairs={{0,1},{1,0},{2,3},{3,2},{4,5},{5,4},{6,7},{7,6},{8,9},{9,8},{10,11... | collective-permute-start | bytes 786440 | tf_op jit(solution)/shard_map/ppermute | solution.py:357
  48.4 1.4 %collective-permute-start.8 = (f32[16,128]{1,0:T(8,128)S(1)}, f32[16,128]{1,0:T(8,128)S(1)}, u32[]{:S(2)}, u32[]{:S(2)}) collective-permute-start(f32[16,128]{1,0:T(8,128)S(1)} %get-tuple-element.23), channel_id=1, source_target_pairs={{0,1},{1,0},{2,3},{3,2},{4,5},{5,4},{6,7},{7,6},{8,9},{9,8},{10,11... | collective-permute-start | bytes 24584 | tf_op jit(solution)/shard_map/ppermute | solution.py:357
  49.8 1.5 %collective-permute-start.9 = (f32[256,256]{1,0:T(8,128)S(1)}, f32[256,256]{1,0:T(8,128)S(1)}, u32[]{:S(2)}, u32[]{:S(2)}) collective-permute-start(f32[256,256]{1,0:T(8,128)S(1)} %collective-permute-done.5.x_ref), channel_id=1, source_target_pairs={{0,1},{1,0},{2,3},{3,2},{4,5},{5,4},{6,7},{7,6},{8,9},{9,8},{10,11... | collective-permute-start | bytes 786440 | tf_op jit(solution)/shard_map/ppermute | solution.py:357

commit v25 on v23

--- a/solution.py
+++ b/solution.py
@@ -245,12 +245,15 @@
     group_c = lax.broadcasted_iota(jnp.int32, (width, width), 1) // NB
     same = group_r == group_c
     ones = jnp.where(same, 1.0, 0.0).astype(jnp.bfloat16)
-    spread = jnp.zeros(stacked.shape, jnp.float32)
-    rest = stacked
+    pieces, rest = [], stacked
     for _ in range(3):
-        piece = rest.astype(jnp.bfloat16)
-        rest = rest - piece.astype(jnp.float32)
-        spread = spread + jnp.dot(piece, ones, preferred_element_type=jnp.float32)
+        pieces.append(rest.astype(jnp.bfloat16))
+        rest = rest - pieces[-1].astype(jnp.float32)
+    spread = jnp.dot(
+        jnp.concatenate(pieces, axis=1),
+        jnp.concatenate([ones] * 3, axis=0),
+        preferred_element_type=jnp.float32,
+    )
     col_re = [[spread[j * NB + 8 * h : j * NB + 8 * h + 8] for h in (0, 1)] for j in range(NB)]
     base = NB * NB
     col_im = [

time: 64.6 us -> 64.5 us (level)
  no operation moved by 1% of the time
where the time goes in v25:
time: 64.5 us; the launch traced here: 64 us
  waiting for transfers between devices  28.3 us (44%)
  Pallas kernels  13.6 us (21%)
  starting transfers between devices  11.5 us (18%)
  blocking collectives  9.84 us (15%)
  between operations  0.83 us (1%)
    ppermute x10, waiting for transfers between devices, partner(): return lax.ppermute(value, axis, [(i, i ^ step) for i in range(size)])  28.3 us
    ppermute x10, starting transfers between devices, partner(): return lax.ppermute(value, axis, [(i, i ^ step) for i in range(size)])  11.5 us
    all_to_all x1, blocking collectives, on_device(): lax.all_to_all(gram, ('space', 'tm'), split_axis=0, concat_axis=0, axis_i...  9.84 us
    pallas_call x7, Pallas kernels, cut(): pl.pallas_call(functools.partial(cut_kernel, n, k, rows, skip), out_shape...  6.98 us
    pallas_call x6, Pallas kernels, early(): pl.pallas_call(functools.partial(early_kernel, n, k, skip), out_shape=jax...  2.44 us
    pallas_call x1, Pallas kernels, finish(): pl.pallas_call(functools.partial(finish_kernel, total), out_shape=(jax.Sh...  2.1 us
    pallas_call x2, Pallas kernels, last_part(): pl.pallas_call(functools.partial(last_part_kernel, n, k, bool(copies)), o...  1.49 us
  transfers between devices with their start and end apart: 10, of which 4 were waited for; matrix products, arithmetic and copies ran while one was open for 0% of the time, Pallas kernels for 15%

profile of v25, /device:TPU:0, one launch (start us, length us, event | category | flops | bytes accessed | tf_op | source)
XLA Modules:
  0.0 64.0 jit_solution(16169541597929732137)
XLA Ops:
  0.6 1.0 %shard_map.54 = f32[16,16,256]{2,1,0:T(8,128)S(1)} custom-call(f32[16,16,4096]{2,1,0:T(8,128)} %x_ref.13), custom_call_target="tpu_custom_call" | custom-call | flops 1 | bytes 1 | tf_op jit(solution)/shard_map/pallas_call | solution.py:82
  1.6 5.1 %collective-permute-start.4 = (f32[256,256]{1,0:T(8,128)S(1)}, f32[256,256]{1,0:T(8,128)S(1)}, u32[]{:S(2)}, u32[]{:S(2)}) collective-permute-start(f32[256,256]{1,0:T(8,128)S(1)} %bitcast.14), channel_id=1, source_target_pairs={{0,12},{4,8},{8,4},{12,0},{1,13},{5,9},{9,5},{13,1},{2,14},{6,10},... | collective-permute-start | bytes 786440 | tf_op jit(solution)/shard_map/ppermute | solution.py:360
  6.7 1.0 %shard_map.53 = f32[16,16,256]{2,1,0:T(8,128)S(1)} custom-call(f32[16,16,4096]{2,1,0:T(8,128)} %x_ref.13), custom_call_target="tpu_custom_call" | custom-call | flops 1 | bytes 1 | tf_op jit(solution)/shard_map/pallas_call | solution.py:82
  7.7 0.1 collective-permute-start.3
  7.8 1.0 %shard_map.52 = f32[16,16,256]{2,1,0:T(8,128)S(1)} custom-call(f32[16,16,4096]{2,1,0:T(8,128)} %x_ref.13), custom_call_target="tpu_custom_call" | custom-call | flops 1 | bytes 1 | tf_op jit(solution)/shard_map/pallas_call | solution.py:82
  8.8 0.6 collective-permute-start.2
  9.4 1.0 %shard_map.51 = f32[16,16,256]{2,1,0:T(8,128)S(1)} custom-call(f32[16,16,4096]{2,1,0:T(8,128)} %x_ref.13), custom_call_target="tpu_custom_call" | custom-call | flops 1 | bytes 1 | tf_op jit(solution)/shard_map/pallas_call | solution.py:82
  10.4 1.5 %collective-permute-start.1 = (f32[256,256]{1,0:T(8,128)S(1)}, f32[256,256]{1,0:T(8,128)S(1)}, u32[]{:S(2)}, u32[]{:S(2)}) collective-permute-start(f32[256,256]{1,0:T(8,128)S(1)} %bitcast.11), channel_id=1, source_target_pairs={{0,4},{4,0},{8,12},{12,8},{1,5},{5,1},{9,13},{13,9},{2,6},{6,2},{1... | collective-permute-start | bytes 786440 | tf_op jit(solution)/shard_map/ppermute | solution.py:360
  11.9 1.0 %shard_map.50 = f32[16,16,256]{2,1,0:T(8,128)S(1)} custom-call(f32[16,16,4096]{2,1,0:T(8,128)} %x_ref.13), custom_call_target="tpu_custom_call" | custom-call | flops 1 | bytes 1 | tf_op jit(solution)/shard_map/pallas_call | solution.py:82
  12.9 3.0 %collective-permute-start = (f32[256,256]{1,0:T(8,128)S(1)}, f32[256,256]{1,0:T(8,128)S(1)}, u32[]{:S(2)}, u32[]{:S(2)}) collective-permute-start(f32[256,256]{1,0:T(8,128)S(1)} %bitcast.10), channel_id=1, source_target_pairs={{0,8},{4,12},{8,0},{12,4},{1,9},{5,13},{9,1},{13,5},{2,10},{6,14},... | collective-permute-start | bytes 786440 | tf_op jit(solution)/shard_map/ppermute | solution.py:360
  15.9 1.1 %shard_map.55 = f32[16,16,512]{2,1,0:T(8,128)S(1)} custom-call(f32[16,16,4096]{2,1,0:T(8,128)} %x_ref.13), custom_call_target="tpu_custom_call" | custom-call | flops 1 | bytes 1 | tf_op jit(solution)/shard_map/pallas_call | solution.py:82
  17.0 1.0 %shard_map.63 = f32[16,16,256]{2,1,0:T(8,128)S(1)} custom-call(f32[16,16,4096]{2,1,0:T(8,128)} %x_ref.13), custom_call_target="tpu_custom_call" | custom-call | flops 1 | bytes 1 | tf_op jit(solution)/shard_map/pallas_call | solution.py:82
  18.0 0.6 shard_map.56.refs_0_
  18.6 0.4 collective-permute-start.5
  19.0 0.4 shard_map.57.refs_0_
  19.4 21.9 %collective-permute-done.3.x_ref = f32[256,256]{1,0:T(8,128)S(1)} collective-permute-done((f32[256,256]{1,0:T(8,128)S(1)}, f32[256,256]{1,0:T(8,128)S(1)}, u32[]{:S(2)}, u32[]{:S(2)}) %collective-permute-start.3) | collective-permute-done | bytes 262176 | tf_op jit(solution)/shard_map/ppermute | solution.py:360
  41.3 0.4 shard_map.58.refs_0_
  41.7 0.4 shard_map.59.refs_0_
  42.1 0.4 shard_map.60.refs_0_
  42.5 4.4 %collective-permute-done.x_ref = f32[256,256]{1,0:T(8,128)S(1)} collective-permute-done((f32[256,256]{1,0:T(8,128)S(1)}, f32[256,256]{1,0:T(8,128)S(1)}, u32[]{:S(2)}, u32[]{:S(2)}) %collective-permute-start) | collective-permute-done | bytes 262176 | tf_op jit(solution)/shard_map/ppermute | solution.py:360
  46.9 0.4 shard_map.61.sum_ref
  47.3 0.5 shard_map.62
  47.8 0.1 collective-permute-start.6
  47.9 0.5 collective-permute-start.7
  48.4 0.1 collective-permute-start.8
  48.5 1.3 %collective-permute-done.8.refs_1_ = f32[16,128]{1,0:T(8,128)S(1)} collective-permute-done((f32[16,128]{1,0:T(8,128)S(1)}, f32[16,128]{1,0:T(8,128)S(1)}, u32[]{:S(2)}, u32[]{:S(2)}) %collective-permute-start.8) | collective-permute-done | bytes 8224 | tf_op jit(solution)/shard_map/ppermute | solution.py:360
  49.8 0.1 collective-permute-start.9
  50.0 0.8 %shard_map.64 = (bf16[256,512]{1,0:T(8,128)(2,1)S(1)}, bf16[256,512]{1,0:T(8,128)(2,1)S(1)}, bf16[256,256]{1,0:T(8,128)(2,1)S(1)}, bf16[256,256]{1,0:T(8,128)(2,1)S(1)}, f32[16,128]{1,0:T(8,128)S(1)}) custom-call(bf16[4,512,768]{2,1,0:T(8,128)(2,1)S(1)} %copy-done, f32[256,256]{1,0:T(8,128)S(1)} %get-tuple-element.20.sum_ref, ...), custom_call_target="tpu_custom_call" | custom-call | flops 1 | bytes 1 | tf_op jit(solution)/shard_map/pallas_call | solution.py:208
  50.8 0.6 collective-permute-done.9.x_ref
  51.4 0.7 %shard_map.65 = (bf16[256,256]{1,0:T(8,128)(2,1)S(1)}, bf16[256,256]{1,0:T(8,128)(2,1)S(1)}, f32[8,16,128]{2,1,0:T(8,128)S(1)}) custom-call(bf16[4,512,768]{2,1,0:T(8,128)(2,1)S(1)} %copy-done, f32[256,256]{1,0:T(8,128)S(1)} %collective-permute-done.7.sum_ref, f32[256,256]{1,0:T(8,128)S(1)} %collective-permute-done.9.x_ref, f32[1,1024]{1,0:T(1,128)S(1)} %bitcast.17, ...), custom_call_target="tpu_custom_call" | custom-call | flops 1 | bytes 1 | tf_op jit(solution)/shard_map/pallas_call | solution.py:208
  52.1 9.8 %all_to_all.5.grams_ref = f32[8,16,128]{2,1,0:T(8,128)S(1)} all-to-all(f32[8,16,128]{2,1,0:T(8,128)S(1)} %get-tuple-element.37), channel_id=1, replica_groups={{14,12,10,8,6,4,2,0},{15,13,11,9,7,5,3,1},{30,28,26,24,22,20,18,16},{31..., dimensions={0} | all-to-all | bytes 131072 | tf_op jit(solution)/shard_map/all_to_all | solution.py:400
  61.9 2.1 %shard_map.66 = (f32[8,2,16,1024]{3,2,1,0:T(8,128)}, f32[2,8,16,16]{3,2,1,0:T(8,128)}) custom-call(bf16[256,512]{1,0:T(8,128)(2,1)S(1)} %get-tuple-element.29.own_high_ref, bf16[256,512]{1,0:T(8,128)(2,1)S(1)} %get-tuple-element.30.own_low_ref, bf16[256,256]{1,0:T(8,128)(2,1)S(1)} %get-tuple-element.31.first_high_ref, ...), custom_call_target="tpu_custom_call" | custom-call | tf_op jit(solution)/shard_map/pallas_call | solution.py:349
  (10 shorter events, 0.0 us)
Async XLA Ops:
  1.6 17.0 %collective-permute-start.4 = (f32[256,256]{1,0:T(8,128)S(1)}, f32[256,256]{1,0:T(8,128)S(1)}, u32[]{:S(2)}, u32[]{:S(2)}) collective-permute-start(f32[256,256]{1,0:T(8,128)S(1)} %bitcast.14), channel_id=1, source_target_pairs={{0,12},{4,8},{8,4},{12,0},{1,13},{5,9},{9,5},{13,1},{2,14},{6,10},... | collective-permute-start | bytes 786440 | tf_op jit(solution)/shard_map/ppermute | solution.py:360
  7.7 33.6 %collective-permute-start.3 = (f32[256,256]{1,0:T(8,128)S(1)}, f32[256,256]{1,0:T(8,128)S(1)}, u32[]{:S(2)}, u32[]{:S(2)}) collective-permute-start(f32[256,256]{1,0:T(8,128)S(1)} %bitcast.13), channel_id=1, source_target_pairs={{0,8},{4,12},{8,0},{12,4},{1,9},{5,13},{9,1},{13,5},{2,10},{6,14},... | collective-permute-start | bytes 786440 | tf_op jit(solution)/shard_map/ppermute | solution.py:360
  8.8 32.9 %collective-permute-start.2 = (f32[256,256]{1,0:T(8,128)S(1)}, f32[256,256]{1,0:T(8,128)S(1)}, u32[]{:S(2)}, u32[]{:S(2)}) collective-permute-start(f32[256,256]{1,0:T(8,128)S(1)} %bitcast.12), channel_id=1, source_target_pairs={{0,4},{4,0},{8,12},{12,8},{1,5},{5,1},{9,13},{13,9},{2,6},{6,2},{1... | collective-permute-start | bytes 786440 | tf_op jit(solution)/shard_map/ppermute | solution.py:360
  10.4 31.7 %collective-permute-start.1 = (f32[256,256]{1,0:T(8,128)S(1)}, f32[256,256]{1,0:T(8,128)S(1)}, u32[]{:S(2)}, u32[]{:S(2)}) collective-permute-start(f32[256,256]{1,0:T(8,128)S(1)} %bitcast.11), channel_id=1, source_target_pairs={{0,4},{4,0},{8,12},{12,8},{1,5},{5,1},{9,13},{13,9},{2,6},{6,2},{1... | collective-permute-start | bytes 786440 | tf_op jit(solution)/shard_map/ppermute | solution.py:360
  12.9 5.1 %copy-start = (bf16[4,512,768]{2,1,0:T(8,128)(2,1)S(1)}, bf16[4,512,768]{2,1,0:T(8,128)(2,1)}, u32[]{:S(2)}) copy-start(bf16[4,512,768]{2,1,0:T(8,128)(2,1)} %constant.2.clone.t_ref) | copy-start | bytes 9437188
  12.9 34.0 %collective-permute-start = (f32[256,256]{1,0:T(8,128)S(1)}, f32[256,256]{1,0:T(8,128)S(1)}, u32[]{:S(2)}, u32[]{:S(2)}) collective-permute-start(f32[256,256]{1,0:T(8,128)S(1)} %bitcast.10), channel_id=1, source_target_pairs={{0,8},{4,12},{8,0},{12,4},{1,9},{5,13},{9,1},{13,5},{2,10},{6,14},... | collective-permute-start | bytes 786440 | tf_op jit(solution)/shard_map/ppermute | solution.py:360
  18.6 29.9 %collective-permute-start.5 = (f32[256,256]{1,0:T(8,128)S(1)}, f32[256,256]{1,0:T(8,128)S(1)}, u32[]{:S(2)}, u32[]{:S(2)}) collective-permute-start(f32[256,256]{1,0:T(8,128)S(1)} %bitcast.9), channel_id=1, source_target_pairs={{0,12},{4,8},{8,4},{12,0},{1,13},{5,9},{9,5},{13,1},{2,14},{6,10},... | collective-permute-start | bytes 786440 | tf_op jit(solution)/shard_map/ppermute | solution.py:360
  42.1 5.2 %copy-start.1 = (f32[1024]{0:T(1024)S(1)}, f32[1024]{0:T(1024)}, u32[]{:S(2)}) copy-start(f32[1024]{0:T(1024)} %param.4) | copy-start | bytes 12292
  47.8 2.0 %collective-permute-start.6 = (f32[256,256]{1,0:T(8,128)S(1)}, f32[256,256]{1,0:T(8,128)S(1)}, u32[]{:S(2)}, u32[]{:S(2)}) collective-permute-start(f32[256,256]{1,0:T(8,128)S(1)} %get-tuple-element.21), channel_id=1, source_target_pairs={{0,1},{1,0},{2,3},{3,2},{4,5},{5,4},{6,7},{7,6},{8,9},{9,8},{10,11... | collective-permute-start | bytes 786440 | tf_op jit(solution)/shard_map/ppermute | solution.py:360
  47.9 1.9 %collective-permute-start.7 = (f32[256,256]{1,0:T(8,128)S(1)}, f32[256,256]{1,0:T(8,128)S(1)}, u32[]{:S(2)}, u32[]{:S(2)}) collective-permute-start(f32[256,256]{1,0:T(8,128)S(1)} %get-tuple-element.22), channel_id=1, source_target_pairs={{0,1},{1,0},{2,3},{3,2},{4,5},{5,4},{6,7},{7,6},{8,9},{9,8},{10,11... | collective-permute-start | bytes 786440 | tf_op jit(solution)/shard_map/ppermute | solution.py:360
  48.4 1.4 %collective-permute-start.8 = (f32[16,128]{1,0:T(8,128)S(1)}, f32[16,128]{1,0:T(8,128)S(1)}, u32[]{:S(2)}, u32[]{:S(2)}) collective-permute-start(f32[16,128]{1,0:T(8,128)S(1)} %get-tuple-element.23), channel_id=1, source_target_pairs={{0,1},{1,0},{2,3},{3,2},{4,5},{5,4},{6,7},{7,6},{8,9},{9,8},{10,11... | collective-permute-start | bytes 24584 | tf_op jit(solution)/shard_map/ppermute | solution.py:360
  49.8 1.5 %collective-permute-start.9 = (f32[256,256]{1,0:T(8,128)S(1)}, f32[256,256]{1,0:T(8,128)S(1)}, u32[]{:S(2)}, u32[]{:S(2)}) collective-permute-start(f32[256,256]{1,0:T(8,128)S(1)} %collective-permute-done.5.x_ref), channel_id=1, source_target_pairs={{0,1},{1,0},{2,3},{3,2},{4,5},{5,4},{6,7},{7,6},{8,9},{9,8},{10,11... | collective-permute-start | bytes 786440 | tf_op jit(solution)/shard_map/ppermute | solution.py:360
